TPU v7x, 32 devices: a whole 2x2x4 slice. The times are simulated.
32 devices in a mesh: dp: 2 (over core), ctx: 16 (over z, y, x).
Axes of the slice: x: 2, y: 2, z: 4, core: 2. Of those that a mesh axis runs over, the one named last changes fastest.
Arguments:
- state_x: bfloat16 [2, 4096, 512], P('dp', 'ctx'), may hold values from -6 to 6
- state_y: bfloat16 [2, 4096, 512], P('dp', 'ctx'), may hold values from -6 to 6
- teacher: bfloat16 [2, 4096, 512], P('dp', 'ctx'), may hold values from -6 to 6
- segment_ids: int32 [2, 4096], P('dp'), may hold values from 0 to 7, never falling along the last dimension, each value on 1 to 2048 neighbouring positions
- valid_mask: int32 [2, 4096], P('dp', 'ctx'), may hold values from 0 to 1, as said below
- w_query: bfloat16 [512, 512], P('dp'), may hold values from -0.25 to 0.25
- w_key: bfloat16 [512, 512], P('dp'), may hold values from -0.25 to 0.25
- w_value: bfloat16 [512, 512], P('dp'), may hold values from -0.25 to 0.25
- w_out: bfloat16 [512, 512], P('dp'), may hold values from -1 to 1
- w_up: bfloat16 [512, 2048], P('dp'), may hold values from -0.25 to 0.25
- w_down: bfloat16 [2048, 512], P('dp'), may hold values from -0.1875 to 0.1875
- gain_attn: bfloat16 [512], P('dp'), may hold values from 0.099609375 to 1.8984375
- gain_ffn: bfloat16 [512], P('dp'), may hold values from 0.099609375 to 1.8984375
- gain_final: bfloat16 [512], P('dp'), may hold values from 0.099609375 to 1.8984375
Outputs:
- loss: float32 [], replicated
- output: bfloat16 [2, 4096, 512], P('dp', 'ctx')
- grad_x: float32 [2, 4096, 512], P('dp', 'ctx')
- grad_y: float32 [2, 4096, 512], P('dp', 'ctx')
- grad_w_query: float32 [512, 512], P(('dp', 'ctx'))
- grad_w_key: float32 [512, 512], P(('dp', 'ctx'))
- grad_w_value: float32 [512, 512], P(('dp', 'ctx'))
- grad_w_out: float32 [512, 512], P(('dp', 'ctx'))
- grad_w_up: float32 [512, 2048], P(('dp', 'ctx'))
- grad_w_down: float32 [2048, 512], P(('dp', 'ctx'))
- grad_gain_attn: float32 [512], P(('dp', 'ctx'))
- grad_gain_ffn: float32 [512], P(('dp', 'ctx'))
- grad_gain_final: float32 [512], P(('dp', 'ctx'))
Inputs may be any that keep to these rules, and one draw needn't show every extreme that they name: `segment_ids`: segment numbers never fall along a sequence; each document has 1 to 2048 tokens and every sequence has one of exactly 2048. `valid_mask`: the last token of every sequence is valid.
All inputs are finite; a program needn't handle non-finite values.
Results may differ from a plain program's by a relative error of at most 0.014.
The roundings to bfloat16 on the way count: a program that leaves them out, or rounds other values in their place, can miss the bound.
Values may be sent and summed in bfloat16 or wider, within the bound.
No kernel may reach another device: no remote copies, remote signals or barrier semaphores. Data moves between devices by JAX's collectives and lax.ppermute only.
A program may use at most 128 MiB of HBM per device.

v0:
```python
import math

import jax
import jax.numpy as jnp
from jax import lax
from jax.sharding import PartitionSpec as P

HEADS = 8


EPSILON = 1e-05
NEGATIVE = -1e30


def passed_along(block, axis, distance):
    devices = range(lax.axis_size(axis))
    route = [((i - distance) % len(devices), i) for i in devices]
    return lax.ppermute(block, axis, route)


def layer_norm(inputs, gain_row):
    centre = jnp.mean(inputs, axis=-1, keepdims=True)
    centred = inputs - centre
    spread = jnp.mean(centred * centred, axis=-1, keepdims=True)
    return centred * lax.rsqrt(spread + EPSILON) * gain_row


def smooth_gate(values):
    return jax.nn.gelu(values, approximate=True)


def norm_back(inputs, gain_row, upstream):
    centre = jnp.mean(inputs, axis=-1, keepdims=True)
    centred = inputs - centre
    spread = jnp.mean(centred * centred, axis=-1, keepdims=True)
    inverse = lax.rsqrt(spread + EPSILON)
    normed = centred * inverse
    gain_grad = jnp.sum(upstream * normed, axis=0)
    scaled = upstream * gain_row
    mean_grad = jnp.mean(scaled, axis=-1, keepdims=True)
    proj_grad = jnp.mean(scaled * normed, axis=-1, keepdims=True)
    return (inverse * (scaled - mean_grad - normed * proj_grad), gain_grad)


def body(
    state_x,
    state_y,
    teacher,
    segment_ids,
    valid_mask,
    w_query,
    w_key,
    w_value,
    w_out,
    w_up,
    w_down,
    gain_attn,
    gain_ffn,
    gain_final,
):
    seq_count, tok_count, feat_count = state_x.shape
    head_count = HEADS
    head_size = feat_count // head_count
    scaling = head_size ** (-0.5)
    cycle_size = lax.axis_size("ctx")
    my_index = lax.axis_index("ctx")
    offset = my_index * tok_count
    row_count = seq_count * tok_count
    query_weights, key_weights, value_weights, out_weights, attn_gain = (
        lax.all_gather(w_query, "dp", axis=0, tiled=True),
        lax.all_gather(w_key, "dp", axis=0, tiled=True),
        lax.all_gather(w_value, "dp", axis=0, tiled=True),
        lax.all_gather(w_out, "dp", axis=0, tiled=True),
        lax.all_gather(gain_attn, "dp", axis=0, tiled=True),
    )
    gain_first = attn_gain.astype(jnp.float32)
    rows_x = state_x.reshape(row_count, feat_count)
    queries = jnp.dot(rows_x, query_weights, preferred_element_type=jnp.float32).astype(
        jnp.bfloat16
    )
    keys_local = jnp.einsum(
        "std,de->tse", state_x, key_weights, preferred_element_type=jnp.float32
    ).astype(jnp.bfloat16)
    values_local = jnp.einsum(
        "std,de->tse", state_x, value_weights, preferred_element_type=jnp.float32
    ).astype(jnp.bfloat16)
    query_heads = queries.reshape(seq_count, tok_count, head_count, head_size)

    def block_scores(query_block, query_start, key_block, key_start):
        key_rows = key_block.shape[0]
        key_heads = key_block.reshape(key_rows, seq_count, head_count, head_size)
        scores = (
            jnp.einsum(
                "sqhd,kshd->shqk", query_block, key_heads, preferred_element_type=jnp.float32
            )
            * scaling
        )
        query_seg = lax.dynamic_slice_in_dim(segment_ids, query_start, tok_count, 1)
        key_seg = lax.dynamic_slice_in_dim(segment_ids, key_start, key_rows, 1)
        allowed = query_seg[:, :, None] == key_seg[:, None, :]
        return (scores, allowed[:, None, :, :], key_heads)

    stats_start = (
        jnp.full((seq_count, head_count, tok_count), NEGATIVE, jnp.float32),
        jnp.zeros((seq_count, head_count, tok_count), jnp.float32),
    )
    key_piece = lax.all_gather(keys_local, "ctx", axis=0, tiled=True)
    piece_rows = key_piece.shape[0]
    block_rows = math.gcd(piece_rows, tok_count)
    block_count = piece_rows // block_rows
    key_blocks = key_piece.reshape(block_count, block_rows, seq_count, feat_count)

    def absorb(carried_state, block_item):
        key_block, number = block_item
        running, totals = carried_state
        scores, allowed, unused_heads = block_scores(
            query_heads, offset, key_block, number * block_rows
        )
        scores = jnp.where(allowed, scores, NEGATIVE)
        highest = jnp.maximum(running, jnp.max(scores, axis=-1))
        factor = jnp.exp(running - highest)
        weights = jnp.where(allowed, jnp.exp(scores - highest[..., None]), 0.0)
        return ((highest, totals * factor + jnp.sum(weights, axis=-1)), None)

    final_state, unused_out = lax.scan(absorb, stats_start, (key_blocks, jnp.arange(block_count)))
    running, totals = final_state
    log_total = running + jnp.log(totals)
    start_state = jnp.zeros((seq_count, head_count, tok_count, head_size), jnp.float32)
    key_piece = lax.all_gather(keys_local, "ctx", axis=0, tiled=True)
    value_piece = lax.all_gather(values_local, "ctx", axis=0, tiled=True)
    piece_rows = key_piece.shape[0]
    fold_block_rows = math.gcd(piece_rows, tok_count)
    block_count = piece_rows // fold_block_rows
    key_blocks = key_piece.reshape(block_count, fold_block_rows, seq_count, feat_count)
    value_blocks = value_piece.reshape(block_count, fold_block_rows, seq_count, feat_count)

    def absorb(accumulated, block_item):
        key_block, value_block, number = block_item
        scores, allowed, unused_heads = block_scores(
            query_heads, offset, key_block, number * fold_block_rows
        )
        weights = jnp.where(allowed, jnp.exp(scores - log_total[..., None]), 0.0).astype(
            jnp.bfloat16
        )
        value_heads = value_block.reshape(fold_block_rows, seq_count, head_count, head_size)
        mixed_part = jnp.einsum(
            "shqk,kshd->shqd", weights, value_heads, preferred_element_type=jnp.float32
        )
        return (accumulated + mixed_part, None)

    final_state, unused_out = lax.scan(
        absorb, start_state, (key_blocks, value_blocks, jnp.arange(block_count))
    )
    attended_seq = final_state.transpose(0, 2, 1, 3)
    attended_low = attended_seq.reshape(row_count, feat_count).astype(jnp.bfloat16)
    branch_a = jnp.dot(attended_low, out_weights, preferred_element_type=jnp.float32)
    input_rows = rows_x.astype(jnp.float32)
    first_sum = input_rows + branch_a
    normed_one = layer_norm(first_sum, gain_first)
    up_weights, down_weights, ffn_gain, final_gain = (
        lax.all_gather(w_up, "dp", axis=0, tiled=True),
        lax.all_gather(w_down, "dp", axis=0, tiled=True),
        lax.all_gather(gain_ffn, "dp", axis=0, tiled=True),
        lax.all_gather(gain_final, "dp", axis=0, tiled=True),
    )
    gain_second = ffn_gain.astype(jnp.float32)
    gain_third = final_gain.astype(jnp.float32)
    normed_low = normed_one.astype(jnp.bfloat16)
    hidden_pre = jnp.dot(normed_low, up_weights, preferred_element_type=jnp.float32)
    hidden_act, gate_pull = jax.vjp(smooth_gate, hidden_pre)
    hidden_low = hidden_act.astype(jnp.bfloat16)
    branch_f = jnp.dot(hidden_low, down_weights, preferred_element_type=jnp.float32)
    second_sum = normed_one + branch_f
    normed_two = layer_norm(second_sum, gain_second)
    carried = state_y.reshape(row_count, feat_count).astype(jnp.float32) + branch_a + branch_f
    result = normed_two + layer_norm(carried, gain_third)
    target_rows = teacher.reshape(row_count, feat_count).astype(jnp.float32)
    mask_rows = valid_mask.reshape(row_count).astype(jnp.float32)
    differ = result - target_rows
    error_sum = jnp.sum(mask_rows * jnp.sum(differ * differ, axis=-1))
    error_total, valid_total = lax.psum((error_sum, jnp.sum(mask_rows)), ("dp", "ctx"))
    loss_value = error_total / valid_total
    upstream = 2.0 / valid_total * mask_rows[:, None] * differ
    grad_carried, grad_third = norm_back(carried, gain_third, upstream)
    grad_second, grad_gain_two = norm_back(second_sum, gain_second, upstream)
    grad_branch_f = (grad_second + grad_carried).astype(jnp.bfloat16)
    grad_down = jnp.einsum(
        "rf,rd->fd", hidden_low, grad_branch_f, preferred_element_type=jnp.float32
    )
    grad_hidden = jnp.einsum(
        "rd,fd->rf", grad_branch_f, down_weights, preferred_element_type=jnp.float32
    )
    grad_pre = gate_pull(grad_hidden)[0].astype(jnp.bfloat16)
    grad_up = jnp.einsum("rd,rf->df", normed_low, grad_pre, preferred_element_type=jnp.float32)
    grad_normed = grad_second + jnp.einsum(
        "rf,df->rd", grad_pre, up_weights, preferred_element_type=jnp.float32
    )
    ffn_grads = (
        lax.psum_scatter(grad_up, ("dp", "ctx"), scatter_dimension=0, tiled=True),
        lax.psum_scatter(grad_down, ("dp", "ctx"), scatter_dimension=0, tiled=True),
        lax.psum_scatter(grad_gain_two, ("dp", "ctx"), scatter_dimension=0, tiled=True),
        lax.psum_scatter(grad_third, ("dp", "ctx"), scatter_dimension=0, tiled=True),
    )
    grad_first, grad_gain_one = norm_back(first_sum, gain_first, grad_normed)
    grad_branch_a = (grad_first + grad_carried).astype(jnp.bfloat16)
    grad_out_w = jnp.einsum(
        "rd,re->de", attended_low, grad_branch_a, preferred_element_type=jnp.float32
    )
    grad_attended = jnp.einsum(
        "re,de->rd", grad_branch_a, out_weights, preferred_element_type=jnp.float32
    ).astype(jnp.bfloat16)
    grad_heads = grad_attended.reshape(seq_count, tok_count, head_count, head_size)
    deltas = jnp.sum(grad_heads.astype(jnp.float32) * attended_seq, axis=-1).transpose(0, 2, 1)

    def block_back(
        query_block,
        grad_block,
        lse_block,
        delta_block,
        query_start,
        key_block,
        value_block,
        key_start,
    ):
        scores, allowed, key_heads = block_scores(query_block, query_start, key_block, key_start)
        probs = jnp.where(allowed, jnp.exp(scores - lse_block[..., None]), 0.0)
        value_heads = value_block.reshape(key_block.shape[0], seq_count, head_count, head_size)
        grad_value = jnp.einsum(
            "shqk,sqhd->kshd",
            probs.astype(jnp.bfloat16),
            grad_block,
            preferred_element_type=jnp.float32,
        )
        grad_probs = jnp.einsum(
            "sqhd,kshd->shqk", grad_block, value_heads, preferred_element_type=jnp.float32
        )
        grad_scores = (probs * (grad_probs - delta_block[..., None])).astype(jnp.bfloat16)
        grad_query = (
            jnp.einsum(
                "shqk,kshd->sqhd", grad_scores, key_heads, preferred_element_type=jnp.float32
            )
            * scaling
        )
        grad_key = (
            jnp.einsum(
                "shqk,sqhd->kshd", grad_scores, query_block, preferred_element_type=jnp.float32
            )
            * scaling
        )
        return (grad_query, grad_key, grad_value)

    zero_keys = jnp.zeros((tok_count, seq_count, head_count, head_size), jnp.float32)
    zero_queries = jnp.zeros((seq_count, tok_count, head_count, head_size), jnp.float32)

    def pass_grads(grad_pair):
        return (
            passed_along(grad_pair[0].astype(jnp.bfloat16), "ctx", 1).astype(jnp.float32),
            passed_along(grad_pair[1].astype(jnp.bfloat16), "ctx", 1).astype(jnp.float32),
        )

    def turn_keys(turn_index, carry_in):
        key_block, value_block, grad_keys, grad_values, grad_queries = carry_in
        anchor = (my_index - turn_index) % cycle_size
        part_query, part_key, part_value = block_back(
            query_heads,
            grad_heads,
            log_total,
            deltas,
            offset,
            key_block,
            value_block,
            anchor * tok_count,
        )
        grad_keys, grad_values = pass_grads((grad_keys + part_key, grad_values + part_value))
        key_block, value_block = passed_along((key_block, value_block), "ctx", 1)
        return (key_block, value_block, grad_keys, grad_values, grad_queries + part_query)

    key_block, value_block, grad_keys, grad_values, grad_queries = lax.fori_loop(
        0, cycle_size - 1, turn_keys, (keys_local, values_local, zero_keys, zero_keys, zero_queries)
    )
    anchor = (my_index + 1) % cycle_size
    part_query, part_key, part_value = block_back(
        query_heads,
        grad_heads,
        log_total,
        deltas,
        offset,
        key_block,
        value_block,
        anchor * tok_count,
    )
    grad_keys, grad_values = pass_grads((grad_keys + part_key, grad_values + part_value))
    grad_queries = grad_queries + part_query
    grad_q_low = grad_queries.reshape(row_count, feat_count).astype(jnp.bfloat16)
    grad_k_low = grad_keys.reshape(tok_count, seq_count, feat_count).astype(jnp.bfloat16)
    grad_v_low = grad_values.reshape(tok_count, seq_count, feat_count).astype(jnp.bfloat16)
    grad_query_w = jnp.einsum("rd,re->de", rows_x, grad_q_low, preferred_element_type=jnp.float32)
    grad_key_w = jnp.einsum("std,tse->de", state_x, grad_k_low, preferred_element_type=jnp.float32)
    grad_value_w = jnp.einsum(
        "std,tse->de", state_x, grad_v_low, preferred_element_type=jnp.float32
    )
    attn_grads = (
        lax.psum_scatter(grad_query_w, ("dp", "ctx"), scatter_dimension=0, tiled=True),
        lax.psum_scatter(grad_key_w, ("dp", "ctx"), scatter_dimension=0, tiled=True),
        lax.psum_scatter(grad_value_w, ("dp", "ctx"), scatter_dimension=0, tiled=True),
        lax.psum_scatter(grad_out_w, ("dp", "ctx"), scatter_dimension=0, tiled=True),
        lax.psum_scatter(grad_gain_one, ("dp", "ctx"), scatter_dimension=0, tiled=True),
    )
    from_keys = jnp.einsum(
        "tse,de->std", grad_k_low, key_weights, preferred_element_type=jnp.float32
    )
    from_values = jnp.einsum(
        "tse,de->std", grad_v_low, value_weights, preferred_element_type=jnp.float32
    )
    from_queries = jnp.einsum(
        "re,de->rd", grad_q_low, query_weights, preferred_element_type=jnp.float32
    )
    grad_input = (
        grad_first + from_queries + (from_keys + from_values).reshape(row_count, feat_count)
    )
    shape_three = (seq_count, tok_count, feat_count)
    return (
        loss_value,
        result.astype(jnp.bfloat16).reshape(shape_three),
        grad_input.reshape(shape_three),
        grad_carried.reshape(shape_three),
        attn_grads[0],
        attn_grads[1],
        attn_grads[2],
        attn_grads[3],
        ffn_grads[0],
        ffn_grads[1],
        attn_grads[4],
        ffn_grads[2],
        ffn_grads[3],
    )


def solution(mesh):
    return jax.shard_map(
        body,
        mesh=mesh,
        in_specs=(
            P("dp", "ctx", None),
            P("dp", "ctx", None),
            P("dp", "ctx", None),
            P("dp", None),
            P("dp", "ctx"),
            P("dp", None),
            P("dp", None),
            P("dp", None),
            P("dp", None),
            P("dp", None),
            P("dp", None),
            P("dp"),
            P("dp"),
            P("dp"),
        ),
        out_specs=(
            P(),
            P("dp", "ctx", None),
            P("dp", "ctx", None),
            P("dp", "ctx", None),
            P(("dp", "ctx"), None),
            P(("dp", "ctx"), None),
            P(("dp", "ctx"), None),
            P(("dp", "ctx"), None),
            P(("dp", "ctx"), None),
            P(("dp", "ctx"), None),
            P(("dp", "ctx")),
            P(("dp", "ctx")),
            P(("dp", "ctx")),
        ),
        check_vma=False,
    )
```

profile of v0, /device:TPU:0, one launch (start us, length us, event | category | flops | bytes accessed | tf_op | source)
XLA Modules:
  0.0 1519.4 jit_solution(13736004728321700707)
XLA Ops:
  28.8 42.4 %psum.15 = f32[]{:T(128)} all-reduce(f32[]{:T(128)} %convert_reduce_fusion), channel_id=1, replica_groups=mesh['dp'=2,'ctx'=16] {'dp','ctx'}, use_global_device_ids=true, to_apply=%region_16.17 | all-reduce | flops 1 | bytes 8 | tf_op jit(solution)/shard_map/psum | solution.py:181
  72.8 29.7 %all-gather.8.cloned.1.call-done = bf16[4096,1,512]{0,2,1:T(8,128)(2,1)} async-done(((bf16[256,1,512]{0,2,1:T(8,128)(2,1)}), bf16[4096,1,512]{0,2,1:T(8,128)(2,1)}) %all-gather.8.cloned.1.call-update) | async-done | bytes 4194320 | tf_op jit(solution)/shard_map/all_gather | solution.py:129
  107.0 66.0 %while.52 = (s32[]{:T(128)}, f32[1,8,256]{2,1,0:T(8,128)S(1)}, f32[1,8,256]{2,1,0:T(8,128)S(1)}, s32[1,256]{1,0:T(1,128)S(1)}, s32[16]{0:T(128)S(1)}, /*index=5*...) while((s32[]{:T(128)}, f32[1,8,256]{2,1,0:T(8,128)S(1)}, ...), condition=%wide.region_3.4_spmd.clone, body=%wide.region_0.3_spmd.clone.sunk | while | flops 71378952 | bytes 5550282 | solution.py:125
  173.1 17.5 %all-gather.10.cloned.1.call-done = bf16[4096,1,512]{0,2,1:T(8,128)(2,1)} async-done(((bf16[256,1,512]{0,2,1:T(8,128)(2,1)}), bf16[4096,1,512]{0,2,1:T(8,128)(2,1)}) %all-gather.10.cloned.1.call-update) | async-done | bytes 4194320 | tf_op jit(solution)/shard_map/all_gather | solution.py:130
  190.6 4.6 copy.74
  195.2 63.1 %while.53 = (s32[]{:T(128)}, f32[1,8,256,64]{2,3,1,0:T(8,128)S(1)}, s32[1,256]{1,0:T(1,128)S(1)}, s32[16]{0:T(128)S(1)}, s32[1,4096]{1,0:T(1,128)}, /*index=5*/b...) while((s32[]{:T(128)}, f32[1,8,256,64]{2,3,1,0:T(8,128)S(1)}, ...), condition=%wide.region_5.6_spmd.clone, body=%wide.region_4.5_spmd.clone.sunk | while | flops 136642560 | bytes 3027153 | solution.py:151
  272.9 385.7 %while.54 = (s32[]{:T(128)}, bf16[256,1,512]{0,2,1:T(8,128)(2,1)}, bf16[256,1,512]{0,2,1:T(8,128)(2,1)S(1)}, f32[256,1,8,64]{0,3,2,1:T(8,128)S(1)}, f32[256,1,8,...) while((s32[]{:T(128)}, bf16[256,1,512]{0,2,1:T(8,128)(2,1)}, ...), condition=%wide.region_25.26_spmd.clone, body=%wide.region_24.25_spmd.clone.sunk | while | flops 340852736 | bytes 27152984 | solution.py:278
  284.2 14.0 collective-permute-done.2
  314.2 14.7 collective-permute-done.2
  343.3 14.5 collective-permute-done.2
  371.6 14.2 collective-permute-done.2
  398.9 13.9 collective-permute-done.2
  425.3 13.6 collective-permute-done.2
  450.7 13.2 collective-permute-done.2
  475.3 12.7 collective-permute-done.2
  499.2 11.9 collective-permute-done.2
  522.5 11.0 collective-permute-done.2
  545.9 10.2 collective-permute-done.2
  570.4 9.0 collective-permute-done.2
  580.4 4.6 collective-permute-done.3
  595.5 8.0 collective-permute-done.2
  620.6 7.9 collective-permute-done.2
  645.5 8.5 collective-permute-done.2
  669.5 10.4 collective-permute-done.4
  683.6 10.5 collective-permute-done.5
  705.0 37.3 %all-reduce.3 = (f32[]{:T(128)}, f32[512]{0:T(512)S(1)}, f32[512]{0:T(512)S(1)}, f32[512]{0:T(512)S(1)}) all-reduce(f32[]{:T(128)} %multiply_reduce_fusion.13, f32[512]{0:T(512)S(1)} %get-tuple-element.754, f32[512]{0:T(512)S(1)} %get-tuple-element.761, f32[512]{0:T(512)S(1)} %get-tuple-element.750), channel_id=1, replica_groups=mesh['dp'=2,'ctx'=16] {'dp','ctx'}, use_global_device_ids=true, to_apply=%region_14.15 | all-reduce | flops 1537 | bytes 12296 | tf_op jit(solution)/shard_map/psum | solution.py:181
  747.3 55.8 %reduce-scatter.19.cloned.1.call-done = f32[16,512]{1,0:T(8,128)} async-done(((f32[512,512]{1,0:T(8,128)}), f32[16,512]{1,0:T(8,128)}) %reduce-scatter.19.cloned.1.call-update) | async-done | bytes 32784
  803.1 138.7 %reduce-scatter.13.cloned.1.call-done = f32[16,512]{1,0:T(8,128)} async-done(((f32[512,512]{1,0:T(8,128)}), f32[16,512]{1,0:T(8,128)}) %reduce-scatter.13.cloned.1.call-update) | async-done | bytes 32784 | tf_op jit(solution)/shard_map/reduce_scatter | solution.py:306
  941.8 138.7 %reduce-scatter.21.cloned.1.call-done = f32[16,512]{1,0:T(8,128)} async-done(((f32[512,512]{1,0:T(8,128)}), f32[16,512]{1,0:T(8,128)}) %reduce-scatter.21.cloned.1.call-update) | async-done | bytes 32784
  1080.5 138.8 %reduce-scatter.23.cloned.1.call-done = f32[16,512]{1,0:T(8,128)} async-done(((f32[512,512]{1,0:T(8,128)}), f32[16,512]{1,0:T(8,128)}) %reduce-scatter.23.cloned.1.call-update) | async-done | bytes 32784
  1219.3 143.1 %reduce-scatter.15.cloned.1.call-done = f32[16,2048]{1,0:T(8,128)} async-done(((f32[512,2048]{1,0:T(8,128)}), f32[16,2048]{1,0:T(8,128)}) %reduce-scatter.15.cloned.1.call-update) | async-done | bytes 131088 | tf_op jit(solution)/shard_map/reduce_scatter | solution.py:199
  1362.5 149.0 %reduce-scatter.17.cloned.1.call-done = f32[64,512]{1,0:T(8,128)} async-done(((f32[2048,512]{1,0:T(8,128)}), f32[64,512]{1,0:T(8,128)}) %reduce-scatter.17.cloned.1.call-update) | async-done | bytes 131088 | tf_op jit(solution)/shard_map/reduce_scatter | solution.py:200
  (777 shorter events, 378.5 us)
Async XLA Ops:
  7.2 95.3 %all-gather.8.cloned.1.call-start = ((), (), s32[]{:S(2)}) async-start(), calls=%async_computation.6 | async-start | bytes 4456448 | tf_op jit(solution)/shard_map/all_gather | solution.py:129
  12.1 178.5 %all-gather.10.cloned.1.call-start = ((), (), s32[]{:S(2)}) async-start(), calls=%async_computation.7 | async-start | bytes 4456448 | tf_op jit(solution)/shard_map/all_gather | solution.py:130
  15.6 244.2 %all-gather.12.cloned.1.call-start = ((), (), s32[]{:S(2)}) async-start(), calls=%async_computation.8 | async-start | bytes 3145728 | tf_op jit(solution)/shard_map/all_gather | solution.py:161
  16.3 245.8 %all-gather.14.cloned.1.call-start = ((), (), s32[]{:S(2)}) async-start(), calls=%async_computation.9 | async-start | bytes 3145728 | tf_op jit(solution)/shard_map/all_gather | solution.py:162
  16.9 786.2 %reduce-scatter.19.cloned.1.call-start = ((), (), s32[]{:S(2)}) async-start(), calls=%async_computation.13 | async-start | bytes 1081344
  274.0 29.8 %collective-permute-start = (bf16[256,1,512]{0,2,1:T(8,128)(2,1)S(1)}, bf16[256,1,512]{0,2,1:T(8,128)(2,1)}, u32[]{:S(2)}, u32[]{:S(2)}) collective-permute-start(bf16[256,1,512]{0,2,1:T(8,128)(2,1)S(1)} %copy.98), channel_id=1, source_target_pairs={{15,0},{0,1},{1,2},{2,3},{3,4},{4,5},{5,6},{6,7},{7,8},{8,9},{9,10... | collective-permute-start | bytes 786440 | tf_op jit(solution)/shard_map/while/body/eval_jaxpr/ppermute | solution.py:18
  275.5 28.2 %collective-permute-start.1 = (bf16[256,1,512]{0,2,1:T(8,128)(2,1)S(1)}, bf16[256,1,512]{0,2,1:T(8,128)(2,1)S(1)}, u32[]{:S(2)}, u32[]{:S(2)}) collective-permute-start(bf16[256,1,512]{0,2,1:T(8,128)(2,1)S(1)} %copy.99), channel_id=1, source_target_pairs={{15,0},{0,1},{1,2},{2,3},{3,4},{4,5},{5,6},{6,7},{7,8},{8,9},{9,10... | collective-permute-start | bytes 786440 | tf_op jit(solution)/shard_map/while/body/eval_jaxpr/ppermute | solution.py:18
  304.7 28.8 %collective-permute-start = (bf16[256,1,512]{0,2,1:T(8,128)(2,1)S(1)}, bf16[256,1,512]{0,2,1:T(8,128)(2,1)}, u32[]{:S(2)}, u32[]{:S(2)}) collective-permute-start(bf16[256,1,512]{0,2,1:T(8,128)(2,1)S(1)} %copy.98), channel_id=1, source_target_pairs={{15,0},{0,1},{1,2},{2,3},{3,4},{4,5},{5,6},{6,7},{7,8},{8,9},{9,10... | collective-permute-start | bytes 786440 | tf_op jit(solution)/shard_map/while/body/eval_jaxpr/ppermute | solution.py:18
  304.7 28.8 %collective-permute-start.1 = (bf16[256,1,512]{0,2,1:T(8,128)(2,1)S(1)}, bf16[256,1,512]{0,2,1:T(8,128)(2,1)S(1)}, u32[]{:S(2)}, u32[]{:S(2)}) collective-permute-start(bf16[256,1,512]{0,2,1:T(8,128)(2,1)S(1)} %copy.99), channel_id=1, source_target_pairs={{15,0},{0,1},{1,2},{2,3},{3,4},{4,5},{5,6},{6,7},{7,8},{8,9},{9,10... | collective-permute-start | bytes 786440 | tf_op jit(solution)/shard_map/while/body/eval_jaxpr/ppermute | solution.py:18
  334.5 27.9 %collective-permute-start = (bf16[256,1,512]{0,2,1:T(8,128)(2,1)S(1)}, bf16[256,1,512]{0,2,1:T(8,128)(2,1)}, u32[]{:S(2)}, u32[]{:S(2)}) collective-permute-start(bf16[256,1,512]{0,2,1:T(8,128)(2,1)S(1)} %copy.98), channel_id=1, source_target_pairs={{15,0},{0,1},{1,2},{2,3},{3,4},{4,5},{5,6},{6,7},{7,8},{8,9},{9,10... | collective-permute-start | bytes 786440 | tf_op jit(solution)/shard_map/while/body/eval_jaxpr/ppermute | solution.py:18
  334.5 27.9 %collective-permute-start.1 = (bf16[256,1,512]{0,2,1:T(8,128)(2,1)S(1)}, bf16[256,1,512]{0,2,1:T(8,128)(2,1)S(1)}, u32[]{:S(2)}, u32[]{:S(2)}) collective-permute-start(bf16[256,1,512]{0,2,1:T(8,128)(2,1)S(1)} %copy.99), channel_id=1, source_target_pairs={{15,0},{0,1},{1,2},{2,3},{3,4},{4,5},{5,6},{6,7},{7,8},{8,9},{9,10... | collective-permute-start | bytes 786440 | tf_op jit(solution)/shard_map/while/body/eval_jaxpr/ppermute | solution.py:18
  363.4 27.0 %collective-permute-start = (bf16[256,1,512]{0,2,1:T(8,128)(2,1)S(1)}, bf16[256,1,512]{0,2,1:T(8,128)(2,1)}, u32[]{:S(2)}, u32[]{:S(2)}) collective-permute-start(bf16[256,1,512]{0,2,1:T(8,128)(2,1)S(1)} %copy.98), channel_id=1, source_target_pairs={{15,0},{0,1},{1,2},{2,3},{3,4},{4,5},{5,6},{6,7},{7,8},{8,9},{9,10... | collective-permute-start | bytes 786440 | tf_op jit(solution)/shard_map/while/body/eval_jaxpr/ppermute | solution.py:18
  363.4 27.0 %collective-permute-start.1 = (bf16[256,1,512]{0,2,1:T(8,128)(2,1)S(1)}, bf16[256,1,512]{0,2,1:T(8,128)(2,1)S(1)}, u32[]{:S(2)}, u32[]{:S(2)}) collective-permute-start(bf16[256,1,512]{0,2,1:T(8,128)(2,1)S(1)} %copy.99), channel_id=1, source_target_pairs={{15,0},{0,1},{1,2},{2,3},{3,4},{4,5},{5,6},{6,7},{7,8},{8,9},{9,10... | collective-permute-start | bytes 786440 | tf_op jit(solution)/shard_map/while/body/eval_jaxpr/ppermute | solution.py:18
  391.3 26.1 %collective-permute-start = (bf16[256,1,512]{0,2,1:T(8,128)(2,1)S(1)}, bf16[256,1,512]{0,2,1:T(8,128)(2,1)}, u32[]{:S(2)}, u32[]{:S(2)}) collective-permute-start(bf16[256,1,512]{0,2,1:T(8,128)(2,1)S(1)} %copy.98), channel_id=1, source_target_pairs={{15,0},{0,1},{1,2},{2,3},{3,4},{4,5},{5,6},{6,7},{7,8},{8,9},{9,10... | collective-permute-start | bytes 786440 | tf_op jit(solution)/shard_map/while/body/eval_jaxpr/ppermute | solution.py:18
  391.3 26.0 %collective-permute-start.1 = (bf16[256,1,512]{0,2,1:T(8,128)(2,1)S(1)}, bf16[256,1,512]{0,2,1:T(8,128)(2,1)S(1)}, u32[]{:S(2)}, u32[]{:S(2)}) collective-permute-start(bf16[256,1,512]{0,2,1:T(8,128)(2,1)S(1)} %copy.99), channel_id=1, source_target_pairs={{15,0},{0,1},{1,2},{2,3},{3,4},{4,5},{5,6},{6,7},{7,8},{8,9},{9,10... | collective-permute-start | bytes 786440 | tf_op jit(solution)/shard_map/while/body/eval_jaxpr/ppermute | solution.py:18
  418.3 25.1 %collective-permute-start = (bf16[256,1,512]{0,2,1:T(8,128)(2,1)S(1)}, bf16[256,1,512]{0,2,1:T(8,128)(2,1)}, u32[]{:S(2)}, u32[]{:S(2)}) collective-permute-start(bf16[256,1,512]{0,2,1:T(8,128)(2,1)S(1)} %copy.98), channel_id=1, source_target_pairs={{15,0},{0,1},{1,2},{2,3},{3,4},{4,5},{5,6},{6,7},{7,8},{8,9},{9,10... | collective-permute-start | bytes 786440 | tf_op jit(solution)/shard_map/while/body/eval_jaxpr/ppermute | solution.py:18
  418.4 25.1 %collective-permute-start.1 = (bf16[256,1,512]{0,2,1:T(8,128)(2,1)S(1)}, bf16[256,1,512]{0,2,1:T(8,128)(2,1)S(1)}, u32[]{:S(2)}, u32[]{:S(2)}) collective-permute-start(bf16[256,1,512]{0,2,1:T(8,128)(2,1)S(1)} %copy.99), channel_id=1, source_target_pairs={{15,0},{0,1},{1,2},{2,3},{3,4},{4,5},{5,6},{6,7},{7,8},{8,9},{9,10... | collective-permute-start | bytes 786440 | tf_op jit(solution)/shard_map/while/body/eval_jaxpr/ppermute | solution.py:18
  444.4 24.1 %collective-permute-start = (bf16[256,1,512]{0,2,1:T(8,128)(2,1)S(1)}, bf16[256,1,512]{0,2,1:T(8,128)(2,1)}, u32[]{:S(2)}, u32[]{:S(2)}) collective-permute-start(bf16[256,1,512]{0,2,1:T(8,128)(2,1)S(1)} %copy.98), channel_id=1, source_target_pairs={{15,0},{0,1},{1,2},{2,3},{3,4},{4,5},{5,6},{6,7},{7,8},{8,9},{9,10... | collective-permute-start | bytes 786440 | tf_op jit(solution)/shard_map/while/body/eval_jaxpr/ppermute | solution.py:18
  444.5 24.1 %collective-permute-start.1 = (bf16[256,1,512]{0,2,1:T(8,128)(2,1)S(1)}, bf16[256,1,512]{0,2,1:T(8,128)(2,1)S(1)}, u32[]{:S(2)}, u32[]{:S(2)}) collective-permute-start(bf16[256,1,512]{0,2,1:T(8,128)(2,1)S(1)} %copy.99), channel_id=1, source_target_pairs={{15,0},{0,1},{1,2},{2,3},{3,4},{4,5},{5,6},{6,7},{7,8},{8,9},{9,10... | collective-permute-start | bytes 786440 | tf_op jit(solution)/shard_map/while/body/eval_jaxpr/ppermute | solution.py:18
  469.5 23.1 %collective-permute-start = (bf16[256,1,512]{0,2,1:T(8,128)(2,1)S(1)}, bf16[256,1,512]{0,2,1:T(8,128)(2,1)}, u32[]{:S(2)}, u32[]{:S(2)}) collective-permute-start(bf16[256,1,512]{0,2,1:T(8,128)(2,1)S(1)} %copy.98), channel_id=1, source_target_pairs={{15,0},{0,1},{1,2},{2,3},{3,4},{4,5},{5,6},{6,7},{7,8},{8,9},{9,10... | collective-permute-start | bytes 786440 | tf_op jit(solution)/shard_map/while/body/eval_jaxpr/ppermute | solution.py:18
  469.5 23.1 %collective-permute-start.1 = (bf16[256,1,512]{0,2,1:T(8,128)(2,1)S(1)}, bf16[256,1,512]{0,2,1:T(8,128)(2,1)S(1)}, u32[]{:S(2)}, u32[]{:S(2)}) collective-permute-start(bf16[256,1,512]{0,2,1:T(8,128)(2,1)S(1)} %copy.99), channel_id=1, source_target_pairs={{15,0},{0,1},{1,2},{2,3},{3,4},{4,5},{5,6},{6,7},{7,8},{8,9},{9,10... | collective-permute-start | bytes 786440 | tf_op jit(solution)/shard_map/while/body/eval_jaxpr/ppermute | solution.py:18
  563.5 23.3 %collective-permute-start = (bf16[256,1,512]{0,2,1:T(8,128)(2,1)S(1)}, bf16[256,1,512]{0,2,1:T(8,128)(2,1)}, u32[]{:S(2)}, u32[]{:S(2)}) collective-permute-start(bf16[256,1,512]{0,2,1:T(8,128)(2,1)S(1)} %copy.98), channel_id=1, source_target_pairs={{15,0},{0,1},{1,2},{2,3},{3,4},{4,5},{5,6},{6,7},{7,8},{8,9},{9,10... | collective-permute-start | bytes 786440 | tf_op jit(solution)/shard_map/while/body/eval_jaxpr/ppermute | solution.py:18
  563.6 23.3 %collective-permute-start.1 = (bf16[256,1,512]{0,2,1:T(8,128)(2,1)S(1)}, bf16[256,1,512]{0,2,1:T(8,128)(2,1)S(1)}, u32[]{:S(2)}, u32[]{:S(2)}) collective-permute-start(bf16[256,1,512]{0,2,1:T(8,128)(2,1)S(1)} %copy.99), channel_id=1, source_target_pairs={{15,0},{0,1},{1,2},{2,3},{3,4},{4,5},{5,6},{6,7},{7,8},{8,9},{9,10... | collective-permute-start | bytes 786440 | tf_op jit(solution)/shard_map/while/body/eval_jaxpr/ppermute | solution.py:18
  587.8 23.1 %collective-permute-start = (bf16[256,1,512]{0,2,1:T(8,128)(2,1)S(1)}, bf16[256,1,512]{0,2,1:T(8,128)(2,1)}, u32[]{:S(2)}, u32[]{:S(2)}) collective-permute-start(bf16[256,1,512]{0,2,1:T(8,128)(2,1)S(1)} %copy.98), channel_id=1, source_target_pairs={{15,0},{0,1},{1,2},{2,3},{3,4},{4,5},{5,6},{6,7},{7,8},{8,9},{9,10... | collective-permute-start | bytes 786440 | tf_op jit(solution)/shard_map/while/body/eval_jaxpr/ppermute | solution.py:18
  587.8 23.0 %collective-permute-start.1 = (bf16[256,1,512]{0,2,1:T(8,128)(2,1)S(1)}, bf16[256,1,512]{0,2,1:T(8,128)(2,1)S(1)}, u32[]{:S(2)}, u32[]{:S(2)}) collective-permute-start(bf16[256,1,512]{0,2,1:T(8,128)(2,1)S(1)} %copy.99), channel_id=1, source_target_pairs={{15,0},{0,1},{1,2},{2,3},{3,4},{4,5},{5,6},{6,7},{7,8},{8,9},{9,10... | collective-permute-start | bytes 786440 | tf_op jit(solution)/shard_map/while/body/eval_jaxpr/ppermute | solution.py:18
  635.1 23.5 %collective-permute-start = (bf16[256,1,512]{0,2,1:T(8,128)(2,1)S(1)}, bf16[256,1,512]{0,2,1:T(8,128)(2,1)}, u32[]{:S(2)}, u32[]{:S(2)}) collective-permute-start(bf16[256,1,512]{0,2,1:T(8,128)(2,1)S(1)} %copy.98), channel_id=1, source_target_pairs={{15,0},{0,1},{1,2},{2,3},{3,4},{4,5},{5,6},{6,7},{7,8},{8,9},{9,10... | collective-permute-start | bytes 786440 | tf_op jit(solution)/shard_map/while/body/eval_jaxpr/ppermute | solution.py:18
  635.1 23.4 %collective-permute-start.1 = (bf16[256,1,512]{0,2,1:T(8,128)(2,1)S(1)}, bf16[256,1,512]{0,2,1:T(8,128)(2,1)S(1)}, u32[]{:S(2)}, u32[]{:S(2)}) collective-permute-start(bf16[256,1,512]{0,2,1:T(8,128)(2,1)S(1)} %copy.99), channel_id=1, source_target_pairs={{15,0},{0,1},{1,2},{2,3},{3,4},{4,5},{5,6},{6,7},{7,8},{8,9},{9,10... | collective-permute-start | bytes 786440 | tf_op jit(solution)/shard_map/while/body/eval_jaxpr/ppermute | solution.py:18
  667.7 274.1 %reduce-scatter.13.cloned.1.call-start = ((), (), s32[]{:S(2)}) async-start(), calls=%async_computation.10 | async-start | bytes 1081344 | tf_op jit(solution)/shard_map/reduce_scatter | solution.py:306
  669.1 411.5 %reduce-scatter.21.cloned.1.call-start = ((), (), s32[]{:S(2)}) async-start(), calls=%async_computation.14 | async-start | bytes 1081344
  681.5 537.8 %reduce-scatter.23.cloned.1.call-start = ((), (), s32[]{:S(2)}) async-start(), calls=%async_computation.15 | async-start | bytes 1081344
  695.7 666.8 %reduce-scatter.15.cloned.1.call-start = ((), (), s32[]{:S(2)}) async-start(), calls=%async_computation.11 | async-start | bytes 4325376 | tf_op jit(solution)/shard_map/reduce_scatter | solution.py:199
  699.8 811.6 %reduce-scatter.17.cloned.1.call-start = ((), (), s32[]{:S(2)}) async-start(), calls=%async_computation.12 | async-start | bytes 4325376 | tf_op jit(solution)/shard_map/reduce_scatter | solution.py:200
  (130 other events, 1259.1 us)
Sparse Core Ops, SparseCore 0:
  12.2 90.2 all-gather.7
  105.2 85.3 all-gather.9
  192.1 8.7 all-gather.11
  202.4 11.7 all-gather.13
  667.8 135.2 reduce-scatter.18
  805.9 135.8 reduce-scatter.12
  944.6 135.8 reduce-scatter.20
  1083.4 135.8 reduce-scatter.22
  1222.2 140.2 reduce-scatter.14
  1365.2 146.2 reduce-scatter.16
where the time goes:
time: 1520 us
  waiting for transfers between devices  1050 us (69%)
  local copies, waits for them, and re-layouts  133 us (9%)
  matrix products  111 us (7%)
  blocking collectives  94.5 us (6%)
  other arithmetic  59.1 us (4%)
  starting transfers between devices  30.7 us (2%)
  loops' own time  24.3 us (2%)
  between operations  18.1 us (1%)
    unnamed x13, waiting for transfers between devices  335 us
    ppermute x62, waiting for transfers between devices, passed_along(): return lax.ppermute(block, axis, route)  236 us
    reduce_scatter x1, waiting for transfers between devices, body(): lax.psum_scatter(grad_down, ('dp', 'ctx'), scatter_dimension=0, tiled=True)  149 us
    reduce_scatter x1, waiting for transfers between devices, body(): lax.psum_scatter(grad_up, ('dp', 'ctx'), scatter_dimension=0, tiled=True)  143 us
    reduce_scatter x1, waiting for transfers between devices, body(): lax.psum_scatter(grad_out_w, ('dp', 'ctx'), scatter_dimension=0, tiled=True)  139 us
    psum x2, blocking collectives, body(): lax.psum((error_sum, jnp.sum(mask_rows)), ('dp', 'ctx'))  79.7 us
    dynamic_slice x64, local copies, waits for them, and re-layouts, body(): lax.scan(absorb, stats_start, (key_blocks, jnp.arange(block_count)))  51.6 us
    dynamic_slice x48, local copies, waits for them, and re-layouts, block_scores(): key_seg = lax.dynamic_slice_in_dim(segment_ids, key_start, key_rows, 1)  32.9 us
  transfers between devices with their start and end apart: 72, of which 40 were waited for; matrix products, arithmetic and copies ran while one was open for 17% of the time, Pallas kernels for 0%

commit v1 on v0

v1 whole, which is shorter than its diff:
```python
import functools

import jax
import jax.numpy as jnp
from jax import lax
from jax.experimental import pallas as pl
from jax.experimental.pallas import tpu as pltpu
from jax.sharding import PartitionSpec as P

HEADS = 8
EPS = 1e-05
SLOTS = 32
FAR = -(2.0**100)
CORE = 0.7978845608028654
CUBE = 0.044715
MIB = 1024 * 1024

BF16 = jnp.bfloat16
F32 = jnp.float32


def dot(left, right):
    return jnp.dot(left, right, preferred_element_type=F32)


def dot_t(left, right):
    return lax.dot_general(left, right, (((1,), (1,)), ((), ())), preferred_element_type=F32)


def vmem(count):
    return [pl.BlockSpec(memory_space=pltpu.VMEM) for _ in range(count)]


def smem():
    return pl.BlockSpec(memory_space=pltpu.SMEM)


def shaped(shape, dtype):
    return jax.ShapeDtypeStruct(shape, dtype)


def swap(block, axis, bit):
    size = lax.axis_size(axis)
    return lax.ppermute(block, axis, [(i, i ^ bit) for i in range(size)])


def project_kernel(x_ref, wq_ref, wk_ref, wv_ref, q_ref, kv_ref):
    x = x_ref[...]
    size = q_ref.shape[1]
    for w_ref, out_ref, base, scale in (
        (wk_ref, kv_ref, 0, 1.0),
        (wv_ref, kv_ref, size, 1.0),
        (wq_ref, q_ref, 0, size**-0.5),
    ):
        flat = dot(x, w_ref[...]) * scale
        turned = flat.astype(BF16).T
        for h in range(HEADS):
            out_ref[h, base : base + size, :] = turned[h * size : (h + 1) * size, :]


def project(x, wq, wk, wv):
    tok, feat = x.shape
    size = feat // HEADS
    return pl.pallas_call(
        project_kernel,
        out_shape=(
            shaped((HEADS, size, tok), BF16),
            shaped((HEADS, 2 * size, tok), BF16),
        ),
        in_specs=vmem(4),
        out_specs=tuple(vmem(2)),
        compiler_params=pltpu.CompilerParams(vmem_limit_bytes=24 * MIB),
        name="project",
    )(x, wq, wk, wv)


def onehot(row, hit, miss):
    number = lax.broadcasted_iota(jnp.int32, (SLOTS, row.shape[1]), 0)
    return jnp.where(number == row, hit, miss).astype(BF16)


def key_range(seg_s, chunk, count, tok):
    first = seg_s[chunk * tok]
    last = seg_s[chunk * tok + tok - 1]
    low = jnp.int32(0)
    high = jnp.int32(0)
    for c in range(count):
        low += (seg_s[c * tok + tok - 1] < first).astype(jnp.int32)
        high += (seg_s[c * tok] <= last).astype(jnp.int32)
    return low // 2, (high + 1) // 2


def place(h, slot, ways, rank, tok):
    chunk = h * ways + lax.rem(rank - slot + ways, ways)
    return chunk, chunk // 2, pl.multiple_of(lax.rem(chunk, 2) * tok, tok)


def forward_kernel(ways, ids_ref, seg_s, seg_ref, q_ref, *refs):
    kv_refs = refs[:ways]
    o_ref, of_ref, lse_ref, kx, vt = refs[ways:]
    count, tok = seg_ref.shape
    size = q_ref.shape[1]
    rank = lax.rem(ids_ref[1], ways)
    for slot in range(ways):

        @pl.loop(0, HEADS)
        def fill(h):
            chunk, pair, start = place(h, slot, ways, rank, tok)
            row = seg_ref[pl.ds(chunk, 1), :]
            wide = jnp.concatenate(
                [kv_refs[slot][h, 0:size, :], onehot(row, 1.0, 0.0)], axis=0
            )
            kx[pair, pl.ds(start, tok), :] = wide.T
            vt[pair, :, pl.ds(start, tok)] = kv_refs[slot][h, size : 2 * size, :]

    @pl.loop(0, HEADS)
    def one(i):
        chunk = i * ways + rank
        low, high = key_range(seg_s, chunk, count, tok)
        row = seg_ref[pl.ds(chunk, 1), :]
        qx = jnp.concatenate([q_ref[i], onehot(row, 0.0, FAR)], axis=0)

        def step(p, carry):
            top, total, acc = carry
            s = dot(kx[p], qx)
            new = jnp.maximum(top, jnp.max(s, axis=0, keepdims=True))
            fade = jnp.exp(top - new)
            w = jnp.exp(s - new)
            total = total * fade + jnp.sum(w, axis=0, keepdims=True)
            acc = acc * fade + dot(vt[p], w.astype(BF16))
            return new, total, acc

        top, total, acc = lax.fori_loop(
            low,
            high,
            step,
            (
                jnp.full((1, tok), -3e38, F32),
                jnp.zeros((1, tok), F32),
                jnp.zeros((size, tok), F32),
            ),
        )
        out = acc / total
        of_ref[i] = out
        o_ref[i] = out.astype(BF16)
        lse_ref[pl.ds(i, 1), :] = top + jnp.log(total)


def attend(ids, seg, seg2, q, kvs):
    ways = len(kvs)
    _, size, tok = q.shape
    count = seg2.shape[0]
    return pl.pallas_call(
        functools.partial(forward_kernel, ways),
        out_shape=(
            shaped((HEADS, size, tok), BF16),
            shaped((HEADS, size, tok), F32),
            shaped((HEADS, tok), F32),
        ),
        in_specs=[smem(), smem()] + vmem(2 + ways),
        out_specs=tuple(vmem(3)),
        scratch_shapes=[
            pltpu.VMEM((count // 2, 2 * tok, size + SLOTS), BF16),
            pltpu.VMEM((count // 2, size, 2 * tok), BF16),
        ],
        compiler_params=pltpu.CompilerParams(vmem_limit_bytes=32 * MIB),
        name="attend",
    )(ids, seg, seg2, q, *kvs)


def backward_kernel(ways, ids_ref, seg_s, seg_ref, q_ref, do_ref, of_ref, lse_ref, *refs):
    kv_refs = refs[:ways]
    dq_ref = refs[ways]
    dkv_refs = refs[ways + 1 : 2 * ways + 1]
    kx, vx, kt, dk, dv = refs[2 * ways + 1 :]
    count, tok = seg_ref.shape
    size = q_ref.shape[1]
    rank = lax.rem(ids_ref[1], ways)
    for slot in range(ways):

        @pl.loop(0, HEADS)
        def fill(h):
            chunk, pair, start = place(h, slot, ways, rank, tok)
            row = seg_ref[pl.ds(chunk, 1), :]
            keys = kv_refs[slot][h, 0:size, :]
            kx[pair, pl.ds(start, tok), :] = jnp.concatenate(
                [keys, onehot(row, 1.0, 0.0)], axis=0
            ).T
            kt[pair, :, pl.ds(start, tok)] = keys
            vx[pair, pl.ds(start, tok), :] = kv_refs[slot][h, size : 2 * size, :].T

    dk[...] = jnp.zeros_like(dk)
    dv[...] = jnp.zeros_like(dv)

    @pl.loop(0, HEADS)
    def one(i):
        chunk = i * ways + rank
        low, high = key_range(seg_s, chunk, count, tok)
        row = seg_ref[pl.ds(chunk, 1), :]
        q = q_ref[i]
        qx = jnp.concatenate([q, onehot(row, 0.0, FAR)], axis=0)
        do = do_ref[i]
        delta = jnp.sum(do.astype(F32) * of_ref[i], axis=0, keepdims=True)
        lse = lse_ref[pl.ds(i, 1), :]

        def step(p, dq):
            w = jnp.exp(dot(kx[p], qx) - lse)
            dp = dot(vx[p], do)
            ds = (w * (dp - delta)).astype(BF16)
            dv[p] += dot_t(do, w.astype(BF16))
            dk[p] += dot_t(q, ds)
            return dq + dot(kt[p], ds)

        dq = lax.fori_loop(low, high, step, jnp.zeros((size, tok), F32))
        dq_ref[i] = (dq * size**-0.5).astype(BF16)

    for slot in range(ways):

        @pl.loop(0, HEADS)
        def drain(h):
            _, pair, start = place(h, slot, ways, rank, tok)
            out = dkv_refs[slot]
            out[h, 0:size, :] = dk[pair, :, pl.ds(start, tok)].astype(out.dtype)
            out[h, size : 2 * size, :] = dv[pair, :, pl.ds(start, tok)].astype(out.dtype)


def attend_back(ids, seg, seg2, q, do, of, lse, kvs):
    ways = len(kvs)
    _, size, tok = q.shape
    count = seg2.shape[0]
    return pl.pallas_call(
        functools.partial(backward_kernel, ways),
        out_shape=(shaped((HEADS, size, tok), BF16), shaped((HEADS, 2 * size, tok), F32))
        + (shaped((HEADS, 2 * size, tok), BF16),) * (ways - 1),
        in_specs=[smem(), smem()] + vmem(5 + ways),
        out_specs=tuple(vmem(1 + ways)),
        scratch_shapes=[
            pltpu.VMEM((count // 2, 2 * tok, size + SLOTS), BF16),
            pltpu.VMEM((count // 2, 2 * tok, size), BF16),
            pltpu.VMEM((count // 2, size, 2 * tok), BF16),
            pltpu.VMEM((count // 2, size, 2 * tok), F32),
            pltpu.VMEM((count // 2, size, 2 * tok), F32),
        ],
        compiler_params=pltpu.CompilerParams(vmem_limit_bytes=40 * MIB),
        name="attend_back",
    )(ids, seg, seg2, q, do, of, lse, *kvs)


def normed(rows):
    centred = rows - jnp.mean(rows, axis=-1, keepdims=True)
    spread = jnp.mean(centred * centred, axis=-1, keepdims=True)
    inverse = lax.rsqrt(spread + EPS)
    return centred * inverse, inverse


def norm_back(n, inverse, gain, up):
    scaled = up * gain
    mean_one = jnp.mean(scaled, axis=-1, keepdims=True)
    mean_two = jnp.mean(scaled * n, axis=-1, keepdims=True)
    grad = inverse * (scaled - mean_one - n * mean_two)
    return grad, jnp.sum(up * n, axis=0, keepdims=True)


def middle_kernel(
    tile,
    ot_ref,
    x_ref,
    y_ref,
    t_ref,
    mask_ref,
    gains_ref,
    wo_ref,
    wu_ref,
    wd_ref,
    out_ref,
    gy_ref,
    gr_ref,
    dot_ref,
    x1_ref,
    h_ref,
    df_ref,
    dz_ref,
    da_ref,
    small_ref,
    slope,
    acc,
):
    rows, feat = x_ref.shape
    steps = wu_ref.shape[1] // tile
    gains = gains_ref[...].astype(F32)
    g1, g2, g3 = gains[0:1], gains[1:2], gains[2:3]
    branch = dot(ot_ref[...].T, wo_ref[...])
    n1, r1 = normed(x_ref[...].astype(F32) + branch)
    x1 = n1 * g1
    x1_ref[...] = x1.astype(BF16)
    acc[...] = jnp.zeros_like(acc)

    @pl.loop(0, steps)
    def up(t):
        cols = pl.ds(pl.multiple_of(t * tile, tile), tile)
        z = dot(x1_ref[...], wu_ref[:, cols])
        z2 = z * z
        th = jnp.tanh(CORE * z * (1.0 + CUBE * z2))
        half = 0.5 * (1.0 + th)
        h = (z * half).astype(BF16)
        slope[:, cols] = half + 0.5 * z * (1.0 - th * th) * (CORE * (1.0 + 3.0 * CUBE * z2))
        h_ref[:, cols] = h
        acc[...] += dot(h, wd_ref[cols, :])

    ffn = acc[...]
    n2, r2 = normed(x1 + ffn)
    n3, r3 = normed(y_ref[...].astype(F32) + branch + ffn)
    result = n2 * g2 + n3 * g3
    out_ref[...] = result.astype(BF16)
    mask_row = mask_ref[...].astype(F32)
    mask = jnp.broadcast_to(mask_row, (8, rows)).T[:, 0:1]
    differ = result - t_ref[...].astype(F32)
    error = jnp.sum(mask * differ * differ)
    valid = jnp.sum(mask_row)
    upstream = 2.0 * mask * differ
    gy, dg3 = norm_back(n3, r3, g3, upstream)
    du, dg2 = norm_back(n2, r2, g2, upstream)
    gy_ref[...] = gy
    df_ref[...] = (du + gy).astype(BF16)
    acc[...] = du

    @pl.loop(0, steps)
    def down(t):
        cols = pl.ds(pl.multiple_of(t * tile, tile), tile)
        dz = (dot_t(df_ref[...], wd_ref[cols, :]) * slope[:, cols]).astype(BF16)
        dz_ref[:, cols] = dz
        acc[...] += dot_t(dz, wu_ref[:, cols])

    gr, dg1 = norm_back(n1, r1, g1, acc[...])
    gr_ref[...] = gr
    da = (gr + gy).astype(BF16)
    da_ref[...] = da
    dot_ref[...] = dot_t(wo_ref[...], da).astype(BF16)
    lane = lax.broadcasted_iota(jnp.int32, (1, feat), 1)
    scalars = jnp.where(lane == 0, error, jnp.where(lane == 1, valid, 0.0))
    small_ref[...] = jnp.concatenate(
        [dg1, dg2, dg3, scalars, jnp.zeros((4, feat), F32)], axis=0
    )


def middle(ot, x, y, teacher, mask, gains, wo, wu, wd):
    tok, feat = x.shape
    wide = wu.shape[1]
    return pl.pallas_call(
        functools.partial(middle_kernel, min(512, wide)),
        out_shape=(
            shaped((tok, feat), BF16),
            shaped((tok, feat), F32),
            shaped((tok, feat), F32),
            shaped((feat, tok), BF16),
            shaped((tok, feat), BF16),
            shaped((tok, wide), BF16),
            shaped((tok, feat), BF16),
            shaped((tok, wide), BF16),
            shaped((tok, feat), BF16),
            shaped((8, feat), F32),
        ),
        in_specs=vmem(9),
        out_specs=tuple(vmem(10)),
        scratch_shapes=[pltpu.VMEM((tok, wide), F32), pltpu.VMEM((tok, feat), F32)],
        compiler_params=pltpu.CompilerParams(vmem_limit_bytes=40 * MIB),
        name="middle",
    )(ot, x, y, teacher, mask, gains, wo, wu, wd)


def split_sum(values):
    high = values.astype(BF16)
    low = (values - high.astype(F32)).astype(BF16)
    return jnp.concatenate([high.astype(F32), low.astype(F32)], axis=0).astype(BF16)


def ffn_grad_kernel(
    tile, ids_ref, x1_ref, h_ref, df_ref, dz_ref, ot_ref, da_ref, small_ref, keep_ref, send_ref, xt
):
    feat = x1_ref.shape[1]
    wide = h_ref.shape[1]
    blocks = keep_ref.shape[0]
    half, wide_half = feat // 2, wide // 2
    step = half // blocks
    wide_step = wide_half // blocks
    parts = wide // feat
    xt[...] = x1_ref[...].T
    small = split_sum(small_ref[...])
    for flip, ref in ((1, send_ref), (0, keep_ref)):
        side = ids_ref[0] if flip == 0 else 1 - ids_ref[0]
        rows = pl.ds(pl.multiple_of(side * half, half), half)
        for j in range(parts):
            g = dot(xt[rows, :], dz_ref[:, j * feat : (j + 1) * feat])
            ref[:, j * step : (j + 1) * step, :] = g.astype(BF16).reshape(blocks, step, feat)
        base = parts * step
        each = tile // wide_step
        for j in range(wide_half // tile):
            cols = pl.ds(pl.multiple_of(side * wide_half + j * tile, tile), tile)
            g = dot(h_ref[:, cols].T, df_ref[...])
            ref[j * each : (j + 1) * each, base : base + wide_step, :] = g.astype(
                BF16
            ).reshape(each, wide_step, feat)
        base += wide_step
        g = dot(ot_ref[rows, :], da_ref[...])
        ref[:, base : base + step, :] = g.astype(BF16).reshape(blocks, step, feat)
        base += step
        ref[:, base : base + 16, :] = jnp.broadcast_to(small[None], (blocks, 16, feat))


def ffn_grads(ids, blocks, x1, h, df, dz, ot, da, small):
    tok, feat = x1.shape
    wide = h.shape[1]
    step = feat // (2 * blocks)
    depth = (wide // feat) * step + wide // (2 * blocks) + step + 16
    return pl.pallas_call(
        functools.partial(ffn_grad_kernel, min(512, wide // 2)),
        out_shape=(shaped((blocks, depth, feat), BF16),) * 2,
        in_specs=[smem()] + vmem(7),
        out_specs=tuple(vmem(2)),
        scratch_shapes=[pltpu.VMEM((feat, tok), BF16)],
        compiler_params=pltpu.CompilerParams(vmem_limit_bytes=32 * MIB),
        name="ffn_grads",
    )(ids, x1, h, df, dz, ot, da, small)


def added(one, two):
    depth = one.shape[0]
    main = one[: depth - 16].astype(F32) + two[: depth - 16].astype(F32)
    tail = one[depth - 16 :].astype(F32) + two[depth - 16 :].astype(F32)
    return main, tail[0:8] + tail[8:16]


def halve_kernel(bit, ids_ref, keep_ref, got_ref, next_ref, send_ref):
    mine = lax.rem(ids_ref[1] // bit, 2)
    depth = keep_ref.shape[1]

    @pl.loop(0, next_ref.shape[0])
    def one(b):
        for ref, which in ((send_ref, 1 - mine), (next_ref, mine)):
            at = 2 * b + which
            main, tail = added(keep_ref[at], got_ref[at])
            ref[b, 0 : depth - 16, :] = main.astype(BF16)
            ref[b, depth - 16 : depth, :] = split_sum(tail)


def halve(ids, bit, keep, got):
    blocks, depth, feat = keep.shape
    return pl.pallas_call(
        functools.partial(halve_kernel, bit),
        out_shape=(shaped((blocks // 2, depth, feat), BF16),) * 2,
        in_specs=[smem()] + vmem(2),
        out_specs=tuple(vmem(2)),
        compiler_params=pltpu.CompilerParams(vmem_limit_bytes=24 * MIB),
        name="halve",
    )(ids, keep, got)


def last_kernel(
    ids_ref, back_ref, x_ref, gr_ref, wq_ref, wk_ref, wv_ref, gx_ref, keep_ref, send_ref, xt
):
    feat = x_ref.shape[1]
    blocks = keep_ref.shape[0]
    half = feat // 2
    step = half // blocks
    size = back_ref.shape[1] // 3
    xt[...] = x_ref[...].T
    total = gr_ref[...]
    for j, w_ref in enumerate((wq_ref, wk_ref, wv_ref)):
        grad_t = jnp.concatenate(
            [back_ref[h, j * size : (j + 1) * size, :] for h in range(HEADS)], axis=0
        )
        total = total + dot_t(grad_t.T, w_ref[...])
        for flip, ref in ((1, send_ref), (0, keep_ref)):
            side = ids_ref[0] if flip == 0 else 1 - ids_ref[0]
            rows = pl.ds(pl.multiple_of(side * half, half), half)
            g = dot_t(xt[rows, :], grad_t)
            ref[:, j * step : (j + 1) * step, :] = g.astype(BF16).reshape(blocks, step, feat)
    gx_ref[...] = total


def last(ids, blocks, back, x, gr, wq, wk, wv):
    tok, feat = x.shape
    step = feat // (2 * blocks)
    return pl.pallas_call(
        last_kernel,
        out_shape=(shaped((tok, feat), F32),) + (shaped((blocks, 3 * step, feat), BF16),) * 2,
        in_specs=[smem()] + vmem(6),
        out_specs=tuple(vmem(3)),
        scratch_shapes=[pltpu.VMEM((feat, tok), BF16)],
        compiler_params=pltpu.CompilerParams(vmem_limit_bytes=24 * MIB),
        name="last",
    )(ids, back, x, gr, wq, wk, wv)


def finish_kernel(
    ids_ref,
    keep_ref,
    got_ref,
    pieces_ref,
    gx_in,
    gy_in,
    loss_ref,
    gx_ref,
    gy_ref,
    gq_ref,
    gk_ref,
    gv_ref,
    go_ref,
    gu_ref,
    gd_ref,
    g1_ref,
    g2_ref,
    g3_ref,
):
    step, feat = gq_ref.shape
    wide_step = gd_ref.shape[0]
    parts = gu_ref.shape[1] // feat
    main, small = added(keep_ref[0], got_ref[0])
    inverse = 1.0 / small[3:4, 1:2]
    loss_ref[...] = small[3:4, 0:1] * inverse
    gx_ref[...] = gx_in[...] * inverse
    gy_ref[...] = gy_in[...] * inverse
    main = main * inverse
    for j in range(parts):
        gu_ref[:, j * feat : (j + 1) * feat] = main[j * step : (j + 1) * step]
    base = parts * step
    gd_ref[...] = main[base : base + wide_step]
    base += wide_step
    go_ref[...] = main[base : base + step]
    summed = jnp.sum(pieces_ref[...].astype(F32), axis=0) * inverse
    gq_ref[...] = summed[0:step]
    gk_ref[...] = summed[step : 2 * step]
    gv_ref[...] = summed[2 * step : 3 * step]
    number = ids_ref[0] * pieces_ref.shape[0] + ids_ref[1]
    turned = pltpu.roll(small * inverse, lax.rem(feat - number * step, feat), 1)
    g1_ref[...] = turned[0:1, 0:step]
    g2_ref[...] = turned[1:2, 0:step]
    g3_ref[...] = turned[2:3, 0:step]


def finish(ids, keep, got, pieces, gx, gy, wide):
    tok, feat = gx.shape
    blocks = pieces.shape[0]
    step = feat // (2 * blocks)
    return pl.pallas_call(
        finish_kernel,
        out_shape=(
            shaped((1, 1), F32),
            shaped((tok, feat), F32),
            shaped((tok, feat), F32),
            shaped((step, feat), F32),
            shaped((step, feat), F32),
            shaped((step, feat), F32),
            shaped((step, feat), F32),
            shaped((step, wide), F32),
            shaped((wide // (2 * blocks), feat), F32),
            shaped((1, step), F32),
            shaped((1, step), F32),
            shaped((1, step), F32),
        ),
        in_specs=[smem()] + vmem(5),
        out_specs=tuple(vmem(12)),
        compiler_params=pltpu.CompilerParams(vmem_limit_bytes=24 * MIB),
        name="finish",
    )(ids, keep, got, pieces, gx, gy)


def body(
    state_x,
    state_y,
    teacher,
    segment_ids,
    valid_mask,
    w_query,
    w_key,
    w_value,
    w_out,
    w_up,
    w_down,
    gain_attn,
    gain_ffn,
    gain_final,
):
    _, tok, feat = state_x.shape
    size = feat // HEADS
    ctx = lax.axis_size("ctx")
    sides = lax.axis_size("dp")
    ways = ctx // HEADS
    groups = [[h * ways + r for h in range(HEADS)] for r in range(ways)]
    ids = jnp.stack([lax.axis_index("dp"), lax.axis_index("ctx")]).astype(jnp.int32)
    seg = segment_ids.reshape(-1)
    seg2 = segment_ids.reshape(ctx, tok)
    x = state_x[0]

    def gathered(block):
        return lax.all_gather(block, "dp", axis=0, tiled=True)

    def exchange(block):
        return lax.all_to_all(block, "ctx", 0, 0, axis_index_groups=groups, tiled=True)

    def around(block, distance):
        route = []
        for g in range(HEADS):
            for r in range(ways):
                route.append((g * ways + r, g * ways + (r + distance) % ways))
        return lax.ppermute(block, "ctx", route)

    wq, wk, wv = gathered(w_query), gathered(w_key), gathered(w_value)
    q, kv = project(x, wq, wk, wv)
    kv = exchange(kv)
    kvs = [kv] + [around(kv, j) for j in range(1, ways)]
    q = exchange(q)
    o, of, lse = attend(ids, seg, seg2, q, kvs)
    wo, wu, wd = gathered(w_out), gathered(w_up), gathered(w_down)
    gains = lax.all_gather(
        jnp.stack([gain_attn, gain_ffn, gain_final]), "dp", axis=1, tiled=True
    )
    ot = exchange(o).reshape(feat, tok)
    result, gy, gr, do, x1, h, df, dz, da, small = middle(
        ot, x, state_y[0], teacher[0], valid_mask, gains, wo, wu, wd
    )
    do = exchange(do.reshape(HEADS, size, tok))
    fast = sides == 2 and (feat // (sides * ctx)) % 16 == 0
    if fast:
        keep, send = ffn_grads(ids, ctx, x1, h, df, dz, ot, da, small)
        got = swap(send, "dp", 1)
        bit = 1
        while bit < ctx:
            keep, send = halve(ids, bit, keep, got)
            got = swap(send, "ctx", bit)
            bit *= 2
    dq, own, *others = attend_back(ids, seg, seg2, q, do, of, lse, kvs)
    for j, other in enumerate(others):
        own = own + around(other, -(j + 1)).astype(F32)
    back = exchange(jnp.concatenate([dq, own.astype(BF16)], axis=1))
    wide = wu.shape[1]
    if fast:
        gx, mine, sent = last(ids, ctx, back, x, gr, wq, wk, wv)
        pieces = mine + swap(sent, "dp", 1)
        pieces = lax.all_to_all(pieces, "ctx", 0, 0, tiled=True)
        loss, gx, gy, gq, gk, gv, go, gu, gd, g1, g2, g3 = finish(
            ids, keep, got, pieces, gx, gy, wide
        )
        gains_out = [g.reshape(-1) for g in (g1, g2, g3)]
        loss = loss.reshape(())
    else:
        both = ("dp", "ctx")
        total = lax.psum(small, both)
        inverse = 1.0 / total[3, 1]
        loss = total[3, 0] * inverse

        def scattered(block):
            block = block * inverse
            return lax.psum_scatter(block, both, scatter_dimension=0, tiled=True)

        parts = [back[:, j * size : (j + 1) * size, :].reshape(feat, tok) for j in range(3)]
        gx = gr
        for part, weight in zip(parts, (wq, wk, wv)):
            gx = gx + dot_t(part.T, weight)
        gq, gk, gv = [scattered(dot_t(x.T, part)) for part in parts]
        go = scattered(dot(ot, da))
        gu = scattered(dot(x1.T, dz))
        gd = scattered(dot(h.T, df))
        gx, gy = gx * inverse, gy * inverse
        step = feat // (sides * ctx)
        number = ids[0] * ctx + ids[1]
        gains_out = [
            lax.dynamic_slice_in_dim(total[k] * inverse, number * step, step)
            for k in range(3)
        ]
    return (
        loss,
        result[None],
        gx[None],
        gy[None],
        gq,
        gk,
        gv,
        go,
        gu,
        gd,
        gains_out[0],
        gains_out[1],
        gains_out[2],
    )


def solution(mesh):
    tokens = P("dp", "ctx", None)
    rows = P("dp", None)
    spread = P(("dp", "ctx"), None)
    gain = P(("dp", "ctx"))
    return jax.shard_map(
        body,
        mesh=mesh,
        in_specs=(tokens,) * 3 + (rows, P("dp", "ctx")) + (rows,) * 6 + (P("dp"),) * 3,
        out_specs=(P(), tokens, tokens, tokens) + (spread,) * 6 + (gain,) * 3,
        check_vma=False,
    )
```

time: 1520 us -> 238 us (0.16)
  waiting for transfers between devices: 1050 us -> 74.9 us
  local copies, waits for them, and re-layouts: 133 us -> 12.5 us
  matrix products: 111 us -> 0 us
  other arithmetic: 59.1 us -> 3.12 us
  Pallas kernels: 0 us -> 52.7 us
  blocking collectives: 94.5 us -> 48.1 us
  loops' own time: 24.3 us -> 0 us
    reduce_scatter x3 -> x0, waiting for transfers between devices: 431 us -> none  [the longest x1 149 us: body(): lax.psum_scatter(grad_down, ('dp', 'ctx'), scatter_dimension=0, tiled=True)]
    unnamed x13 -> x2, waiting for transfers between devices: 335 us -> 1.38 us
    ppermute x62 -> x8, waiting for transfers between devices: 236 us -> 50 us  [the longest x6 39.1 us: swap(): return lax.ppermute(block, axis, [(i, i ^ bit) for i in range(size)])]
    dot_general x130 -> x0, matrix products: 111 us -> none  [the longest x32 23.4 us: block_scores(): jnp.einsum('sqhd,kshd->shqk', query_block, key_heads, preferred_element_t...]
    dynamic_slice x112 -> x0, local copies, waits for them, and re-layouts: 84.5 us -> none  [the longest x64 51.6 us: body(): lax.scan(absorb, stats_start, (key_blocks, jnp.arange(block_count)))]
    psum x2 -> x0, blocking collectives: 79.7 us -> none  [body(): lax.psum((error_sum, jnp.sum(mask_rows)), ('dp', 'ctx'))]
    pallas_call x0 -> x11, Pallas kernels: none -> 52.7 us  [the longest x1 16.2 us: attend_back(): pl.pallas_call(functools.partial(backward_kernel, ways), out_shape=(shape...]
    all_gather x4 -> x2, waiting for transfers between devices: 47.2 us -> 0.01 us  [gathered(): return lax.all_gather(block, 'dp', axis=0, tiled=True)]
  transfers between devices with their start and end apart: 72 -> 14, of which waited for: 40 -> 9; matrix products, arithmetic and copies ran while one was open for 17% -> 2% of each run, Pallas kernels for 0% -> 17%
where the time goes in v1:
time: 238 us; the launch traced here: 237 us
  waiting for transfers between devices  74.9 us (31%)
  Pallas kernels  52.7 us (22%)
  blocking collectives  48.1 us (20%)
  starting transfers between devices  30.9 us (13%)
  between operations  14.3 us (6%)
  local copies, waits for them, and re-layouts  12.5 us (5%)
  other arithmetic  3.12 us (1%)
    ppermute x6, waiting for transfers between devices, swap(): return lax.ppermute(block, axis, [(i, i ^ bit) for i in range(size)])  39.1 us
    all_to_all x2, blocking collectives, exchange(): lax.all_to_all(block, 'ctx', 0, 0, axis_index_groups=groups, tiled=True)  34.9 us
    all_to_all x3, waiting for transfers between devices, exchange(): lax.all_to_all(block, 'ctx', 0, 0, axis_index_groups=groups, tiled=True)  23.5 us
    pallas_call x1, Pallas kernels, attend_back(): pl.pallas_call(functools.partial(backward_kernel, ways), out_shape=(shape...  16.2 us
    pallas_call x1, Pallas kernels, attend(): pl.pallas_call(functools.partial(forward_kernel, ways), out_shape=(shaped...  14.6 us
    unnamed x61, local copies, waits for them, and re-layouts  12.4 us
    all_to_all x3, starting transfers between devices, exchange(): lax.all_to_all(block, 'ctx', 0, 0, axis_index_groups=groups, tiled=True)  11.1 us
    ppermute x2, waiting for transfers between devices, around(): return lax.ppermute(block, 'ctx', route)  10.9 us
  transfers between devices with their start and end apart: 14, of which 9 were waited for; matrix products, arithmetic and copies ran while one was open for 2% of the time, Pallas kernels for 17%

profile of v1, /device:TPU:0, one launch (start us, length us, event | category | flops | bytes accessed | tf_op | source)
XLA Modules:
  0.0 236.6 jit_solution(3170489942760167229)
XLA Ops:
  8.7 2.3 all_gather.21.wq_ref
  11.0 2.2 all_gather.22.wk_ref
  13.1 2.2 all_gather.23.wv_ref
  16.0 21.9 %all_to_all.30.refs_0_ = bf16[8,128,256]{2,1,0:T(8,128)(2,1)S(1)} all-to-all(bf16[8,128,256]{2,1,0:T(8,128)(2,1)S(1)} %get-tuple-element.57), channel_id=1, replica_groups={{0,2,4,6,8,10,12,14},{1,3,5,7,9,11,13,15},{16,18,20,22,24,26,28,30},{17..., dimensions={0} | all-to-all | bytes 1048576 | tf_op jit(solution)/shard_map/all_to_all | solution.py:599
  39.4 3.8 %all-to-all-start = ((bf16[8,64,256]{2,1,0:T(8,128)(2,1)}), bf16[8,64,256]{2,1,0:T(8,128)(2,1)S(1)}, u32[]{:S(2)}, u32[]{:S(2)}) async-start(bf16[8,64,256]{2,1,0:T(8,128)(2,1)} %copy-done.20), calls=%async_computation | async-start | bytes 524288 | tf_op jit(solution)/shard_map/all_to_all | solution.py:599
  44.5 7.1 %all-to-all-done.q_ref = bf16[8,64,256]{2,1,0:T(8,128)(2,1)S(1)} async-done(((bf16[8,64,256]{2,1,0:T(8,128)(2,1)}), bf16[8,64,256]{2,1,0:T(8,128)(2,1)S(1)}, u32[]{:S(2)}, u32[]{:S(2)}) %all-to-all-start) | async-done | bytes 262176 | tf_op jit(solution)/shard_map/all_to_all | solution.py:599
  51.7 14.6 %attend.1 = (bf16[8,64,256]{2,1,0:T(8,128)(2,1)S(1)}, f32[8,64,256]{2,1,0:T(8,128)S(1)}, f32[8,256]{1,0:T(8,128)S(1)}) custom-call(s32[2]{0:T(128)S(1)} %pad_add_fusion.ids_ref, s32[4096]{0:T(1024)S(1)} %bitcast.23, s32[16,256]{1,0:T(8,128)S(1)} %reshape.51.seg_ref, bf16[8,64,256]{2,1,0:T(8,128)(2,1)S(1)} %all-to-all-done.q_ref, ...), custom_call_target="tpu_custom_call" | custom-call | tf_op jit(solution)/shard_map/attend/pallas_call | solution.py:153
  67.8 3.4 %all-to-all-start.2 = ((bf16[8,64,256]{2,1,0:T(8,128)(2,1)}), bf16[8,64,256]{2,1,0:T(8,128)(2,1)S(1)}, u32[]{:S(2)}, u32[]{:S(2)}) async-start(bf16[8,64,256]{2,1,0:T(8,128)(2,1)} %copy-done.21), calls=%async_computation.2 | async-start | bytes 524288 | tf_op jit(solution)/shard_map/all_to_all | solution.py:599
  71.3 2.6 %all_gather.24.gains_ref = bf16[3,512]{1,0:T(4,128)(2,1)S(1)} all-gather(bf16[3,256]{1,0:T(4,128)(2,1)S(1)} %pad_maximum_fusion.1), channel_id=1, replica_groups=mesh['dp'=2,'ctx'=16] {'dp'}, dimensions={1}, use_global_device_ids=true | all-gather | bytes 4608 | tf_op jit(solution)/shard_map/all_gather | solution.py:615
  73.8 4.0 %all_gather.25.wo_ref = bf16[512,512]{1,0:T(8,128)(2,1)} all-gather(bf16[256,512]{1,0:T(8,128)(2,1)} %param.22), channel_id=1, replica_groups=mesh['dp'=2,'ctx'=16] {'dp'}, dimensions={0}, use_global_device_ids=true | all-gather | bytes 786432 | tf_op jit(solution)/shard_map/all_gather | solution.py:596
  77.8 3.5 %all-to-all-done.2 = bf16[8,64,256]{2,1,0:T(8,128)(2,1)S(1)} async-done(((bf16[8,64,256]{2,1,0:T(8,128)(2,1)}), bf16[8,64,256]{2,1,0:T(8,128)(2,1)S(1)}, u32[]{:S(2)}, u32[]{:S(2)}) %all-to-all-start.2) | async-done | bytes 262176 | tf_op jit(solution)/shard_map/all_to_all | solution.py:599
  86.5 7.8 %middle.1 = (bf16[256,512]{1,0:T(8,128)(2,1)}, f32[256,512]{1,0:T(8,128)S(1)}, f32[256,512]{1,0:T(8,128)S(1)}, bf16[512,256]{1,0:T(8,128)(2,1)S(1)}, bf16[256,51...) custom-call(bf16[512,256]{1,0:T(8,128)(2,1)S(1)} %bitcast.18, ...), custom_call_target="tpu_custom_call" | custom-call | tf_op jit(solution)/shard_map/middle/pallas_call | solution.py:349
  94.3 3.5 %ffn_grads.1 = (bf16[16,160,512]{2,1,0:T(8,128)(2,1)S(1)}, bf16[16,160,512]{2,1,0:T(8,128)(2,1)}) custom-call(s32[2]{0:T(128)S(1)} %pad_add_fusion.ids_ref, bf16[256,512]{1,0:T(8,128)(2,1)S(1)} %get-tuple-element.59.x1_ref, bf16[256,2048]{1,0:T(8,128)(2,1)S(1)} %get-tuple-element.60.h_ref, bf16[256,512]{1,0:T(8,128)(2,1)S(1)} %get-tuple-element.61.df_ref, ...), custom_call_target="tpu_custom_call" | custom-call | tf_op jit(solution)/shard_map/ffn_grads/pallas_call | solution.py:415
  99.5 13.0 %all_to_all.31.do_ref = bf16[8,64,256]{2,1,0:T(8,128)(2,1)S(1)} all-to-all(bf16[8,64,256]{2,1,0:T(8,128)(2,1)S(1)} %bitcast.22), channel_id=1, replica_groups={{0,2,4,6,8,10,12,14},{1,3,5,7,9,11,13,15},{16,18,20,22,24,26,28,30},{17..., dimensions={0} | all-to-all | bytes 524288 | tf_op jit(solution)/shard_map/all_to_all | solution.py:599
  112.6 16.2 %attend_back.1 = (bf16[8,64,256]{2,1,0:T(8,128)(2,1)S(1)}, f32[8,128,256]{2,1,0:T(8,128)S(1)}, bf16[8,128,256]{2,1,0:T(8,128)(2,1)S(1)}) custom-call(s32[2]{0:T(128)S(1)} %pad_add_fusion.ids_ref, s32[4096]{0:T(1024)S(1)} %bitcast.24, s32[16,256]{1,0:T(8,128)S(1)} %reshape.51.seg_ref, bf16[8,64,256]{2,1,0:T(8,128)(2,1)S(1)} %all-to-all-done.q_ref, ...), custom_call_target="tpu_custom_call" | custom-call | tf_op jit(solution)/shard_map/attend_back/pallas_call | solution.py:231
  128.8 2.3 collective-permute-start.6
  131.1 10.9 %collective-permute-done.6 = bf16[8,128,256]{2,1,0:T(8,128)(2,1)S(1)} collective-permute-done((bf16[8,128,256]{2,1,0:T(8,128)(2,1)S(1)}, bf16[8,128,256]{2,1,0:T(8,128)(2,1)S(1)}, u32[]{:S(2)}, u32[]{:S(2)}) %collective-permute-start.6) | collective-permute-done | bytes 524320 | tf_op jit(solution)/shard_map/ppermute | solution.py:606
  143.1 3.9 %all-to-all-start.4 = ((bf16[8,192,256]{2,1,0:T(8,128)(2,1)}), bf16[8,192,256]{2,1,0:T(8,128)(2,1)S(1)}, u32[]{:S(2)}, u32[]{:S(2)}) async-start(bf16[8,192,256]{2,1,0:T(8,128)(2,1)} %pad_maximum_fusion), calls=%async_computation.4 | async-start | bytes 1572864 | tf_op jit(solution)/shard_map/all_to_all | solution.py:599
  147.0 1.7 copy-done.1
  148.8 3.5 %halve.4 = (bf16[8,160,512]{2,1,0:T(8,128)(2,1)S(1)}, bf16[8,160,512]{2,1,0:T(8,128)(2,1)}) custom-call(s32[2]{0:T(128)S(1)} %pad_add_fusion.ids_ref, bf16[16,160,512]{2,1,0:T(8,128)(2,1)S(1)} %copy-done.1, bf16[16,160,512]{2,1,0:T(8,128)(2,1)} %collective-permute-done.1.got_ref), custom_call_target="tpu_custom_call" | custom-call | tf_op jit(solution)/shard_map/halve/pallas_call | solution.py:448
  153.4 2.3 collective-permute-start.2
  155.8 12.9 %all-to-all-done.4.back_ref = bf16[8,192,256]{2,1,0:T(8,128)(2,1)S(1)} async-done(((bf16[8,192,256]{2,1,0:T(8,128)(2,1)}), bf16[8,192,256]{2,1,0:T(8,128)(2,1)S(1)}, u32[]{:S(2)}, u32[]{:S(2)}) %all-to-all-start.4) | async-done | bytes 786464 | tf_op jit(solution)/shard_map/all_to_all | solution.py:599
  171.2 2.1 collective-permute-done.7
  174.5 5.5 %all-to-all-start.5 = ((bf16[16,48,512]{2,1,0:T(8,128)(2,1)}), bf16[16,48,512]{2,1,0:T(8,128)(2,1)S(1)}, u32[]{:S(2)}, u32[]{:S(2)}) async-start(bf16[16,48,512]{2,1,0:T(8,128)(2,1)} %add.7), calls=%async_computation.5 | async-start | bytes 1572864 | tf_op jit(solution)/shard_map/all_to_all | solution.py:640
  179.9 5.5 %collective-permute-done.2.got_ref = bf16[8,160,512]{2,1,0:T(8,128)(2,1)} collective-permute-done((bf16[8,160,512]{2,1,0:T(8,128)(2,1)}, bf16[8,160,512]{2,1,0:T(8,128)(2,1)}, u32[]{:S(2)}, u32[]{:S(2)}) %collective-permute-start.2) | collective-permute-done | bytes 1310752 | tf_op jit(solution)/shard_map/ppermute | solution.py:44
  187.1 2.8 %collective-permute-start.3 = (bf16[4,160,512]{2,1,0:T(8,128)(2,1)S(1)}, bf16[4,160,512]{2,1,0:T(8,128)(2,1)S(1)}, u32[]{:S(2)}, u32[]{:S(2)}) collective-permute-start(bf16[4,160,512]{2,1,0:T(8,128)(2,1)S(1)} %get-tuple-element.70), channel_id=1, source_target_pairs={{0,2},{1,3},{2,0},{3,1},{4,6},{5,7},{6,4},{7,5},{8,10},{9,11},{10,... | collective-permute-start | bytes 1966088 | tf_op jit(solution)/shard_map/ppermute | solution.py:44
  189.9 17.8 %collective-permute-done.3.got_ref = bf16[4,160,512]{2,1,0:T(8,128)(2,1)S(1)} collective-permute-done((bf16[4,160,512]{2,1,0:T(8,128)(2,1)S(1)}, bf16[4,160,512]{2,1,0:T(8,128)(2,1)S(1)}, u32[]{:S(2)}, u32[]{:S(2)}) %collective-permute-start.3) | collective-permute-done | bytes 655392 | tf_op jit(solution)/shard_map/ppermute | solution.py:44
  208.5 2.3 collective-permute-start.4
  210.8 7.2 %collective-permute-done.4.got_ref = bf16[2,160,512]{2,1,0:T(8,128)(2,1)S(1)} collective-permute-done((bf16[2,160,512]{2,1,0:T(8,128)(2,1)S(1)}, bf16[2,160,512]{2,1,0:T(8,128)(2,1)S(1)}, u32[]{:S(2)}, u32[]{:S(2)}) %collective-permute-start.4) | collective-permute-done | bytes 327712 | tf_op jit(solution)/shard_map/ppermute | solution.py:44
  218.6 2.8 %collective-permute-start.5 = (bf16[1,160,512]{2,1,0:T(8,128)(2,1)S(1)}, bf16[1,160,512]{2,1,0:T(8,128)(2,1)S(1)}, u32[]{:S(2)}, u32[]{:S(2)}) collective-permute-start(bf16[1,160,512]{2,1,0:T(8,128)(2,1)S(1)} %get-tuple-element.74), channel_id=1, source_target_pairs={{0,8},{1,9},{2,10},{3,11},{4,12},{5,13},{6,14},{7,15},{8,0},{9,1},... | collective-permute-start | bytes 491528 | tf_op jit(solution)/shard_map/ppermute | solution.py:44
  221.4 6.5 %collective-permute-done.5.got_ref = bf16[1,160,512]{2,1,0:T(8,128)(2,1)S(1)} collective-permute-done((bf16[1,160,512]{2,1,0:T(8,128)(2,1)S(1)}, bf16[1,160,512]{2,1,0:T(8,128)(2,1)S(1)}, u32[]{:S(2)}, u32[]{:S(2)}) %collective-permute-start.5) | collective-permute-done | bytes 163872 | tf_op jit(solution)/shard_map/ppermute | solution.py:44
  227.9 1.8 finish.1
  (87 shorter events, 22.3 us)
Async XLA Ops:
  7.2 3.8 %copy-start.25 = (bf16[256,512]{1,0:T(8,128)(2,1)S(1)}, bf16[256,512]{1,0:T(8,128)(2,1)}, u32[]{:S(2)}) copy-start(bf16[256,512]{1,0:T(8,128)(2,1)} %param.20) | copy-start | bytes 786436
  7.2 74.2 %all-gather.3.cloned.1.call-start = ((), (), s32[]{:S(2)}) async-start(), calls=%async_computation.6 | async-start | bytes 3145728 | tf_op jit(solution)/shard_map/all_gather | solution.py:596
  7.9 5.2 %copy-start.26 = (bf16[256,512]{1,0:T(8,128)(2,1)S(1)}, bf16[256,512]{1,0:T(8,128)(2,1)}, u32[]{:S(2)}) copy-start(bf16[256,512]{1,0:T(8,128)(2,1)} %param.21) | copy-start | bytes 786436
  7.9 7.4 %copy-start.2 = (bf16[1,256,512]{2,1,0:T(8,128)(2,1)S(1)}, bf16[1,256,512]{2,1,0:T(8,128)(2,1)}, u32[]{:S(2)}) copy-start(bf16[1,256,512]{2,1,0:T(8,128)(2,1)} %param.14) | copy-start | bytes 786436
  8.0 73.4 %all-gather.5.cloned.1.call-start = ((), (), s32[]{:S(2)}) async-start(), calls=%async_computation.7 | async-start | bytes 3145728 | tf_op jit(solution)/shard_map/all_gather | solution.py:596
  15.3 28.4 %copy-start.22 = (s32[1,4096]{1,0:T(1,128)S(1)}, s32[1,4096]{1,0:T(1,128)}, u32[]{:S(2)}) copy-start(s32[1,4096]{1,0:T(1,128)} %param.17) | copy-start | bytes 49156
  16.0 23.5 %copy-start.20 = (bf16[8,64,256]{2,1,0:T(8,128)(2,1)}, bf16[8,64,256]{2,1,0:T(8,128)(2,1)S(1)}, u32[]{:S(2)}) copy-start(bf16[8,64,256]{2,1,0:T(8,128)(2,1)S(1)} %get-tuple-element.56) | copy-start | bytes 786436
  16.0 55.2 %copy-start.27 = (bf16[256]{0:T(256)(128)(2,1)S(1)}, bf16[256]{0:T(256)(128)(2,1)}, u32[]{:S(2)}) copy-start(bf16[256]{0:T(256)(128)(2,1)} %param.25) | copy-start | bytes 1540
  16.0 55.2 %copy-start.28 = (bf16[256]{0:T(256)(128)(2,1)S(1)}, bf16[256]{0:T(256)(128)(2,1)}, u32[]{:S(2)}) copy-start(bf16[256]{0:T(256)(128)(2,1)} %param.26) | copy-start | bytes 1540
  16.0 55.2 %copy-start.29 = (bf16[256]{0:T(256)(128)(2,1)S(1)}, bf16[256]{0:T(256)(128)(2,1)}, u32[]{:S(2)}) copy-start(bf16[256]{0:T(256)(128)(2,1)} %param.27) | copy-start | bytes 1540
  38.0 13.7 %collective-permute-start = (bf16[8,128,256]{2,1,0:T(8,128)(2,1)S(1)}, bf16[8,128,256]{2,1,0:T(8,128)(2,1)S(1)}, u32[]{:S(2)}, u32[]{:S(2)}) collective-permute-start(bf16[8,128,256]{2,1,0:T(8,128)(2,1)S(1)} %all_to_all.30.refs_0_), channel_id=1, source_target_pairs={{0,1},{1,0},{2,3},{3,2},{4,5},{5,4},{6,7},{7,6},{8,9},{9,8},{10,11... | collective-permute-start | bytes 1572872 | tf_op jit(solution)/shard_map/ppermute | solution.py:606
  39.4 41.9 %copy-start.18 = (bf16[1,256,512]{2,1,0:T(8,128)(2,1)S(1)}, bf16[1,256,512]{2,1,0:T(8,128)(2,1)}, u32[]{:S(2)}) copy-start(bf16[1,256,512]{2,1,0:T(8,128)(2,1)} %param.15) | copy-start | bytes 786436
  39.4 41.9 %copy-start.23 = (s32[1,256]{1,0:T(1,128)S(1)}, s32[1,256]{1,0:T(1,128)}, u32[]{:S(2)}) copy-start(s32[1,256]{1,0:T(1,128)} %mask_ref.1) | copy-start | bytes 3076
  39.4 12.2 %all-to-all-start = ((bf16[8,64,256]{2,1,0:T(8,128)(2,1)}), bf16[8,64,256]{2,1,0:T(8,128)(2,1)S(1)}, u32[]{:S(2)}, u32[]{:S(2)}) async-start(bf16[8,64,256]{2,1,0:T(8,128)(2,1)} %copy-done.20), calls=%async_computation | async-start | bytes 524288 | tf_op jit(solution)/shard_map/all_to_all | solution.py:599
  51.7 16.1 %copy-start.3 = (bf16[8,128,256]{2,1,0:T(8,128)(2,1)}, bf16[8,128,256]{2,1,0:T(8,128)(2,1)S(1)}, u32[]{:S(2)}) copy-start(bf16[8,128,256]{2,1,0:T(8,128)(2,1)S(1)} %collective-permute-done.refs_1_) | copy-start | bytes 1572868
  67.8 13.6 %all-to-all-start.2 = ((bf16[8,64,256]{2,1,0:T(8,128)(2,1)}), bf16[8,64,256]{2,1,0:T(8,128)(2,1)S(1)}, u32[]{:S(2)}, u32[]{:S(2)}) async-start(bf16[8,64,256]{2,1,0:T(8,128)(2,1)} %copy-done.21), calls=%async_computation.2 | async-start | bytes 524288 | tf_op jit(solution)/shard_map/all_to_all | solution.py:599
  94.3 3.5 %copy-start.16 = (f32[256,512]{1,0:T(8,128)}, f32[256,512]{1,0:T(8,128)S(1)}, u32[]{:S(2)}) copy-start(f32[256,512]{1,0:T(8,128)S(1)} %get-tuple-element.81.gr_ref) | copy-start | bytes 1572868
  94.3 18.2 %copy-start.4 = (bf16[8,128,256]{2,1,0:T(8,128)(2,1)S(1)}, bf16[8,128,256]{2,1,0:T(8,128)(2,1)}, u32[]{:S(2)}) copy-start(bf16[8,128,256]{2,1,0:T(8,128)(2,1)} %copy-done.3) | copy-start | bytes 1572868
  94.3 18.2 %copy-start.15 = (f32[8,64,256]{2,1,0:T(8,128)S(1)}, f32[8,64,256]{2,1,0:T(8,128)}, u32[]{:S(2)}) copy-start(f32[8,64,256]{2,1,0:T(8,128)} %copy-done.14) | copy-start | bytes 1572868
  99.4 47.6 %collective-permute-start.1 = (bf16[16,160,512]{2,1,0:T(8,128)(2,1)}, bf16[16,160,512]{2,1,0:T(8,128)(2,1)}, u32[]{:S(2)}, u32[]{:S(2)}) collective-permute-start(bf16[16,160,512]{2,1,0:T(8,128)(2,1)} %get-tuple-element.66), channel_id=1, source_target_pairs={{0,16},{16,0},{1,17},{17,1},{2,18},{18,2},{3,19},{19,3},{4,20},{20... | collective-permute-start | bytes 7864328 | tf_op jit(solution)/shard_map/ppermute | solution.py:44
  128.8 13.1 %collective-permute-start.6 = (bf16[8,128,256]{2,1,0:T(8,128)(2,1)S(1)}, bf16[8,128,256]{2,1,0:T(8,128)(2,1)S(1)}, u32[]{:S(2)}, u32[]{:S(2)}) collective-permute-start(bf16[8,128,256]{2,1,0:T(8,128)(2,1)S(1)} %get-tuple-element.80), channel_id=1, source_target_pairs={{0,1},{1,0},{2,3},{3,2},{4,5},{5,4},{6,7},{7,6},{8,9},{9,8},{10,11... | collective-permute-start | bytes 1572872 | tf_op jit(solution)/shard_map/ppermute | solution.py:606
  143.1 25.5 %all-to-all-start.4 = ((bf16[8,192,256]{2,1,0:T(8,128)(2,1)}), bf16[8,192,256]{2,1,0:T(8,128)(2,1)S(1)}, u32[]{:S(2)}, u32[]{:S(2)}) async-start(bf16[8,192,256]{2,1,0:T(8,128)(2,1)} %pad_maximum_fusion), calls=%async_computation.4 | async-start | bytes 1572864 | tf_op jit(solution)/shard_map/all_to_all | solution.py:599
  148.8 19.9 %copy-start.17 = (f32[256,512]{1,0:T(8,128)S(1)}, f32[256,512]{1,0:T(8,128)}, u32[]{:S(2)}) copy-start(f32[256,512]{1,0:T(8,128)} %copy-done.16) | copy-start | bytes 1572868
  153.4 32.0 %collective-permute-start.2 = (bf16[8,160,512]{2,1,0:T(8,128)(2,1)}, bf16[8,160,512]{2,1,0:T(8,128)(2,1)}, u32[]{:S(2)}, u32[]{:S(2)}) collective-permute-start(bf16[8,160,512]{2,1,0:T(8,128)(2,1)} %get-tuple-element.68), channel_id=1, source_target_pairs={{0,1},{1,0},{2,3},{3,2},{4,5},{5,4},{6,7},{7,6},{8,9},{9,8},{10,11... | collective-permute-start | bytes 3932168 | tf_op jit(solution)/shard_map/ppermute | solution.py:44
  171.0 2.3 collective-permute-start.7
  173.3 12.1 %copy-start.9 = (bf16[8,160,512]{2,1,0:T(8,128)(2,1)S(1)}, bf16[8,160,512]{2,1,0:T(8,128)(2,1)}, u32[]{:S(2)}) copy-start(bf16[8,160,512]{2,1,0:T(8,128)(2,1)} %copy-done.8) | copy-start | bytes 3932164
  174.5 46.9 %all-to-all-start.5 = ((bf16[16,48,512]{2,1,0:T(8,128)(2,1)}), bf16[16,48,512]{2,1,0:T(8,128)(2,1)S(1)}, u32[]{:S(2)}, u32[]{:S(2)}) async-start(bf16[16,48,512]{2,1,0:T(8,128)(2,1)} %add.7), calls=%async_computation.5 | async-start | bytes 1572864 | tf_op jit(solution)/shard_map/all_to_all | solution.py:640
  187.1 40.8 %copy-start.11 = (f32[256,512]{1,0:T(8,128)S(1)}, f32[256,512]{1,0:T(8,128)}, u32[]{:S(2)}) copy-start(f32[256,512]{1,0:T(8,128)} %copy-done.10) | copy-start | bytes 1572868
  187.1 40.8 %copy-start.13 = (f32[256,512]{1,0:T(8,128)S(1)}, f32[256,512]{1,0:T(8,128)}, u32[]{:S(2)}) copy-start(f32[256,512]{1,0:T(8,128)} %copy-done.12) | copy-start | bytes 1572868
  187.1 20.7 %collective-permute-start.3 = (bf16[4,160,512]{2,1,0:T(8,128)(2,1)S(1)}, bf16[4,160,512]{2,1,0:T(8,128)(2,1)S(1)}, u32[]{:S(2)}, u32[]{:S(2)}) collective-permute-start(bf16[4,160,512]{2,1,0:T(8,128)(2,1)S(1)} %get-tuple-element.70), channel_id=1, source_target_pairs={{0,2},{1,3},{2,0},{3,1},{4,6},{5,7},{6,4},{7,5},{8,10},{9,11},{10,... | collective-permute-start | bytes 1966088 | tf_op jit(solution)/shard_map/ppermute | solution.py:44
  208.5 9.5 %collective-permute-start.4 = (bf16[2,160,512]{2,1,0:T(8,128)(2,1)S(1)}, bf16[2,160,512]{2,1,0:T(8,128)(2,1)S(1)}, u32[]{:S(2)}, u32[]{:S(2)}) collective-permute-start(bf16[2,160,512]{2,1,0:T(8,128)(2,1)S(1)} %get-tuple-element.72), channel_id=1, source_target_pairs={{0,4},{1,5},{2,6},{3,7},{4,0},{5,1},{6,2},{7,3},{8,12},{9,13},{10,... | collective-permute-start | bytes 983048 | tf_op jit(solution)/shard_map/ppermute | solution.py:44
  218.6 9.3 %collective-permute-start.5 = (bf16[1,160,512]{2,1,0:T(8,128)(2,1)S(1)}, bf16[1,160,512]{2,1,0:T(8,128)(2,1)S(1)}, u32[]{:S(2)}, u32[]{:S(2)}) collective-permute-start(bf16[1,160,512]{2,1,0:T(8,128)(2,1)S(1)} %get-tuple-element.74), channel_id=1, source_target_pairs={{0,8},{1,9},{2,10},{3,11},{4,12},{5,13},{6,14},{7,15},{8,0},{9,1},... | collective-permute-start | bytes 491528 | tf_op jit(solution)/shard_map/ppermute | solution.py:44
  (12 other events, 16.9 us)
Sparse Core Ops, SparseCore 0:
  9.6 13.2 all-gather.2
  24.4 11.7 all-gather.4

commit v2 on v1

v2 whole, which is shorter than its diff:
```python
import functools

import jax
import jax.numpy as jnp
from jax import lax
from jax.experimental import pallas as pl
from jax.experimental.pallas import tpu as pltpu
from jax.sharding import PartitionSpec as P

HEADS = 8
EPS = 1e-05
LANES = 32
DOCS = 24
UNROLL = 4
INNER = (0, 1, 3, 2)
RING = (0, 2, 4, 6, 7, 5, 3, 1)
GROUP = 8
LOG2E = 1.4426950408889634
FAR = -(2.0**100)
CORE = 0.7978845608028654
CUBE = 0.044715
MIB = 1024 * 1024

BF16 = jnp.bfloat16
F32 = jnp.float32


def dot(left, right):
    return jnp.dot(left, right, preferred_element_type=F32)


def dot_t(left, right):
    return lax.dot_general(left, right, (((1,), (1,)), ((), ())), preferred_element_type=F32)


def vmem(count):
    return [pl.BlockSpec(memory_space=pltpu.VMEM) for _ in range(count)]


def hbm(count):
    return [pl.BlockSpec(memory_space=pltpu.HBM) for _ in range(count)]


def smem():
    return pl.BlockSpec(memory_space=pltpu.SMEM)


def kept(shape, dtype):
    return pltpu.VMEM(shape, dtype)


def near(array):
    return pltpu.with_memory_space_constraint(array, pltpu.VMEM)


def apart(shape, dtype):
    return pltpu.HBM(shape, dtype)


def far(array):
    return pltpu.with_memory_space_constraint(array, pltpu.HBM)


def shaped(shape, dtype):
    return jax.ShapeDtypeStruct(shape, dtype)


def cost(us):
    return pl.CostEstimate(flops=int(us * 1.1e9), bytes_accessed=1024, transcendentals=0)


def swap(block, axis, bit):
    size = lax.axis_size(axis)
    return lax.ppermute(block, axis, [(i, i ^ bit) for i in range(size)])


def rows_of(ids_ref, blocks, number, total):
    size = total // blocks
    if blocks == 1:
        return pl.ds(0, size)
    return pl.ds(pl.multiple_of((ids_ref[0] + number) % 2 * size, size), size)


def fetch(sources, targets, sems):
    copies = [
        pltpu.make_async_copy(source, target, sems.at[k])
        for k, (source, target) in enumerate(zip(sources, targets))
    ]
    for copy in copies:
        copy.start()
    return copies


def project_kernel(blocks, ids_ref, x_ref, *refs):
    out_ref, held, sems = refs[3 * blocks :]
    feat = x_ref.shape[1]
    size = feat // HEADS
    each = feat // blocks
    targets = [
        held.at[part, pl.ds(j * each, each), :] for part in range(3) for j in range(blocks)
    ]
    copies = fetch(refs[: 3 * blocks], targets, sems)
    x = jnp.concatenate(
        [x_ref[:, rows_of(ids_ref, blocks, j, feat)] for j in range(blocks)], axis=1
    )
    for part, scale in ((0, size**-0.5), (1, 1.0), (2, 1.0)):
        for copy in copies[part * blocks : (part + 1) * blocks]:
            copy.wait()
        turned = (dot(x, held[part]) * scale).astype(BF16).T
        for h in range(HEADS):
            out_ref[h, part * size : (part + 1) * size, :] = turned[h * size : (h + 1) * size, :]


def project(ids, x, weights):
    tok, feat = x.shape
    flat = [block for weight in weights for block in weight]
    return pl.pallas_call(
        functools.partial(project_kernel, len(weights[0])),
        out_shape=shaped((HEADS, 3 * feat // HEADS, tok), BF16),
        in_specs=[smem()] + vmem(1) + hbm(len(flat)),
        out_specs=vmem(1)[0],
        scratch_shapes=[
            pltpu.VMEM((3, feat, feat), BF16),
            pltpu.SemaphoreType.DMA((len(flat),)),
        ],
        compiler_params=pltpu.CompilerParams(vmem_limit_bytes=12 * MIB),
        cost_estimate=cost(1.4),
        name="project",
    )(ids, x, *map(far, flat))


def mask_rows(row, hit, miss, extra):
    number = lax.broadcasted_iota(jnp.int32, (LANES, row.shape[1]), 0)
    base = jnp.where(number == row, hit, miss)
    base = jnp.where(number < DOCS, base, 0.0)
    for k, value in enumerate(extra):
        base = jnp.where(number == DOCS + k, value, base)
    return base.astype(BF16)


def parts_of(value, count):
    found = []
    for _ in range(count):
        part = value.astype(BF16).astype(F32)
        found.append(part)
        value = value - part
    return found


def query_rows(q, row, extra):
    wide = q.astype(F32) * LOG2E
    high, low = parts_of(wide, 2)
    return jnp.concatenate(
        [high.astype(BF16), low.astype(BF16), mask_rows(row, 0.0, FAR, extra)], axis=0
    ).T


def key_rows(k, row):
    return jnp.concatenate([k, k, mask_rows(row, 1.0, 0.0, (1.0, 1.0, 1.0))], axis=0)


def list_size(count):
    return HEADS * count + 2 * GROUP


def plan_kernel(ways, count, tok, ids_ref, *refs):
    out_ref = refs[-1]
    rank = ids_ref[2]
    length = list_size(count)

    def number(at):
        if len(refs) == 2:
            return refs[0][at]
        return jnp.where(ids_ref[3] == 0, refs[0][at], refs[1][at])

    firsts = [number(c * tok) for c in range(count)]
    lasts = [number(c * tok + tok - 1) for c in range(count)]

    def one(i, found):
        chunk = i * ways + rank
        first = number(chunk * tok)
        last = number(chunk * tok + tok - 1)
        low = sum((value < first).astype(jnp.int32) for value in lasts)
        high = sum((value <= last).astype(jnp.int32) for value in firsts)

        def other(c, found):
            own = (lax.rem(c, ways) == rank).astype(jnp.int32)
            every, mine, rest = found
            out_ref[every] = i
            out_ref[length + every] = c
            at = jnp.where(own == 1, 2 * length + mine, 4 * length + rest)
            out_ref[at] = i
            out_ref[at + length] = c
            return every + 1, mine + own, rest + 1 - own

        return lax.fori_loop(low, high, other, found)

    found = lax.fori_loop(0, HEADS, one, (jnp.int32(0),) * 3)
    for k, ended in enumerate(found):
        for g in range(GROUP):
            out_ref[2 * k * length + ended + g] = HEADS
            out_ref[(2 * k + 1) * length + ended + g] = 0
        out_ref[6 * length + k] = (ended + GROUP - 1) // GROUP


def plan_of(ids, segs, ways, count, tok):
    size = 6 * list_size(count) + 8
    return pl.pallas_call(
        functools.partial(plan_kernel, ways, count, tok),
        out_shape=shaped((size,), jnp.int32),
        in_specs=[smem()] * (1 + len(segs)),
        out_specs=smem(),
        cost_estimate=cost(1),
        name="plan",
    )(ids, *[seg.reshape(-1) for seg in segs])


def chosen(ids_ref, seg_refs):
    if len(seg_refs) == 1:
        return seg_refs[0][...]
    return jnp.where(ids_ref[3] == 0, seg_refs[0][...], seg_refs[1][...])


def tiles_of(plan_ref, kind, length, g):
    found = []
    for k in range(GROUP):
        at = 2 * kind * length + g * GROUP + k
        found.append((plan_ref[at], plan_ref[at + length]))
    return found


def chunk_of(h, slot, ways, rank):
    return h * ways + lax.rem(rank - slot + ways, ways)


def forward_kernel(ways, texts, ids_ref, plan_ref, *refs):
    seg_refs, refs = refs[:texts], refs[texts:]
    kv_refs = refs[:ways]
    q_ref = kv_refs[0]
    o_ref, of_out, lse_ref, kx, vx, qx, acc, seg_ref, of_ref, sem = refs[ways:]
    seg_ref[...] = chosen(ids_ref, seg_refs)
    count, tok = seg_ref.shape
    size = q_ref.shape[1] // 3
    rank = ids_ref[2]
    length = list_size(count)
    ones = (lax.broadcasted_iota(jnp.int32, (16, tok), 0) == 0).astype(F32).astype(BF16)
    for slot in range(ways):

        @pl.loop(0, HEADS, unroll=UNROLL)
        def fill(h):
            chunk = chunk_of(h, slot, ways, rank)
            keys = kv_refs[slot][h, size : 2 * size, :]
            kx[chunk] = key_rows(keys, seg_ref[pl.ds(chunk, 1), :])
            vx[chunk] = jnp.concatenate([kv_refs[slot][h, 2 * size : 3 * size, :], ones], axis=0)

    @pl.loop(0, HEADS, unroll=UNROLL)
    def fill_query(i):
        qx[i] = query_rows(q_ref[i, 0:size, :], seg_ref[pl.ds(i * ways + rank, 1), :], ())
        acc[i] = jnp.zeros_like(acc[i])

    qx[HEADS] = query_rows(jnp.zeros((size, tok), BF16), jnp.full((1, tok), -1, jnp.int32), ())
    acc[HEADS] = jnp.zeros_like(acc[0])

    @pl.loop(0, plan_ref[6 * length])
    def group(g):
        tiles = tiles_of(plan_ref, 0, length, g)
        weights = [jnp.exp2(dot(qx[i], kx[c])).astype(BF16) for i, c in tiles]
        mixed = [dot_t(vx[c], w) for (i, c), w in zip(tiles, weights)]
        for (i, c), part in zip(tiles, mixed):
            acc[i] += part

    smallest = jnp.full((1, tok), 1.0, F32)
    largest = jnp.full((1, tok), 1.0, F32)
    for i in range(HEADS):
        total = acc[i, size : size + 1, :]
        smallest = jnp.minimum(smallest, total)
        largest = jnp.maximum(largest, total)
        out = acc[i, 0:size, :] / total
        of_ref[i] = out
        o_ref[i] = out.astype(BF16)
        lse_ref[i : i + 1, :] = jnp.log(total) * LOG2E
    good = (jnp.min(smallest) > 2.0**-90) & (jnp.max(largest) < 2.0**90)

    @pl.when(jnp.logical_not(good))
    def any_scores():
        @pl.loop(0, HEADS)
        def one(i):
            query = qx[i]

            def step(c, carry):
                top, total, mixed = carry
                s = dot(query, kx[c])
                new = jnp.maximum(top, jnp.max(s, axis=1, keepdims=True))
                fade = jnp.exp2(top - new)
                w = jnp.exp2(s - new)
                total = total * fade + jnp.sum(w, axis=1, keepdims=True)
                mixed = mixed * fade + dot_t(w.astype(BF16), vx[c])
                return new, total, mixed

            top, total, mixed = lax.fori_loop(
                0,
                count,
                step,
                (
                    jnp.full((tok, 1), -3e38, F32),
                    jnp.zeros((tok, 1), F32),
                    jnp.zeros((tok, size + 16), F32),
                ),
            )
            out = (mixed / total).T[0:size, :]
            of_ref[i] = out
            o_ref[i] = out.astype(BF16)
            lse = jnp.broadcast_to(top + jnp.log(total) * LOG2E, (tok, 128)).T
            lse_ref[pl.ds(i, 1), :] = lse[0:1, :]

    fetch([of_ref], [of_out], sem)[0].wait()


def attend(ids, plan, segs, kvs):
    ways = len(kvs)
    _, size, tok = kvs[0].shape
    size = size // 3
    count = segs[0].shape[0]
    depth = 2 * size + LANES
    return pl.pallas_call(
        functools.partial(forward_kernel, ways, len(segs)),
        out_shape=(
            shaped((HEADS, size, tok), BF16),
            apart((HEADS, size, tok), F32),
            shaped((HEADS, tok), F32),
        ),
        in_specs=[smem(), smem()] + vmem(len(segs) + ways),
        out_specs=(vmem(1)[0], hbm(1)[0], vmem(1)[0]),
        scratch_shapes=[
            pltpu.VMEM((count, depth, tok), BF16),
            pltpu.VMEM((count, size + 16, tok), BF16),
            pltpu.VMEM((HEADS + 1, tok, depth), BF16),
            pltpu.VMEM((HEADS + 1, size + 16, tok), F32),
            pltpu.VMEM(segs[0].shape, jnp.int32),
            pltpu.VMEM((HEADS, size, tok), F32),
            pltpu.SemaphoreType.DMA((1,)),
        ],
        compiler_params=pltpu.CompilerParams(vmem_limit_bytes=16 * MIB),
        cost_estimate=cost(7),
        name="attend",
    )(ids, plan, *segs, *kvs)


def backward_kernel(ways, slots, final, texts, ids_ref, plan_ref, *refs):
    seg_refs, refs = refs[:texts], refs[texts:]
    q_ref, do_ref, of_in, lse_ref = refs[:4]
    refs = refs[4:]
    many = len(slots)
    kv_refs = refs[:many]
    refs = refs[many:]
    if final:
        part_ref, refs = refs[0], refs[1:]
    dq_ref = refs[0]
    dkv_refs = refs[1 : 1 + many]
    kx, vx, qx, dx, dk, dv, dq, seg_ref, of_ref, sem = refs[1 + many :]
    (copy,) = fetch([of_in], [of_ref], sem)
    seg_ref[...] = chosen(ids_ref, seg_refs)
    count, tok = seg_ref.shape
    size = do_ref.shape[1]
    rank = ids_ref[2]
    ones = (lax.broadcasted_iota(jnp.int32, (16, tok), 0) < 2).astype(F32).astype(BF16)
    for slot, kv_ref in zip(slots, kv_refs):

        @pl.loop(0, HEADS, unroll=UNROLL)
        def fill(h):
            chunk = chunk_of(h, slot, ways, rank)
            kx[chunk] = key_rows(kv_ref[h, size : 2 * size, :], seg_ref[pl.ds(chunk, 1), :])
            vx[chunk] = jnp.concatenate([kv_ref[h, 2 * size : 3 * size, :], ones], axis=0)
            dk[chunk] = jnp.zeros_like(dk[chunk])
            dv[chunk] = jnp.zeros_like(dv[chunk])

    copy.wait()

    @pl.loop(0, HEADS, unroll=UNROLL)
    def fill_query(i):
        lse = parts_of(-lse_ref[pl.ds(i, 1), :], 3)
        qx[i] = query_rows(q_ref[i, 0:size, :], seg_ref[pl.ds(i * ways + rank, 1), :], lse)
        do = do_ref[i].astype(F32)
        delta = parts_of(-jnp.sum(do * of_ref[i], axis=0, keepdims=True), 3)
        number = lax.broadcasted_iota(jnp.int32, (16, tok), 0)
        tail = jnp.where(number == 0, delta[0], jnp.where(number == 1, delta[1], 0.0))
        dx[i] = jnp.concatenate([do_ref[i], tail.astype(BF16)], axis=0).T
        dq[i] = part_ref[i] if final else jnp.zeros_like(dq[i])

    qx[HEADS] = query_rows(jnp.zeros((size, tok), BF16), jnp.full((1, tok), -1, jnp.int32), ())
    dx[HEADS] = jnp.zeros_like(dx[0])
    dq[HEADS] = jnp.zeros_like(dq[0])

    kind = 1 if slots == (0,) else 2
    length = list_size(count)

    @pl.loop(0, plan_ref[6 * length + kind])
    def group(g):
        tiles = tiles_of(plan_ref, kind, length, g)
        weights = [jnp.exp2(dot(qx[i], kx[c])) for i, c in tiles]
        pulls = [dot(dx[i], vx[c]) for i, c in tiles]
        scores = [(w * p).astype(BF16) for w, p in zip(weights, pulls)]
        for (i, c), w, ds in zip(tiles, weights, scores):
            j = jnp.minimum(i, HEADS - 1)
            dv[c] += dot(do_ref[j], w.astype(BF16))
            dk[c] += dot(q_ref[j, 0:size, :], ds)
            dq[i] += dot_t(kx[c, 0:size, :], ds)

    for slot, kv_ref, out in zip(slots, kv_refs, dkv_refs):

        @pl.loop(0, HEADS, unroll=UNROLL)
        def drain(h):
            chunk = chunk_of(h, slot, ways, rank)
            out[h, 0:size, :] = dk[chunk].astype(out.dtype)
            out[h, size : 2 * size, :] = dv[chunk].astype(out.dtype)

    @pl.loop(0, HEADS, unroll=UNROLL)
    def drain_query(i):
        if final:
            dq_ref[i] = (dq[i] * size**-0.5).astype(BF16)
        else:
            dq_ref[i] = dq[i]


def attend_back(ids, plan, segs, q, do, of, lse, kvs, ways, slots, part):
    many = len(slots)
    final = part is not None
    _, size, tok = do.shape
    count = segs[0].shape[0]
    depth = 2 * size + LANES
    return pl.pallas_call(
        functools.partial(backward_kernel, ways, slots, final, len(segs)),
        out_shape=(shaped((HEADS, size, tok), BF16 if final else F32),)
        + (shaped((HEADS, 2 * size, tok), F32 if slots == (0,) else BF16),) * many,
        in_specs=[smem(), smem()]
        + vmem(len(segs) + 2)
        + hbm(1)
        + vmem(1 + many + final),
        out_specs=tuple(vmem(1 + many)),
        scratch_shapes=[
            pltpu.VMEM((count, depth, tok), BF16),
            pltpu.VMEM((count, size + 16, tok), BF16),
            pltpu.VMEM((HEADS + 1, tok, depth), BF16),
            pltpu.VMEM((HEADS + 1, tok, size + 16), BF16),
            pltpu.VMEM((count, size, tok), F32),
            pltpu.VMEM((count, size, tok), F32),
            pltpu.VMEM((HEADS + 1, size, tok), F32),
            pltpu.VMEM(segs[0].shape, jnp.int32),
            pltpu.VMEM((HEADS, size, tok), F32),
            pltpu.SemaphoreType.DMA((1,)),
        ],
        compiler_params=pltpu.CompilerParams(vmem_limit_bytes=20 * MIB),
        cost_estimate=cost(7.5),
        name="attend_back",
    )(ids, plan, *segs, q, do, far(of), lse, *kvs, *((part,) if final else ()))


def normed(rows):
    centred = rows - jnp.mean(rows, axis=-1, keepdims=True)
    spread = jnp.mean(centred * centred, axis=-1, keepdims=True)
    inverse = lax.rsqrt(spread + EPS)
    return centred * inverse, inverse


def norm_back(n, inverse, gain, up):
    scaled = up * gain
    mean_one = jnp.mean(scaled, axis=-1, keepdims=True)
    mean_two = jnp.mean(scaled * n, axis=-1, keepdims=True)
    grad = inverse * (scaled - mean_one - n * mean_two)
    return grad, jnp.sum(up * n, axis=0, keepdims=True)


def middle_kernel(blocks, tile, ids_ref, ot_ref, x_ref, y_in, t_in, mask_ref, *refs):
    gains_refs, wo_refs, wu_refs, wd_refs = [refs[k * blocks : (k + 1) * blocks] for k in range(4)]
    (
        out_ref,
        gy_ref,
        gr_out,
        dot_ref,
        x1_ref,
        h_ref,
        df_ref,
        dz_ref,
        da_ref,
        small_ref,
        slope,
        acc,
        x1_turned,
        y_ref,
        t_ref,
        gr_ref,
        sems,
    ) = refs[4 * blocks :]
    copies = fetch([y_in, t_in], [y_ref, t_ref], sems)
    rows, feat = x_ref.shape
    wide = h_ref.shape[1]
    each = wide // blocks
    halves = [rows_of(ids_ref, blocks, j, feat) for j in range(blocks)]
    gains = gains_refs[0][...].astype(F32)
    if blocks == 2:
        other = gains_refs[1][...].astype(F32)
        gains = jnp.where(
            ids_ref[0] == 0,
            jnp.concatenate([gains, other], axis=1),
            jnp.concatenate([other, gains], axis=1),
        )
    g1, g2, g3 = gains[0:1], gains[1:2], gains[2:3]
    branch = dot(
        jnp.concatenate([ot_ref[rows_j, :] for rows_j in halves], axis=0).T,
        jnp.concatenate([ref[...] for ref in wo_refs], axis=0),
    )
    n1, r1 = normed(x_ref[...].astype(F32) + branch)
    x1 = n1 * g1
    x1_ref[...] = x1.astype(BF16)
    for j in range(blocks):
        size = feat // blocks
        x1_turned[:, j * size : (j + 1) * size] = x1_ref[:, halves[j]]
    acc[...] = jnp.zeros_like(acc)

    def hidden(k, t):
        start = 0 if blocks == 1 else (ids_ref[0] + k) % 2 * each
        return pl.ds(pl.multiple_of(start + t * tile, tile), tile)

    for k in range(blocks):

        @pl.loop(0, each // tile)
        def up(t):
            cols = hidden(k, t)
            z = dot(
                x1_turned[...], jnp.concatenate([ref[:, cols] for ref in wu_refs], axis=0)
            )
            z2 = z * z
            th = jnp.tanh(CORE * z * (1.0 + CUBE * z2))
            half = 0.5 * (1.0 + th)
            h = (z * half).astype(BF16)
            slope[:, cols] = half + 0.5 * z * (1.0 - th * th) * (CORE * (1.0 + 3.0 * CUBE * z2))
            h_ref[:, cols] = h
            acc[...] += dot(h, wd_refs[k][pl.ds(pl.multiple_of(t * tile, tile), tile), :])

    ffn = acc[...]
    n2, r2 = normed(x1 + ffn)
    for copy in copies:
        copy.wait()
    n3, r3 = normed(y_ref[...].astype(F32) + branch + ffn)
    result = n2 * g2 + n3 * g3
    out_ref[...] = result.astype(BF16)
    mask_row = mask_ref[...].astype(F32)
    mask = jnp.broadcast_to(mask_row, (8, rows)).T[:, 0:1]
    differ = result - t_ref[...].astype(F32)
    error = jnp.sum(mask * differ * differ)
    valid = jnp.sum(mask_row)
    upstream = 2.0 * mask * differ
    gy, dg3 = norm_back(n3, r3, g3, upstream)
    du, dg2 = norm_back(n2, r2, g2, upstream)
    gy_ref[...] = gy.astype(gy_ref.dtype)
    df_ref[...] = (du + gy).astype(BF16)
    acc[...] = du

    for k in range(blocks):

        @pl.loop(0, each // tile)
        def down(t):
            cols = hidden(k, t)
            block = wd_refs[k][pl.ds(pl.multiple_of(t * tile, tile), tile), :]
            dz = (dot_t(df_ref[...], block) * slope[:, cols]).astype(BF16)
            dz_ref[:, cols] = dz
            for j in range(blocks):
                acc[:, halves[j]] += dot_t(dz, wu_refs[j][:, cols])

    gr, dg1 = norm_back(n1, r1, g1, acc[...])
    gr_ref[...] = gr
    (copy,) = fetch([gr_ref], [gr_out], sems)
    da = (gr + gy).astype(BF16)
    da_ref[...] = da
    for j in range(blocks):
        dot_ref[halves[j], :] = dot_t(wo_refs[j][...], da).astype(BF16)
    lane = lax.broadcasted_iota(jnp.int32, (1, feat), 1)
    scalars = jnp.where(lane == 0, error, jnp.where(lane == 1, valid, 0.0))
    sums = jnp.concatenate([dg1, dg2, dg3, scalars], axis=0)
    small_ref[...] = jnp.concatenate([sums[:, : feat // 2], sums[:, feat // 2 :]], axis=0)
    copy.wait()


def middle(ids, ot, x, y, teacher, mask, gains, wo, wu, wd, gy_type):
    tok, feat = x.shape
    wide = wu[0].shape[1]
    blocks = len(wo)
    return pl.pallas_call(
        functools.partial(middle_kernel, blocks, min(512, wide // blocks)),
        out_shape=(
            shaped((tok, feat), BF16),
            shaped((tok, feat), gy_type),
            apart((tok, feat), F32),
            shaped((feat, tok), BF16),
            shaped((tok, feat), BF16),
            shaped((tok, wide), BF16),
            shaped((tok, feat), BF16),
            shaped((tok, wide), BF16),
            shaped((tok, feat), BF16),
            shaped((8, feat // 2), F32),
        ),
        in_specs=[smem()] + vmem(2) + hbm(2) + vmem(1 + 4 * blocks),
        out_specs=tuple(vmem(2) + hbm(1) + vmem(7)),
        scratch_shapes=[
            pltpu.VMEM((tok, wide), F32),
            pltpu.VMEM((tok, feat), F32),
            pltpu.VMEM((tok, feat), BF16),
            pltpu.VMEM((tok, feat), BF16),
            pltpu.VMEM((tok, feat), BF16),
            pltpu.VMEM((tok, feat), F32),
            pltpu.SemaphoreType.DMA((2,)),
        ],
        compiler_params=pltpu.CompilerParams(vmem_limit_bytes=24 * MIB),
        cost_estimate=cost(8),
        name="middle",
    )(ids, ot, x, far(y), far(teacher), mask, *gains, *wo, *wu, *wd)


def split_sum(values):
    high = values.astype(BF16)
    low = (values - high.astype(F32)).astype(BF16)
    return jnp.concatenate([high.astype(F32), low.astype(F32)], axis=0).astype(BF16)


def ffn_grad_kernel(
    tile, flip, ids_ref, x1_ref, h_ref, df_ref, dz_ref, ot_ref, da_ref, *refs
):
    got_ref, ref, xt = (None, *refs) if len(refs) == 2 else refs
    feat = x1_ref.shape[1]
    wide = h_ref.shape[1]
    blocks = ref.shape[0]
    half, wide_half = feat // 2, wide // 2
    step = half // blocks
    wide_step = wide_half // blocks
    parts = wide // feat
    side = (ids_ref[0] + flip) % 2
    rows = pl.ds(pl.multiple_of(side * half, half), half)
    xt[...] = x1_ref[:, rows].T

    def put(ref, first, base, size, values):
        for k in range(values.shape[0] // size):
            c = first + k
            at = INNER.index(c % len(INNER)) * (blocks // len(INNER)) + c // len(INNER)
            block = values[k * size : (k + 1) * size]
            if got_ref is not None:
                block = block + got_ref[at, base : base + size, :].astype(F32)
            ref[at, base : base + size, :] = block.astype(BF16)

    for j in range(parts):
        put(ref, 0, j * step, step, dot(xt[...], dz_ref[:, j * feat : (j + 1) * feat]))
    base = parts * step
    for j in range(wide_half // tile):
        cols = pl.ds(pl.multiple_of(side * wide_half + j * tile, tile), tile)
        put(ref, j * (tile // wide_step), base, wide_step, dot(h_ref[:, cols].T, df_ref[...]))
    base += wide_step
    put(ref, 0, base, step, dot(ot_ref[rows, :], da_ref[...]))


def ffn_grads(ids, blocks, flip, got, x1, h, df, dz, ot, da):
    tok, feat = x1.shape
    wide = h.shape[1]
    step = feat // (2 * blocks)
    depth = (wide // feat) * step + wide // (2 * blocks) + step
    return pl.pallas_call(
        functools.partial(ffn_grad_kernel, min(512, wide // 2), flip),
        out_shape=shaped((blocks, depth, feat), BF16),
        in_specs=[smem()] + vmem(6 + len(got)),
        out_specs=vmem(1)[0],
        scratch_shapes=[pltpu.VMEM((feat // 2, tok), BF16)],
        compiler_params=pltpu.CompilerParams(vmem_limit_bytes=16 * MIB),
        cost_estimate=cost(2),
        name="ffn_grads",
    )(ids, x1, h, df, dz, ot, da, *got)


def added(one, two, tail):
    total = one.astype(F32) + two.astype(F32)
    if not tail:
        return total.astype(BF16)
    depth = total.shape[0]
    high, low = depth - tail, depth - tail // 2
    return jnp.concatenate(
        [total[:high].astype(BF16), split_sum(total[high:low] + total[low:])], axis=0
    )


def halve_kernel(bit, under, tail, ids_ref, keep_ref, got_ref, next_ref, send_ref):
    mine = lax.rem(ids_ref[1] // bit, 2)

    @pl.loop(0, next_ref.shape[0])
    def one(b):
        for ref, which in ((send_ref, 1 - mine), (next_ref, mine)):
            at = (b // under) * 2 * under + which * under + lax.rem(b, under)
            ref[b] = added(keep_ref[at], got_ref[at], tail)


def halve(ids, bit, under, tail, keep, got):
    blocks, depth, feat = keep.shape
    return pl.pallas_call(
        functools.partial(halve_kernel, bit, under, tail),
        out_shape=(shaped((blocks // 2, depth, feat), BF16),) * 2,
        in_specs=[smem()] + vmem(2),
        out_specs=tuple(vmem(2)),
        compiler_params=pltpu.CompilerParams(vmem_limit_bytes=12 * MIB),
        cost_estimate=cost(1),
        name="halve",
    )(ids, keep, got)


def merge_kernel(tail, one_ref, two_ref, out_ref):
    for b in range(out_ref.shape[0]):
        out_ref[b] = added(one_ref[b], two_ref[b], tail)


def merge(tail, one, two):
    return pl.pallas_call(
        functools.partial(merge_kernel, tail),
        out_shape=shaped(one.shape, BF16),
        in_specs=vmem(2),
        out_specs=vmem(1)[0],
        cost_estimate=cost(0.5),
        name="merge",
    )(one, two)


def head_grad_kernel(ids_ref, back_ref, x_in, small_ref, keep_ref, send_ref, x_ref, sems):
    copies = fetch(
        [x_in.at[h] for h in range(HEADS)], [x_ref.at[h] for h in range(HEADS)], sems
    )
    total = 0.0
    for h in range(HEADS):
        copies[h].wait()
        total = total + dot(back_ref[RING[h]], x_ref[h])
    turned = total.T
    feat, size = turned.shape
    blocks, depth, lanes = keep_ref.shape
    step = feat // (2 * blocks)
    turned = jnp.concatenate([turned, jnp.zeros((feat, lanes - size), F32)], axis=1).astype(BF16)
    small = split_sum(small_ref[...])
    for flip in range(2):
        ref = (keep_ref, send_ref)[flip]
        for side in range(2):

            @pl.when(ids_ref[0] == (side + flip) % 2)
            def store():
                half = turned[side * feat // 2 : (side + 1) * feat // 2]
                ref[:, 0:step, :] = half.reshape(blocks, step, lanes)

        ref[:, step:depth, :] = jnp.broadcast_to(small[None], (blocks,) + small.shape)


def head_grads(ids, blocks, back, x, small):
    feat = x.shape[2]
    step = feat // (2 * blocks)
    lanes = small.shape[1]
    return pl.pallas_call(
        head_grad_kernel,
        out_shape=(shaped((blocks, step + 16, lanes), BF16),) * 2,
        in_specs=[smem()] + vmem(1) + hbm(1) + vmem(1),
        out_specs=tuple(vmem(2)),
        scratch_shapes=[
            pltpu.VMEM(x.shape, BF16),
            pltpu.SemaphoreType.DMA((HEADS,)),
        ],
        compiler_params=pltpu.CompilerParams(vmem_limit_bytes=16 * MIB),
        cost_estimate=cost(1.5),
        name="head_grads",
    )(ids, back, far(x), small)


def last_kernel(blocks, ids_ref, back_ref, gr_in, *refs):
    gx_ref, held, gr_ref, sems = refs[3 * blocks :]
    feat = gr_ref.shape[1]
    size = feat // HEADS
    each = feat // blocks
    targets = [
        held.at[part, pl.ds(j * each, each), :] for part in range(3) for j in range(blocks)
    ]
    copies = fetch([gr_in, *refs[: 3 * blocks]], [gr_ref, *targets], sems)
    grads = []
    for part in range(3):
        turned = jnp.concatenate(
            [back_ref[h, part * size : (part + 1) * size, :] for h in range(HEADS)], axis=0
        )
        grads.append(turned.T)
    for copy in copies:
        copy.wait()
    total = 0.0
    for part in range(3):
        total = total + dot_t(grads[part], held[part])
    for j in range(blocks):
        rows = rows_of(ids_ref, blocks, j, feat)
        gx_ref[:, rows] = (gr_ref[:, rows] + total[:, j * each : (j + 1) * each]).astype(
            gx_ref.dtype
        )


def last(ids, back, gr, weights, kind):
    flat = [block for weight in weights for block in weight]
    feat = gr.shape[1]
    return pl.pallas_call(
        functools.partial(last_kernel, len(weights[0])),
        out_shape=shaped(gr.shape, kind),
        in_specs=[smem()] + vmem(1) + hbm(1 + len(flat)),
        out_specs=vmem(1)[0],
        scratch_shapes=[
            pltpu.VMEM((3, feat, feat), BF16),
            pltpu.VMEM(gr.shape, F32),
            pltpu.SemaphoreType.DMA((1 + len(flat),)),
        ],
        compiler_params=pltpu.CompilerParams(vmem_limit_bytes=16 * MIB),
        cost_estimate=cost(1.5),
        name="last",
    )(ids, back, far(gr), *map(far, flat))


def finish_kernel(
    ids_ref,
    sums_ref,
    pieces_ref,
    gx_in,
    gy_in,
    out_in,
    loss_ref,
    out_ref,
    gx_ref,
    gy_ref,
    gq_ref,
    gk_ref,
    gv_ref,
    go_ref,
    gu_ref,
    gd_ref,
    g1_ref,
    g2_ref,
    g3_ref,
):
    step, feat = gq_ref.shape
    wide_step = gd_ref.shape[0]
    parts = gu_ref.shape[1] // feat
    size = feat // HEADS
    halves = jnp.sum(pieces_ref[:, step : step + 16, :].astype(F32), axis=0)
    halves = halves[0:8] + halves[8:16]
    small = jnp.concatenate([halves[0:4], halves[4:8]], axis=1)
    inverse = 1.0 / small[3:4, 1:2]
    loss_ref[...] = small[3:4, 0:1] * inverse
    gx_ref[...] = gx_in[...].astype(F32) * inverse
    gy_ref[...] = gy_in[...].astype(F32) * inverse
    out_ref[...] = out_in[...]
    main = sums_ref[0].astype(F32) * inverse
    for j in range(parts):
        gu_ref[:, j * feat : (j + 1) * feat] = main[j * step : (j + 1) * step]
    base = parts * step
    gd_ref[...] = main[base : base + wide_step]
    base += wide_step
    go_ref[...] = main[base : base + step]
    for h in range(HEADS):
        block = pieces_ref[h, 0:step, :].astype(F32) * inverse
        for part, ref in enumerate((gq_ref, gk_ref, gv_ref)):
            ref[:, h * size : (h + 1) * size] = block[:, part * size : (part + 1) * size]
    number = ids_ref[0] * (2 * pieces_ref.shape[0]) + ids_ref[1]
    eight = jnp.concatenate([small, small], axis=0) * inverse
    turned = pltpu.roll(eight, lax.rem(feat - number * step, feat), 1)
    g1_ref[...] = turned[0:1, 0:step]
    g2_ref[...] = turned[1:2, 0:step]
    g3_ref[...] = turned[2:3, 0:step]


def finish(ids, sums, pieces, gx, gy, result, wide):
    tok, feat = gx.shape
    step = pieces.shape[1] - 16
    return pl.pallas_call(
        finish_kernel,
        out_shape=(
            shaped((1, 1), F32),
            shaped((tok, feat), BF16),
            shaped((tok, feat), F32),
            shaped((tok, feat), F32),
            shaped((step, feat), F32),
            shaped((step, feat), F32),
            shaped((step, feat), F32),
            shaped((step, feat), F32),
            shaped((step, wide), F32),
            shaped((wide * step // feat, feat), F32),
            shaped((1, step), F32),
            shaped((1, step), F32),
            shaped((1, step), F32),
        ),
        in_specs=[smem()] + vmem(5),
        out_specs=tuple(vmem(13)),
        compiler_params=pltpu.CompilerParams(vmem_limit_bytes=12 * MIB),
        cost_estimate=cost(1.8),
        name="finish",
    )(ids, sums, pieces, gx, gy, result)


def body(
    state_x,
    state_y,
    teacher,
    segment_ids,
    valid_mask,
    w_query,
    w_key,
    w_value,
    w_out,
    w_up,
    w_down,
    gain_attn,
    gain_ffn,
    gain_final,
):
    _, tok, feat = state_x.shape
    size = feat // HEADS
    ctx = lax.axis_size("ctx")
    sides = lax.axis_size("dp")
    ways = ctx // HEADS
    groups = [[h * ways + r for h in range(HEADS)] for r in range(ways)]
    side, place = lax.axis_index("dp"), lax.axis_index("ctx")
    wide = w_up.shape[1]
    cross = sides == 2 and ways == 2 and (feat // (sides * ctx)) % 16 == 0
    rank = side if cross else place % ways
    flip = (side + place) % 2 if cross else 0
    ids = jnp.stack([jnp.int32(v) for v in (side, place, rank, flip)])
    both = ("dp", "ctx")

    def moved(block):
        if not cross:
            return block
        route = []
        for s in range(2):
            for c in range(ctx):
                route.append((s * ctx + c, (c % 2) * ctx + c - c % 2 + s))
        return lax.ppermute(block, both, route)

    def shared(block):
        if sides == 2:
            return [block, swap(block, "dp", 1)]
        return [lax.all_gather(block, "dp", axis=0, tiled=True)]

    def exchange(block):
        return lax.all_to_all(block, "ctx", 0, 0, axis_index_groups=groups, tiled=True)

    def around(block, distance):
        if cross:
            return swap(block, "dp", 1)
        route = []
        for g in range(HEADS):
            for r in range(ways):
                route.append((g * ways + r, g * ways + (r + distance) % ways))
        return lax.ppermute(block, "ctx", route)

    x = moved(state_x[0])
    attn_weights = [shared(w) for w in (w_query, w_key, w_value)]
    segs = [segment_ids.reshape(ctx, tok)]
    if cross:
        segs.append(swap(segs[0], "dp", 1))
    y, target, mask = moved(state_y[0]), moved(teacher[0]), moved(valid_mask)
    qkv = project(ids, x, attn_weights)
    plan = plan_of(ids, segs, ways, ctx, tok)
    qkv = exchange(qkv)
    qkv, plan, mask = lax.optimization_barrier((qkv, plan, mask))
    kvs = [qkv] + [around(qkv, j) for j in range(1, ways)]
    o, of, lse = attend(ids, plan, segs, kvs)
    gains = jnp.stack([gain_attn, gain_ffn, gain_final])
    if sides == 2:
        gains = shared(gains)
    else:
        gains = [lax.all_gather(gains, "dp", axis=1, tiled=True)]
    wo, wu, wd = shared(w_out), shared(w_up), shared(w_down)
    ot = exchange(o).reshape(feat, tok)
    result, gy, gr, do, x1, h, df, dz, da, small = middle(
        ids, ot, x, y, target, mask, gains, wo, wu, wd, BF16 if cross else F32
    )
    do = do.reshape(HEADS, size, tok)
    if cross:
        rings = [[h * ways + r for h in RING] for r in range(ways)]
        gathered = lax.all_gather(x, "ctx", axis=0, axis_index_groups=rings)
    do = exchange(do)
    if cross:
        arrays = (x1, h, df, dz, ot, da)
        send = ffn_grads(ids, ctx, 1, (), *arrays)
        sums = ffn_grads(ids, ctx, 0, (near(swap(send, "dp", 1)),), *arrays)
        do, sums, gathered = lax.optimization_barrier((do, sums, gathered))
        inner = [[g + k for k in INNER] for g in range(0, ctx, len(INNER))]
        outer = [list(range(k, ctx, len(INNER))) for k in range(len(INNER))]
        sums = lax.psum_scatter(
            sums, "ctx", scatter_dimension=0, axis_index_groups=inner, tiled=True
        )
    back_args = (ids, plan, segs, qkv, do, of, lse)
    part = jnp.zeros((HEADS, size, tok), F32)
    others = ()
    if ways > 1:
        part, *others = attend_back(*back_args, kvs[1:], ways, tuple(range(1, ways)), None)
    others = [around(other, -(j + 1)) for j, other in enumerate(others)]
    dq, own = attend_back(*back_args, kvs[:1], ways, (0,), part)
    for other in others:
        own = own + other.astype(F32)
    sent = jnp.concatenate([dq, own.astype(BF16)], axis=1)
    back = exchange(sent)
    if cross:
        mine, away = head_grads(ids, ctx, sent, gathered, small)
        mine, away = halve(ids, 1, 1, 16, mine, swap(away, "dp", 1))
        pieces = merge(16, mine, swap(away, "ctx", 1))
        result, gy = moved(result), moved(gy)
        pieces, sums = lax.optimization_barrier((pieces, sums))
        sums = lax.psum_scatter(
            sums, "ctx", scatter_dimension=0, axis_index_groups=outer, tiled=True
        )
        pieces = exchange(pieces)
        gx = moved(last(ids, back, gr, attn_weights, BF16))
        loss, result, gx, gy, gq, gk, gv, go, gu, gd, g1, g2, g3 = finish(
            ids, sums, pieces, gx, gy, result, wide
        )
        gains_out = [g.reshape(-1) for g in (g1, g2, g3)]
        loss = loss.reshape(())
    else:
        total = lax.psum(small, both)
        inverse = 1.0 / total[3, 1]
        loss = total[3, 0] * inverse

        def scattered(block):
            block = block * inverse
            return lax.psum_scatter(block, both, scatter_dimension=0, tiled=True)

        gx = last(ids, back, gr, attn_weights, F32)
        parts = [back[:, j * size : (j + 1) * size, :].reshape(feat, tok) for j in range(3)]
        gq, gk, gv = [scattered(dot_t(x.T, part)) for part in parts]
        go = scattered(dot(ot, da))
        gu = scattered(dot(x1.T, dz))
        gd = scattered(dot(h.T, df))
        gx, gy = gx * inverse, gy * inverse
        step = feat // (sides * ctx)
        number = ids[0] * ctx + ids[1]
        gains_out = [
            lax.dynamic_slice_in_dim(
                jnp.concatenate([total[k], total[k + 4]]) * inverse, number * step, step
            )
            for k in range(3)
        ]
    return (
        loss,
        result[None],
        gx[None],
        gy[None],
        gq,
        gk,
        gv,
        go,
        gu,
        gd,
        gains_out[0],
        gains_out[1],
        gains_out[2],
    )


def solution(mesh):
    tokens = P("dp", "ctx", None)
    rows = P("dp", None)
    spread = P(("dp", "ctx"), None)
    gain = P(("dp", "ctx"))
    return jax.shard_map(
        body,
        mesh=mesh,
        in_specs=(tokens,) * 3 + (rows, P("dp", "ctx")) + (rows,) * 6 + (P("dp"),) * 3,
        out_specs=(P(), tokens, tokens, tokens) + (spread,) * 6 + (gain,) * 3,
        check_vma=False,
    )
```

time: 238 us -> 182 us (0.76)
  blocking collectives: 48.1 us -> 0 us
  waiting for transfers between devices: 74.9 us -> 47.2 us
  starting transfers between devices: 30.9 us -> 47.4 us
  Pallas kernels: 52.7 us -> 58.4 us
    all_to_all x2 -> x0, blocking collectives: 34.9 us -> none  [exchange(): lax.all_to_all(block, 'ctx', 0, 0, axis_index_groups=groups, tiled=True)]
    ppermute x6 -> x13, waiting for transfers between devices: 39.1 us -> 9.81 us  [swap(): return lax.ppermute(block, axis, [(i, i ^ bit) for i in range(size)])]
    all_gather x5 -> x0, blocking collectives: 13.2 us -> none  [the longest x4 10.6 us: gathered(): return lax.all_gather(block, 'dp', axis=0, tiled=True)]
    all_to_all x3 -> x5, starting transfers between devices: 11.1 us -> 22.7 us  [exchange(): lax.all_to_all(block, 'ctx', 0, 0, axis_index_groups=groups, tiled=True)]
    ppermute x2 -> x7, waiting for transfers between devices: 10.9 us -> 0.02 us  [moved(): return lax.ppermute(block, both, route)]
    reduce_scatter x0 -> x2, waiting for transfers between devices: none -> 7.93 us  [the longest x1 5.91 us: body(): lax.psum_scatter(sums, 'ctx', scatter_dimension=0, axis_index_groups=oute...]
    ppermute x2 -> x7, starting transfers between devices: 3.77 us -> 11.5 us  [moved(): return lax.ppermute(block, both, route)]
    pallas_call x10 -> x12, Pallas kernels: 50.9 us -> 56.4 us  [the longest x2 15.6 us: attend_back(): pl.pallas_call(functools.partial(backward_kernel, ways, slots, final, len...]
  transfers between devices with their start and end apart: 14 -> 28, of which waited for: 9 -> 15; matrix products, arithmetic and copies ran while one was open for 2% -> 2% of each run, Pallas kernels for 17% -> 29%
where the time goes in v2:
time: 182 us; the launch traced here: 181 us
  Pallas kernels  58.4 us (32%)
  starting transfers between devices  47.4 us (26%)
  waiting for transfers between devices  47.2 us (26%)
  between operations  14.3 us (8%)
  local copies, waits for them, and re-layouts  11.4 us (6%)
  other arithmetic  1.98 us (1%)
    all_to_all x5, waiting for transfers between devices, exchange(): lax.all_to_all(block, 'ctx', 0, 0, axis_index_groups=groups, tiled=True)  26.6 us
    all_to_all x5, starting transfers between devices, exchange(): lax.all_to_all(block, 'ctx', 0, 0, axis_index_groups=groups, tiled=True)  22.7 us
    pallas_call x2, Pallas kernels, attend_back(): pl.pallas_call(functools.partial(backward_kernel, ways, slots, final, len...  15.6 us
    ppermute x13, starting transfers between devices, swap(): return lax.ppermute(block, axis, [(i, i ^ bit) for i in range(size)])  13.1 us
    ppermute x7, starting transfers between devices, moved(): return lax.ppermute(block, both, route)  11.5 us
    unnamed x74, local copies, waits for them, and re-layouts  11.4 us
    pallas_call x1, Pallas kernels, middle(): pl.pallas_call(functools.partial(middle_kernel, blocks, min(512, wide //...  10.6 us
    ppermute x13, waiting for transfers between devices, swap(): return lax.ppermute(block, axis, [(i, i ^ bit) for i in range(size)])  9.81 us
  transfers between devices with their start and end apart: 28, of which 15 were waited for; matrix products, arithmetic and copies ran while one was open for 2% of the time, Pallas kernels for 29%

profile of v2, /device:TPU:0, one launch (start us, length us, event | category | flops | bytes accessed | tf_op | source)
XLA Modules:
  0.0 180.7 jit_solution(13923414685473984050)
XLA Ops:
  7.2 1.6 collective-permute-start
  8.8 3.4 %collective-permute-start.1 = (bf16[256,512]{1,0:T(8,128)(2,1)}, bf16[256,512]{1,0:T(8,128)(2,1)S(1)}, u32[]{:S(2)}, u32[]{:S(2)}) collective-permute-start(bf16[256,512]{1,0:T(8,128)(2,1)} %refs_0_.3), channel_id=1, source_target_pairs={{0,16},{16,0},{1,17},{17,1},{2,18},{18,2},{3,19},{19,3},{4,20},{20... | collective-permute-start | bytes 786440 | tf_op jit(solution)/shard_map/ppermute | solution.py:74
  15.4 3.7 %project.1 = bf16[8,192,256]{2,1,0:T(8,128)(2,1)} custom-call(s32[4]{0:T(128)S(1)} %pad_add_fusion.ids_ref, bf16[256,512]{1,0:T(8,128)(2,1)S(1)} %collective-permute-done.x_ref, bf16[256,512]{1,0:T(8,128)(2,1)} %refs_0_.3, bf16[256,512]{1,0:T(8,128)(2,1)} %copy-done.28, bf16[256,512]{1,0:T(8,128)(2,1)} %refs_2_.5, bf16[256,512]{1,0:T(8,128)(2,1)} %copy-done.29, ...), custom_call_target="tpu_custom_call" | custom-call | flops 1540000000 | bytes 1024 | tf_op jit(solution)/shard_map/project/pallas_call | solution.py:117
  19.1 5.8 %all-to-all-start = ((bf16[8,192,256]{2,1,0:T(8,128)(2,1)}), bf16[8,192,256]{2,1,0:T(8,128)(2,1)S(1)}, u32[]{:S(2)}, u32[]{:S(2)}) async-start(bf16[8,192,256]{2,1,0:T(8,128)(2,1)} %project.1), calls=%async_computation | async-start | bytes 1572864 | tf_op jit(solution)/shard_map/all_to_all | solution.py:942
  26.3 2.3 %collective-permute-start.4 = (s32[16,256]{1,0:T(8,128)S(1)}, s32[16,256]{1,0:T(8,128)S(1)}, u32[]{:S(2)}, u32[]{:S(2)}) collective-permute-start(s32[16,256]{1,0:T(8,128)S(1)} %reshape.50.refs_0_), channel_id=1, source_target_pairs={{0,16},{16,0},{1,17},{17,1},{2,18},{18,2},{3,19},{19,3},{4,20},{20... | collective-permute-start | bytes 49160 | tf_op jit(solution)/shard_map/ppermute | solution.py:74
  30.1 3.1 %plan.1.plan_ref = s32[872]{0:T(1024)} custom-call(s32[4]{0:T(128)} %copy-done.2, s32[4096]{0:T(1024)} %bitcast.23, s32[4096]{0:T(1024)} %bitcast.24), custom_call_target="tpu_custom_call" | custom-call | flops 1100000000 | bytes 1024 | tf_op jit(solution)/shard_map/plan/pallas_call | solution.py:208
  33.2 12.2 %all-to-all-done.refs_2_.refs_6_ = bf16[8,192,256]{2,1,0:T(8,128)(2,1)S(1)} async-done(((bf16[8,192,256]{2,1,0:T(8,128)(2,1)}), bf16[8,192,256]{2,1,0:T(8,128)(2,1)S(1)}, u32[]{:S(2)}, u32[]{:S(2)}) %all-to-all-start) | async-done | bytes 786464 | tf_op jit(solution)/shard_map/all_to_all | solution.py:942
  46.9 2.5 %collective-permute-done.6.refs_3_.refs_6_ = bf16[8,192,256]{2,1,0:T(8,128)(2,1)S(1)} collective-permute-done((bf16[8,192,256]{2,1,0:T(8,128)(2,1)S(1)}, bf16[8,192,256]{2,1,0:T(8,128)(2,1)S(1)}, u32[]{:S(2)}, u32[]{:S(2)}) %collective-permute-start.6) | collective-permute-done | bytes 786464 | tf_op jit(solution)/shard_map/ppermute | solution.py:74
  50.1 8.4 %attend.1 = (bf16[8,64,256]{2,1,0:T(8,128)(2,1)}, f32[8,64,256]{2,1,0:T(8,128)}, f32[8,256]{1,0:T(8,128)S(1)}) custom-call(s32[4]{0:T(128)S(1)} %copy-done.3, s32[872]{0:T(1024)S(1)} %copy-done.25, s32[16,256]{1,0:T(8,128)S(1)} %reshape.50.refs_0_, s32[16,256]{1,0:T(8,128)S(1)} %collective-permute-done.4.refs_1_, ...), custom_call_target="tpu_custom_call" | custom-call | flops 7699999744 | bytes 1024 | tf_op jit(solution)/shard_map/attend/pallas_call | solution.py:325
  58.4 3.4 %all-to-all-start.1 = ((bf16[8,64,256]{2,1,0:T(8,128)(2,1)}), bf16[8,64,256]{2,1,0:T(8,128)(2,1)S(1)}, u32[]{:S(2)}, u32[]{:S(2)}) async-start(bf16[8,64,256]{2,1,0:T(8,128)(2,1)} %get-tuple-element.57), calls=%async_computation.1 | async-start | bytes 524288 | tf_op jit(solution)/shard_map/all_to_all | solution.py:942
  62.6 3.6 %collective-permute-start.7 = (bf16[256,512]{1,0:T(8,128)(2,1)}, bf16[256,512]{1,0:T(8,128)(2,1)}, u32[]{:S(2)}, u32[]{:S(2)}) collective-permute-start(bf16[256,512]{1,0:T(8,128)(2,1)} %bitcast.27), channel_id=1, source_target_pairs={{0,0},{1,16},{2,2},{3,18},{4,4},{5,20},{6,6},{7,22},{8,8},{9,24},{... | collective-permute-start | bytes 786440 | tf_op jit(solution)/shard_map/ppermute | solution.py:934
  66.2 3.6 %collective-permute-start.8 = (bf16[256,512]{1,0:T(8,128)(2,1)}, bf16[256,512]{1,0:T(8,128)(2,1)}, u32[]{:S(2)}, u32[]{:S(2)}) collective-permute-start(bf16[256,512]{1,0:T(8,128)(2,1)} %bitcast.28), channel_id=1, source_target_pairs={{0,0},{1,16},{2,2},{3,18},{4,4},{5,20},{6,6},{7,22},{8,8},{9,24},{... | collective-permute-start | bytes 786440 | tf_op jit(solution)/shard_map/ppermute | solution.py:934
  71.3 10.6 %middle.1 = (bf16[256,512]{1,0:T(8,128)(2,1)S(1)}, bf16[256,512]{1,0:T(8,128)(2,1)S(1)}, f32[256,512]{1,0:T(8,128)}, bf16[512,256]{1,0:T(8,128)(2,1)}, bf16[256,...) custom-call(s32[4]{0:T(128)S(1)} %copy-done.3, ...), custom_call_target="tpu_custom_call" | custom-call | flops 8800000000 | bytes 1024 | tf_op jit(solution)/shard_map/middle/pallas_call | solution.py:588
  82.0 2.8 %ffn_grads.2 = bf16[16,144,512]{2,1,0:T(8,128)(2,1)} custom-call(s32[4]{0:T(128)S(1)} %copy-done.3, bf16[256,512]{1,0:T(8,128)(2,1)S(1)} %get-tuple-element.60.x1_ref, bf16[256,2048]{1,0:T(8,128)(2,1)S(1)} %get-tuple-element.61.h_ref, bf16[256,512]{1,0:T(8,128)(2,1)S(1)} %get-tuple-element.62.df_ref, bf16[256,2048]{1,0:T(8,128)(2,1)S(1)} %get-tuple-element.63.dz_ref, ...), custom_call_target="tpu_custom_call" | custom-call | flops 2200000000 | bytes 1024 | tf_op jit(solution)/shard_map/ffn_grads/pallas_call | solution.py:664
  84.8 3.2 %collective-permute-start.13 = (bf16[16,144,512]{2,1,0:T(8,128)(2,1)}, bf16[16,144,512]{2,1,0:T(8,128)(2,1)}, u32[]{:S(2)}, u32[]{:S(2)}) collective-permute-start(bf16[16,144,512]{2,1,0:T(8,128)(2,1)} %ffn_grads.2), channel_id=1, source_target_pairs={{0,16},{16,0},{1,17},{17,1},{2,18},{18,2},{3,19},{19,3},{4,20},{20... | collective-permute-start | bytes 7077896 | tf_op jit(solution)/shard_map/ppermute | solution.py:74
  88.0 5.9 %all-to-all-start.2 = ((bf16[8,64,256]{2,1,0:T(8,128)(2,1)}), bf16[8,64,256]{2,1,0:T(8,128)(2,1)S(1)}, u32[]{:S(2)}, u32[]{:S(2)}) async-start(bf16[8,64,256]{2,1,0:T(8,128)(2,1)} %bitcast.8), calls=%async_computation.2 | async-start | bytes 524288 | tf_op jit(solution)/shard_map/all_to_all | solution.py:942
  99.3 4.0 %ffn_grads.3 = bf16[16,144,512]{2,1,0:T(8,128)(2,1)} custom-call(s32[4]{0:T(128)S(1)} %copy-done.3, bf16[256,512]{1,0:T(8,128)(2,1)S(1)} %copy-done.19, bf16[256,2048]{1,0:T(8,128)(2,1)S(1)} %copy-done.15, bf16[256,512]{1,0:T(8,128)(2,1)S(1)} %copy-done.21, bf16[256,2048]{1,0:T(8,128)(2,1)S(1)} %copy-done.17, bf16[512,256]{1,0:T(8,128)(2,1)S(1)} %bitcast.21, ...), custom_call_target="tpu_custom_call" | custom-call | flops 2200000000 | bytes 1024 | tf_op jit(solution)/shard_map/ffn_grads/pallas_call | solution.py:664
  103.2 2.8 %all-to-all-done.2.refs_3_ = bf16[8,64,256]{2,1,0:T(8,128)(2,1)S(1)} async-done(((bf16[8,64,256]{2,1,0:T(8,128)(2,1)}), bf16[8,64,256]{2,1,0:T(8,128)(2,1)S(1)}, u32[]{:S(2)}, u32[]{:S(2)}) %all-to-all-start.2) | async-done | bytes 262176 | tf_op jit(solution)/shard_map/all_to_all | solution.py:942
  106.0 2.7 %all-gather.3.cloned.1.call-done = bf16[2048,512]{1,0:T(8,128)(2,1)} async-done(((bf16[256,512]{1,0:T(8,128)(2,1)}), bf16[2048,512]{1,0:T(8,128)(2,1)}) %all-gather.3.cloned.1.call-update) | async-done | bytes 2097168 | tf_op jit(solution)/shard_map/all_gather | solution.py:978
  108.8 7.7 %attend_back.2 = (f32[8,64,256]{2,1,0:T(8,128)S(1)}, bf16[8,128,256]{2,1,0:T(8,128)(2,1)S(1)}) custom-call(s32[4]{0:T(128)S(1)} %copy-done.3, s32[872]{0:T(1024)S(1)} %copy-done.26, s32[16,256]{1,0:T(8,128)S(1)} %reshape.50.refs_0_, s32[16,256]{1,0:T(8,128)S(1)} %collective-permute-done.4.refs_1_, bf16[8,192,256]{2,1,0:T(8,128)(2,1)S(1)} %all-to-all-done.refs_2_.refs_6_, ...), custom_call_target="tpu_custom_call" | custom-call | flops 8249999872 | bytes 1024 | tf_op jit(solution)/shard_map/attend_back/pallas_call | solution.py:431
  116.6 7.9 %attend_back.3 = (bf16[8,64,256]{2,1,0:T(8,128)(2,1)S(1)}, f32[8,128,256]{2,1,0:T(8,128)S(1)}) custom-call(s32[4]{0:T(128)S(1)} %copy-done.3, s32[872]{0:T(1024)S(1)} %copy-done.26, s32[16,256]{1,0:T(8,128)S(1)} %reshape.50.refs_0_, s32[16,256]{1,0:T(8,128)S(1)} %collective-permute-done.4.refs_1_, bf16[8,192,256]{2,1,0:T(8,128)(2,1)S(1)} %all-to-all-done.refs_2_.refs_6_, ...), custom_call_target="tpu_custom_call" | custom-call | flops 8249999872 | bytes 1024 | tf_op jit(solution)/shard_map/attend_back/pallas_call | solution.py:431
  125.6 4.0 %all-to-all-start.4 = ((bf16[8,192,256]{2,1,0:T(8,128)(2,1)}), bf16[8,192,256]{2,1,0:T(8,128)(2,1)S(1)}, u32[]{:S(2)}, u32[]{:S(2)}) async-start(bf16[8,192,256]{2,1,0:T(8,128)(2,1)} %pad_maximum_fusion.back_ref), calls=%async_computation.6 | async-start | bytes 1572864 | tf_op jit(solution)/shard_map/all_to_all | solution.py:942
  129.7 3.2 %head_grads.1 = (bf16[16,32,256]{2,1,0:T(8,128)(2,1)S(1)}, bf16[16,32,256]{2,1,0:T(8,128)(2,1)S(1)}) custom-call(s32[4]{0:T(128)S(1)} %copy-done.3, bf16[8,192,256]{2,1,0:T(8,128)(2,1)} %pad_maximum_fusion.back_ref, bf16[8,256,512]{2,1,0:T(8,128)(2,1)} %bitcast.25, f32[8,256]{1,0:T(8,128)S(1)} %get-tuple-element.73.small_ref), custom_call_target="tpu_custom_call" | custom-call | flops 1650000000 | bytes 1024 | tf_op jit(solution)/shard_map/head_grads/pallas_call | solution.py:756
  137.3 4.2 %collective-permute-done.16.two_ref = bf16[8,32,256]{2,1,0:T(8,128)(2,1)S(1)} collective-permute-done((bf16[8,32,256]{2,1,0:T(8,128)(2,1)S(1)}, bf16[8,32,256]{2,1,0:T(8,128)(2,1)S(1)}, u32[]{:S(2)}, u32[]{:S(2)}) %collective-permute-start.16) | collective-permute-done | bytes 131104 | tf_op jit(solution)/shard_map/ppermute | solution.py:74
  142.1 1.7 merge.1
  143.8 2.0 %reduce-scatter.3.cloned.1.call-done = bf16[4,144,512]{2,1,0:T(8,128)(2,1)} async-done(((bf16[16,144,512]{2,1,0:T(8,128)(2,1)}), bf16[4,144,512]{2,1,0:T(8,128)(2,1)}) %reduce-scatter.3.cloned.1.call-update) | async-done | bytes 589840 | tf_op jit(solution)/shard_map/reduce_scatter | solution.py:987
  147.2 2.1 %all-to-all-done.4.back_ref = bf16[8,192,256]{2,1,0:T(8,128)(2,1)S(1)} async-done(((bf16[8,192,256]{2,1,0:T(8,128)(2,1)}), bf16[8,192,256]{2,1,0:T(8,128)(2,1)S(1)}, u32[]{:S(2)}, u32[]{:S(2)}) %all-to-all-start.4) | async-done | bytes 786464 | tf_op jit(solution)/shard_map/all_to_all | solution.py:942
  149.3 2.7 %last.1 = bf16[256,512]{1,0:T(8,128)(2,1)S(1)} custom-call(s32[4]{0:T(128)S(1)} %copy-done.3, bf16[8,192,256]{2,1,0:T(8,128)(2,1)S(1)} %all-to-all-done.4.back_ref, f32[256,512]{1,0:T(8,128)} %get-tuple-element.81.gr_in, bf16[256,512]{1,0:T(8,128)(2,1)} %refs_0_.3, bf16[256,512]{1,0:T(8,128)(2,1)} %copy-done.28, bf16[256,512]{1,0:T(8,128)(2,1)} %refs_2_.5, ...), custom_call_target="tpu_custom_call" | custom-call | flops 1650000000 | bytes 1024 | tf_op jit(solution)/shard_map/last/pallas_call | solution.py:801
  152.7 3.6 %all-to-all-start.3 = ((bf16[8,32,256]{2,1,0:T(8,128)(2,1)}), bf16[8,32,256]{2,1,0:T(8,128)(2,1)S(1)}, u32[]{:S(2)}, u32[]{:S(2)}) async-start(bf16[8,32,256]{2,1,0:T(8,128)(2,1)} %merge.1), calls=%async_computation.5 | async-start | bytes 262144 | tf_op jit(solution)/shard_map/all_to_all | solution.py:942
  156.3 9.0 %all-to-all-done.3.pieces_ref = bf16[8,32,256]{2,1,0:T(8,128)(2,1)S(1)} async-done(((bf16[8,32,256]{2,1,0:T(8,128)(2,1)}), bf16[8,32,256]{2,1,0:T(8,128)(2,1)S(1)}, u32[]{:S(2)}, u32[]{:S(2)}) %all-to-all-start.3) | async-done | bytes 131104 | tf_op jit(solution)/shard_map/all_to_all | solution.py:942
  165.4 5.9 %reduce-scatter.5.cloned.1.call-done.sums_ref = bf16[1,144,512]{2,1,0:T(8,128)(2,1)} async-done(((bf16[4,144,512]{2,1,0:T(8,128)(2,1)}), bf16[1,144,512]{2,1,0:T(8,128)(2,1)}) %reduce-scatter.5.cloned.1.call-update) | async-done | bytes 147472 | tf_op jit(solution)/shard_map/reduce_scatter | solution.py:1007
  172.2 1.9 %finish.1 = (f32[1,1]{1,0:T(1,128)}, bf16[256,512]{1,0:T(8,128)(2,1)}, f32[256,512]{1,0:T(8,128)}, f32[256,512]{1,0:T(8,128)}, f32[16,512]{1,0:T(8,128)}, /*inde...) custom-call(s32[4]{0:T(128)S(1)} %copy-done.3, ...), custom_call_target="tpu_custom_call" | custom-call | flops 1980000000 | bytes 1024 | tf_op jit(solution)/shard_map/finish/pallas_call | solution.py:872
  (123 shorter events, 24.8 us)
Async XLA Ops:
  7.2 5.6 %collective-permute-start = (bf16[256,512]{1,0:T(8,128)(2,1)}, bf16[256,512]{1,0:T(8,128)(2,1)S(1)}, u32[]{:S(2)}, u32[]{:S(2)}) collective-permute-start(bf16[256,512]{1,0:T(8,128)(2,1)} %bitcast.26), channel_id=1, source_target_pairs={{0,0},{1,16},{2,2},{3,18},{4,4},{5,20},{6,6},{7,22},{8,8},{9,24},{... | collective-permute-start | bytes 786440 | tf_op jit(solution)/shard_map/ppermute | solution.py:934
  8.8 4.8 %collective-permute-start.1 = (bf16[256,512]{1,0:T(8,128)(2,1)}, bf16[256,512]{1,0:T(8,128)(2,1)S(1)}, u32[]{:S(2)}, u32[]{:S(2)}) collective-permute-start(bf16[256,512]{1,0:T(8,128)(2,1)} %refs_0_.3), channel_id=1, source_target_pairs={{0,16},{16,0},{1,17},{17,1},{2,18},{18,2},{3,19},{19,3},{4,20},{20... | collective-permute-start | bytes 786440 | tf_op jit(solution)/shard_map/ppermute | solution.py:74
  12.2 1.7 collective-permute-start.2
  12.3 2.0 %collective-permute-start.3 = (bf16[256,512]{1,0:T(8,128)(2,1)}, bf16[256,512]{1,0:T(8,128)(2,1)S(1)}, u32[]{:S(2)}, u32[]{:S(2)}) collective-permute-start(bf16[256,512]{1,0:T(8,128)(2,1)} %refs_4_.5), channel_id=1, source_target_pairs={{0,16},{16,0},{1,17},{17,1},{2,18},{18,2},{3,19},{19,3},{4,20},{20... | collective-permute-start | bytes 786440 | tf_op jit(solution)/shard_map/ppermute | solution.py:74
  19.1 26.3 %all-to-all-start = ((bf16[8,192,256]{2,1,0:T(8,128)(2,1)}), bf16[8,192,256]{2,1,0:T(8,128)(2,1)S(1)}, u32[]{:S(2)}, u32[]{:S(2)}) async-start(bf16[8,192,256]{2,1,0:T(8,128)(2,1)} %project.1), calls=%async_computation | async-start | bytes 1572864 | tf_op jit(solution)/shard_map/all_to_all | solution.py:942
  26.3 3.2 %collective-permute-start.4 = (s32[16,256]{1,0:T(8,128)S(1)}, s32[16,256]{1,0:T(8,128)S(1)}, u32[]{:S(2)}, u32[]{:S(2)}) collective-permute-start(s32[16,256]{1,0:T(8,128)S(1)} %reshape.50.refs_0_), channel_id=1, source_target_pairs={{0,16},{16,0},{1,17},{17,1},{2,18},{18,2},{3,19},{19,3},{4,20},{20... | collective-permute-start | bytes 49160 | tf_op jit(solution)/shard_map/ppermute | solution.py:74
  28.6 4.6 %collective-permute-start.5 = (s32[1,256]{1,0:T(1,128)S(1)}, s32[1,256]{1,0:T(1,128)S(1)}, u32[]{:S(2)}, u32[]{:S(2)}) collective-permute-start(s32[1,256]{1,0:T(1,128)S(1)} %copy-done.32), channel_id=1, source_target_pairs={{0,0},{1,16},{2,2},{3,18},{4,4},{5,20},{6,6},{7,22},{8,8},{9,24},{... | collective-permute-start | bytes 3080 | tf_op jit(solution)/shard_map/ppermute | solution.py:934
  30.1 31.9 %copy-start.33 = (bf16[256]{0:T(256)(128)(2,1)S(1)}, bf16[256]{0:T(256)(128)(2,1)}, u32[]{:S(2)}) copy-start(bf16[256]{0:T(256)(128)(2,1)} %param.25) | copy-start | bytes 1540
  30.1 31.9 %copy-start.34 = (bf16[256]{0:T(256)(128)(2,1)S(1)}, bf16[256]{0:T(256)(128)(2,1)}, u32[]{:S(2)}) copy-start(bf16[256]{0:T(256)(128)(2,1)} %param.26) | copy-start | bytes 1540
  30.1 31.9 %copy-start.35 = (bf16[256]{0:T(256)(128)(2,1)S(1)}, bf16[256]{0:T(256)(128)(2,1)}, u32[]{:S(2)}) copy-start(bf16[256]{0:T(256)(128)(2,1)} %param.27) | copy-start | bytes 1540
  33.2 37.1 %copy-start.1 = (bf16[256,512]{1,0:T(8,128)(2,1)S(1)}, bf16[256,512]{1,0:T(8,128)(2,1)}, u32[]{:S(2)}) copy-start(bf16[256,512]{1,0:T(8,128)(2,1)} %copy-done) | copy-start | bytes 786436
  45.4 4.0 %collective-permute-start.6 = (bf16[8,192,256]{2,1,0:T(8,128)(2,1)S(1)}, bf16[8,192,256]{2,1,0:T(8,128)(2,1)S(1)}, u32[]{:S(2)}, u32[]{:S(2)}) collective-permute-start(bf16[8,192,256]{2,1,0:T(8,128)(2,1)S(1)} %all-to-all-done.refs_2_.refs_6_), channel_id=1, source_target_pairs={{0,16},{16,0},{1,17},{17,1},{2,18},{18,2},{3,19},{19,3},{4,20},{20... | collective-permute-start | bytes 2359304 | tf_op jit(solution)/shard_map/ppermute | solution.py:74
  46.4 23.4 %collective-permute-start.11 = (bf16[256,2048]{1,0:T(8,128)(2,1)S(1)}, bf16[256,2048]{1,0:T(8,128)(2,1)}, u32[]{:S(2)}, u32[]{:S(2)}) collective-permute-start(bf16[256,2048]{1,0:T(8,128)(2,1)S(1)} %copy-done.4), channel_id=1, source_target_pairs={{0,16},{16,0},{1,17},{17,1},{2,18},{18,2},{3,19},{19,3},{4,20},{20... | collective-permute-start | bytes 3145736 | tf_op jit(solution)/shard_map/ppermute | solution.py:74
  46.4 23.4 %collective-permute-start.12 = (bf16[1024,512]{1,0:T(8,128)(2,1)S(1)}, bf16[1024,512]{1,0:T(8,128)(2,1)}, u32[]{:S(2)}, u32[]{:S(2)}) collective-permute-start(bf16[1024,512]{1,0:T(8,128)(2,1)S(1)} %copy-done.5), channel_id=1, source_target_pairs={{0,16},{16,0},{1,17},{17,1},{2,18},{18,2},{3,19},{19,3},{4,20},{20... | collective-permute-start | bytes 3145736 | tf_op jit(solution)/shard_map/ppermute | solution.py:74
  58.4 11.9 %all-to-all-start.1 = ((bf16[8,64,256]{2,1,0:T(8,128)(2,1)}), bf16[8,64,256]{2,1,0:T(8,128)(2,1)S(1)}, u32[]{:S(2)}, u32[]{:S(2)}) async-start(bf16[8,64,256]{2,1,0:T(8,128)(2,1)} %get-tuple-element.57), calls=%async_computation.1 | async-start | bytes 524288 | tf_op jit(solution)/shard_map/all_to_all | solution.py:942
  61.9 46.9 %all-gather.3.cloned.1.call-start = ((), (), s32[]{:S(2)}) async-start(), calls=%async_computation.9 | async-start | bytes 2359296 | tf_op jit(solution)/shard_map/all_gather | solution.py:978
  62.0 4.2 %collective-permute-start.9 = (bf16[3,256]{1,0:T(4,128)(2,1)S(1)}, bf16[3,256]{1,0:T(4,128)(2,1)S(1)}, u32[]{:S(2)}, u32[]{:S(2)}) collective-permute-start(bf16[3,256]{1,0:T(4,128)(2,1)S(1)} %pad_maximum_fusion.1.refs_0_), channel_id=1, source_target_pairs={{0,16},{16,0},{1,17},{17,1},{2,18},{18,2},{3,19},{19,3},{4,20},{20... | collective-permute-start | bytes 4616 | tf_op jit(solution)/shard_map/ppermute | solution.py:74
  62.1 7.7 %collective-permute-start.10 = (bf16[256,512]{1,0:T(8,128)(2,1)}, bf16[256,512]{1,0:T(8,128)(2,1)}, u32[]{:S(2)}, u32[]{:S(2)}) collective-permute-start(bf16[256,512]{1,0:T(8,128)(2,1)} %refs_2_.4), channel_id=1, source_target_pairs={{0,16},{16,0},{1,17},{17,1},{2,18},{18,2},{3,19},{19,3},{4,20},{20... | collective-permute-start | bytes 786440 | tf_op jit(solution)/shard_map/ppermute | solution.py:74
  62.6 7.2 %collective-permute-start.7 = (bf16[256,512]{1,0:T(8,128)(2,1)}, bf16[256,512]{1,0:T(8,128)(2,1)}, u32[]{:S(2)}, u32[]{:S(2)}) collective-permute-start(bf16[256,512]{1,0:T(8,128)(2,1)} %bitcast.27), channel_id=1, source_target_pairs={{0,0},{1,16},{2,2},{3,18},{4,4},{5,20},{6,6},{7,22},{8,8},{9,24},{... | collective-permute-start | bytes 786440 | tf_op jit(solution)/shard_map/ppermute | solution.py:934
  66.2 3.6 %collective-permute-start.8 = (bf16[256,512]{1,0:T(8,128)(2,1)}, bf16[256,512]{1,0:T(8,128)(2,1)}, u32[]{:S(2)}, u32[]{:S(2)}) collective-permute-start(bf16[256,512]{1,0:T(8,128)(2,1)} %bitcast.28), channel_id=1, source_target_pairs={{0,0},{1,16},{2,2},{3,18},{4,4},{5,20},{6,6},{7,22},{8,8},{9,24},{... | collective-permute-start | bytes 786440 | tf_op jit(solution)/shard_map/ppermute | solution.py:934
  84.8 9.1 %collective-permute-start.13 = (bf16[16,144,512]{2,1,0:T(8,128)(2,1)}, bf16[16,144,512]{2,1,0:T(8,128)(2,1)}, u32[]{:S(2)}, u32[]{:S(2)}) collective-permute-start(bf16[16,144,512]{2,1,0:T(8,128)(2,1)} %ffn_grads.2), channel_id=1, source_target_pairs={{0,16},{16,0},{1,17},{17,1},{2,18},{18,2},{3,19},{19,3},{4,20},{20... | collective-permute-start | bytes 7077896 | tf_op jit(solution)/shard_map/ppermute | solution.py:74
  88.0 18.0 %all-to-all-start.2 = ((bf16[8,64,256]{2,1,0:T(8,128)(2,1)}), bf16[8,64,256]{2,1,0:T(8,128)(2,1)S(1)}, u32[]{:S(2)}, u32[]{:S(2)}) async-start(bf16[8,64,256]{2,1,0:T(8,128)(2,1)} %bitcast.8), calls=%async_computation.2 | async-start | bytes 524288 | tf_op jit(solution)/shard_map/all_to_all | solution.py:942
  93.9 51.9 %reduce-scatter.3.cloned.1.call-start = ((), (), s32[]{:S(2)}) async-start(), calls=%async_computation.7 | async-start | bytes 2949120 | tf_op jit(solution)/shard_map/reduce_scatter | solution.py:987
  116.5 8.0 %collective-permute-start.14 = (bf16[8,128,256]{2,1,0:T(8,128)(2,1)S(1)}, bf16[8,128,256]{2,1,0:T(8,128)(2,1)S(1)}, u32[]{:S(2)}, u32[]{:S(2)}) collective-permute-start(bf16[8,128,256]{2,1,0:T(8,128)(2,1)S(1)} %get-tuple-element.71), channel_id=1, source_target_pairs={{0,16},{16,0},{1,17},{17,1},{2,18},{18,2},{3,19},{19,3},{4,20},{20... | collective-permute-start | bytes 1572872 | tf_op jit(solution)/shard_map/ppermute | solution.py:74
  125.6 23.7 %all-to-all-start.4 = ((bf16[8,192,256]{2,1,0:T(8,128)(2,1)}), bf16[8,192,256]{2,1,0:T(8,128)(2,1)S(1)}, u32[]{:S(2)}, u32[]{:S(2)}) async-start(bf16[8,192,256]{2,1,0:T(8,128)(2,1)} %pad_maximum_fusion.back_ref), calls=%async_computation.6 | async-start | bytes 1572864 | tf_op jit(solution)/shard_map/all_to_all | solution.py:942
  129.7 41.6 %reduce-scatter.5.cloned.1.call-start = ((), (), s32[]{:S(2)}) async-start(), calls=%async_computation.8 | async-start | bytes 737280 | tf_op jit(solution)/shard_map/reduce_scatter | solution.py:1007
  133.0 1.6 collective-permute-start.15
  135.9 5.5 %collective-permute-start.16 = (bf16[8,32,256]{2,1,0:T(8,128)(2,1)S(1)}, bf16[8,32,256]{2,1,0:T(8,128)(2,1)S(1)}, u32[]{:S(2)}, u32[]{:S(2)}) collective-permute-start(bf16[8,32,256]{2,1,0:T(8,128)(2,1)S(1)} %get-tuple-element.77), channel_id=1, source_target_pairs={{0,1},{1,0},{2,3},{3,2},{4,5},{5,4},{6,7},{7,6},{8,9},{9,8},{10,11... | collective-permute-start | bytes 393224 | tf_op jit(solution)/shard_map/ppermute | solution.py:74
  145.8 10.5 %collective-permute-start.18 = (bf16[256,512]{1,0:T(8,128)(2,1)S(1)}, bf16[256,512]{1,0:T(8,128)(2,1)S(1)}, u32[]{:S(2)}, u32[]{:S(2)}) collective-permute-start(bf16[256,512]{1,0:T(8,128)(2,1)S(1)} %copy-done.12), channel_id=1, source_target_pairs={{0,0},{1,16},{2,2},{3,18},{4,4},{5,20},{6,6},{7,22},{8,8},{9,24},{... | collective-permute-start | bytes 786440 | tf_op jit(solution)/shard_map/ppermute | solution.py:934
  146.5 9.8 %collective-permute-start.19 = (bf16[256,512]{1,0:T(8,128)(2,1)S(1)}, bf16[256,512]{1,0:T(8,128)(2,1)S(1)}, u32[]{:S(2)}, u32[]{:S(2)}) collective-permute-start(bf16[256,512]{1,0:T(8,128)(2,1)S(1)} %copy-done.10), channel_id=1, source_target_pairs={{0,0},{1,16},{2,2},{3,18},{4,4},{5,20},{6,6},{7,22},{8,8},{9,24},{... | collective-permute-start | bytes 786440 | tf_op jit(solution)/shard_map/ppermute | solution.py:934
  152.1 4.3 %collective-permute-start.17 = (bf16[256,512]{1,0:T(8,128)(2,1)S(1)}, bf16[256,512]{1,0:T(8,128)(2,1)S(1)}, u32[]{:S(2)}, u32[]{:S(2)}) collective-permute-start(bf16[256,512]{1,0:T(8,128)(2,1)S(1)} %last.1), channel_id=1, source_target_pairs={{0,0},{1,16},{2,2},{3,18},{4,4},{5,20},{6,6},{7,22},{8,8},{9,24},{... | collective-permute-start | bytes 786440 | tf_op jit(solution)/shard_map/ppermute | solution.py:934
  152.7 12.6 %all-to-all-start.3 = ((bf16[8,32,256]{2,1,0:T(8,128)(2,1)}), bf16[8,32,256]{2,1,0:T(8,128)(2,1)S(1)}, u32[]{:S(2)}, u32[]{:S(2)}) async-start(bf16[8,32,256]{2,1,0:T(8,128)(2,1)} %merge.1), calls=%async_computation.5 | async-start | bytes 262144 | tf_op jit(solution)/shard_map/all_to_all | solution.py:942
  (32 other events, 179.6 us)
Sparse Core Ops, SparseCore 0:
  69.9 38.8 all-gather.2
  111.1 34.6 reduce-scatter.2
  148.1 23.1 reduce-scatter.4

commit v3 on v2

v3 whole, which is shorter than its diff:
```python
import functools

import jax
import jax.numpy as jnp
from jax import lax
from jax.experimental import pallas as pl
from jax.experimental.pallas import tpu as pltpu
from jax.sharding import PartitionSpec as P

HEADS = 8
EPS = 1e-05
LANES = 32
DOCS = 24
UNROLL = 4
INNER = (0, 1, 3, 2)
OUTER = (0, 1, 3, 2)
RING = (0, 2, 4, 6, 7, 5, 3, 1)
GROUP = 8
GROUP_BACK = 4
LOG2E = 1.4426950408889634
FAR = -(2.0**100)
CORE = 0.7978845608028654
CUBE = 0.044715
MIB = 1024 * 1024

BF16 = jnp.bfloat16
F32 = jnp.float32


def dot(left, right):
    return jnp.dot(left, right, preferred_element_type=F32)


def dot_t(left, right):
    return lax.dot_general(left, right, (((1,), (1,)), ((), ())), preferred_element_type=F32)


def vmem(count):
    return [pl.BlockSpec(memory_space=pltpu.VMEM) for _ in range(count)]


def hbm(count):
    return [pl.BlockSpec(memory_space=pltpu.HBM) for _ in range(count)]


def smem():
    return pl.BlockSpec(memory_space=pltpu.SMEM)


def kept(shape, dtype):
    return pltpu.VMEM(shape, dtype)


def near(array):
    return pltpu.with_memory_space_constraint(array, pltpu.VMEM)


def apart(shape, dtype):
    return pltpu.HBM(shape, dtype)


def far(array):
    return pltpu.with_memory_space_constraint(array, pltpu.HBM)


def shaped(shape, dtype):
    return jax.ShapeDtypeStruct(shape, dtype)


def cost(us):
    return pl.CostEstimate(flops=1000, bytes_accessed=1024, transcendentals=0)


def swap(block, axis, bit):
    size = lax.axis_size(axis)
    return lax.ppermute(block, axis, [(i, i ^ bit) for i in range(size)])


def rank_of(ways, texts):
    if texts == 2:
        return lax.axis_index("dp")
    return lax.rem(lax.axis_index("ctx"), ways)


def rows_of(blocks, number, total):
    size = total // blocks
    if blocks == 1:
        return pl.ds(0, size)
    return pl.ds(pl.multiple_of((lax.axis_index("dp") + number) % 2 * size, size), size)


def fetch(sources, targets, sems, first=0):
    copies = [
        pltpu.make_async_copy(source, target, sems.at[first + k])
        for k, (source, target) in enumerate(zip(sources, targets))
    ]
    for copy in copies:
        copy.start()
    return copies


def stage_kernel(layout, *refs):
    outs, sems = refs[len(layout) : -1], refs[-1]
    targets = [outs[k].at[pl.ds(start, size), :] for k, start, size in layout]
    for copy in fetch(refs[: len(layout)], targets, sems):
        copy.wait()


def stage(*groups):
    layout, shapes = [], []
    for k, group in enumerate(groups):
        start = 0
        for array in group:
            layout.append((k, start, array.shape[0]))
            start += array.shape[0]
        shapes.append(kept((start, group[0].shape[1]), group[0].dtype))
    flat = [far(array) for group in groups for array in group]
    return pl.pallas_call(
        functools.partial(stage_kernel, tuple(layout)),
        out_shape=tuple(shapes),
        in_specs=hbm(len(flat)),
        out_specs=tuple(vmem(len(groups))),
        scratch_shapes=[pltpu.SemaphoreType.DMA((len(flat),))],
        compiler_params=pltpu.CompilerParams(vmem_limit_bytes=4 * MIB),
        cost_estimate=cost(0.01),
        name="stage",
    )(*flat)


def project_kernel(blocks, x_in, *refs):
    ins, others = refs[:3], refs[3 : 3 * blocks]
    out_ref, held, x_ref, sems = refs[3 * blocks :]
    feat = x_ref.shape[1]
    size = feat // HEADS
    each = feat // blocks
    first, *copies = fetch(
        [x_in, *ins], [x_ref, *[held.at[part] for part in range(3)]], sems
    )
    first.wait()
    x = jnp.concatenate(
        [x_ref[:, rows_of(blocks, j, feat)] for j in range(blocks)], axis=1
    )
    for part, scale in ((0, size**-0.5), (1, 1.0), (2, 1.0)):
        copies[part].wait()
        weight = [held[part]] + [ref[...] for ref in others[part : part + 1]]
        turned = (dot(x, jnp.concatenate(weight, axis=0)) * scale).astype(BF16).T
        for h in range(HEADS):
            out_ref[h, part * size : (part + 1) * size, :] = turned[h * size : (h + 1) * size, :]


def project(x, weights):
    tok, feat = x.shape
    blocks = len(weights[0])
    mine = [weight[0] for weight in weights]
    others = [weight[1] for weight in weights if blocks == 2]
    return pl.pallas_call(
        functools.partial(project_kernel, blocks),
        out_shape=kept((HEADS, 3 * feat // HEADS, tok), BF16),
        in_specs=hbm(4) + vmem(len(others)),
        out_specs=vmem(1)[0],
        scratch_shapes=[
            pltpu.VMEM((3, feat // blocks, feat), BF16),
            pltpu.VMEM((tok, feat), BF16),
            pltpu.SemaphoreType.DMA((4,)),
        ],
        compiler_params=pltpu.CompilerParams(vmem_limit_bytes=6 * MIB),
        cost_estimate=cost(1.4),
        name="project",
    )(far(x), *map(far, mine), *map(near, others))


def mask_rows(row, hit, miss, extra):
    number = lax.broadcasted_iota(jnp.int32, (LANES, row.shape[1]), 0)
    base = jnp.where(number == row, hit, miss)
    base = jnp.where(number < DOCS, base, 0.0)
    for k, value in enumerate(extra):
        base = jnp.where(number == DOCS + k, value, base)
    return base.astype(BF16)


def parts_of(value, count):
    found = []
    for _ in range(count):
        part = value.astype(BF16).astype(F32)
        found.append(part)
        value = value - part
    return found


def query_rows(q, row, extra):
    wide = q.astype(F32) * LOG2E
    high, low = parts_of(wide, 2)
    return jnp.concatenate(
        [high.astype(BF16), low.astype(BF16), mask_rows(row, 0.0, FAR, extra)], axis=0
    ).T


def key_rows(k, row):
    return jnp.concatenate([k, k, mask_rows(row, 1.0, 0.0, (1.0, 1.0, 1.0))], axis=0)


def list_size(count):
    return HEADS * count + 2 * GROUP


def plan_kernel(ways, count, tok, *refs):
    out_ref = refs[-1]
    rank = rank_of(ways, len(refs) - 1)
    flip = (lax.axis_index("dp") + lax.axis_index("ctx")) % 2
    length = list_size(count)

    def number(at):
        if len(refs) == 2:
            return refs[0][at]
        return jnp.where(flip == 0, refs[0][at], refs[1][at])

    firsts = [number(c * tok) for c in range(count)]
    lasts = [number(c * tok + tok - 1) for c in range(count)]

    def one(i, found):
        chunk = i * ways + rank
        first = number(chunk * tok)
        last = number(chunk * tok + tok - 1)
        low = sum((value < first).astype(jnp.int32) for value in lasts)
        high = sum((value <= last).astype(jnp.int32) for value in firsts)

        def other(c, found):
            own = (lax.rem(c, ways) == rank).astype(jnp.int32)
            every, mine, rest = found
            out_ref[every] = i
            out_ref[length + every] = c
            at = jnp.where(own == 1, 2 * length + mine, 4 * length + rest)
            out_ref[at] = i
            out_ref[at + length] = c
            return every + 1, mine + own, rest + 1 - own

        return lax.fori_loop(low, high, other, found)

    found = lax.fori_loop(0, HEADS, one, (jnp.int32(0),) * 3)
    for k, ended in enumerate(found):
        for g in range(GROUP):
            out_ref[2 * k * length + ended + g] = HEADS
            out_ref[(2 * k + 1) * length + ended + g] = 0
        size = GROUP if k == 0 else GROUP_BACK
        out_ref[6 * length + k] = (ended + size - 1) // size


def plan_of(segs, ways, count, tok):
    size = 6 * list_size(count) + 8
    return pl.pallas_call(
        functools.partial(plan_kernel, ways, count, tok),
        out_shape=shaped((size,), jnp.int32),
        in_specs=[smem()] * len(segs),
        out_specs=smem(),
        cost_estimate=cost(1),
        compiler_params=pltpu.CompilerParams(vmem_limit_bytes=1 * MIB),
        name="plan",
    )(*[seg.reshape(-1) for seg in segs])


def chosen(seg_refs):
    if len(seg_refs) == 1:
        return seg_refs[0][...]
    flip = (lax.axis_index("dp") + lax.axis_index("ctx")) % 2
    return jnp.where(flip == 0, seg_refs[0][...], seg_refs[1][...])


def tiles_of(plan_ref, kind, length, g):
    found = []
    size = GROUP if kind == 0 else GROUP_BACK
    for k in range(size):
        at = 2 * kind * length + g * size + k
        found.append((plan_ref[at], plan_ref[at + length]))
    return found


def chunk_of(h, slot, ways, rank):
    return h * ways + lax.rem(rank - slot + ways, ways)


def forward_kernel(ways, texts, plan_ref, *refs):
    seg_refs, refs = refs[:texts], refs[texts:]
    kv_refs = refs[:ways]
    q_ref = kv_refs[0]
    o_ref, of_out, lse_ref, kx, vx, qx, acc, seg_ref, of_ref, sem = refs[ways:]
    seg_ref[...] = chosen(seg_refs)
    count, tok = seg_ref.shape
    size = q_ref.shape[1] // 3
    rank = rank_of(ways, texts)
    length = list_size(count)
    ones = (lax.broadcasted_iota(jnp.int32, (16, tok), 0) == 0).astype(F32).astype(BF16)
    for slot in range(ways):

        @pl.loop(0, HEADS, unroll=UNROLL)
        def fill(h):
            chunk = chunk_of(h, slot, ways, rank)
            keys = kv_refs[slot][h, size : 2 * size, :]
            kx[chunk] = key_rows(keys, seg_ref[pl.ds(chunk, 1), :])
            vx[chunk] = jnp.concatenate([kv_refs[slot][h, 2 * size : 3 * size, :], ones], axis=0)

    @pl.loop(0, HEADS, unroll=UNROLL)
    def fill_query(i):
        qx[i] = query_rows(q_ref[i, 0:size, :], seg_ref[pl.ds(i * ways + rank, 1), :], ())
        acc[i] = jnp.zeros_like(acc[i])

    qx[HEADS] = query_rows(jnp.zeros((size, tok), BF16), jnp.full((1, tok), -1, jnp.int32), ())
    acc[HEADS] = jnp.zeros_like(acc[0])

    @pl.loop(0, plan_ref[6 * length])
    def group(g):
        tiles = tiles_of(plan_ref, 0, length, g)
        weights = [jnp.exp2(dot(qx[i], kx[c])).astype(BF16) for i, c in tiles]
        mixed = [dot_t(vx[c], w) for (i, c), w in zip(tiles, weights)]
        for (i, c), part in zip(tiles, mixed):
            acc[i] += part

    smallest = jnp.full((1, tok), 1.0, F32)
    largest = jnp.full((1, tok), 1.0, F32)
    for i in range(HEADS):
        total = acc[i, size : size + 1, :]
        smallest = jnp.minimum(smallest, total)
        largest = jnp.maximum(largest, total)
        out = acc[i, 0:size, :] / total
        of_ref[i] = out
        o_ref[i] = out.astype(BF16)
        lse_ref[i : i + 1, :] = jnp.log(total) * LOG2E
    good = (jnp.min(smallest) > 2.0**-90) & (jnp.max(largest) < 2.0**90)

    @pl.when(jnp.logical_not(good))
    def any_scores():
        @pl.loop(0, HEADS)
        def one(i):
            query = qx[i]

            def step(c, carry):
                top, total, mixed = carry
                s = dot(query, kx[c])
                new = jnp.maximum(top, jnp.max(s, axis=1, keepdims=True))
                fade = jnp.exp2(top - new)
                w = jnp.exp2(s - new)
                total = total * fade + jnp.sum(w, axis=1, keepdims=True)
                mixed = mixed * fade + dot_t(w.astype(BF16), vx[c])
                return new, total, mixed

            top, total, mixed = lax.fori_loop(
                0,
                count,
                step,
                (
                    jnp.full((tok, 1), -3e38, F32),
                    jnp.zeros((tok, 1), F32),
                    jnp.zeros((tok, size + 16), F32),
                ),
            )
            out = (mixed / total).T[0:size, :]
            of_ref[i] = out
            o_ref[i] = out.astype(BF16)
            lse = jnp.broadcast_to(top + jnp.log(total) * LOG2E, (tok, 128)).T
            lse_ref[pl.ds(i, 1), :] = lse[0:1, :]

    fetch([of_ref], [of_out], sem)[0].wait()


def attend(plan, segs, kvs):
    ways = len(kvs)
    _, size, tok = kvs[0].shape
    size = size // 3
    count = segs[0].shape[0]
    depth = 2 * size + LANES
    return pl.pallas_call(
        functools.partial(forward_kernel, ways, len(segs)),
        out_shape=(
            kept((HEADS, size, tok), BF16),
            apart((HEADS, size, tok), F32),
            kept((HEADS, tok), F32),
        ),
        in_specs=[smem()] + vmem(len(segs) + ways),
        out_specs=(vmem(1)[0], hbm(1)[0], vmem(1)[0]),
        scratch_shapes=[
            pltpu.VMEM((count, depth, tok), BF16),
            pltpu.VMEM((count, size + 16, tok), BF16),
            pltpu.VMEM((HEADS + 1, tok, depth), BF16),
            pltpu.VMEM((HEADS + 1, size + 16, tok), F32),
            pltpu.VMEM(segs[0].shape, jnp.int32),
            pltpu.VMEM((HEADS, size, tok), F32),
            pltpu.SemaphoreType.DMA((1,)),
        ],
        compiler_params=pltpu.CompilerParams(vmem_limit_bytes=12 * MIB),
        cost_estimate=cost(7),
        name="attend",
    )(far(plan), *segs, *map(near, kvs))


def backward_kernel(ways, slots, final, texts, plan_ref, *refs):
    seg_refs, refs = refs[:texts], refs[texts:]
    q_ref, do_ref, of_in, lse_ref = refs[:4]
    refs = refs[4:]
    many = len(slots)
    kv_refs = refs[:many]
    refs = refs[many:]
    if final:
        part_ref, refs = refs[0], refs[1:]
    dq_ref = refs[0]
    dkv_refs = refs[1 : 1 + many]
    kx, vx, qx, dx, dk, dv, dq, seg_ref, of_ref, sem = refs[1 + many :]
    (copy,) = fetch([of_in], [of_ref], sem)
    seg_ref[...] = chosen(seg_refs)
    count, tok = seg_ref.shape
    size = do_ref.shape[1]
    rank = rank_of(ways, texts)
    ones = (lax.broadcasted_iota(jnp.int32, (16, tok), 0) < 2).astype(F32).astype(BF16)
    for slot, kv_ref in zip(slots, kv_refs):

        @pl.loop(0, HEADS, unroll=UNROLL)
        def fill(h):
            chunk = chunk_of(h, slot, ways, rank)
            kx[chunk] = key_rows(kv_ref[h, size : 2 * size, :], seg_ref[pl.ds(chunk, 1), :])
            vx[chunk] = jnp.concatenate([kv_ref[h, 2 * size : 3 * size, :], ones], axis=0)
            dk[chunk] = jnp.zeros_like(dk[chunk])
            dv[chunk] = jnp.zeros_like(dv[chunk])

    copy.wait()

    @pl.loop(0, HEADS, unroll=UNROLL)
    def fill_query(i):
        lse = parts_of(-lse_ref[pl.ds(i, 1), :], 3)
        qx[i] = query_rows(q_ref[i, 0:size, :], seg_ref[pl.ds(i * ways + rank, 1), :], lse)
        do = do_ref[i].astype(F32)
        delta = parts_of(-jnp.sum(do * of_ref[i], axis=0, keepdims=True), 3)
        number = lax.broadcasted_iota(jnp.int32, (16, tok), 0)
        tail = jnp.where(number == 0, delta[0], jnp.where(number == 1, delta[1], 0.0))
        dx[i] = jnp.concatenate([do_ref[i], tail.astype(BF16)], axis=0).T
        dq[i] = part_ref[i] if final else jnp.zeros_like(dq[i])

    qx[HEADS] = query_rows(jnp.zeros((size, tok), BF16), jnp.full((1, tok), -1, jnp.int32), ())
    dx[HEADS] = jnp.zeros_like(dx[0])
    dq[HEADS] = jnp.zeros_like(dq[0])

    kind = 1 if slots == (0,) else 2
    length = list_size(count)

    @pl.loop(0, plan_ref[6 * length + kind])
    def group(g):
        tiles = tiles_of(plan_ref, kind, length, g)
        weights = [jnp.exp2(dot(qx[i], kx[c])) for i, c in tiles]
        pulls = [dot(dx[i], vx[c]) for i, c in tiles]
        scores = [(w * p).astype(BF16) for w, p in zip(weights, pulls)]
        for (i, c), w, ds in zip(tiles, weights, scores):
            j = jnp.minimum(i, HEADS - 1)
            dv[c] += dot(do_ref[j], w.astype(BF16))
            dk[c] += dot(q_ref[j, 0:size, :], ds)
            dq[i] += dot_t(kx[c, 0:size, :], ds)

    for slot, kv_ref, out in zip(slots, kv_refs, dkv_refs):

        @pl.loop(0, HEADS, unroll=UNROLL)
        def drain(h):
            chunk = chunk_of(h, slot, ways, rank)
            out[h, 0:size, :] = dk[chunk].astype(out.dtype)
            out[h, size : 2 * size, :] = dv[chunk].astype(out.dtype)

    @pl.loop(0, HEADS, unroll=UNROLL)
    def drain_query(i):
        if final:
            dq_ref[i] = (dq[i] * size**-0.5).astype(BF16)
        else:
            dq_ref[i] = dq[i]


def attend_back(plan, segs, q, do, of, lse, kvs, ways, slots, part):
    many = len(slots)
    final = part is not None
    _, size, tok = do.shape
    count = segs[0].shape[0]
    depth = 2 * size + LANES
    return pl.pallas_call(
        functools.partial(backward_kernel, ways, slots, final, len(segs)),
        out_shape=(kept((HEADS, size, tok), BF16 if final else F32),)
        + (kept((HEADS, 2 * size, tok), F32 if slots == (0,) else BF16),) * many,
        in_specs=[smem()]
        + vmem(len(segs) + 2)
        + hbm(1)
        + vmem(1 + many + final),
        out_specs=tuple(vmem(1 + many)),
        scratch_shapes=[
            pltpu.VMEM((count, depth, tok), BF16),
            pltpu.VMEM((count, size + 16, tok), BF16),
            pltpu.VMEM((HEADS + 1, tok, depth), BF16),
            pltpu.VMEM((HEADS + 1, tok, size + 16), BF16),
            pltpu.VMEM((count, size, tok), F32),
            pltpu.VMEM((count, size, tok), F32),
            pltpu.VMEM((HEADS + 1, size, tok), F32),
            pltpu.VMEM(segs[0].shape, jnp.int32),
            pltpu.VMEM((HEADS, size, tok), F32),
            pltpu.SemaphoreType.DMA((1,)),
        ],
        compiler_params=pltpu.CompilerParams(vmem_limit_bytes=16 * MIB),
        cost_estimate=cost(7.5),
        name="attend_back",
    )(far(plan), *segs, near(q), near(do), far(of), near(lse), *map(near, kvs), *((near(part),) if final else ()))


def normed(rows):
    centred = rows - jnp.mean(rows, axis=-1, keepdims=True)
    spread = jnp.mean(centred * centred, axis=-1, keepdims=True)
    inverse = lax.rsqrt(spread + EPS)
    return centred * inverse, inverse


def norm_back(n, inverse, gain, up):
    scaled = up * gain
    mean_one = jnp.mean(scaled, axis=-1, keepdims=True)
    mean_two = jnp.mean(scaled * n, axis=-1, keepdims=True)
    grad = inverse * (scaled - mean_one - n * mean_two)
    return grad, jnp.sum(up * n, axis=0, keepdims=True)


def middle_kernel(blocks, tile, *refs):
    ot_ref, mask_ref = refs[:2]
    gains_refs = refs[2 : 2 + blocks]
    refs = refs[2 + blocks :]
    x_in, y_in, t_in = refs[:3]
    wo_in, wu_in, wd_in = [refs[3 + k * blocks : 3 + (k + 1) * blocks] for k in range(3)]
    (
        result_out,
        gy_out,
        gr_out,
        dot_ref,
        small_ref,
        *grad_outs,
        x1_ref,
        h_ref,
        df_ref,
        dz_ref,
        da_ref,
        slope,
        acc,
        gr_ref,
        x_ref,
        y_ref,
        t_ref,
        wo_ref,
        wu_ref,
        wd_ref,
        xt,
        sum_refs,
        out_ref,
        gy_ref,
        sems,
        tile_sems,
        sum_sems,
    ) = refs[3 + 3 * blocks :]
    part_rows = wo_ref.shape[0] // blocks
    early = fetch(
        [*wo_in, x_in], [*[wo_ref.at[pl.ds(j * part_rows, part_rows), :] for j in range(blocks)], x_ref], sems
    )
    wide = h_ref.shape[1]
    each = wide // blocks

    def columns(start):
        if blocks == 2:
            start = (start + lax.axis_index("dp") * each) % wide
        return pl.ds(pl.multiple_of(start, tile), tile)

    tiles = []
    for k, start in enumerate(range(0, wide, tile)):
        cols = columns(start)
        tiles.append(
            fetch(
                [*[ref.at[:, cols] for ref in wu_in], wd_in[start // each].at[pl.ds(start % each, tile), :]],
                [
                    *[wu_ref.at[pl.ds(j * part_rows, part_rows), cols] for j in range(blocks)],
                    wd_ref.at[pl.ds(start, tile), :],
                ],
                tile_sems,
                k * (blocks + 1),
            )
        )
    late = fetch([y_in, t_in], [y_ref, t_ref], sems, blocks + 1)
    for copy in early:
        copy.wait()
    rows, feat = x_ref.shape
    halves = [rows_of(blocks, j, feat) for j in range(blocks)]

    def ordered(values):
        if blocks == 1:
            return values
        low, high = values[:, : feat // 2], values[:, feat // 2 :]
        turned = jnp.concatenate([high, low], axis=1)
        return jnp.where(lax.axis_index("dp") == 0, values, turned)

    gains = gains_refs[0][...].astype(F32)
    if blocks == 2:
        other = gains_refs[1][...].astype(F32)
        gains = jnp.where(
            lax.axis_index("dp") == 0,
            jnp.concatenate([gains, other], axis=1),
            jnp.concatenate([other, gains], axis=1),
        )
    g1, g2, g3 = gains[0:1], gains[1:2], gains[2:3]
    branch = dot(
        jnp.concatenate([ot_ref[rows_j, :] for rows_j in halves], axis=0).T,
        wo_ref[...],
    )
    n1, r1 = normed(x_ref[...].astype(F32) + branch)
    x1 = n1 * g1
    x1_ref[...] = ordered(x1).astype(BF16)

    def weight_up(start):
        return wu_ref[:, columns(start)]

    for start in range(0, wide, tile):
        cols = slice(start, start + tile)
        for copy in tiles[start // tile]:
            copy.wait()
        z = dot(x1_ref[...], weight_up(start))
        z2 = z * z
        th = jnp.tanh(z * (CORE + (CORE * CUBE) * z2))
        half = 0.5 + 0.5 * th
        h = (z * half).astype(BF16)
        slope[:, cols] = half + z * (1.0 - th * th) * (0.5 * CORE + (1.5 * CORE * CUBE) * z2)
        h_ref[:, cols] = h
        part = dot(h, wd_ref[start : start + tile, :])
        if start:
            acc[...] += part
        else:
            acc[...] = part

    ffn = acc[...]
    n2, r2 = normed(x1 + ffn)
    for copy in late:
        copy.wait()
    n3, r3 = normed(y_ref[...].astype(F32) + branch + ffn)
    result = n2 * g2 + n3 * g3
    out_ref[...] = result.astype(BF16)
    mask_row = mask_ref[...].astype(F32)
    mask = jnp.broadcast_to(mask_row, (8, rows)).T[:, 0:1]
    differ = result - t_ref[...].astype(F32)
    error = jnp.sum(mask * differ * differ)
    valid = jnp.sum(mask_row)
    upstream = 2.0 * mask * differ
    gy, dg3 = norm_back(n3, r3, g3, upstream)
    du, dg2 = norm_back(n2, r2, g2, upstream)
    gy_ref[...] = gy.astype(gy_ref.dtype)
    df_ref[...] = (du + gy).astype(BF16)
    going = [] if len(grad_outs) == 2 else None
    if going is not None:
        count, depth, _ = grad_outs[0].shape
        step = feat // (2 * count)
        wide_step = wide // (2 * count)
        parts = wide // feat

        def put(flip, first, base, size, values):
            for k in range(values.shape[0] // size):
                c = first + k
                at = INNER.index(c % 4) * 4 + OUTER.index(c // 4)
                sum_refs[flip, at, pl.ds(base, size), :] = values[
                    k * size : (k + 1) * size
                ].astype(BF16)

        def send(flip, base, size):
            span = pl.ds(base, size)
            going.extend(
                fetch(
                    [sum_refs.at[flip, :, span, :]],
                    [grad_outs[flip].at[:, span, :]],
                    sum_sems,
                    len(going),
                )
            )

        xt[...] = x1_ref[...].T
        for flip in (1, 0):
            for start in range(0, wide // 2, tile):
                cols = slice(flip * (wide // 2) + start, flip * (wide // 2) + start + tile)
                g = dot(h_ref[:, cols].T, df_ref[...])
                put(flip, start // wide_step, parts * step, wide_step, g)
            send(flip, parts * step, wide_step)
    for start in range(0, wide, tile):
        cols = slice(start, start + tile)
        dz = (dot_t(df_ref[...], wd_ref[start : start + tile, :]) * slope[:, cols]).astype(BF16)
        dz_ref[:, cols] = dz
        if going is not None:
            g = dot(xt[...], dz)
            base = (start + lax.axis_index("dp") * each) % wide // feat * step
            for flip in (1, 0):
                half_g = g[flip * (feat // 2) : (flip + 1) * (feat // 2)]
                put(flip, 0, pl.multiple_of(base, step), step, half_g)
                send(flip, pl.multiple_of(base, step), step)
        part = dot_t(dz, weight_up(start))
        if start:
            acc[...] += part
        else:
            acc[...] = part

    gr, dg1 = norm_back(n1, r1, g1, du + ordered(acc[...]))
    gr_ref[...] = gr
    leaving = fetch([gr_ref, out_ref, gy_ref], [gr_out, result_out, gy_out], sems)
    da = (gr + gy).astype(BF16)
    da_ref[...] = da
    turned = dot_t(wo_ref[...], da).astype(BF16)
    for j in range(blocks):
        size = feat // blocks
        dot_ref[halves[j], :] = turned[j * size : (j + 1) * size]
    lane = lax.broadcasted_iota(jnp.int32, (1, feat), 1)
    scalars = jnp.where(lane == 0, error, jnp.where(lane == 1, valid, 0.0))
    sums = jnp.concatenate([dg1, dg2, dg3, scalars], axis=0)
    small_ref[...] = jnp.concatenate([sums[:, : feat // 2], sums[:, feat // 2 :]], axis=0)
    if going is None:
        for out, ref in zip(grad_outs, (x1_ref, h_ref, df_ref, dz_ref, da_ref)):
            out[...] = ref[...]
    else:
        for flip in (1, 0):
            side = (lax.axis_index("dp") + flip) % 2
            part = pl.ds(pl.multiple_of(side * (feat // 2), feat // 2), feat // 2)
            put(flip, 0, parts * step + wide_step, step, dot(ot_ref[part, :], da))
            send(flip, parts * step + wide_step, step)
    for copy in leaving + (going or []):
        copy.wait()


def middle(ot, mask, gains, x, y, teacher, wo, wu, wd, gy_type, scattered):
    tok, feat = x.shape
    wide = wu[0].shape[1]
    blocks = len(gains)
    tile = min(512, wide // blocks)
    return pl.pallas_call(
        functools.partial(middle_kernel, blocks, tile),
        out_shape=(
            apart((tok, feat), BF16),
            apart((tok, feat), gy_type),
            apart((tok, feat), F32),
            kept((feat, tok), BF16),
            kept((8, feat // 2), F32),
        )
        + (
            tuple(apart(shape, BF16) for shape in scattered)
            or tuple(shaped((tok, size), BF16) for size in (feat, wide, feat, wide, feat))
        ),
        in_specs=vmem(2 + blocks) + hbm(3 + 3 * blocks),
        out_specs=tuple(hbm(3) + vmem(2) + (hbm(len(scattered)) or vmem(5))),
        scratch_shapes=[
            pltpu.VMEM((tok, feat), BF16),
            pltpu.VMEM((tok, wide), BF16),
            pltpu.VMEM((tok, feat), BF16),
            pltpu.VMEM((tok, wide), BF16),
            pltpu.VMEM((tok, feat), BF16),
            pltpu.VMEM((tok, wide), F32),
            pltpu.VMEM((tok, feat), F32),
            pltpu.VMEM((tok, feat), F32),
            pltpu.VMEM((tok, feat), BF16),
            pltpu.VMEM((tok, feat), BF16),
            pltpu.VMEM((tok, feat), BF16),
            pltpu.VMEM((feat, feat), BF16),
            pltpu.VMEM((feat, wide), BF16),
            pltpu.VMEM((wide, feat), BF16),
            pltpu.VMEM((feat, tok), BF16),
            pltpu.VMEM((2, *(scattered[0] if scattered else (8, 16, 128))), BF16),
            pltpu.VMEM((tok, feat), BF16),
            pltpu.VMEM((tok, feat), gy_type),
            pltpu.SemaphoreType.DMA((blocks + 3,)),
            pltpu.SemaphoreType.DMA((wide // tile * (blocks + 1),)),
            pltpu.SemaphoreType.DMA((2 * PIECES,)),
        ],
        compiler_params=pltpu.CompilerParams(vmem_limit_bytes=36 * MIB),
        cost_estimate=cost(8),
        name="middle",
    )(near(ot), mask, *gains, *map(far, (x, y, teacher, *wo, *wu, *wd)))


def split_sum(values):
    high = values.astype(BF16)
    low = (values - high.astype(F32)).astype(BF16)
    return jnp.concatenate([high.astype(F32), low.astype(F32)], axis=0).astype(BF16)


PIECES = 8


def ffn_shape(blocks, feat, wide):
    step = feat // (2 * blocks)
    return (blocks, (wide // feat) * step + wide // (2 * blocks) + step, feat)


def join_kernel(one_in, two_in, out, one_ref, two_ref, ref, sems):
    blocks = one_in.shape[0]
    spans = [pl.ds(k * blocks // PIECES, blocks // PIECES) for k in range(PIECES)]
    ones = fetch([one_in.at[k] for k in spans], [one_ref.at[k] for k in spans], sems)
    twos = fetch([two_in.at[k] for k in spans], [two_ref.at[k] for k in spans], sems, PIECES)
    going = []
    for k, (span, one, two) in enumerate(zip(spans, ones, twos)):
        one.wait()
        two.wait()
        for b in range(k * blocks // PIECES, (k + 1) * blocks // PIECES):
            ref[b] = added(one_ref[b], two_ref[b], 0)
        going += fetch([ref.at[span]], [out.at[span]], sems, 2 * PIECES + k)
    for copy in going:
        copy.wait()


def join(one, two):
    return pl.pallas_call(
        join_kernel,
        out_shape=apart(one.shape, BF16),
        in_specs=hbm(2),
        out_specs=hbm(1)[0],
        scratch_shapes=[pltpu.VMEM(one.shape, BF16)] * 3
        + [pltpu.SemaphoreType.DMA((3 * PIECES,))],
        compiler_params=pltpu.CompilerParams(vmem_limit_bytes=12 * MIB),
        cost_estimate=cost(0.01),
        name="join",
    )(far(one), far(two))


def added(one, two, tail):
    total = one.astype(F32) + two.astype(F32)
    if not tail:
        return total.astype(BF16)
    depth = total.shape[0]
    high, low = depth - tail, depth - tail // 2
    return jnp.concatenate(
        [total[:high].astype(BF16), split_sum(total[high:low] + total[low:])], axis=0
    )


def halve_kernel(bit, under, tail, keep_ref, got_ref, next_ref, send_ref):
    mine = lax.rem(lax.axis_index("ctx") // bit, 2)

    @pl.loop(0, next_ref.shape[0])
    def one(b):
        for ref, which in ((send_ref, 1 - mine), (next_ref, mine)):
            at = (b // under) * 2 * under + which * under + lax.rem(b, under)
            ref[b] = added(keep_ref[at], got_ref[at], tail)


def halve(bit, under, tail, keep, got):
    blocks, depth, feat = keep.shape
    return pl.pallas_call(
        functools.partial(halve_kernel, bit, under, tail),
        out_shape=(kept((blocks // 2, depth, feat), BF16),) * 2,
        in_specs=vmem(2),
        out_specs=tuple(vmem(2)),
        compiler_params=pltpu.CompilerParams(vmem_limit_bytes=12 * MIB),
        cost_estimate=cost(1),
        name="halve",
    )(near(keep), near(got))


def merge_kernel(tail, one_ref, two_ref, out_ref):
    for b in range(out_ref.shape[0]):
        out_ref[b] = added(one_ref[b], two_ref[b], tail)


def merge(tail, one, two):
    return pl.pallas_call(
        functools.partial(merge_kernel, tail),
        out_shape=kept(one.shape, BF16),
        in_specs=vmem(2),
        out_specs=vmem(1)[0],
        cost_estimate=cost(0.5),
        compiler_params=pltpu.CompilerParams(vmem_limit_bytes=3 * MIB),
        name="merge",
    )(near(one), near(two))


def head_grad_kernel(back_ref, x_in, small_ref, keep_ref, send_ref, x_ref, sems):
    copies = fetch(
        [x_in.at[h] for h in range(HEADS)], [x_ref.at[h] for h in range(HEADS)], sems
    )
    total = 0.0
    for h in range(HEADS):
        copies[h].wait()
        total = total + dot(back_ref[RING[h]], x_ref[h])
    turned = total.T
    feat, size = turned.shape
    blocks, depth, lanes = keep_ref.shape
    step = feat // (2 * blocks)
    turned = jnp.concatenate([turned, jnp.zeros((feat, lanes - size), F32)], axis=1).astype(BF16)
    small = split_sum(small_ref[...])
    for flip in range(2):
        ref = (keep_ref, send_ref)[flip]
        for side in range(2):

            @pl.when(lax.axis_index("dp") == (side + flip) % 2)
            def store():
                half = turned[side * feat // 2 : (side + 1) * feat // 2]
                ref[:, 0:step, :] = half.reshape(blocks, step, lanes)

        ref[:, step:depth, :] = jnp.broadcast_to(small[None], (blocks,) + small.shape)


def head_grads(blocks, back, x, small):
    feat = x.shape[2]
    step = feat // (2 * blocks)
    lanes = small.shape[1]
    return pl.pallas_call(
        head_grad_kernel,
        out_shape=(kept((blocks, step + 16, lanes), BF16),) * 2,
        in_specs=vmem(1) + hbm(1) + vmem(1),
        out_specs=tuple(vmem(2)),
        scratch_shapes=[
            pltpu.VMEM(x.shape, BF16),
            pltpu.SemaphoreType.DMA((HEADS,)),
        ],
        compiler_params=pltpu.CompilerParams(vmem_limit_bytes=8 * MIB),
        cost_estimate=cost(1.5),
        name="head_grads",
    )(near(back), far(x), near(small))


def last_kernel(blocks, back_ref, gr_ref, *refs):
    gx_ref = refs[-1]
    feat = gr_ref.shape[1]
    size = feat // HEADS
    each = feat // blocks
    total = 0.0
    for part in range(3):
        turned = jnp.concatenate(
            [back_ref[h, part * size : (part + 1) * size, :] for h in range(HEADS)], axis=0
        )
        total = total + dot_t(turned.T, refs[part][...])
    for j in range(blocks):
        rows = rows_of(blocks, j, feat)
        gx_ref[:, rows] = (gr_ref[:, rows] + total[:, j * each : (j + 1) * each]).astype(
            gx_ref.dtype
        )


def last(blocks, back, gr, weights, kind):
    return pl.pallas_call(
        functools.partial(last_kernel, blocks),
        out_shape=(shaped if kind == F32 else kept)(gr.shape, kind),
        in_specs=vmem(2 + len(weights)),
        out_specs=vmem(1)[0],
        compiler_params=pltpu.CompilerParams(vmem_limit_bytes=6 * MIB),
        cost_estimate=cost(0.01),
        name="last",
    )(*map(near, (back, gr, *weights)))


def finish_kernel(
    pieces_ref,
    gx_in,
    gy_in,
    out_in,
    loss_ref,
    out_ref,
    gx_ref,
    gy_ref,
    gq_ref,
    gk_ref,
    gv_ref,
    g1_ref,
    g2_ref,
    g3_ref,
    inverse_ref,
):
    step, feat = gq_ref.shape
    size = feat // HEADS
    halves = jnp.sum(pieces_ref[:, step : step + 16, :].astype(F32), axis=0)
    halves = halves[0:8] + halves[8:16]
    small = jnp.concatenate([halves[0:4], halves[4:8]], axis=1)
    inverse = 1.0 / small[3:4, 1:2]
    inverse_ref[...] = jnp.broadcast_to(inverse, inverse_ref.shape)
    loss_ref[...] = small[3:4, 0:1] * inverse
    out_ref[...] = out_in[...]
    gx_ref[...] = gx_in[...].astype(F32) * inverse
    gy_ref[...] = gy_in[...].astype(F32) * inverse
    for h in range(HEADS):
        block = pieces_ref[h, 0:step, :].astype(F32) * inverse
        for part, ref in enumerate((gq_ref, gk_ref, gv_ref)):
            ref[:, h * size : (h + 1) * size] = block[:, part * size : (part + 1) * size]
    number = lax.axis_index("dp") * (2 * pieces_ref.shape[0]) + lax.axis_index("ctx")
    eight = jnp.concatenate([small, small], axis=0) * inverse
    turned = pltpu.roll(eight, lax.rem(feat - number * step, feat), 1)
    g1_ref[...] = turned[0:1, 0:step]
    g2_ref[...] = turned[1:2, 0:step]
    g3_ref[...] = turned[2:3, 0:step]


def finish(pieces, gx, gy, result):
    tok, feat = gx.shape
    step = pieces.shape[1] - 16
    return pl.pallas_call(
        finish_kernel,
        out_shape=(
            shaped((1, 1), F32),
            shaped((tok, feat), BF16),
            shaped((tok, feat), F32),
            shaped((tok, feat), F32),
            shaped((step, feat), F32),
            shaped((step, feat), F32),
            shaped((step, feat), F32),
            shaped((1, step), F32),
            shaped((1, step), F32),
            shaped((1, step), F32),
            kept((8, 128), F32),
        ),
        in_specs=vmem(4),
        out_specs=tuple(vmem(11)),
        compiler_params=pltpu.CompilerParams(vmem_limit_bytes=8 * MIB),
        cost_estimate=cost(1.8),
        name="finish",
    )(near(pieces), gx, gy, result)


def spread_kernel(sums_in, inverse_ref, go_ref, gu_ref, gd_ref, sums_ref, sem):
    (copy,) = fetch([sums_in], [sums_ref], sem)
    step, feat = go_ref.shape
    wide_step = gd_ref.shape[0]
    parts = gu_ref.shape[1] // feat
    copy.wait()
    main = sums_ref[0].astype(F32) * inverse_ref[0:1, 0:1]
    for j in range(parts):
        gu_ref[:, j * feat : (j + 1) * feat] = main[j * step : (j + 1) * step]
    base = parts * step
    gd_ref[...] = main[base : base + wide_step]
    base += wide_step
    go_ref[...] = main[base : base + step]


def spread(sums, inverse, step, wide):
    feat = sums.shape[2]
    return pl.pallas_call(
        spread_kernel,
        out_shape=(
            shaped((step, feat), F32),
            shaped((step, wide), F32),
            shaped((wide * step // feat, feat), F32),
        ),
        in_specs=hbm(1) + vmem(1),
        out_specs=tuple(vmem(3)),
        scratch_shapes=[pltpu.VMEM(sums.shape, BF16), pltpu.SemaphoreType.DMA((1,))],
        compiler_params=pltpu.CompilerParams(vmem_limit_bytes=4 * MIB),
        cost_estimate=cost(1),
        name="spread",
    )(far(sums), near(inverse))


def body(
    state_x,
    state_y,
    teacher,
    segment_ids,
    valid_mask,
    w_query,
    w_key,
    w_value,
    w_out,
    w_up,
    w_down,
    gain_attn,
    gain_ffn,
    gain_final,
):
    _, tok, feat = state_x.shape
    size = feat // HEADS
    ctx = lax.axis_size("ctx")
    sides = lax.axis_size("dp")
    ways = ctx // HEADS
    groups = [[h * ways + r for h in range(HEADS)] for r in range(ways)]
    side, place = lax.axis_index("dp"), lax.axis_index("ctx")
    wide = w_up.shape[1]
    cross = sides == 2 and ways == 2 and (feat // (sides * ctx)) % 16 == 0
    both = ("dp", "ctx")

    def moved(block):
        if not cross:
            return block
        route = []
        for s in range(2):
            for c in range(ctx):
                route.append((s * ctx + c, (c % 2) * ctx + c - c % 2 + s))
        return lax.ppermute(block, both, route)

    def shared(block):
        if sides == 2:
            return [block, swap(block, "dp", 1)]
        return [lax.all_gather(block, "dp", axis=0, tiled=True)]

    def exchange(block):
        return lax.all_to_all(block, "ctx", 0, 0, axis_index_groups=groups, tiled=True)

    def around(block, distance):
        if cross:
            return swap(block, "dp", 1)
        route = []
        for g in range(HEADS):
            for r in range(ways):
                route.append((g * ways + r, g * ways + (r + distance) % ways))
        return lax.ppermute(block, "ctx", route)

    x = moved(state_x[0])
    attn_weights = [shared(w) for w in (w_query, w_key, w_value)]
    segs = [segment_ids.reshape(ctx, tok)]
    if cross:
        segs.append(swap(segs[0], "dp", 1))
    y, target, mask = moved(state_y[0]), moved(teacher[0]), moved(valid_mask)
    qkv = project(x, attn_weights)
    plan = plan_of(segs, ways, ctx, tok)
    qkv = exchange(qkv)
    qkv, plan, mask, late_x = lax.optimization_barrier((qkv, plan, mask, x))
    kvs = [qkv] + [around(qkv, j) for j in range(1, ways)]
    o, of, lse = attend(plan, segs, kvs)
    gains = jnp.stack([gain_attn, gain_ffn, gain_final])
    if sides == 2:
        gains = shared(gains)
    else:
        gains = [lax.all_gather(gains, "dp", axis=1, tiled=True)]
    wo, wu, wd = shared(w_out), shared(w_up), shared(w_down)
    blocks = len(wo)
    ot = exchange(o)
    ot = ot.reshape(feat, tok)
    result, gy, gr, do, small, *halves = middle(
        ot,
        mask,
        gains,
        x,
        y,
        target,
        wo,
        wu,
        wd,
        BF16 if cross else F32,
        [ffn_shape(ctx, feat, wide)] * (2 * cross),
    )
    do = do.reshape(HEADS, size, tok)
    if cross:
        rings = [[h * ways + r for h in RING] for r in range(ways)]
        gathered = lax.all_gather(late_x, "ctx", axis=0, axis_index_groups=rings)
    do = exchange(do)
    if cross:
        sums = join(halves[0], swap(halves[1], "dp", 1))
        do, sums, gathered, result, gy = lax.optimization_barrier(
            (do, sums, gathered, moved(result), moved(gy))
        )
        inner = [[4 * z + k for k in INNER] for z in range(4)]
        outer = [[4 * z + k for z in OUTER] for k in range(4)]
        sums = lax.psum_scatter(
            sums, "ctx", scatter_dimension=0, axis_index_groups=inner, tiled=True
        )
    back_args = (plan, segs, qkv, do, of, lse)
    part = jnp.zeros((HEADS, size, tok), F32)
    others = ()
    if ways > 1:
        part, *others = attend_back(*back_args, kvs[1:], ways, tuple(range(1, ways)), None)
    others = [around(other, -(j + 1)) for j, other in enumerate(others)]
    dq, own = attend_back(*back_args, kvs[:1], ways, (0,), part)
    for other in others:
        own = own + other.astype(F32)
    sent = jnp.concatenate([dq, own.astype(BF16)], axis=1)
    back = exchange(sent)
    back, *staged = lax.optimization_barrier((back, *stage([gr], *attn_weights)))
    if cross:
        mine, away = head_grads(ctx, sent, gathered, small)
        mine, away = halve(1, 1, 16, mine, swap(away, "dp", 1))
        pieces = merge(16, mine, swap(away, "ctx", 1))
        pieces, sums = lax.optimization_barrier((pieces, sums))
        sums = lax.psum_scatter(
            sums, "ctx", scatter_dimension=0, axis_index_groups=outer, tiled=True
        )
        pieces = exchange(pieces)
        gx = moved(last(blocks, back, staged[0], staged[1:], BF16))
        loss, result, gx, gy, gq, gk, gv, g1, g2, g3, inverse = finish(pieces, gx, gy, result)
        go, gu, gd = spread(sums, inverse, gq.shape[0], wide)
        gains_out = [g.reshape(-1) for g in (g1, g2, g3)]
        loss = loss.reshape(())
    else:
        x1, h, df, dz, da = halves
        total = lax.psum(small, both)
        inverse = 1.0 / total[3, 1]
        loss = total[3, 0] * inverse

        def scattered(block):
            block = block * inverse
            return lax.psum_scatter(block, both, scatter_dimension=0, tiled=True)

        gx = last(blocks, back, staged[0], staged[1:], F32)
        parts = [back[:, j * size : (j + 1) * size, :].reshape(feat, tok) for j in range(3)]
        gq, gk, gv = [scattered(dot_t(x.T, part)) for part in parts]
        go = scattered(dot(ot, da))
        gu = scattered(dot(x1.T, dz))
        gd = scattered(dot(h.T, df))
        gx, gy = gx * inverse, gy * inverse
        step = feat // (sides * ctx)
        number = side * ctx + place
        gains_out = [
            lax.dynamic_slice_in_dim(
                jnp.concatenate([total[k], total[k + 4]]) * inverse, number * step, step
            )
            for k in range(3)
        ]
    return (
        loss,
        result[None],
        gx[None],
        gy[None],
        gq,
        gk,
        gv,
        go,
        gu,
        gd,
        gains_out[0],
        gains_out[1],
        gains_out[2],
    )


def solution(mesh):
    tokens = P("dp", "ctx", None)
    rows = P("dp", None)
    spread = P(("dp", "ctx"), None)
    gain = P(("dp", "ctx"))
    return jax.shard_map(
        body,
        mesh=mesh,
        in_specs=(tokens,) * 3 + (rows, P("dp", "ctx")) + (rows,) * 6 + (P("dp"),) * 3,
        out_specs=(P(), tokens, tokens, tokens) + (spread,) * 6 + (gain,) * 3,
        check_vma=False,
    )
```

time: 182 us -> 171 us (0.940)
  local copies, waits for them, and re-layouts: 11.4 us -> 1.2 us
  Pallas kernels: 58.4 us -> 51.5 us
  starting transfers between devices: 47.4 us -> 51 us
  waiting for transfers between devices: 47.2 us -> 50.2 us
    all_to_all x5, waiting for transfers between devices: 26.6 us -> 38.6 us  [exchange(): lax.all_to_all(block, 'ctx', 0, 0, axis_index_groups=groups, tiled=True)]
    unnamed x74 -> x32, local copies, waits for them, and re-layouts: 11.4 us -> 1.18 us
    reduce_scatter x1, waiting for transfers between devices: 5.91 us -> 1.16 us  [body(): lax.psum_scatter(sums, 'ctx', scatter_dimension=0, axis_index_groups=oute...]
    ppermute x13, starting transfers between devices: 13.1 us -> 16.1 us  [swap(): return lax.ppermute(block, axis, [(i, i ^ bit) for i in range(size)])]
    all_gather x1, waiting for transfers between devices: 2.73 us -> 0.01 us  [body(): gathered = lax.all_gather(late_x, 'ctx', axis=0, axis_index_groups=rings)]
    all_to_all x5, starting transfers between devices: 22.7 us -> 25.4 us  [exchange(): lax.all_to_all(block, 'ctx', 0, 0, axis_index_groups=groups, tiled=True)]
    pallas_call x7 -> x8, Pallas kernels: 28.7 us -> 26.4 us  [the longest x1 11.4 us: middle(): pl.pallas_call(functools.partial(middle_kernel, blocks, tile), out_shape=...]
    ppermute x7, starting transfers between devices: 11.5 us -> 9.46 us  [moved(): return lax.ppermute(block, both, route)]
  transfers between devices with their start and end apart: 28 -> 28, of which waited for: 15 -> 15; matrix products, arithmetic and copies ran while one was open for 2% -> 1% of each run, Pallas kernels for 29% -> 27%
where the time goes in v3:
time: 171 us; the launch traced here: 170 us
  Pallas kernels  51.5 us (30%)
  starting transfers between devices  51 us (30%)
  waiting for transfers between devices  50.2 us (29%)
  between operations  14.1 us (8%)
  other arithmetic  1.82 us (1%)
    all_to_all x5, waiting for transfers between devices, exchange(): lax.all_to_all(block, 'ctx', 0, 0, axis_index_groups=groups, tiled=True)  38.6 us
    all_to_all x5, starting transfers between devices, exchange(): lax.all_to_all(block, 'ctx', 0, 0, axis_index_groups=groups, tiled=True)  25.4 us
    ppermute x13, starting transfers between devices, swap(): return lax.ppermute(block, axis, [(i, i ^ bit) for i in range(size)])  16.1 us
    pallas_call x2, Pallas kernels, attend_back(): pl.pallas_call(functools.partial(backward_kernel, ways, slots, final, len...  13.8 us
    pallas_call x1, Pallas kernels, middle(): pl.pallas_call(functools.partial(middle_kernel, blocks, tile), out_shape=...  11.4 us
    ppermute x7, starting transfers between devices, moved(): return lax.ppermute(block, both, route)  9.46 us
    ppermute x13, waiting for transfers between devices, swap(): return lax.ppermute(block, axis, [(i, i ^ bit) for i in range(size)])  9.2 us
    pallas_call x1, Pallas kernels, attend(): pl.pallas_call(functools.partial(forward_kernel, ways, len(segs)), out_sh...  7.11 us
  transfers between devices with their start and end apart: 28, of which 15 were waited for; matrix products, arithmetic and copies ran while one was open for 1% of the time, Pallas kernels for 27%

profile of v3, /device:TPU:0, one launch (start us, length us, event | category | flops | bytes accessed | tf_op | source)
XLA Modules:
  0.0 169.9 jit_solution(10610454868908170081)
XLA Ops:
  7.2 1.7 %collective-permute-start = (bf16[256,512]{1,0:T(8,128)(2,1)}, bf16[256,512]{1,0:T(8,128)(2,1)S(1)}, u32[]{:S(2)}, u32[]{:S(2)}) collective-permute-start(bf16[256,512]{1,0:T(8,128)(2,1)} %bitcast.23), channel_id=1, source_target_pairs={{0,0},{1,16},{2,2},{3,18},{4,4},{5,20},{6,6},{7,22},{8,8},{9,24},{... | collective-permute-start | bytes 786440 | tf_op jit(solution)/shard_map/ppermute | solution.py:1074
  8.9 3.4 %collective-permute-start.1 = (bf16[256,512]{1,0:T(8,128)(2,1)}, bf16[256,512]{1,0:T(8,128)(2,1)S(1)}, u32[]{:S(2)}, u32[]{:S(2)}) collective-permute-start(bf16[256,512]{1,0:T(8,128)(2,1)} %refs_1_.3), channel_id=1, source_target_pairs={{0,16},{16,0},{1,17},{17,1},{2,18},{18,2},{3,19},{19,3},{4,20},{20... | collective-permute-start | bytes 786440 | tf_op jit(solution)/shard_map/ppermute | solution.py:76
  14.5 3.2 %project.1 = bf16[8,192,256]{2,1,0:T(8,128)(2,1)} custom-call(bf16[256,512]{1,0:T(8,128)(2,1)} %copy-done.5, bf16[256,512]{1,0:T(8,128)(2,1)} %refs_1_.3, bf16[256,512]{1,0:T(8,128)(2,1)} %refs_3_.1, bf16[256,512]{1,0:T(8,128)(2,1)} %refs_5_.1, bf16[256,512]{1,0:T(8,128)(2,1)S(1)} %collective-permute-done.1.refs_3_.refs_2_, ...), custom_call_target="tpu_custom_call" | custom-call | flops 1000 | bytes 1024 | tf_op jit(solution)/shard_map/project/pallas_call | solution.py:156
  17.7 6.0 %all-to-all-start = ((bf16[8,192,256]{2,1,0:T(8,128)(2,1)}), bf16[8,192,256]{2,1,0:T(8,128)(2,1)S(1)}, u32[]{:S(2)}, u32[]{:S(2)}) async-start(bf16[8,192,256]{2,1,0:T(8,128)(2,1)} %project.1), calls=%async_computation | async-start | bytes 1572864 | tf_op jit(solution)/shard_map/all_to_all | solution.py:1082
  25.0 2.5 %collective-permute-start.4 = (s32[16,256]{1,0:T(8,128)S(1)}, s32[16,256]{1,0:T(8,128)S(1)}, u32[]{:S(2)}, u32[]{:S(2)}) collective-permute-start(s32[16,256]{1,0:T(8,128)S(1)} %reshape.50.refs_0_), channel_id=1, source_target_pairs={{0,16},{16,0},{1,17},{17,1},{2,18},{18,2},{3,19},{19,3},{4,20},{20... | collective-permute-start | bytes 49160 | tf_op jit(solution)/shard_map/ppermute | solution.py:76
  28.4 2.8 %plan.1.plan_ref = s32[872]{0:T(1024)S(1)} custom-call(s32[4096]{0:T(1024)S(1)} %bitcast.18, s32[4096]{0:T(1024)S(1)} %bitcast.19), custom_call_target="tpu_custom_call" | custom-call | flops 1000 | bytes 1024 | tf_op jit(solution)/shard_map/plan/pallas_call | solution.py:250
  31.8 12.1 %all-to-all-done.refs_2_.refs_6_ = bf16[8,192,256]{2,1,0:T(8,128)(2,1)S(1)} async-done(((bf16[8,192,256]{2,1,0:T(8,128)(2,1)}), bf16[8,192,256]{2,1,0:T(8,128)(2,1)S(1)}, u32[]{:S(2)}, u32[]{:S(2)}) %all-to-all-start) | async-done | bytes 786464 | tf_op jit(solution)/shard_map/all_to_all | solution.py:1082
  45.8 1.7 %collective-permute-done.6.refs_3_.refs_6_ = bf16[8,192,256]{2,1,0:T(8,128)(2,1)S(1)} collective-permute-done((bf16[8,192,256]{2,1,0:T(8,128)(2,1)S(1)}, bf16[8,192,256]{2,1,0:T(8,128)(2,1)S(1)}, u32[]{:S(2)}, u32[]{:S(2)}) %collective-permute-start.6) | collective-permute-done | bytes 786464 | tf_op jit(solution)/shard_map/ppermute | solution.py:76
  47.5 7.1 %attend.1 = (bf16[8,64,256]{2,1,0:T(8,128)(2,1)}, f32[8,64,256]{2,1,0:T(8,128)}, f32[8,256]{1,0:T(8,128)S(1)}) custom-call(s32[872]{0:T(1024)} %copy-done.3, s32[16,256]{1,0:T(8,128)S(1)} %reshape.50.refs_0_, s32[16,256]{1,0:T(8,128)S(1)} %collective-permute-done.4.refs_1_, bf16[8,192,256]{2,1,0:T(8,128)(2,1)S(1)} %all-to-all-done.refs_2_.refs_6_, ...), custom_call_target="tpu_custom_call" | custom-call | flops 1000 | bytes 1024 | tf_op jit(solution)/shard_map/attend/pallas_call | solution.py:370
  54.7 3.6 %all-to-all-start.1 = ((bf16[8,64,256]{2,1,0:T(8,128)(2,1)}), bf16[8,64,256]{2,1,0:T(8,128)(2,1)S(1)}, u32[]{:S(2)}, u32[]{:S(2)}) async-start(bf16[8,64,256]{2,1,0:T(8,128)(2,1)} %get-tuple-element.67), calls=%async_computation.1 | async-start | bytes 524288 | tf_op jit(solution)/shard_map/all_to_all | solution.py:1082
  58.4 1.6 collective-permute-start.7
  60.8 1.6 collective-permute-start.9
  62.5 8.9 %all-to-all-done.1 = bf16[8,64,256]{2,1,0:T(8,128)(2,1)S(1)} async-done(((bf16[8,64,256]{2,1,0:T(8,128)(2,1)}), bf16[8,64,256]{2,1,0:T(8,128)(2,1)S(1)}, u32[]{:S(2)}, u32[]{:S(2)}) %all-to-all-start.1) | async-done | bytes 262176 | tf_op jit(solution)/shard_map/all_to_all | solution.py:1082
  71.4 11.4 %middle.1 = (bf16[256,512]{1,0:T(8,128)(2,1)}, bf16[256,512]{1,0:T(8,128)(2,1)}, f32[256,512]{1,0:T(8,128)}, bf16[512,256]{1,0:T(8,128)(2,1)}, f32[8,256]{1,0:T(...) custom-call(bf16[512,256]{1,0:T(8,128)(2,1)S(1)} %bitcast.16, ...), custom_call_target="tpu_custom_call" | custom-call | flops 1000 | bytes 1024 | tf_op jit(solution)/shard_map/middle/pallas_call | solution.py:727
  83.5 5.2 %all-to-all-start.2 = ((bf16[8,64,256]{2,1,0:T(8,128)(2,1)}), bf16[8,64,256]{2,1,0:T(8,128)(2,1)S(1)}, u32[]{:S(2)}, u32[]{:S(2)}) async-start(bf16[8,64,256]{2,1,0:T(8,128)(2,1)} %bitcast.5), calls=%async_computation.2 | async-start | bytes 524288 | tf_op jit(solution)/shard_map/all_to_all | solution.py:1082
  88.8 1.6 collective-permute-start.14
  90.4 1.6 collective-permute-start.15
  92.0 3.4 %join.1 = bf16[16,144,512]{2,1,0:T(8,128)(2,1)} custom-call(bf16[16,144,512]{2,1,0:T(8,128)(2,1)} %get-tuple-element.70.one_in, bf16[16,144,512]{2,1,0:T(8,128)(2,1)} %collective-permute-done.13.two_in), custom_call_target="tpu_custom_call" | custom-call | flops 1000 | bytes 1024 | tf_op jit(solution)/shard_map/join/pallas_call | solution.py:802
  95.5 2.4 %all-to-all-done.2.refs_3_ = bf16[8,64,256]{2,1,0:T(8,128)(2,1)S(1)} async-done(((bf16[8,64,256]{2,1,0:T(8,128)(2,1)}), bf16[8,64,256]{2,1,0:T(8,128)(2,1)S(1)}, u32[]{:S(2)}, u32[]{:S(2)}) %all-to-all-start.2) | async-done | bytes 262176 | tf_op jit(solution)/shard_map/all_to_all | solution.py:1082
  97.9 7.7 %attend_back.2 = (f32[8,64,256]{2,1,0:T(8,128)S(1)}, bf16[8,128,256]{2,1,0:T(8,128)(2,1)S(1)}) custom-call(s32[872]{0:T(1024)} %copy-done.3, s32[16,256]{1,0:T(8,128)S(1)} %reshape.50.refs_0_, s32[16,256]{1,0:T(8,128)S(1)} %collective-permute-done.4.refs_1_, bf16[8,192,256]{2,1,0:T(8,128)(2,1)S(1)} %all-to-all-done.refs_2_.refs_6_, ...), custom_call_target="tpu_custom_call" | custom-call | flops 1000 | bytes 1024 | tf_op jit(solution)/shard_map/attend_back/pallas_call | solution.py:476
  105.7 1.9 %collective-permute-start.16 = (bf16[8,128,256]{2,1,0:T(8,128)(2,1)S(1)}, bf16[8,128,256]{2,1,0:T(8,128)(2,1)S(1)}, u32[]{:S(2)}, u32[]{:S(2)}) collective-permute-start(bf16[8,128,256]{2,1,0:T(8,128)(2,1)S(1)} %get-tuple-element.81), channel_id=1, source_target_pairs={{0,16},{16,0},{1,17},{17,1},{2,18},{18,2},{3,19},{19,3},{4,20},{20... | collective-permute-start | bytes 1572872 | tf_op jit(solution)/shard_map/ppermute | solution.py:76
  107.5 6.1 %attend_back.3 = (bf16[8,64,256]{2,1,0:T(8,128)(2,1)S(1)}, f32[8,128,256]{2,1,0:T(8,128)S(1)}) custom-call(s32[872]{0:T(1024)} %copy-done.3, s32[16,256]{1,0:T(8,128)S(1)} %reshape.50.refs_0_, s32[16,256]{1,0:T(8,128)S(1)} %collective-permute-done.4.refs_1_, bf16[8,192,256]{2,1,0:T(8,128)(2,1)S(1)} %all-to-all-done.refs_2_.refs_6_, ...), custom_call_target="tpu_custom_call" | custom-call | flops 1000 | bytes 1024 | tf_op jit(solution)/shard_map/attend_back/pallas_call | solution.py:476
  114.8 6.0 %all-to-all-start.4 = ((bf16[8,192,256]{2,1,0:T(8,128)(2,1)}), bf16[8,192,256]{2,1,0:T(8,128)(2,1)S(1)}, u32[]{:S(2)}, u32[]{:S(2)}) async-start(bf16[8,192,256]{2,1,0:T(8,128)(2,1)} %pad_maximum_fusion.back_ref), calls=%async_computation.5 | async-start | bytes 1572864 | tf_op jit(solution)/shard_map/all_to_all | solution.py:1082
  120.8 3.2 %head_grads.1 = (bf16[16,32,256]{2,1,0:T(8,128)(2,1)S(1)}, bf16[16,32,256]{2,1,0:T(8,128)(2,1)S(1)}) custom-call(bf16[8,192,256]{2,1,0:T(8,128)(2,1)} %pad_maximum_fusion.back_ref, bf16[8,256,512]{2,1,0:T(8,128)(2,1)} %bitcast.20, f32[8,256]{1,0:T(8,128)S(1)} %get-tuple-element.83.small_ref), custom_call_target="tpu_custom_call" | custom-call | flops 1000 | bytes 1024 | tf_op jit(solution)/shard_map/head_grads/pallas_call | solution.py:896
  124.0 2.0 %collective-permute-start.17 = (bf16[16,32,256]{2,1,0:T(8,128)(2,1)S(1)}, bf16[16,32,256]{2,1,0:T(8,128)(2,1)S(1)}, u32[]{:S(2)}, u32[]{:S(2)}) collective-permute-start(bf16[16,32,256]{2,1,0:T(8,128)(2,1)S(1)} %get-tuple-element.85), channel_id=1, source_target_pairs={{0,16},{16,0},{1,17},{17,1},{2,18},{18,2},{3,19},{19,3},{4,20},{20... | collective-permute-start | bytes 786440 | tf_op jit(solution)/shard_map/ppermute | solution.py:76
  128.7 4.5 %collective-permute-done.18.two_ref = bf16[8,32,256]{2,1,0:T(8,128)(2,1)S(1)} collective-permute-done((bf16[8,32,256]{2,1,0:T(8,128)(2,1)S(1)}, bf16[8,32,256]{2,1,0:T(8,128)(2,1)S(1)}, u32[]{:S(2)}, u32[]{:S(2)}) %collective-permute-start.18) | collective-permute-done | bytes 131104 | tf_op jit(solution)/shard_map/ppermute | solution.py:76
  135.0 1.6 stage.1
  136.6 4.8 %all-to-all-done.4.back_ref = bf16[8,192,256]{2,1,0:T(8,128)(2,1)S(1)} async-done(((bf16[8,192,256]{2,1,0:T(8,128)(2,1)}), bf16[8,192,256]{2,1,0:T(8,128)(2,1)S(1)}, u32[]{:S(2)}, u32[]{:S(2)}) %all-to-all-start.4) | async-done | bytes 786464 | tf_op jit(solution)/shard_map/all_to_all | solution.py:1082
  142.6 1.6 collective-permute-start.19
  144.2 4.6 %all-to-all-start.3 = ((bf16[8,32,256]{2,1,0:T(8,128)(2,1)}), bf16[8,32,256]{2,1,0:T(8,128)(2,1)S(1)}, u32[]{:S(2)}, u32[]{:S(2)}) async-start(bf16[8,32,256]{2,1,0:T(8,128)(2,1)} %merge.1), calls=%async_computation.4 | async-start | bytes 262144 | tf_op jit(solution)/shard_map/all_to_all | solution.py:1082
  148.8 10.5 %all-to-all-done.3.pieces_ref = bf16[8,32,256]{2,1,0:T(8,128)(2,1)S(1)} async-done(((bf16[8,32,256]{2,1,0:T(8,128)(2,1)}), bf16[8,32,256]{2,1,0:T(8,128)(2,1)S(1)}, u32[]{:S(2)}, u32[]{:S(2)}) %all-to-all-start.3) | async-done | bytes 131104 | tf_op jit(solution)/shard_map/all_to_all | solution.py:1082
  161.7 1.7 spread.1
  (81 shorter events, 17.8 us)
Async XLA Ops:
  7.2 5.7 %collective-permute-start = (bf16[256,512]{1,0:T(8,128)(2,1)}, bf16[256,512]{1,0:T(8,128)(2,1)S(1)}, u32[]{:S(2)}, u32[]{:S(2)}) collective-permute-start(bf16[256,512]{1,0:T(8,128)(2,1)} %bitcast.23), channel_id=1, source_target_pairs={{0,0},{1,16},{2,2},{3,18},{4,4},{5,20},{6,6},{7,22},{8,8},{9,24},{... | collective-permute-start | bytes 786440 | tf_op jit(solution)/shard_map/ppermute | solution.py:1074
  8.9 4.8 %collective-permute-start.1 = (bf16[256,512]{1,0:T(8,128)(2,1)}, bf16[256,512]{1,0:T(8,128)(2,1)S(1)}, u32[]{:S(2)}, u32[]{:S(2)}) collective-permute-start(bf16[256,512]{1,0:T(8,128)(2,1)} %refs_1_.3), channel_id=1, source_target_pairs={{0,16},{16,0},{1,17},{17,1},{2,18},{18,2},{3,19},{19,3},{4,20},{20... | collective-permute-start | bytes 786440 | tf_op jit(solution)/shard_map/ppermute | solution.py:76
  12.4 1.7 %collective-permute-start.2 = (bf16[256,512]{1,0:T(8,128)(2,1)}, bf16[256,512]{1,0:T(8,128)(2,1)S(1)}, u32[]{:S(2)}, u32[]{:S(2)}) collective-permute-start(bf16[256,512]{1,0:T(8,128)(2,1)} %refs_3_.1), channel_id=1, source_target_pairs={{0,16},{16,0},{1,17},{17,1},{2,18},{18,2},{3,19},{19,3},{4,20},{20... | collective-permute-start | bytes 786440 | tf_op jit(solution)/shard_map/ppermute | solution.py:76
  12.4 2.0 %collective-permute-start.3 = (bf16[256,512]{1,0:T(8,128)(2,1)}, bf16[256,512]{1,0:T(8,128)(2,1)S(1)}, u32[]{:S(2)}, u32[]{:S(2)}) collective-permute-start(bf16[256,512]{1,0:T(8,128)(2,1)} %refs_5_.1), channel_id=1, source_target_pairs={{0,16},{16,0},{1,17},{17,1},{2,18},{18,2},{3,19},{19,3},{4,20},{20... | collective-permute-start | bytes 786440 | tf_op jit(solution)/shard_map/ppermute | solution.py:76
  13.7 40.9 %copy-start = (bf16[256,512]{1,0:T(8,128)(2,1)}, bf16[256,512]{1,0:T(8,128)(2,1)S(1)}, u32[]{:S(2)}) copy-start(bf16[256,512]{1,0:T(8,128)(2,1)S(1)} %collective-permute-done.1.refs_3_.refs_2_) | copy-start | bytes 786436
  17.7 40.7 %copy-start.14 = (bf16[256]{0:T(256)(128)(2,1)S(1)}, bf16[256]{0:T(256)(128)(2,1)}, u32[]{:S(2)}) copy-start(bf16[256]{0:T(256)(128)(2,1)} %param.27) | copy-start | bytes 1540
  17.7 42.3 %copy-start.6 = (bf16[256,512]{1,0:T(8,128)(2,1)S(1)}, bf16[256,512]{1,0:T(8,128)(2,1)}, u32[]{:S(2)}) copy-start(bf16[256,512]{1,0:T(8,128)(2,1)} %refs_7_.1) | copy-start | bytes 786436
  17.7 42.4 %copy-start.10 = (bf16[1,256,512]{2,1,0:T(8,128)(2,1)S(1)}, bf16[1,256,512]{2,1,0:T(8,128)(2,1)}, u32[]{:S(2)}) copy-start(bf16[1,256,512]{2,1,0:T(8,128)(2,1)} %param.15) | copy-start | bytes 786436
  17.7 26.2 %all-to-all-start = ((bf16[8,192,256]{2,1,0:T(8,128)(2,1)}), bf16[8,192,256]{2,1,0:T(8,128)(2,1)S(1)}, u32[]{:S(2)}, u32[]{:S(2)}) async-start(bf16[8,192,256]{2,1,0:T(8,128)(2,1)} %project.1), calls=%async_computation | async-start | bytes 1572864 | tf_op jit(solution)/shard_map/all_to_all | solution.py:1082
  23.7 74.2 %all-gather.3.cloned.1.call-start = ((), (), s32[]{:S(2)}) async-start(), calls=%async_computation.9 | async-start | bytes 2359296 | tf_op jit(solution)/shard_map/all_gather | solution.py:1130
  25.0 3.4 %collective-permute-start.4 = (s32[16,256]{1,0:T(8,128)S(1)}, s32[16,256]{1,0:T(8,128)S(1)}, u32[]{:S(2)}, u32[]{:S(2)}) collective-permute-start(s32[16,256]{1,0:T(8,128)S(1)} %reshape.50.refs_0_), channel_id=1, source_target_pairs={{0,16},{16,0},{1,17},{17,1},{2,18},{18,2},{3,19},{19,3},{4,20},{20... | collective-permute-start | bytes 49160 | tf_op jit(solution)/shard_map/ppermute | solution.py:76
  27.5 4.3 %collective-permute-start.5 = (s32[1,256]{1,0:T(1,128)S(1)}, s32[1,256]{1,0:T(1,128)S(1)}, u32[]{:S(2)}, u32[]{:S(2)}) collective-permute-start(s32[1,256]{1,0:T(1,128)S(1)} %copy-done.11), channel_id=1, source_target_pairs={{0,0},{1,16},{2,2},{3,18},{4,4},{5,20},{6,6},{7,22},{8,8},{9,24},{... | collective-permute-start | bytes 3080 | tf_op jit(solution)/shard_map/ppermute | solution.py:1074
  44.0 3.6 %collective-permute-start.6 = (bf16[8,192,256]{2,1,0:T(8,128)(2,1)S(1)}, bf16[8,192,256]{2,1,0:T(8,128)(2,1)S(1)}, u32[]{:S(2)}, u32[]{:S(2)}) collective-permute-start(bf16[8,192,256]{2,1,0:T(8,128)(2,1)S(1)} %all-to-all-done.refs_2_.refs_6_), channel_id=1, source_target_pairs={{0,16},{16,0},{1,17},{17,1},{2,18},{18,2},{3,19},{19,3},{4,20},{20... | collective-permute-start | bytes 2359304 | tf_op jit(solution)/shard_map/ppermute | solution.py:76
  45.3 17.2 %collective-permute-start.11 = (bf16[256,2048]{1,0:T(8,128)(2,1)}, bf16[256,2048]{1,0:T(8,128)(2,1)}, u32[]{:S(2)}, u32[]{:S(2)}) collective-permute-start(bf16[256,2048]{1,0:T(8,128)(2,1)} %refs_9_.1), channel_id=1, source_target_pairs={{0,16},{16,0},{1,17},{17,1},{2,18},{18,2},{3,19},{19,3},{4,20},{20... | collective-permute-start | bytes 3145736 | tf_op jit(solution)/shard_map/ppermute | solution.py:76
  45.4 17.1 %collective-permute-start.12 = (bf16[1024,512]{1,0:T(8,128)(2,1)}, bf16[1024,512]{1,0:T(8,128)(2,1)}, u32[]{:S(2)}, u32[]{:S(2)}) collective-permute-start(bf16[1024,512]{1,0:T(8,128)(2,1)} %refs_11_.1), channel_id=1, source_target_pairs={{0,16},{16,0},{1,17},{17,1},{2,18},{18,2},{3,19},{19,3},{4,20},{20... | collective-permute-start | bytes 3145736 | tf_op jit(solution)/shard_map/ppermute | solution.py:76
  54.7 16.7 %all-to-all-start.1 = ((bf16[8,64,256]{2,1,0:T(8,128)(2,1)}), bf16[8,64,256]{2,1,0:T(8,128)(2,1)S(1)}, u32[]{:S(2)}, u32[]{:S(2)}) async-start(bf16[8,64,256]{2,1,0:T(8,128)(2,1)} %get-tuple-element.67), calls=%async_computation.1 | async-start | bytes 524288 | tf_op jit(solution)/shard_map/all_to_all | solution.py:1082
  58.4 2.4 %collective-permute-start.7 = (bf16[3,256]{1,0:T(4,128)(2,1)S(1)}, bf16[3,256]{1,0:T(4,128)(2,1)S(1)}, u32[]{:S(2)}, u32[]{:S(2)}) collective-permute-start(bf16[3,256]{1,0:T(4,128)(2,1)S(1)} %pad_maximum_fusion.1.refs_2_), channel_id=1, source_target_pairs={{0,16},{16,0},{1,17},{17,1},{2,18},{18,2},{3,19},{19,3},{4,20},{20... | collective-permute-start | bytes 4616 | tf_op jit(solution)/shard_map/ppermute | solution.py:76
  60.0 2.4 %collective-permute-start.10 = (bf16[256,512]{1,0:T(8,128)(2,1)S(1)}, bf16[256,512]{1,0:T(8,128)(2,1)S(1)}, u32[]{:S(2)}, u32[]{:S(2)}) collective-permute-start(bf16[256,512]{1,0:T(8,128)(2,1)S(1)} %copy-done.6), channel_id=1, source_target_pairs={{0,16},{16,0},{1,17},{17,1},{2,18},{18,2},{3,19},{19,3},{4,20},{20... | collective-permute-start | bytes 786440 | tf_op jit(solution)/shard_map/ppermute | solution.py:76
  60.1 2.3 %collective-permute-start.8 = (bf16[256,512]{1,0:T(8,128)(2,1)S(1)}, bf16[256,512]{1,0:T(8,128)(2,1)S(1)}, u32[]{:S(2)}, u32[]{:S(2)}) collective-permute-start(bf16[256,512]{1,0:T(8,128)(2,1)S(1)} %bitcast.24), channel_id=1, source_target_pairs={{0,0},{1,16},{2,2},{3,18},{4,4},{5,20},{6,6},{7,22},{8,8},{9,24},{... | collective-permute-start | bytes 786440 | tf_op jit(solution)/shard_map/ppermute | solution.py:1074
  60.8 1.6 collective-permute-start.9
  82.8 9.3 %collective-permute-start.13 = (bf16[16,144,512]{2,1,0:T(8,128)(2,1)}, bf16[16,144,512]{2,1,0:T(8,128)(2,1)}, u32[]{:S(2)}, u32[]{:S(2)}) collective-permute-start(bf16[16,144,512]{2,1,0:T(8,128)(2,1)} %get-tuple-element.71), channel_id=1, source_target_pairs={{0,16},{16,0},{1,17},{17,1},{2,18},{18,2},{3,19},{19,3},{4,20},{20... | collective-permute-start | bytes 7077896 | tf_op jit(solution)/shard_map/ppermute | solution.py:76
  83.5 14.4 %all-to-all-start.2 = ((bf16[8,64,256]{2,1,0:T(8,128)(2,1)}), bf16[8,64,256]{2,1,0:T(8,128)(2,1)S(1)}, u32[]{:S(2)}, u32[]{:S(2)}) async-start(bf16[8,64,256]{2,1,0:T(8,128)(2,1)} %bitcast.5), calls=%async_computation.2 | async-start | bytes 524288 | tf_op jit(solution)/shard_map/all_to_all | solution.py:1082
  88.8 46.2 %reduce-scatter.3.cloned.1.call-start = ((), (), s32[]{:S(2)}) async-start(), calls=%async_computation.7 | async-start | bytes 2949120 | tf_op jit(solution)/shard_map/reduce_scatter | solution.py:1139
  88.8 6.6 %collective-permute-start.14 = (bf16[256,512]{1,0:T(8,128)(2,1)}, bf16[256,512]{1,0:T(8,128)(2,1)S(1)}, u32[]{:S(2)}, u32[]{:S(2)}) collective-permute-start(bf16[256,512]{1,0:T(8,128)(2,1)} %get-tuple-element.73), channel_id=1, source_target_pairs={{0,0},{1,16},{2,2},{3,18},{4,4},{5,20},{6,6},{7,22},{8,8},{9,24},{... | collective-permute-start | bytes 786440 | tf_op jit(solution)/shard_map/ppermute | solution.py:1074
  90.4 5.0 %collective-permute-start.15 = (bf16[256,512]{1,0:T(8,128)(2,1)}, bf16[256,512]{1,0:T(8,128)(2,1)S(1)}, u32[]{:S(2)}, u32[]{:S(2)}) collective-permute-start(bf16[256,512]{1,0:T(8,128)(2,1)} %get-tuple-element.74), channel_id=1, source_target_pairs={{0,0},{1,16},{2,2},{3,18},{4,4},{5,20},{6,6},{7,22},{8,8},{9,24},{... | collective-permute-start | bytes 786440 | tf_op jit(solution)/shard_map/ppermute | solution.py:1074
  105.7 8.0 %collective-permute-start.16 = (bf16[8,128,256]{2,1,0:T(8,128)(2,1)S(1)}, bf16[8,128,256]{2,1,0:T(8,128)(2,1)S(1)}, u32[]{:S(2)}, u32[]{:S(2)}) collective-permute-start(bf16[8,128,256]{2,1,0:T(8,128)(2,1)S(1)} %get-tuple-element.81), channel_id=1, source_target_pairs={{0,16},{16,0},{1,17},{17,1},{2,18},{18,2},{3,19},{19,3},{4,20},{20... | collective-permute-start | bytes 1572872 | tf_op jit(solution)/shard_map/ppermute | solution.py:76
  114.8 26.6 %all-to-all-start.4 = ((bf16[8,192,256]{2,1,0:T(8,128)(2,1)}), bf16[8,192,256]{2,1,0:T(8,128)(2,1)S(1)}, u32[]{:S(2)}, u32[]{:S(2)}) async-start(bf16[8,192,256]{2,1,0:T(8,128)(2,1)} %pad_maximum_fusion.back_ref), calls=%async_computation.5 | async-start | bytes 1572864 | tf_op jit(solution)/shard_map/all_to_all | solution.py:1082
  120.7 40.9 %reduce-scatter.5.cloned.1.call-start = ((), (), s32[]{:S(2)}) async-start(), calls=%async_computation.8 | async-start | bytes 737280 | tf_op jit(solution)/shard_map/reduce_scatter | solution.py:1159
  124.0 3.2 %collective-permute-start.17 = (bf16[16,32,256]{2,1,0:T(8,128)(2,1)S(1)}, bf16[16,32,256]{2,1,0:T(8,128)(2,1)S(1)}, u32[]{:S(2)}, u32[]{:S(2)}) collective-permute-start(bf16[16,32,256]{2,1,0:T(8,128)(2,1)S(1)} %get-tuple-element.85), channel_id=1, source_target_pairs={{0,16},{16,0},{1,17},{17,1},{2,18},{18,2},{3,19},{19,3},{4,20},{20... | collective-permute-start | bytes 786440 | tf_op jit(solution)/shard_map/ppermute | solution.py:76
  127.3 5.8 %collective-permute-start.18 = (bf16[8,32,256]{2,1,0:T(8,128)(2,1)S(1)}, bf16[8,32,256]{2,1,0:T(8,128)(2,1)S(1)}, u32[]{:S(2)}, u32[]{:S(2)}) collective-permute-start(bf16[8,32,256]{2,1,0:T(8,128)(2,1)S(1)} %get-tuple-element.87), channel_id=1, source_target_pairs={{0,1},{1,0},{2,3},{3,2},{4,5},{5,4},{6,7},{7,6},{8,9},{9,8},{10,11... | collective-permute-start | bytes 393224 | tf_op jit(solution)/shard_map/ppermute | solution.py:76
  142.6 6.2 %collective-permute-start.19 = (bf16[256,512]{1,0:T(8,128)(2,1)}, bf16[256,512]{1,0:T(8,128)(2,1)S(1)}, u32[]{:S(2)}, u32[]{:S(2)}) collective-permute-start(bf16[256,512]{1,0:T(8,128)(2,1)} %last.1), channel_id=1, source_target_pairs={{0,0},{1,16},{2,2},{3,18},{4,4},{5,20},{6,6},{7,22},{8,8},{9,24},{... | collective-permute-start | bytes 786440 | tf_op jit(solution)/shard_map/ppermute | solution.py:1074
  144.2 15.0 %all-to-all-start.3 = ((bf16[8,32,256]{2,1,0:T(8,128)(2,1)}), bf16[8,32,256]{2,1,0:T(8,128)(2,1)S(1)}, u32[]{:S(2)}, u32[]{:S(2)}) async-start(bf16[8,32,256]{2,1,0:T(8,128)(2,1)} %merge.1), calls=%async_computation.4 | async-start | bytes 262144 | tf_op jit(solution)/shard_map/all_to_all | solution.py:1082
  (11 other events, 228.4 us)
Sparse Core Ops, SparseCore 0:
  44.1 37.5 all-gather.2
  98.1 36.8 reduce-scatter.2
  137.3 24.3 reduce-scatter.4

commit v4 on v3

--- a/solution.py
+++ b/solution.py
@@ -127,22 +127,13 @@
     )(*flat)
 
 
-def project_kernel(blocks, x_in, *refs):
-    ins, others = refs[:3], refs[3 : 3 * blocks]
-    out_ref, held, x_ref, sems = refs[3 * blocks :]
+def project_kernel(blocks, x_ref, *refs):
+    out_ref = refs[-1]
     feat = x_ref.shape[1]
     size = feat // HEADS
-    each = feat // blocks
-    first, *copies = fetch(
-        [x_in, *ins], [x_ref, *[held.at[part] for part in range(3)]], sems
-    )
-    first.wait()
-    x = jnp.concatenate(
-        [x_ref[:, rows_of(blocks, j, feat)] for j in range(blocks)], axis=1
-    )
+    x = jnp.concatenate([x_ref[:, rows_of(blocks, j, feat)] for j in range(blocks)], axis=1)
     for part, scale in ((0, size**-0.5), (1, 1.0), (2, 1.0)):
-        copies[part].wait()
-        weight = [held[part]] + [ref[...] for ref in others[part : part + 1]]
+        weight = [refs[j * 3 + part][...] for j in range(blocks)]
         turned = (dot(x, jnp.concatenate(weight, axis=0)) * scale).astype(BF16).T
         for h in range(HEADS):
             out_ref[h, part * size : (part + 1) * size, :] = turned[h * size : (h + 1) * size, :]
@@ -150,23 +141,17 @@
 
 def project(x, weights):
     tok, feat = x.shape
-    blocks = len(weights[0])
-    mine = [weight[0] for weight in weights]
-    others = [weight[1] for weight in weights if blocks == 2]
-    return pl.pallas_call(
-        functools.partial(project_kernel, blocks),
+    flat = stage(*[[weight[0]] for weight in weights])
+    flat += tuple(block for weight in weights for block in weight[1:])
+    return pl.pallas_call(
+        functools.partial(project_kernel, len(weights[0])),
         out_shape=kept((HEADS, 3 * feat // HEADS, tok), BF16),
-        in_specs=hbm(4) + vmem(len(others)),
+        in_specs=vmem(1 + len(flat)),
         out_specs=vmem(1)[0],
-        scratch_shapes=[
-            pltpu.VMEM((3, feat // blocks, feat), BF16),
-            pltpu.VMEM((tok, feat), BF16),
-            pltpu.SemaphoreType.DMA((4,)),
-        ],
         compiler_params=pltpu.CompilerParams(vmem_limit_bytes=6 * MIB),
         cost_estimate=cost(1.4),
         name="project",
-    )(far(x), *map(far, mine), *map(near, others))
+    )(near(x), *map(near, flat))
 
 
 def mask_rows(row, hit, miss, extra):
@@ -314,6 +299,7 @@
         for (i, c), part in zip(tiles, mixed):
             acc[i] += part
 
+    leaving = []
     smallest = jnp.full((1, tok), 1.0, F32)
     largest = jnp.full((1, tok), 1.0, F32)
     for i in range(HEADS):
@@ -322,8 +308,11 @@
         largest = jnp.maximum(largest, total)
         out = acc[i, 0:size, :] / total
         of_ref[i] = out
+        leaving += fetch([of_ref.at[i]], [of_out.at[i]], sem, i)
         o_ref[i] = out.astype(BF16)
         lse_ref[i : i + 1, :] = jnp.log(total) * LOG2E
+    for copy in leaving:
+        copy.wait()
     good = (jnp.min(smallest) > 2.0**-90) & (jnp.max(largest) < 2.0**90)
 
     @pl.when(jnp.logical_not(good))
@@ -358,7 +347,7 @@
             lse = jnp.broadcast_to(top + jnp.log(total) * LOG2E, (tok, 128)).T
             lse_ref[pl.ds(i, 1), :] = lse[0:1, :]
 
-    fetch([of_ref], [of_out], sem)[0].wait()
+        fetch([of_ref], [of_out], sem)[0].wait()
 
 
 def attend(plan, segs, kvs):
@@ -383,7 +372,7 @@
             pltpu.VMEM((HEADS + 1, size + 16, tok), F32),
             pltpu.VMEM(segs[0].shape, jnp.int32),
             pltpu.VMEM((HEADS, size, tok), F32),
-            pltpu.SemaphoreType.DMA((1,)),
+            pltpu.SemaphoreType.DMA((HEADS,)),
         ],
         compiler_params=pltpu.CompilerParams(vmem_limit_bytes=12 * MIB),
         cost_estimate=cost(7),
@@ -391,50 +380,106 @@
     )(far(plan), *segs, *map(near, kvs))
 
 
-def backward_kernel(ways, slots, final, texts, plan_ref, *refs):
+def prepare_kernel(ways, texts, lse_ref, *refs):
     seg_refs, refs = refs[:texts], refs[texts:]
-    q_ref, do_ref, of_in, lse_ref = refs[:4]
-    refs = refs[4:]
-    many = len(slots)
-    kv_refs = refs[:many]
-    refs = refs[many:]
-    if final:
-        part_ref, refs = refs[0], refs[1:]
-    dq_ref = refs[0]
-    dkv_refs = refs[1 : 1 + many]
-    kx, vx, qx, dx, dk, dv, dq, seg_ref, of_ref, sem = refs[1 + many :]
-    (copy,) = fetch([of_in], [of_ref], sem)
+    kv_ins = refs[:ways]
+    kx, qx, seg_ref, k_ref, q_ref, sems = refs[ways:]
+    size = q_ref.shape[1]
+    there = (slice(None), pl.ds(size, size), slice(None))
+    copies = fetch([kv.at[there] for kv in kv_ins], [k_ref.at[k] for k in range(ways)], sems)
+    there = (slice(None), pl.ds(0, size), slice(None))
+    copies += fetch([kv_ins[0].at[there]], [q_ref], sems, ways)
     seg_ref[...] = chosen(seg_refs)
-    count, tok = seg_ref.shape
-    size = do_ref.shape[1]
+    tok = seg_ref.shape[1]
     rank = rank_of(ways, texts)
-    ones = (lax.broadcasted_iota(jnp.int32, (16, tok), 0) < 2).astype(F32).astype(BF16)
-    for slot, kv_ref in zip(slots, kv_refs):
+    for slot in range(ways):
+        copies[slot].wait()
 
         @pl.loop(0, HEADS, unroll=UNROLL)
         def fill(h):
             chunk = chunk_of(h, slot, ways, rank)
-            kx[chunk] = key_rows(kv_ref[h, size : 2 * size, :], seg_ref[pl.ds(chunk, 1), :])
-            vx[chunk] = jnp.concatenate([kv_ref[h, 2 * size : 3 * size, :], ones], axis=0)
-            dk[chunk] = jnp.zeros_like(dk[chunk])
-            dv[chunk] = jnp.zeros_like(dv[chunk])
-
-    copy.wait()
+            kx[chunk] = key_rows(k_ref[slot, h], seg_ref[pl.ds(chunk, 1), :])
+
+    copies[ways].wait()
 
     @pl.loop(0, HEADS, unroll=UNROLL)
     def fill_query(i):
         lse = parts_of(-lse_ref[pl.ds(i, 1), :], 3)
-        qx[i] = query_rows(q_ref[i, 0:size, :], seg_ref[pl.ds(i * ways + rank, 1), :], lse)
+        qx[i] = query_rows(q_ref[i], seg_ref[pl.ds(i * ways + rank, 1), :], lse)
+
+    qx[HEADS] = query_rows(jnp.zeros((size, tok), BF16), jnp.full((1, tok), -1, jnp.int32), ())
+
+
+def prepare(segs, lse, kvs):
+    ways = len(kvs)
+    count, tok = segs[0].shape
+    size = kvs[0].shape[1] // 3
+    depth = 2 * size + LANES
+    return pl.pallas_call(
+        functools.partial(prepare_kernel, ways, len(segs)),
+        out_shape=(kept((count, depth, tok), BF16), kept((HEADS + 1, tok, depth), BF16)),
+        in_specs=vmem(1 + len(segs)) + hbm(ways),
+        out_specs=tuple(vmem(2)),
+        scratch_shapes=[
+            pltpu.VMEM(segs[0].shape, jnp.int32),
+            pltpu.VMEM((ways, HEADS, size, tok), BF16),
+            pltpu.VMEM((HEADS, size, tok), BF16),
+            pltpu.SemaphoreType.DMA((ways + 1,)),
+        ],
+        compiler_params=pltpu.CompilerParams(vmem_limit_bytes=12 * MIB),
+        cost_estimate=cost(2),
+        name="prepare",
+    )(near(lse), *segs, *map(far, kvs))
+
+
+def backward_kernel(ways, slots, final, texts, plan_ref, kx, qx, do_ref, *refs):
+    many = len(slots)
+    q_in, kv_ins, refs = refs[0], refs[1 : 1 + many], refs[1 + many :]
+    if final:
+        part_ref, dx, dq_ref, *dkv_refs = refs[: 3 + many]
+        refs = refs[3 + many :]
+    else:
+        of_in, dq_ref, dx, *dkv_refs = refs[: 3 + many]
+        refs = refs[3 + many :]
+    vx, dk, dv, dq, q_ref, v_ref, of_ref, sems = refs
+    count, _, tok = kx.shape
+    size = do_ref.shape[1]
+    copies = []
+    if not final:
+        copies += fetch([of_in], [of_ref], sems, 1 + many)
+    for k, kv in enumerate(kv_ins):
+        there = (slice(None), pl.ds(2 * size, size), slice(None))
+        copies += fetch([kv.at[there]], [v_ref.at[k]], sems, 1 + k)
+    there = (slice(None), pl.ds(0, size), slice(None))
+    copies += fetch([q_in.at[there]], [q_ref], sems)
+    rank = rank_of(ways, texts)
+    ones = (lax.broadcasted_iota(jnp.int32, (16, tok), 0) < 2).astype(F32).astype(BF16)
+
+    def open_query(i):
         do = do_ref[i].astype(F32)
         delta = parts_of(-jnp.sum(do * of_ref[i], axis=0, keepdims=True), 3)
         number = lax.broadcasted_iota(jnp.int32, (16, tok), 0)
         tail = jnp.where(number == 0, delta[0], jnp.where(number == 1, delta[1], 0.0))
         dx[i] = jnp.concatenate([do_ref[i], tail.astype(BF16)], axis=0).T
-        dq[i] = part_ref[i] if final else jnp.zeros_like(dq[i])
-
-    qx[HEADS] = query_rows(jnp.zeros((size, tok), BF16), jnp.full((1, tok), -1, jnp.int32), ())
-    dx[HEADS] = jnp.zeros_like(dx[0])
+
+    if final:
+        dq[0:HEADS] = part_ref[...]
+    else:
+        copies.pop(0).wait()
+        pl.loop(0, HEADS, unroll=UNROLL)(open_query)
+        dx[HEADS] = jnp.zeros_like(dx[0])
+        dq[0:HEADS] = jnp.zeros_like(dq[0:HEADS])
     dq[HEADS] = jnp.zeros_like(dq[0])
+    for copy in copies:
+        copy.wait()
+    for k, slot in enumerate(slots):
+
+        @pl.loop(0, HEADS, unroll=UNROLL)
+        def fill(h):
+            chunk = chunk_of(h, slot, ways, rank)
+            vx[chunk] = jnp.concatenate([v_ref[k, h], ones], axis=0)
+            dk[chunk] = jnp.zeros_like(dk[chunk])
+            dv[chunk] = jnp.zeros_like(dv[chunk])
 
     kind = 1 if slots == (0,) else 2
     length = list_size(count)
@@ -448,10 +493,10 @@
         for (i, c), w, ds in zip(tiles, weights, scores):
             j = jnp.minimum(i, HEADS - 1)
             dv[c] += dot(do_ref[j], w.astype(BF16))
-            dk[c] += dot(q_ref[j, 0:size, :], ds)
+            dk[c] += dot(q_ref[j], ds)
             dq[i] += dot_t(kx[c, 0:size, :], ds)
 
-    for slot, kv_ref, out in zip(slots, kv_refs, dkv_refs):
+    for slot, out in zip(slots, dkv_refs):
 
         @pl.loop(0, HEADS, unroll=UNROLL)
         def drain(h):
@@ -467,37 +512,42 @@
             dq_ref[i] = dq[i]
 
 
-def attend_back(plan, segs, q, do, of, lse, kvs, ways, slots, part):
+def attend_back(plan, kx, qx, do, q, kvs, ways, texts, slots, of=None, part=None, dx=None):
     many = len(slots)
     final = part is not None
     _, size, tok = do.shape
-    count = segs[0].shape[0]
-    depth = 2 * size + LANES
-    return pl.pallas_call(
-        functools.partial(backward_kernel, ways, slots, final, len(segs)),
-        out_shape=(kept((HEADS, size, tok), BF16 if final else F32),)
-        + (kept((HEADS, 2 * size, tok), F32 if slots == (0,) else BF16),) * many,
+    count, depth, _ = kx.shape
+    queries = kept((HEADS, size, tok), BF16 if final else F32)
+    grads = (kept((HEADS, 2 * size, tok), F32 if slots == (0,) else BF16),) * many
+    pulls = kept((HEADS + 1, tok, size + 16), BF16)
+    return pl.pallas_call(
+        functools.partial(backward_kernel, ways, slots, final, texts),
+        out_shape=(queries,) + ((pulls,) * (not final)) + grads,
         in_specs=[smem()]
-        + vmem(len(segs) + 2)
-        + hbm(1)
-        + vmem(1 + many + final),
-        out_specs=tuple(vmem(1 + many)),
+        + vmem(3)
+        + hbm(1 + many)
+        + (vmem(2) if final else hbm(1)),
+        out_specs=tuple(vmem(1 + many + (not final))),
         scratch_shapes=[
-            pltpu.VMEM((count, depth, tok), BF16),
             pltpu.VMEM((count, size + 16, tok), BF16),
-            pltpu.VMEM((HEADS + 1, tok, depth), BF16),
-            pltpu.VMEM((HEADS + 1, tok, size + 16), BF16),
             pltpu.VMEM((count, size, tok), F32),
             pltpu.VMEM((count, size, tok), F32),
             pltpu.VMEM((HEADS + 1, size, tok), F32),
-            pltpu.VMEM(segs[0].shape, jnp.int32),
+            pltpu.VMEM((HEADS, size, tok), BF16),
+            pltpu.VMEM((many, HEADS, size, tok), BF16),
             pltpu.VMEM((HEADS, size, tok), F32),
-            pltpu.SemaphoreType.DMA((1,)),
+            pltpu.SemaphoreType.DMA((2 + many,)),
         ],
         compiler_params=pltpu.CompilerParams(vmem_limit_bytes=16 * MIB),
         cost_estimate=cost(7.5),
         name="attend_back",
-    )(far(plan), *segs, near(q), near(do), far(of), near(lse), *map(near, kvs), *((near(part),) if final else ()))
+    )(
+        far(plan),
+        *map(near, (kx, qx, do)),
+        far(q),
+        *map(far, kvs),
+        *((near(part), near(dx)) if final else (far(of),)),
+    )
 
 
 def normed(rows):
@@ -519,11 +569,10 @@
     ot_ref, mask_ref = refs[:2]
     gains_refs = refs[2 : 2 + blocks]
     refs = refs[2 + blocks :]
-    x_in, y_in, t_in = refs[:3]
-    wo_in, wu_in, wd_in = [refs[3 + k * blocks : 3 + (k + 1) * blocks] for k in range(3)]
+    x_ref, wo_ref, both_in = refs[:3]
+    wu_in, wd_in = [refs[3 + k * blocks : 3 + (k + 1) * blocks] for k in range(2)]
     (
-        result_out,
-        gy_out,
+        both_out,
         gr_out,
         dot_ref,
         small_ref,
@@ -536,10 +585,8 @@
         slope,
         acc,
         gr_ref,
-        x_ref,
         y_ref,
         t_ref,
-        wo_ref,
         wu_ref,
         wd_ref,
         xt,
@@ -549,11 +596,8 @@
         sems,
         tile_sems,
         sum_sems,
-    ) = refs[3 + 3 * blocks :]
+    ) = refs[3 + 2 * blocks :]
     part_rows = wo_ref.shape[0] // blocks
-    early = fetch(
-        [*wo_in, x_in], [*[wo_ref.at[pl.ds(j * part_rows, part_rows), :] for j in range(blocks)], x_ref], sems
-    )
     wide = h_ref.shape[1]
     each = wide // blocks
 
@@ -576,9 +620,13 @@
                 k * (blocks + 1),
             )
         )
-    late = fetch([y_in, t_in], [y_ref, t_ref], sems, blocks + 1)
-    for copy in early:
-        copy.wait()
+    tok = x_ref.shape[0]
+    late = fetch(
+        [both_in.at[pl.ds(0, tok), :], both_in.at[pl.ds(tok, tok), :]],
+        [y_ref, t_ref],
+        sems,
+        blocks + 1,
+    )
     rows, feat = x_ref.shape
     halves = [rows_of(blocks, j, feat) for j in range(blocks)]
 
@@ -695,7 +743,11 @@
 
     gr, dg1 = norm_back(n1, r1, g1, du + ordered(acc[...]))
     gr_ref[...] = gr
-    leaving = fetch([gr_ref, out_ref, gy_ref], [gr_out, result_out, gy_out], sems)
+    leaving = fetch(
+        [gr_ref, out_ref, gy_ref],
+        [gr_out, both_out.at[pl.ds(0, tok), :], both_out.at[pl.ds(tok, tok), :]],
+        sems,
+    )
     da = (gr + gy).astype(BF16)
     da_ref[...] = da
     turned = dot_t(wo_ref[...], da).astype(BF16)
@@ -719,7 +771,7 @@
         copy.wait()
 
 
-def middle(ot, mask, gains, x, y, teacher, wo, wu, wd, gy_type, scattered):
+def middle(ot, mask, gains, x, pair, wo, wu, wd, scattered):
     tok, feat = x.shape
     wide = wu[0].shape[1]
     blocks = len(gains)
@@ -727,8 +779,7 @@
     return pl.pallas_call(
         functools.partial(middle_kernel, blocks, tile),
         out_shape=(
-            apart((tok, feat), BF16),
-            apart((tok, feat), gy_type),
+            apart((2 * tok, feat), BF16),
             apart((tok, feat), F32),
             kept((feat, tok), BF16),
             kept((8, feat // 2), F32),
@@ -737,8 +788,8 @@
             tuple(apart(shape, BF16) for shape in scattered)
             or tuple(shaped((tok, size), BF16) for size in (feat, wide, feat, wide, feat))
         ),
-        in_specs=vmem(2 + blocks) + hbm(3 + 3 * blocks),
-        out_specs=tuple(hbm(3) + vmem(2) + (hbm(len(scattered)) or vmem(5))),
+        in_specs=vmem(4 + blocks) + hbm(1 + 2 * blocks),
+        out_specs=tuple(hbm(2) + vmem(2) + (hbm(len(scattered)) or vmem(5))),
         scratch_shapes=[
             pltpu.VMEM((tok, feat), BF16),
             pltpu.VMEM((tok, wide), BF16),
@@ -750,14 +801,12 @@
             pltpu.VMEM((tok, feat), F32),
             pltpu.VMEM((tok, feat), BF16),
             pltpu.VMEM((tok, feat), BF16),
-            pltpu.VMEM((tok, feat), BF16),
-            pltpu.VMEM((feat, feat), BF16),
             pltpu.VMEM((feat, wide), BF16),
             pltpu.VMEM((wide, feat), BF16),
             pltpu.VMEM((feat, tok), BF16),
             pltpu.VMEM((2, *(scattered[0] if scattered else (8, 16, 128))), BF16),
             pltpu.VMEM((tok, feat), BF16),
-            pltpu.VMEM((tok, feat), gy_type),
+            pltpu.VMEM((tok, feat), BF16),
             pltpu.SemaphoreType.DMA((blocks + 3,)),
             pltpu.SemaphoreType.DMA((wide // tile * (blocks + 1),)),
             pltpu.SemaphoreType.DMA((2 * PIECES,)),
@@ -765,7 +814,7 @@
         compiler_params=pltpu.CompilerParams(vmem_limit_bytes=36 * MIB),
         cost_estimate=cost(8),
         name="middle",
-    )(near(ot), mask, *gains, *map(far, (x, y, teacher, *wo, *wu, *wd)))
+    )(near(ot), mask, *gains, near(x), near(wo), *map(far, (pair, *wu, *wd)))
 
 
 def split_sum(values):
@@ -782,18 +831,16 @@
     return (blocks, (wide // feat) * step + wide // (2 * blocks) + step, feat)
 
 
-def join_kernel(one_in, two_in, out, one_ref, two_ref, ref, sems):
-    blocks = one_in.shape[0]
+def join_kernel(two_ref, one_in, out, one_ref, ref, sems):
+    blocks = two_ref.shape[0]
     spans = [pl.ds(k * blocks // PIECES, blocks // PIECES) for k in range(PIECES)]
     ones = fetch([one_in.at[k] for k in spans], [one_ref.at[k] for k in spans], sems)
-    twos = fetch([two_in.at[k] for k in spans], [two_ref.at[k] for k in spans], sems, PIECES)
     going = []
-    for k, (span, one, two) in enumerate(zip(spans, ones, twos)):
+    for k, (span, one) in enumerate(zip(spans, ones)):
         one.wait()
-        two.wait()
         for b in range(k * blocks // PIECES, (k + 1) * blocks // PIECES):
             ref[b] = added(one_ref[b], two_ref[b], 0)
-        going += fetch([ref.at[span]], [out.at[span]], sems, 2 * PIECES + k)
+        going += fetch([ref.at[span]], [out.at[span]], sems, PIECES + k)
     for copy in going:
         copy.wait()
 
@@ -802,14 +849,14 @@
     return pl.pallas_call(
         join_kernel,
         out_shape=apart(one.shape, BF16),
-        in_specs=hbm(2),
+        in_specs=vmem(1) + hbm(1),
         out_specs=hbm(1)[0],
-        scratch_shapes=[pltpu.VMEM(one.shape, BF16)] * 3
-        + [pltpu.SemaphoreType.DMA((3 * PIECES,))],
-        compiler_params=pltpu.CompilerParams(vmem_limit_bytes=12 * MIB),
+        scratch_shapes=[pltpu.VMEM(one.shape, BF16)] * 2
+        + [pltpu.SemaphoreType.DMA((2 * PIECES,))],
+        compiler_params=pltpu.CompilerParams(vmem_limit_bytes=10 * MIB),
         cost_estimate=cost(0.01),
         name="join",
-    )(far(one), far(two))
+    )(near(two), far(one))
 
 
 def added(one, two, tail):
@@ -938,22 +985,8 @@
     )(*map(near, (back, gr, *weights)))
 
 
-def finish_kernel(
-    pieces_ref,
-    gx_in,
-    gy_in,
-    out_in,
-    loss_ref,
-    out_ref,
-    gx_ref,
-    gy_ref,
-    gq_ref,
-    gk_ref,
-    gv_ref,
-    g1_ref,
-    g2_ref,
-    g3_ref,
-    inverse_ref,
+def settle_kernel(
+    pieces_ref, loss_ref, gq_ref, gk_ref, gv_ref, g1_ref, g2_ref, g3_ref, inverse_ref
 ):
     step, feat = gq_ref.shape
     size = feat // HEADS
@@ -963,9 +996,6 @@
     inverse = 1.0 / small[3:4, 1:2]
     inverse_ref[...] = jnp.broadcast_to(inverse, inverse_ref.shape)
     loss_ref[...] = small[3:4, 0:1] * inverse
-    out_ref[...] = out_in[...]
-    gx_ref[...] = gx_in[...].astype(F32) * inverse
-    gy_ref[...] = gy_in[...].astype(F32) * inverse
     for h in range(HEADS):
         block = pieces_ref[h, 0:step, :].astype(F32) * inverse
         for part, ref in enumerate((gq_ref, gk_ref, gv_ref)):
@@ -978,16 +1008,12 @@
     g3_ref[...] = turned[2:3, 0:step]
 
 
-def finish(pieces, gx, gy, result):
-    tok, feat = gx.shape
+def settle(pieces, feat):
     step = pieces.shape[1] - 16
     return pl.pallas_call(
-        finish_kernel,
+        settle_kernel,
         out_shape=(
             shaped((1, 1), F32),
-            shaped((tok, feat), BF16),
-            shaped((tok, feat), F32),
-            shaped((tok, feat), F32),
             shaped((step, feat), F32),
             shaped((step, feat), F32),
             shaped((step, feat), F32),
@@ -996,12 +1022,39 @@
             shaped((1, step), F32),
             kept((8, 128), F32),
         ),
-        in_specs=vmem(4),
-        out_specs=tuple(vmem(11)),
-        compiler_params=pltpu.CompilerParams(vmem_limit_bytes=8 * MIB),
-        cost_estimate=cost(1.8),
+        in_specs=vmem(1),
+        out_specs=tuple(vmem(8)),
+        compiler_params=pltpu.CompilerParams(vmem_limit_bytes=4 * MIB),
+        cost_estimate=pl.CostEstimate(
+            flops=5500000000, bytes_accessed=1024, transcendentals=0
+        ),
+        name="settle",
+    )(near(pieces))
+
+
+def finish_kernel(inverse_ref, gx_in, pair_in, out_ref, gx_ref, gy_ref):
+    inverse = inverse_ref[0:1, 0:1]
+    tok = out_ref.shape[0]
+    out_ref[...] = pair_in[0:tok]
+    gx_ref[...] = gx_in[...].astype(F32) * inverse
+    gy_ref[...] = pair_in[tok : 2 * tok].astype(F32) * inverse
+
+
+def finish(inverse, gx, pair):
+    tok, feat = gx.shape
+    return pl.pallas_call(
+        finish_kernel,
+        out_shape=(
+            shaped((tok, feat), BF16),
+            shaped((tok, feat), F32),
+            shaped((tok, feat), F32),
+        ),
+        in_specs=vmem(3),
+        out_specs=tuple(vmem(3)),
+        compiler_params=pltpu.CompilerParams(vmem_limit_bytes=6 * MIB),
+        cost_estimate=cost(1),
         name="finish",
-    )(near(pieces), gx, gy, result)
+    )(near(inverse), gx, pair)
 
 
 def spread_kernel(sums_in, inverse_ref, go_ref, gu_ref, gd_ref, sums_ref, sem):
@@ -1095,11 +1148,12 @@
     segs = [segment_ids.reshape(ctx, tok)]
     if cross:
         segs.append(swap(segs[0], "dp", 1))
-    y, target, mask = moved(state_y[0]), moved(teacher[0]), moved(valid_mask)
+    mask = moved(valid_mask)
+    pair = jnp.concatenate([state_y[0], teacher[0]], axis=0)
     qkv = project(x, attn_weights)
     plan = plan_of(segs, ways, ctx, tok)
     qkv = exchange(qkv)
-    qkv, plan, mask, late_x = lax.optimization_barrier((qkv, plan, mask, x))
+    qkv, plan, mask, late_x, pair = lax.optimization_barrier((qkv, plan, mask, x, pair))
     kvs = [qkv] + [around(qkv, j) for j in range(1, ways)]
     o, of, lse = attend(plan, segs, kvs)
     gains = jnp.stack([gain_attn, gain_ffn, gain_final])
@@ -1108,20 +1162,20 @@
     else:
         gains = [lax.all_gather(gains, "dp", axis=1, tiled=True)]
     wo, wu, wd = shared(w_out), shared(w_up), shared(w_down)
-    blocks = len(wo)
+    blocks = len(wu)
+    o, pair = lax.optimization_barrier((o, moved(pair)))
     ot = exchange(o)
+    ot, x_near, wo = lax.optimization_barrier((ot, *stage([x], wo)))
     ot = ot.reshape(feat, tok)
-    result, gy, gr, do, small, *halves = middle(
+    pair, gr, do, small, *halves = middle(
         ot,
         mask,
         gains,
-        x,
-        y,
-        target,
+        x_near,
+        pair,
         wo,
         wu,
         wd,
-        BF16 if cross else F32,
         [ffn_shape(ctx, feat, wide)] * (2 * cross),
     )
     do = do.reshape(HEADS, size, tok)
@@ -1131,21 +1185,24 @@
     do = exchange(do)
     if cross:
         sums = join(halves[0], swap(halves[1], "dp", 1))
-        do, sums, gathered, result, gy = lax.optimization_barrier(
-            (do, sums, gathered, moved(result), moved(gy))
-        )
+        lse, sums = lax.optimization_barrier((lse, sums))
+        kx, qx = prepare(segs, lse, kvs)
+        do, kx, qx, sums, gathered = lax.optimization_barrier((do, kx, qx, sums, gathered))
         inner = [[4 * z + k for k in INNER] for z in range(4)]
         outer = [[4 * z + k for z in OUTER] for k in range(4)]
         sums = lax.psum_scatter(
             sums, "ctx", scatter_dimension=0, axis_index_groups=inner, tiled=True
         )
-    back_args = (plan, segs, qkv, do, of, lse)
-    part = jnp.zeros((HEADS, size, tok), F32)
-    others = ()
-    if ways > 1:
-        part, *others = attend_back(*back_args, kvs[1:], ways, tuple(range(1, ways)), None)
+    else:
+        kx, qx = prepare(segs, lse, kvs)
+    back_args = (plan, kx, qx, do, qkv)
+    part, dx, *others = attend_back(
+        *back_args, kvs[1:], ways, len(segs), tuple(range(1, ways)), of=of
+    )
     others = [around(other, -(j + 1)) for j, other in enumerate(others)]
-    dq, own = attend_back(*back_args, kvs[:1], ways, (0,), part)
+    dq, own = attend_back(
+        *back_args, kvs[:1], ways, len(segs), (0,), part=part, dx=dx
+    )
     for other in others:
         own = own + other.astype(F32)
     sent = jnp.concatenate([dq, own.astype(BF16)], axis=1)
@@ -1155,18 +1212,21 @@
         mine, away = head_grads(ctx, sent, gathered, small)
         mine, away = halve(1, 1, 16, mine, swap(away, "dp", 1))
         pieces = merge(16, mine, swap(away, "ctx", 1))
-        pieces, sums = lax.optimization_barrier((pieces, sums))
+        pieces, sums, pair = lax.optimization_barrier((pieces, sums, pair))
+        pair = moved(pair)
         sums = lax.psum_scatter(
             sums, "ctx", scatter_dimension=0, axis_index_groups=outer, tiled=True
         )
         pieces = exchange(pieces)
         gx = moved(last(blocks, back, staged[0], staged[1:], BF16))
-        loss, result, gx, gy, gq, gk, gv, g1, g2, g3, inverse = finish(pieces, gx, gy, result)
+        loss, gq, gk, gv, g1, g2, g3, inverse = settle(pieces, feat)
+        result, gx, gy = finish(inverse, gx, pair)
         go, gu, gd = spread(sums, inverse, gq.shape[0], wide)
         gains_out = [g.reshape(-1) for g in (g1, g2, g3)]
         loss = loss.reshape(())
     else:
         x1, h, df, dz, da = halves
+        result, gy = pair[:tok], pair[tok:].astype(F32)
         total = lax.psum(small, both)
         inverse = 1.0 / total[3, 1]
         loss = total[3, 0] * inverse

time: 171 us -> 164 us (0.959)
  starting transfers between devices: 51 us -> 39 us
  waiting for transfers between devices: 50.2 us -> 53.6 us
    ppermute x7 -> x5, starting transfers between devices: 9.46 us -> 4.31 us  [moved(): return lax.ppermute(block, both, route)]
    reduce_scatter x1, waiting for transfers between devices: 1.16 us -> 5.68 us  [body(): lax.psum_scatter(sums, 'ctx', scatter_dimension=0, axis_index_groups=oute...]
    all_to_all x5, starting transfers between devices: 25.4 us -> 21.7 us  [exchange(): lax.all_to_all(block, 'ctx', 0, 0, axis_index_groups=groups, tiled=True)]
    ppermute x13, starting transfers between devices: 16.1 us -> 12.9 us  [swap(): return lax.ppermute(block, axis, [(i, i ^ bit) for i in range(size)])]
    pallas_call x1 -> x3, Pallas kernels: 1.57 us -> 3.85 us  [stage(): pl.pallas_call(functools.partial(stage_kernel, tuple(layout)), out_shape=...]
    pallas_call x5 -> x7, Pallas kernels: 21.6 us -> 21.5 us  [the longest x2 13.8 us: attend_back(): pl.pallas_call(functools.partial(backward_kernel, ways, slots, final, tex...]
  transfers between devices with their start and end apart: 28 -> 26, of which waited for: 15 -> 15; matrix products, arithmetic and copies ran while one was open for 1% -> 1% of each run, Pallas kernels for 27% -> 31%
where the time goes in v4:
time: 164 us
  waiting for transfers between devices  53.6 us (33%)
  Pallas kernels  53.2 us (32%)
  starting transfers between devices  39 us (24%)
  between operations  14.2 us (9%)
  local copies, waits for them, and re-layouts  1.9 us (1%)
  other arithmetic  1.8 us (1%)
    all_to_all x5, waiting for transfers between devices, exchange(): lax.all_to_all(block, 'ctx', 0, 0, axis_index_groups=groups, tiled=True)  37.6 us
    all_to_all x5, starting transfers between devices, exchange(): lax.all_to_all(block, 'ctx', 0, 0, axis_index_groups=groups, tiled=True)  21.7 us
    pallas_call x2, Pallas kernels, attend_back(): pl.pallas_call(functools.partial(backward_kernel, ways, slots, final, tex...  13.8 us
    ppermute x13, starting transfers between devices, swap(): return lax.ppermute(block, axis, [(i, i ^ bit) for i in range(size)])  12.9 us
    pallas_call x1, Pallas kernels, middle(): pl.pallas_call(functools.partial(middle_kernel, blocks, tile), out_shape=...  10.7 us
    ppermute x13, waiting for transfers between devices, swap(): return lax.ppermute(block, axis, [(i, i ^ bit) for i in range(size)])  8.24 us
    pallas_call x1, Pallas kernels, attend(): pl.pallas_call(functools.partial(forward_kernel, ways, len(segs)), out_sh...  7.85 us
    reduce_scatter x1, waiting for transfers between devices, body(): lax.psum_scatter(sums, 'ctx', scatter_dimension=0, axis_index_groups=oute...  5.68 us
  transfers between devices with their start and end apart: 26, of which 15 were waited for; matrix products, arithmetic and copies ran while one was open for 1% of the time, Pallas kernels for 31%

profile of v4, /device:TPU:0, one launch (start us, length us, event | category | flops | bytes accessed | tf_op | source)
XLA Modules:
  0.0 163.6 jit_solution(12491671949374265517)
XLA Ops:
  7.2 1.6 collective-permute-start
  8.8 3.4 %collective-permute-start.1 = (bf16[256,512]{1,0:T(8,128)(2,1)}, bf16[256,512]{1,0:T(8,128)(2,1)S(1)}, u32[]{:S(2)}, u32[]{:S(2)}) collective-permute-start(bf16[256,512]{1,0:T(8,128)(2,1)} %refs_1_.5), channel_id=1, source_target_pairs={{0,16},{16,0},{1,17},{17,1},{2,18},{18,2},{3,19},{19,3},{4,20},{20... | collective-permute-start | bytes 786440 | tf_op jit(solution)/shard_map/ppermute | solution.py:76
  14.4 1.6 project.1
  15.9 5.8 %all-to-all-start = ((bf16[8,192,256]{2,1,0:T(8,128)(2,1)}), bf16[8,192,256]{2,1,0:T(8,128)(2,1)S(1)}, u32[]{:S(2)}, u32[]{:S(2)}) async-start(bf16[8,192,256]{2,1,0:T(8,128)(2,1)} %project.1), calls=%async_computation | async-start | bytes 1572864 | tf_op jit(solution)/shard_map/all_to_all | solution.py:1135
  23.1 1.9 %collective-permute-start.4 = (s32[16,256]{1,0:T(8,128)S(1)}, s32[16,256]{1,0:T(8,128)S(1)}, u32[]{:S(2)}, u32[]{:S(2)}) collective-permute-start(s32[16,256]{1,0:T(8,128)S(1)} %reshape.50.refs_0_), channel_id=1, source_target_pairs={{0,16},{16,0},{1,17},{17,1},{2,18},{18,2},{3,19},{19,3},{4,20},{20... | collective-permute-start | bytes 49160 | tf_op jit(solution)/shard_map/ppermute | solution.py:76
  25.9 2.8 %plan.1.plan_ref = s32[872]{0:T(1024)S(1)} custom-call(s32[4096]{0:T(1024)S(1)} %bitcast.18, s32[4096]{0:T(1024)S(1)} %bitcast.19), custom_call_target="tpu_custom_call" | custom-call | flops 1000 | bytes 1024 | tf_op jit(solution)/shard_map/plan/pallas_call | solution.py:235
  29.3 13.2 %all-to-all-done.refs_2_.refs_0_.refs_1_ = bf16[8,192,256]{2,1,0:T(8,128)(2,1)S(1)} async-done(((bf16[8,192,256]{2,1,0:T(8,128)(2,1)}), bf16[8,192,256]{2,1,0:T(8,128)(2,1)S(1)}, u32[]{:S(2)}, u32[]{:S(2)}) %all-to-all-start) | async-done | bytes 786464 | tf_op jit(solution)/shard_map/all_to_all | solution.py:1135
  45.6 7.8 %attend.1 = (bf16[8,64,256]{2,1,0:T(8,128)(2,1)}, f32[8,64,256]{2,1,0:T(8,128)}, f32[8,256]{1,0:T(8,128)S(1)}) custom-call(s32[872]{0:T(1024)} %copy-done.7, s32[16,256]{1,0:T(8,128)S(1)} %reshape.50.refs_0_, s32[16,256]{1,0:T(8,128)S(1)} %collective-permute-done.4.refs_1_, bf16[8,192,256]{2,1,0:T(8,128)(2,1)S(1)} %all-to-all-done.refs_2_.refs_0_.refs_1_, ...), custom_call_target="tpu_custom_call" | custom-call | flops 1000 | bytes 1024 | tf_op jit(solution)/shard_map/attend/pallas_call | solution.py:359
  53.4 3.7 %all-to-all-start.1 = ((bf16[8,64,256]{2,1,0:T(8,128)(2,1)}), bf16[8,64,256]{2,1,0:T(8,128)(2,1)S(1)}, u32[]{:S(2)}, u32[]{:S(2)}) async-start(bf16[8,64,256]{2,1,0:T(8,128)(2,1)} %get-tuple-element.88), calls=%async_computation.1 | async-start | bytes 524288 | tf_op jit(solution)/shard_map/all_to_all | solution.py:1135
  57.2 1.5 collective-permute-start.8
  60.6 1.1 stage.4
  61.7 8.0 %all-to-all-done.1 = bf16[8,64,256]{2,1,0:T(8,128)(2,1)S(1)} async-done(((bf16[8,64,256]{2,1,0:T(8,128)(2,1)}), bf16[8,64,256]{2,1,0:T(8,128)(2,1)S(1)}, u32[]{:S(2)}, u32[]{:S(2)}) %all-to-all-start.1) | async-done | bytes 262176 | tf_op jit(solution)/shard_map/all_to_all | solution.py:1135
  69.7 10.7 %middle.1 = (bf16[512,512]{1,0:T(8,128)(2,1)}, f32[256,512]{1,0:T(8,128)}, bf16[512,256]{1,0:T(8,128)(2,1)}, f32[8,256]{1,0:T(8,128)S(1)}, bf16[16,144,512]{2,1,0:T(8,128)(2,1)}, /*index=5*/bf16[16,144,512]{2,1,0:T(8,128)(2,1)}) custom-call(bf16[512,256]{1,0:T(8,128)(2,1)S(1)} %bitcast.16, s32[1,256]{1,0:T(1,128)S(1)} %collective-permute-done.5.refs_1_, ...), custom_call_target="tpu_custom_call" | custom-call | flops 1000 | bytes 1024 | tf_op jit(solution)/shard_map/middle/pallas_call | solution.py:779
  80.6 4.1 %all-to-all-start.2 = ((bf16[8,64,256]{2,1,0:T(8,128)(2,1)}), bf16[8,64,256]{2,1,0:T(8,128)(2,1)S(1)}, u32[]{:S(2)}, u32[]{:S(2)}) async-start(bf16[8,64,256]{2,1,0:T(8,128)(2,1)} %bitcast.5), calls=%async_computation.2 | async-start | bytes 524288 | tf_op jit(solution)/shard_map/all_to_all | solution.py:1135
  85.2 2.6 %join.1 = bf16[16,144,512]{2,1,0:T(8,128)(2,1)} custom-call(bf16[16,144,512]{2,1,0:T(8,128)(2,1)S(1)} %collective-permute-done.12.two_ref, bf16[16,144,512]{2,1,0:T(8,128)(2,1)} %get-tuple-element.99.one_in), custom_call_target="tpu_custom_call" | custom-call | flops 1000 | bytes 1024 | tf_op jit(solution)/shard_map/join/pallas_call | solution.py:849
  87.8 1.6 prepare.1
  89.4 4.7 %all-to-all-done.2.do_ref = bf16[8,64,256]{2,1,0:T(8,128)(2,1)S(1)} async-done(((bf16[8,64,256]{2,1,0:T(8,128)(2,1)}), bf16[8,64,256]{2,1,0:T(8,128)(2,1)S(1)}, u32[]{:S(2)}, u32[]{:S(2)}) %all-to-all-start.2) | async-done | bytes 262176 | tf_op jit(solution)/shard_map/all_to_all | solution.py:1135
  94.2 7.5 %attend_back.2 = (f32[8,64,256]{2,1,0:T(8,128)S(1)}, bf16[9,256,80]{2,1,0:T(8,128)(2,1)S(1)}, bf16[8,128,256]{2,1,0:T(8,128)(2,1)S(1)}) custom-call(s32[872]{0:T(1024)} %copy-done.7, bf16[16,160,256]{2,1,0:T(8,128)(2,1)S(1)} %get-tuple-element.105.kx, bf16[9,256,160]{2,1,0:T(8,128)(2,1)S(1)} %get-tuple-element.106.qx, ...), custom_call_target="tpu_custom_call" | custom-call | flops 1000 | bytes 1024 | tf_op jit(solution)/shard_map/attend_back/pallas_call | solution.py:523
  101.8 6.3 %attend_back.3 = (bf16[8,64,256]{2,1,0:T(8,128)(2,1)S(1)}, f32[8,128,256]{2,1,0:T(8,128)S(1)}) custom-call(s32[872]{0:T(1024)} %copy-done.7, bf16[16,160,256]{2,1,0:T(8,128)(2,1)S(1)} %get-tuple-element.105.kx, bf16[9,256,160]{2,1,0:T(8,128)(2,1)S(1)} %get-tuple-element.106.qx, bf16[8,64,256]{2,1,0:T(8,128)(2,1)S(1)} %all-to-all-done.2.do_ref, ...), custom_call_target="tpu_custom_call" | custom-call | flops 1000 | bytes 1024 | tf_op jit(solution)/shard_map/attend_back/pallas_call | solution.py:523
  109.2 3.6 %all-to-all-start.4 = ((bf16[8,192,256]{2,1,0:T(8,128)(2,1)}), bf16[8,192,256]{2,1,0:T(8,128)(2,1)S(1)}, u32[]{:S(2)}, u32[]{:S(2)}) async-start(bf16[8,192,256]{2,1,0:T(8,128)(2,1)} %pad_maximum_fusion.back_ref), calls=%async_computation.5 | async-start | bytes 1572864 | tf_op jit(solution)/shard_map/all_to_all | solution.py:1135
  112.9 3.3 %head_grads.1 = (bf16[16,32,256]{2,1,0:T(8,128)(2,1)S(1)}, bf16[16,32,256]{2,1,0:T(8,128)(2,1)S(1)}) custom-call(bf16[8,192,256]{2,1,0:T(8,128)(2,1)} %pad_maximum_fusion.back_ref, bf16[8,256,512]{2,1,0:T(8,128)(2,1)} %bitcast.20, f32[8,256]{1,0:T(8,128)S(1)} %get-tuple-element.115.small_ref), custom_call_target="tpu_custom_call" | custom-call | flops 1000 | bytes 1024 | tf_op jit(solution)/shard_map/head_grads/pallas_call | solution.py:943
  116.2 2.0 %collective-permute-start.14 = (bf16[16,32,256]{2,1,0:T(8,128)(2,1)S(1)}, bf16[16,32,256]{2,1,0:T(8,128)(2,1)S(1)}, u32[]{:S(2)}, u32[]{:S(2)}) collective-permute-start(bf16[16,32,256]{2,1,0:T(8,128)(2,1)S(1)} %get-tuple-element.117), channel_id=1, source_target_pairs={{0,16},{16,0},{1,17},{17,1},{2,18},{18,2},{3,19},{19,3},{4,20},{20... | collective-permute-start | bytes 786440 | tf_op jit(solution)/shard_map/ppermute | solution.py:76
  118.1 1.2 collective-permute-done.14.got_ref
  119.4 1.9 %collective-permute-start.15 = (bf16[8,32,256]{2,1,0:T(8,128)(2,1)S(1)}, bf16[8,32,256]{2,1,0:T(8,128)(2,1)S(1)}, u32[]{:S(2)}, u32[]{:S(2)}) collective-permute-start(bf16[8,32,256]{2,1,0:T(8,128)(2,1)S(1)} %get-tuple-element.119), channel_id=1, source_target_pairs={{0,1},{1,0},{2,3},{3,2},{4,5},{5,4},{6,7},{7,6},{8,9},{9,8},{10,11... | collective-permute-start | bytes 393224 | tf_op jit(solution)/shard_map/ppermute | solution.py:76
  121.4 4.0 %collective-permute-done.15.two_ref = bf16[8,32,256]{2,1,0:T(8,128)(2,1)S(1)} collective-permute-done((bf16[8,32,256]{2,1,0:T(8,128)(2,1)S(1)}, bf16[8,32,256]{2,1,0:T(8,128)(2,1)S(1)}, u32[]{:S(2)}, u32[]{:S(2)}) %collective-permute-start.15) | collective-permute-done | bytes 131104 | tf_op jit(solution)/shard_map/ppermute | solution.py:76
  126.1 2.0 %reduce-scatter.3.cloned.1.call-done = bf16[4,144,512]{2,1,0:T(8,128)(2,1)} async-done(((bf16[16,144,512]{2,1,0:T(8,128)(2,1)}), bf16[4,144,512]{2,1,0:T(8,128)(2,1)}) %reduce-scatter.3.cloned.1.call-update) | async-done | bytes 589840 | tf_op jit(solution)/shard_map/reduce_scatter | solution.py:1193
  128.1 5.5 %all-to-all-done.4.back_ref = bf16[8,192,256]{2,1,0:T(8,128)(2,1)S(1)} async-done(((bf16[8,192,256]{2,1,0:T(8,128)(2,1)}), bf16[8,192,256]{2,1,0:T(8,128)(2,1)S(1)}, u32[]{:S(2)}, u32[]{:S(2)}) %all-to-all-start.4) | async-done | bytes 786464 | tf_op jit(solution)/shard_map/all_to_all | solution.py:1135
  133.6 4.4 %all-to-all-start.3 = ((bf16[8,32,256]{2,1,0:T(8,128)(2,1)}), bf16[8,32,256]{2,1,0:T(8,128)(2,1)S(1)}, u32[]{:S(2)}, u32[]{:S(2)}) async-start(bf16[8,32,256]{2,1,0:T(8,128)(2,1)} %merge.1), calls=%async_computation.4 | async-start | bytes 262144 | tf_op jit(solution)/shard_map/all_to_all | solution.py:1135
  138.7 1.6 stage.5
  141.6 6.2 %all-to-all-done.3.pieces_ref = bf16[8,32,256]{2,1,0:T(8,128)(2,1)S(1)} async-done(((bf16[8,32,256]{2,1,0:T(8,128)(2,1)}), bf16[8,32,256]{2,1,0:T(8,128)(2,1)S(1)}, u32[]{:S(2)}, u32[]{:S(2)}) %all-to-all-start.3) | async-done | bytes 131104 | tf_op jit(solution)/shard_map/all_to_all | solution.py:1135
  149.7 5.7 %reduce-scatter.5.cloned.1.call-done.sums_in = bf16[1,144,512]{2,1,0:T(8,128)(2,1)} async-done(((bf16[4,144,512]{2,1,0:T(8,128)(2,1)}), bf16[1,144,512]{2,1,0:T(8,128)(2,1)}) %reduce-scatter.5.cloned.1.call-update) | async-done | bytes 147472 | tf_op jit(solution)/shard_map/reduce_scatter | solution.py:1217
  155.4 1.7 %spread.1 = (f32[16,512]{1,0:T(8,128)}, f32[16,2048]{1,0:T(8,128)}, f32[64,512]{1,0:T(8,128)}) custom-call(bf16[1,144,512]{2,1,0:T(8,128)(2,1)} %reduce-scatter.5.cloned.1.call-done.sums_in, f32[8,128]{1,0:T(8,128)S(1)} %get-tuple-element.124.inverse_ref), custom_call_target="tpu_custom_call" | custom-call | flops 1000 | bytes 1024 | tf_op jit(solution)/shard_map/spread/pallas_call | solution.py:1077
  (88 shorter events, 16.3 us)
Async XLA Ops:
  7.2 6.7 %collective-permute-start = (bf16[256,512]{1,0:T(8,128)(2,1)}, bf16[256,512]{1,0:T(8,128)(2,1)S(1)}, u32[]{:S(2)}, u32[]{:S(2)}) collective-permute-start(bf16[256,512]{1,0:T(8,128)(2,1)} %bitcast.25), channel_id=1, source_target_pairs={{0,0},{1,16},{2,2},{3,18},{4,4},{5,20},{6,6},{7,22},{8,8},{9,24},{... | collective-permute-start | bytes 786440 | tf_op jit(solution)/shard_map/ppermute | solution.py:1127
  8.8 5.1 %collective-permute-start.1 = (bf16[256,512]{1,0:T(8,128)(2,1)}, bf16[256,512]{1,0:T(8,128)(2,1)S(1)}, u32[]{:S(2)}, u32[]{:S(2)}) collective-permute-start(bf16[256,512]{1,0:T(8,128)(2,1)} %refs_1_.5), channel_id=1, source_target_pairs={{0,16},{16,0},{1,17},{17,1},{2,18},{18,2},{3,19},{19,3},{4,20},{20... | collective-permute-start | bytes 786440 | tf_op jit(solution)/shard_map/ppermute | solution.py:76
  12.2 1.7 %collective-permute-start.2 = (bf16[256,512]{1,0:T(8,128)(2,1)}, bf16[256,512]{1,0:T(8,128)(2,1)S(1)}, u32[]{:S(2)}, u32[]{:S(2)}) collective-permute-start(bf16[256,512]{1,0:T(8,128)(2,1)} %refs_3_.1), channel_id=1, source_target_pairs={{0,16},{16,0},{1,17},{17,1},{2,18},{18,2},{3,19},{19,3},{4,20},{20... | collective-permute-start | bytes 786440 | tf_op jit(solution)/shard_map/ppermute | solution.py:76
  12.3 2.0 %collective-permute-start.3 = (bf16[256,512]{1,0:T(8,128)(2,1)}, bf16[256,512]{1,0:T(8,128)(2,1)S(1)}, u32[]{:S(2)}, u32[]{:S(2)}) collective-permute-start(bf16[256,512]{1,0:T(8,128)(2,1)} %refs_5_.1), channel_id=1, source_target_pairs={{0,16},{16,0},{1,17},{17,1},{2,18},{18,2},{3,19},{19,3},{4,20},{20... | collective-permute-start | bytes 786440 | tf_op jit(solution)/shard_map/ppermute | solution.py:76
  15.9 26.6 %all-to-all-start = ((bf16[8,192,256]{2,1,0:T(8,128)(2,1)}), bf16[8,192,256]{2,1,0:T(8,128)(2,1)S(1)}, u32[]{:S(2)}, u32[]{:S(2)}) async-start(bf16[8,192,256]{2,1,0:T(8,128)(2,1)} %project.1), calls=%async_computation | async-start | bytes 1572864 | tf_op jit(solution)/shard_map/all_to_all | solution.py:1135
  21.8 35.4 %copy-start.9 = (bf16[256,512]{1,0:T(8,128)(2,1)S(1)}, bf16[256,512]{1,0:T(8,128)(2,1)}, u32[]{:S(2)}) copy-start(bf16[256,512]{1,0:T(8,128)(2,1)} %refs_1_.4) | copy-start | bytes 786436
  21.8 36.9 %copy-start.15 = (bf16[256]{0:T(256)(128)(2,1)S(1)}, bf16[256]{0:T(256)(128)(2,1)}, u32[]{:S(2)}) copy-start(bf16[256]{0:T(256)(128)(2,1)} %param.25) | copy-start | bytes 1540
  21.8 36.9 %copy-start.16 = (bf16[256]{0:T(256)(128)(2,1)S(1)}, bf16[256]{0:T(256)(128)(2,1)}, u32[]{:S(2)}) copy-start(bf16[256]{0:T(256)(128)(2,1)} %param.26) | copy-start | bytes 1540
  21.8 36.9 %copy-start.17 = (bf16[256]{0:T(256)(128)(2,1)S(1)}, bf16[256]{0:T(256)(128)(2,1)}, u32[]{:S(2)}) copy-start(bf16[256]{0:T(256)(128)(2,1)} %param.27) | copy-start | bytes 1540
  21.8 72.3 %all-gather.3.cloned.1.call-start = ((), (), s32[]{:S(2)}) async-start(), calls=%async_computation.9 | async-start | bytes 2359296 | tf_op jit(solution)/shard_map/all_gather | solution.py:1184
  23.1 2.8 %collective-permute-start.4 = (s32[16,256]{1,0:T(8,128)S(1)}, s32[16,256]{1,0:T(8,128)S(1)}, u32[]{:S(2)}, u32[]{:S(2)}) collective-permute-start(s32[16,256]{1,0:T(8,128)S(1)} %reshape.50.refs_0_), channel_id=1, source_target_pairs={{0,16},{16,0},{1,17},{17,1},{2,18},{18,2},{3,19},{19,3},{4,20},{20... | collective-permute-start | bytes 49160 | tf_op jit(solution)/shard_map/ppermute | solution.py:76
  25.0 4.3 %collective-permute-start.5 = (s32[1,256]{1,0:T(1,128)S(1)}, s32[1,256]{1,0:T(1,128)S(1)}, u32[]{:S(2)}, u32[]{:S(2)}) collective-permute-start(s32[1,256]{1,0:T(1,128)S(1)} %copy-done.14), channel_id=1, source_target_pairs={{0,0},{1,16},{2,2},{3,18},{4,4},{5,20},{6,6},{7,22},{8,8},{9,24},{... | collective-permute-start | bytes 3080 | tf_op jit(solution)/shard_map/ppermute | solution.py:1127
  42.5 37.9 %copy-start = (bf16[8,192,256]{2,1,0:T(8,128)(2,1)}, bf16[8,192,256]{2,1,0:T(8,128)(2,1)S(1)}, u32[]{:S(2)}) copy-start(bf16[8,192,256]{2,1,0:T(8,128)(2,1)S(1)} %all-to-all-done.refs_2_.refs_0_.refs_1_) | copy-start | bytes 2359300
  42.6 3.0 %collective-permute-start.6 = (bf16[8,192,256]{2,1,0:T(8,128)(2,1)S(1)}, bf16[8,192,256]{2,1,0:T(8,128)(2,1)S(1)}, u32[]{:S(2)}, u32[]{:S(2)}) collective-permute-start(bf16[8,192,256]{2,1,0:T(8,128)(2,1)S(1)} %all-to-all-done.refs_2_.refs_0_.refs_1_), channel_id=1, source_target_pairs={{0,16},{16,0},{1,17},{17,1},{2,18},{18,2},{3,19},{19,3},{4,20},{20... | collective-permute-start | bytes 2359304 | tf_op jit(solution)/shard_map/ppermute | solution.py:76
  43.3 26.4 %collective-permute-start.10 = (bf16[256,2048]{1,0:T(8,128)(2,1)}, bf16[256,2048]{1,0:T(8,128)(2,1)}, u32[]{:S(2)}, u32[]{:S(2)}) collective-permute-start(bf16[256,2048]{1,0:T(8,128)(2,1)} %refs_7_.1), channel_id=1, source_target_pairs={{0,16},{16,0},{1,17},{17,1},{2,18},{18,2},{3,19},{19,3},{4,20},{20... | collective-permute-start | bytes 3145736 | tf_op jit(solution)/shard_map/ppermute | solution.py:76
  43.4 26.3 %collective-permute-start.11 = (bf16[1024,512]{1,0:T(8,128)(2,1)}, bf16[1024,512]{1,0:T(8,128)(2,1)}, u32[]{:S(2)}, u32[]{:S(2)}) collective-permute-start(bf16[1024,512]{1,0:T(8,128)(2,1)} %refs_9_.1), channel_id=1, source_target_pairs={{0,16},{16,0},{1,17},{17,1},{2,18},{18,2},{3,19},{19,3},{4,20},{20... | collective-permute-start | bytes 3145736 | tf_op jit(solution)/shard_map/ppermute | solution.py:76
  43.8 9.6 %collective-permute-start.7 = (bf16[512,512]{1,0:T(8,128)(2,1)S(1)}, bf16[512,512]{1,0:T(8,128)(2,1)S(1)}, u32[]{:S(2)}, u32[]{:S(2)}) collective-permute-start(bf16[512,512]{1,0:T(8,128)(2,1)S(1)} %pad_maximum_fusion.1), channel_id=1, source_target_pairs={{0,0},{1,16},{2,2},{3,18},{4,4},{5,20},{6,6},{7,22},{8,8},{9,24},{... | collective-permute-start | bytes 1572872 | tf_op jit(solution)/shard_map/ppermute | solution.py:1127
  45.6 34.8 %copy-start.1 = (bf16[8,192,256]{2,1,0:T(8,128)(2,1)}, bf16[8,192,256]{2,1,0:T(8,128)(2,1)S(1)}, u32[]{:S(2)}) copy-start(bf16[8,192,256]{2,1,0:T(8,128)(2,1)S(1)} %collective-permute-done.6.refs_3_.refs_1_) | copy-start | bytes 2359300
  53.4 16.2 %all-to-all-start.1 = ((bf16[8,64,256]{2,1,0:T(8,128)(2,1)}), bf16[8,64,256]{2,1,0:T(8,128)(2,1)S(1)}, u32[]{:S(2)}, u32[]{:S(2)}) async-start(bf16[8,64,256]{2,1,0:T(8,128)(2,1)} %get-tuple-element.88), calls=%async_computation.1 | async-start | bytes 524288 | tf_op jit(solution)/shard_map/all_to_all | solution.py:1135
  57.2 2.7 %collective-permute-start.8 = (bf16[256,512]{1,0:T(8,128)(2,1)S(1)}, bf16[256,512]{1,0:T(8,128)(2,1)S(1)}, u32[]{:S(2)}, u32[]{:S(2)}) collective-permute-start(bf16[256,512]{1,0:T(8,128)(2,1)S(1)} %copy-done.9), channel_id=1, source_target_pairs={{0,16},{16,0},{1,17},{17,1},{2,18},{18,2},{3,19},{19,3},{4,20},{20... | collective-permute-start | bytes 786440 | tf_op jit(solution)/shard_map/ppermute | solution.py:76
  58.8 10.9 %collective-permute-start.9 = (bf16[3,256]{1,0:T(4,128)(2,1)S(1)}, bf16[3,256]{1,0:T(4,128)(2,1)S(1)}, u32[]{:S(2)}, u32[]{:S(2)}) collective-permute-start(bf16[3,256]{1,0:T(4,128)(2,1)S(1)} %pad_maximum_fusion.2.refs_2_), channel_id=1, source_target_pairs={{0,16},{16,0},{1,17},{17,1},{2,18},{18,2},{3,19},{19,3},{4,20},{20... | collective-permute-start | bytes 4616 | tf_op jit(solution)/shard_map/ppermute | solution.py:76
  80.4 4.8 %collective-permute-start.12 = (bf16[16,144,512]{2,1,0:T(8,128)(2,1)}, bf16[16,144,512]{2,1,0:T(8,128)(2,1)S(1)}, u32[]{:S(2)}, u32[]{:S(2)}) collective-permute-start(bf16[16,144,512]{2,1,0:T(8,128)(2,1)} %get-tuple-element.98), channel_id=1, source_target_pairs={{0,16},{16,0},{1,17},{17,1},{2,18},{18,2},{3,19},{19,3},{4,20},{20... | collective-permute-start | bytes 7077896 | tf_op jit(solution)/shard_map/ppermute | solution.py:76
  80.6 13.6 %all-to-all-start.2 = ((bf16[8,64,256]{2,1,0:T(8,128)(2,1)}), bf16[8,64,256]{2,1,0:T(8,128)(2,1)S(1)}, u32[]{:S(2)}, u32[]{:S(2)}) async-start(bf16[8,64,256]{2,1,0:T(8,128)(2,1)} %bitcast.5), calls=%async_computation.2 | async-start | bytes 524288 | tf_op jit(solution)/shard_map/all_to_all | solution.py:1135
  84.7 43.4 %reduce-scatter.3.cloned.1.call-start = ((), (), s32[]{:S(2)}) async-start(), calls=%async_computation.7 | async-start | bytes 2949120 | tf_op jit(solution)/shard_map/reduce_scatter | solution.py:1193
  101.7 6.4 %collective-permute-start.13 = (bf16[8,128,256]{2,1,0:T(8,128)(2,1)S(1)}, bf16[8,128,256]{2,1,0:T(8,128)(2,1)S(1)}, u32[]{:S(2)}, u32[]{:S(2)}) collective-permute-start(bf16[8,128,256]{2,1,0:T(8,128)(2,1)S(1)} %get-tuple-element.113), channel_id=1, source_target_pairs={{0,16},{16,0},{1,17},{17,1},{2,18},{18,2},{3,19},{19,3},{4,20},{20... | collective-permute-start | bytes 1572872 | tf_op jit(solution)/shard_map/ppermute | solution.py:76
  109.2 24.4 %all-to-all-start.4 = ((bf16[8,192,256]{2,1,0:T(8,128)(2,1)}), bf16[8,192,256]{2,1,0:T(8,128)(2,1)S(1)}, u32[]{:S(2)}, u32[]{:S(2)}) async-start(bf16[8,192,256]{2,1,0:T(8,128)(2,1)} %pad_maximum_fusion.back_ref), calls=%async_computation.5 | async-start | bytes 1572864 | tf_op jit(solution)/shard_map/all_to_all | solution.py:1135
  112.8 42.6 %reduce-scatter.5.cloned.1.call-start = ((), (), s32[]{:S(2)}) async-start(), calls=%async_computation.8 | async-start | bytes 737280 | tf_op jit(solution)/shard_map/reduce_scatter | solution.py:1217
  116.2 3.1 %collective-permute-start.14 = (bf16[16,32,256]{2,1,0:T(8,128)(2,1)S(1)}, bf16[16,32,256]{2,1,0:T(8,128)(2,1)S(1)}, u32[]{:S(2)}, u32[]{:S(2)}) collective-permute-start(bf16[16,32,256]{2,1,0:T(8,128)(2,1)S(1)} %get-tuple-element.117), channel_id=1, source_target_pairs={{0,16},{16,0},{1,17},{17,1},{2,18},{18,2},{3,19},{19,3},{4,20},{20... | collective-permute-start | bytes 786440 | tf_op jit(solution)/shard_map/ppermute | solution.py:76
  119.4 6.0 %collective-permute-start.15 = (bf16[8,32,256]{2,1,0:T(8,128)(2,1)S(1)}, bf16[8,32,256]{2,1,0:T(8,128)(2,1)S(1)}, u32[]{:S(2)}, u32[]{:S(2)}) collective-permute-start(bf16[8,32,256]{2,1,0:T(8,128)(2,1)S(1)} %get-tuple-element.119), channel_id=1, source_target_pairs={{0,1},{1,0},{2,3},{3,2},{4,5},{5,4},{6,7},{7,6},{8,9},{9,8},{10,11... | collective-permute-start | bytes 393224 | tf_op jit(solution)/shard_map/ppermute | solution.py:76
  133.6 14.2 %all-to-all-start.3 = ((bf16[8,32,256]{2,1,0:T(8,128)(2,1)}), bf16[8,32,256]{2,1,0:T(8,128)(2,1)S(1)}, u32[]{:S(2)}, u32[]{:S(2)}) async-start(bf16[8,32,256]{2,1,0:T(8,128)(2,1)} %merge.1), calls=%async_computation.4 | async-start | bytes 262144 | tf_op jit(solution)/shard_map/all_to_all | solution.py:1135
  138.0 10.7 %collective-permute-start.17 = (bf16[512,512]{1,0:T(8,128)(2,1)S(1)}, bf16[512,512]{1,0:T(8,128)(2,1)S(1)}, u32[]{:S(2)}, u32[]{:S(2)}) collective-permute-start(bf16[512,512]{1,0:T(8,128)(2,1)S(1)} %copy-done.13), channel_id=1, source_target_pairs={{0,0},{1,16},{2,2},{3,18},{4,4},{5,20},{6,6},{7,22},{8,8},{9,24},{... | collective-permute-start | bytes 1572872 | tf_op jit(solution)/shard_map/ppermute | solution.py:1127
  140.9 7.7 %collective-permute-start.16 = (bf16[256,512]{1,0:T(8,128)(2,1)S(1)}, bf16[256,512]{1,0:T(8,128)(2,1)S(1)}, u32[]{:S(2)}, u32[]{:S(2)}) collective-permute-start(bf16[256,512]{1,0:T(8,128)(2,1)S(1)} %last.1), channel_id=1, source_target_pairs={{0,0},{1,16},{2,2},{3,18},{4,4},{5,20},{6,6},{7,22},{8,8},{9,24},{... | collective-permute-start | bytes 786440 | tf_op jit(solution)/shard_map/ppermute | solution.py:1127
  (12 other events, 91.8 us)
Sparse Core Ops, SparseCore 0:
  42.7 36.9 all-gather.2
  94.3 33.7 reduce-scatter.2
  130.4 24.9 reduce-scatter.4

commit v5 on v4

--- a/solution.py
+++ b/solution.py
@@ -87,6 +87,10 @@
     if blocks == 1:
         return pl.ds(0, size)
     return pl.ds(pl.multiple_of((lax.axis_index("dp") + number) % 2 * size, size), size)
+
+
+def turned_by(side, first, second):
+    return jnp.where(side == 0, first, second)
 
 
 def fetch(sources, targets, sems, first=0):
@@ -699,9 +703,11 @@
         parts = wide // feat
 
         def put(flip, first, base, size, values):
+            side = (lax.axis_index("dp") + flip) % 2
             for k in range(values.shape[0] // size):
                 c = first + k
                 at = INNER.index(c % 4) * 4 + OUTER.index(c // 4)
+                at = turned_by(side, at, 15 - at)
                 sum_refs[flip, at, pl.ds(base, size), :] = values[
                     k * size : (k + 1) * size
                 ].astype(BF16)
@@ -831,76 +837,117 @@
     return (blocks, (wide // feat) * step + wide // (2 * blocks) + step, feat)
 
 
-def join_kernel(two_ref, one_in, out, one_ref, ref, sems):
-    blocks = two_ref.shape[0]
+def join_kernel(two_ref, one_in, out, side_ref, one_ref, ref, sems):
+    blocks, depth, feat = two_ref.shape
+    main = ref.shape[1]
+    step = depth - main
     spans = [pl.ds(k * blocks // PIECES, blocks // PIECES) for k in range(PIECES)]
     ones = fetch([one_in.at[k] for k in spans], [one_ref.at[k] for k in spans], sems)
     going = []
     for k, (span, one) in enumerate(zip(spans, ones)):
         one.wait()
         for b in range(k * blocks // PIECES, (k + 1) * blocks // PIECES):
-            ref[b] = added(one_ref[b], two_ref[b], 0)
+            total = added(one_ref[b], two_ref[b])
+            ref[b] = total[:main]
+            places = [OUTER[at % 4] * 4 + INNER[at // 4] for at in (b, 15 - b)]
+            c = turned_by(lax.axis_index("dp"), *places)
+            side_ref[c, 0:step, :] = total[main:, : feat // 2]
+            side_ref[c, step : 2 * step, :] = total[main:, feat // 2 :]
         going += fetch([ref.at[span]], [out.at[span]], sems, PIECES + k)
     for copy in going:
         copy.wait()
 
 
-def join(one, two):
+def join(one, two, step):
+    blocks, depth, feat = one.shape
     return pl.pallas_call(
         join_kernel,
-        out_shape=apart(one.shape, BF16),
+        out_shape=(
+            apart((blocks, depth - step, feat), BF16),
+            kept((blocks, 2 * step, feat // 2), BF16),
+        ),
         in_specs=vmem(1) + hbm(1),
-        out_specs=hbm(1)[0],
-        scratch_shapes=[pltpu.VMEM(one.shape, BF16)] * 2
-        + [pltpu.SemaphoreType.DMA((2 * PIECES,))],
+        out_specs=tuple(hbm(1) + vmem(1)),
+        scratch_shapes=[
+            pltpu.VMEM(one.shape, BF16),
+            pltpu.VMEM((blocks, depth - step, feat), BF16),
+            pltpu.SemaphoreType.DMA((2 * PIECES,)),
+        ],
         compiler_params=pltpu.CompilerParams(vmem_limit_bytes=10 * MIB),
         cost_estimate=cost(0.01),
         name="join",
     )(near(two), far(one))
 
 
-def added(one, two, tail):
+def added(one, two):
+    return (one.astype(F32) + two.astype(F32)).astype(BF16)
+
+
+def added_block(width, one, two):
     total = one.astype(F32) + two.astype(F32)
-    if not tail:
-        return total.astype(BF16)
-    depth = total.shape[0]
-    high, low = depth - tail, depth - tail // 2
-    return jnp.concatenate(
-        [total[:high].astype(BF16), split_sum(total[high:low] + total[low:])], axis=0
-    )
-
-
-def halve_kernel(bit, under, tail, keep_ref, got_ref, next_ref, send_ref):
-    mine = lax.rem(lax.axis_index("ctx") // bit, 2)
+    parts = split_sum(total[0:8] + total[8:16]).astype(F32)
+    lane = lax.broadcasted_iota(jnp.int32, total.shape, 1)
+    return jnp.where(lane < width, total, parts).astype(BF16)
+
+
+def halve_kernel(width, keep_ref, got_ref, side_ref, next_ref, send_ref):
+    mine = lax.rem(lax.axis_index("ctx"), 2)
 
     @pl.loop(0, next_ref.shape[0])
     def one(b):
         for ref, which in ((send_ref, 1 - mine), (next_ref, mine)):
-            at = (b // under) * 2 * under + which * under + lax.rem(b, under)
-            ref[b] = added(keep_ref[at], got_ref[at], tail)
-
-
-def halve(bit, under, tail, keep, got):
-    blocks, depth, feat = keep.shape
-    return pl.pallas_call(
-        functools.partial(halve_kernel, bit, under, tail),
-        out_shape=(kept((blocks // 2, depth, feat), BF16),) * 2,
-        in_specs=vmem(2),
+            at = 2 * b + which
+            total = added_block(width, keep_ref[at], got_ref[at])
+            ref[b] = jnp.concatenate([total, side_ref[at]], axis=0)
+
+
+def halve(width, keep, got, side):
+    blocks, depth, lanes = keep.shape
+    depth += side.shape[1]
+    return pl.pallas_call(
+        functools.partial(halve_kernel, width),
+        out_shape=(kept((blocks // 2, depth, lanes), BF16),) * 2,
+        in_specs=vmem(3),
         out_specs=tuple(vmem(2)),
-        compiler_params=pltpu.CompilerParams(vmem_limit_bytes=12 * MIB),
+        compiler_params=pltpu.CompilerParams(vmem_limit_bytes=6 * MIB),
         cost_estimate=cost(1),
         name="halve",
-    )(near(keep), near(got))
-
-
-def merge_kernel(tail, one_ref, two_ref, out_ref):
+    )(near(keep), near(got), near(side))
+
+
+def pack_kernel(dq_ref, own_ref, *refs):
+    others, out_ref = refs[:-1], refs[-1]
+    size = dq_ref.shape[1]
+    for h in range(HEADS):
+        total = own_ref[h]
+        for ref in others:
+            total = total + ref[h].astype(F32)
+        out_ref[h, 0:size, :] = dq_ref[h]
+        out_ref[h, size : 3 * size, :] = total.astype(BF16)
+
+
+def pack(dq, own, others):
+    heads, size, tok = dq.shape
+    return pl.pallas_call(
+        pack_kernel,
+        out_shape=kept((heads, 3 * size, tok), BF16),
+        in_specs=vmem(2 + len(others)),
+        out_specs=vmem(1)[0],
+        compiler_params=pltpu.CompilerParams(vmem_limit_bytes=6 * MIB),
+        cost_estimate=cost(0.5),
+        name="pack",
+    )(*map(near, (dq, own, *others)))
+
+
+def merge_kernel(width, one_ref, two_ref, out_ref):
     for b in range(out_ref.shape[0]):
-        out_ref[b] = added(one_ref[b], two_ref[b], tail)
-
-
-def merge(tail, one, two):
-    return pl.pallas_call(
-        functools.partial(merge_kernel, tail),
+        out_ref[b, 0:16, :] = added_block(width, one_ref[b, 0:16, :], two_ref[b, 0:16, :])
+        out_ref[b, 16:, :] = added(one_ref[b, 16:, :], two_ref[b, 16:, :])
+
+
+def merge(width, one, two):
+    return pl.pallas_call(
+        functools.partial(merge_kernel, width),
         out_shape=kept(one.shape, BF16),
         in_specs=vmem(2),
         out_specs=vmem(1)[0],
@@ -917,23 +964,29 @@
     total = 0.0
     for h in range(HEADS):
         copies[h].wait()
-        total = total + dot(back_ref[RING[h]], x_ref[h])
+        at = turned_by(lax.axis_index("dp"), RING[h], RING[HEADS - 1 - h])
+        total = total + dot(back_ref[at], x_ref[h])
     turned = total.T
     feat, size = turned.shape
-    blocks, depth, lanes = keep_ref.shape
-    step = feat // (2 * blocks)
-    turned = jnp.concatenate([turned, jnp.zeros((feat, lanes - size), F32)], axis=1).astype(BF16)
-    small = split_sum(small_ref[...])
-    for flip in range(2):
-        ref = (keep_ref, send_ref)[flip]
-        for side in range(2):
+    blocks, step, lanes = keep_ref.shape
+    small = small_ref[...]
+    row = lax.broadcasted_iota(jnp.int32, (step, step), 0)
+    empty = jnp.zeros((step, lanes - size - step), F32)
+    for side in range(2):
+        sums = jnp.concatenate([small[4 * side : 4 * side + 3], small[3:4], small[0:4] * 0.0], axis=0)
+        sums = split_sum(sums).astype(F32)
+        found = []
+        for c in range(blocks):
+            values = jnp.where(row % 8 == 3, sums[:, 0:step], sums[:, c * step : (c + 1) * step])
+            start = side * feat // 2 + c * step
+            block = [turned[start : start + step], values, empty]
+            found.append(jnp.concatenate(block, axis=1).astype(BF16))
+        for flip, ref in enumerate((keep_ref, send_ref)):
 
             @pl.when(lax.axis_index("dp") == (side + flip) % 2)
             def store():
-                half = turned[side * feat // 2 : (side + 1) * feat // 2]
-                ref[:, 0:step, :] = half.reshape(blocks, step, lanes)
-
-        ref[:, step:depth, :] = jnp.broadcast_to(small[None], (blocks,) + small.shape)
+                for c in range(blocks):
+                    ref[c] = found[c]
 
 
 def head_grads(blocks, back, x, small):
@@ -942,7 +995,7 @@
     lanes = small.shape[1]
     return pl.pallas_call(
         head_grad_kernel,
-        out_shape=(kept((blocks, step + 16, lanes), BF16),) * 2,
+        out_shape=(kept((blocks, step, lanes), BF16),) * 2,
         in_specs=vmem(1) + hbm(1) + vmem(1),
         out_specs=tuple(vmem(2)),
         scratch_shapes=[
@@ -986,34 +1039,33 @@
 
 
 def settle_kernel(
-    pieces_ref, loss_ref, gq_ref, gk_ref, gv_ref, g1_ref, g2_ref, g3_ref, inverse_ref
+    pieces_ref, loss_ref, gq_ref, gk_ref, gv_ref, go_ref, g1_ref, g2_ref, g3_ref, inverse_ref
 ):
     step, feat = gq_ref.shape
     size = feat // HEADS
-    halves = jnp.sum(pieces_ref[:, step : step + 16, :].astype(F32), axis=0)
-    halves = halves[0:8] + halves[8:16]
-    small = jnp.concatenate([halves[0:4], halves[4:8]], axis=1)
-    inverse = 1.0 / small[3:4, 1:2]
+    width = 3 * size
+    totals = jnp.sum(pieces_ref[...].astype(F32), axis=0)
+    small = totals[0:8] + totals[8:16]
+    sides = totals[step:]
+    inverse = 1.0 / small[3:4, width + 1 : width + 2]
     inverse_ref[...] = jnp.broadcast_to(inverse, inverse_ref.shape)
-    loss_ref[...] = small[3:4, 0:1] * inverse
+    loss_ref[...] = small[3:4, width : width + 1] * inverse
+    go_ref[...] = jnp.concatenate([sides[:step], sides[step:]], axis=1) * inverse
     for h in range(HEADS):
         block = pieces_ref[h, 0:step, :].astype(F32) * inverse
         for part, ref in enumerate((gq_ref, gk_ref, gv_ref)):
             ref[:, h * size : (h + 1) * size] = block[:, part * size : (part + 1) * size]
-    number = lax.axis_index("dp") * (2 * pieces_ref.shape[0]) + lax.axis_index("ctx")
-    eight = jnp.concatenate([small, small], axis=0) * inverse
-    turned = pltpu.roll(eight, lax.rem(feat - number * step, feat), 1)
-    g1_ref[...] = turned[0:1, 0:step]
-    g2_ref[...] = turned[1:2, 0:step]
-    g3_ref[...] = turned[2:3, 0:step]
+    for k, ref in enumerate((g1_ref, g2_ref, g3_ref)):
+        ref[...] = small[k : k + 1, width : width + step] * inverse
 
 
 def settle(pieces, feat):
-    step = pieces.shape[1] - 16
+    step = pieces.shape[1] // 3
     return pl.pallas_call(
         settle_kernel,
         out_shape=(
             shaped((1, 1), F32),
+            shaped((step, feat), F32),
             shaped((step, feat), F32),
             shaped((step, feat), F32),
             shaped((step, feat), F32),
@@ -1023,7 +1075,7 @@
             kept((8, 128), F32),
         ),
         in_specs=vmem(1),
-        out_specs=tuple(vmem(8)),
+        out_specs=tuple(vmem(9)),
         compiler_params=pltpu.CompilerParams(vmem_limit_bytes=4 * MIB),
         cost_estimate=pl.CostEstimate(
             flops=5500000000, bytes_accessed=1024, transcendentals=0
@@ -1057,32 +1109,24 @@
     )(near(inverse), gx, pair)
 
 
-def spread_kernel(sums_in, inverse_ref, go_ref, gu_ref, gd_ref, sums_ref, sem):
+def spread_kernel(sums_in, inverse_ref, gu_ref, gd_ref, sums_ref, sem):
     (copy,) = fetch([sums_in], [sums_ref], sem)
-    step, feat = go_ref.shape
-    wide_step = gd_ref.shape[0]
-    parts = gu_ref.shape[1] // feat
+    wide_step, feat = gd_ref.shape
+    step = gu_ref.shape[0]
     copy.wait()
     main = sums_ref[0].astype(F32) * inverse_ref[0:1, 0:1]
-    for j in range(parts):
+    for j in range(gu_ref.shape[1] // feat):
         gu_ref[:, j * feat : (j + 1) * feat] = main[j * step : (j + 1) * step]
-    base = parts * step
-    gd_ref[...] = main[base : base + wide_step]
-    base += wide_step
-    go_ref[...] = main[base : base + step]
+    gd_ref[...] = main[main.shape[0] - wide_step :]
 
 
 def spread(sums, inverse, step, wide):
     feat = sums.shape[2]
     return pl.pallas_call(
         spread_kernel,
-        out_shape=(
-            shaped((step, feat), F32),
-            shaped((step, wide), F32),
-            shaped((wide * step // feat, feat), F32),
-        ),
+        out_shape=(shaped((step, wide), F32), shaped((wide * step // feat, feat), F32)),
         in_specs=hbm(1) + vmem(1),
-        out_specs=tuple(vmem(3)),
+        out_specs=tuple(vmem(2)),
         scratch_shapes=[pltpu.VMEM(sums.shape, BF16), pltpu.SemaphoreType.DMA((1,))],
         compiler_params=pltpu.CompilerParams(vmem_limit_bytes=4 * MIB),
         cost_estimate=cost(1),
@@ -1116,6 +1160,9 @@
     wide = w_up.shape[1]
     cross = sides == 2 and ways == 2 and (feat // (sides * ctx)) % 16 == 0
     both = ("dp", "ctx")
+
+    def both_ways(rings):
+        return rings + [[ctx + place for place in reversed(ring)] for ring in rings]
 
     def moved(block):
         if not cross:
@@ -1180,18 +1227,18 @@
     )
     do = do.reshape(HEADS, size, tok)
     if cross:
-        rings = [[h * ways + r for h in RING] for r in range(ways)]
-        gathered = lax.all_gather(late_x, "ctx", axis=0, axis_index_groups=rings)
+        rings = both_ways([[h * ways + r for h in RING] for r in range(ways)])
+        gathered = lax.all_gather(late_x, both, axis=0, axis_index_groups=rings)
     do = exchange(do)
     if cross:
-        sums = join(halves[0], swap(halves[1], "dp", 1))
+        sums, sides = join(halves[0], swap(halves[1], "dp", 1), feat // (2 * ctx))
         lse, sums = lax.optimization_barrier((lse, sums))
         kx, qx = prepare(segs, lse, kvs)
         do, kx, qx, sums, gathered = lax.optimization_barrier((do, kx, qx, sums, gathered))
-        inner = [[4 * z + k for k in INNER] for z in range(4)]
-        outer = [[4 * z + k for z in OUTER] for k in range(4)]
+        inner = both_ways([[4 * z + k for k in INNER] for z in range(4)])
+        outer = both_ways([[4 * z + k for z in OUTER] for k in range(4)])
         sums = lax.psum_scatter(
-            sums, "ctx", scatter_dimension=0, axis_index_groups=inner, tiled=True
+            sums, both, scatter_dimension=0, axis_index_groups=inner, tiled=True
         )
     else:
         kx, qx = prepare(segs, lse, kvs)
@@ -1203,25 +1250,23 @@
     dq, own = attend_back(
         *back_args, kvs[:1], ways, len(segs), (0,), part=part, dx=dx
     )
-    for other in others:
-        own = own + other.astype(F32)
-    sent = jnp.concatenate([dq, own.astype(BF16)], axis=1)
+    sent = pack(dq, own, others)
     back = exchange(sent)
     back, *staged = lax.optimization_barrier((back, *stage([gr], *attn_weights)))
     if cross:
         mine, away = head_grads(ctx, sent, gathered, small)
-        mine, away = halve(1, 1, 16, mine, swap(away, "dp", 1))
-        pieces = merge(16, mine, swap(away, "ctx", 1))
+        mine, away = halve(3 * size, mine, swap(away, "dp", 1), sides)
+        pieces = merge(3 * size, mine, swap(away, "ctx", 1))
         pieces, sums, pair = lax.optimization_barrier((pieces, sums, pair))
         pair = moved(pair)
         sums = lax.psum_scatter(
-            sums, "ctx", scatter_dimension=0, axis_index_groups=outer, tiled=True
+            sums, both, scatter_dimension=0, axis_index_groups=outer, tiled=True
         )
         pieces = exchange(pieces)
         gx = moved(last(blocks, back, staged[0], staged[1:], BF16))
-        loss, gq, gk, gv, g1, g2, g3, inverse = settle(pieces, feat)
+        loss, gq, gk, gv, go, g1, g2, g3, inverse = settle(pieces, feat)
         result, gx, gy = finish(inverse, gx, pair)
-        go, gu, gd = spread(sums, inverse, gq.shape[0], wide)
+        gu, gd = spread(sums, inverse, gq.shape[0], wide)
         gains_out = [g.reshape(-1) for g in (g1, g2, g3)]
         loss = loss.reshape(())
     else:

time: 164 us -> 162 us (0.988)
  waiting for transfers between devices: 53.6 us -> 50.5 us
  Pallas kernels: 53.2 us -> 55 us
    reduce_scatter x2, waiting for transfers between devices: 7.66 us -> 0.01 us  [the longest x1 0.01 us: body(): lax.psum_scatter(sums, both, scatter_dimension=0, axis_index_groups=inner...]
    all_to_all x5, waiting for transfers between devices: 37.6 us -> 39.9 us  [exchange(): lax.all_to_all(block, 'ctx', 0, 0, axis_index_groups=groups, tiled=True)]
    ppermute x13, waiting for transfers between devices: 8.24 us -> 10.5 us  [swap(): return lax.ppermute(block, axis, [(i, i ^ bit) for i in range(size)])]
    pallas_call x5 -> x6, Pallas kernels: 8.35 us -> 9.5 us  [the longest x1 3.47 us: head_grads(): pl.pallas_call(head_grad_kernel, out_shape=(kept((blocks, step, lanes), B...]
  transfers between devices with their start and end apart: 26 -> 26, of which waited for: 15 -> 13; matrix products, arithmetic and copies ran while one was open for 1% -> 1% of each run, Pallas kernels for 31% -> 32%
where the time goes in v5:
time: 162 us; the launch traced here: 161 us
  Pallas kernels  55 us (34%)
  waiting for transfers between devices  50.5 us (31%)
  starting transfers between devices  39.1 us (24%)
  between operations  14.2 us (9%)
  local copies, waits for them, and re-layouts  1.9 us (1%)
    all_to_all x5, waiting for transfers between devices, exchange(): lax.all_to_all(block, 'ctx', 0, 0, axis_index_groups=groups, tiled=True)  39.9 us
    all_to_all x5, starting transfers between devices, exchange(): lax.all_to_all(block, 'ctx', 0, 0, axis_index_groups=groups, tiled=True)  21.9 us
    pallas_call x2, Pallas kernels, attend_back(): pl.pallas_call(functools.partial(backward_kernel, ways, slots, final, tex...  14.6 us
    ppermute x13, starting transfers between devices, swap(): return lax.ppermute(block, axis, [(i, i ^ bit) for i in range(size)])  12.8 us
    pallas_call x1, Pallas kernels, middle(): pl.pallas_call(functools.partial(middle_kernel, blocks, tile), out_shape=...  10.7 us
    ppermute x13, waiting for transfers between devices, swap(): return lax.ppermute(block, axis, [(i, i ^ bit) for i in range(size)])  10.5 us
    pallas_call x1, Pallas kernels, attend(): pl.pallas_call(functools.partial(forward_kernel, ways, len(segs)), out_sh...  7.85 us
    ppermute x5, starting transfers between devices, moved(): return lax.ppermute(block, both, route)  4.31 us
  transfers between devices with their start and end apart: 26, of which 13 were waited for; matrix products, arithmetic and copies ran while one was open for 1% of the time, Pallas kernels for 32%

profile of v5, /device:TPU:0, one launch (start us, length us, event | category | flops | bytes accessed | tf_op | source)
XLA Modules:
  0.0 161.4 jit_solution(8811473135456329537)
XLA Ops:
  7.2 1.6 collective-permute-start
  8.8 3.4 %collective-permute-start.1 = (bf16[256,512]{1,0:T(8,128)(2,1)}, bf16[256,512]{1,0:T(8,128)(2,1)S(1)}, u32[]{:S(2)}, u32[]{:S(2)}) collective-permute-start(bf16[256,512]{1,0:T(8,128)(2,1)} %refs_1_.5), channel_id=1, source_target_pairs={{0,16},{16,0},{1,17},{17,1},{2,18},{18,2},{3,19},{19,3},{4,20},{20... | collective-permute-start | bytes 786440 | tf_op jit(solution)/shard_map/ppermute | solution.py:76
  12.7 1.1 stage.3
  14.4 1.6 project.1
  15.9 5.8 %all-to-all-start = ((bf16[8,192,256]{2,1,0:T(8,128)(2,1)}), bf16[8,192,256]{2,1,0:T(8,128)(2,1)S(1)}, u32[]{:S(2)}, u32[]{:S(2)}) async-start(bf16[8,192,256]{2,1,0:T(8,128)(2,1)} %project.1), calls=%async_computation | async-start | bytes 1572864 | tf_op jit(solution)/shard_map/all_to_all | solution.py:1182
  23.1 1.9 %collective-permute-start.4 = (s32[16,256]{1,0:T(8,128)S(1)}, s32[16,256]{1,0:T(8,128)S(1)}, u32[]{:S(2)}, u32[]{:S(2)}) collective-permute-start(s32[16,256]{1,0:T(8,128)S(1)} %reshape.50.refs_0_), channel_id=1, source_target_pairs={{0,16},{16,0},{1,17},{17,1},{2,18},{18,2},{3,19},{19,3},{4,20},{20... | collective-permute-start | bytes 49160 | tf_op jit(solution)/shard_map/ppermute | solution.py:76
  25.9 2.9 %plan.1.plan_ref = s32[872]{0:T(1024)S(1)} custom-call(s32[4096]{0:T(1024)S(1)} %bitcast.18, s32[4096]{0:T(1024)S(1)} %bitcast.19), custom_call_target="tpu_custom_call" | custom-call | flops 1000 | bytes 1024 | tf_op jit(solution)/shard_map/plan/pallas_call | solution.py:239
  29.3 13.2 %all-to-all-done.refs_2_.refs_0_.refs_1_ = bf16[8,192,256]{2,1,0:T(8,128)(2,1)S(1)} async-done(((bf16[8,192,256]{2,1,0:T(8,128)(2,1)}), bf16[8,192,256]{2,1,0:T(8,128)(2,1)S(1)}, u32[]{:S(2)}, u32[]{:S(2)}) %all-to-all-start) | async-done | bytes 786464 | tf_op jit(solution)/shard_map/all_to_all | solution.py:1182
  44.5 1.0 collective-permute-done.6.refs_3_.refs_1_
  45.6 7.9 %attend.1 = (bf16[8,64,256]{2,1,0:T(8,128)(2,1)}, f32[8,64,256]{2,1,0:T(8,128)}, f32[8,256]{1,0:T(8,128)S(1)}) custom-call(s32[872]{0:T(1024)} %copy-done.7, s32[16,256]{1,0:T(8,128)S(1)} %reshape.50.refs_0_, s32[16,256]{1,0:T(8,128)S(1)} %collective-permute-done.4.refs_1_, bf16[8,192,256]{2,1,0:T(8,128)(2,1)S(1)} %all-to-all-done.refs_2_.refs_0_.refs_1_, ...), custom_call_target="tpu_custom_call" | custom-call | flops 1000 | bytes 1024 | tf_op jit(solution)/shard_map/attend/pallas_call | solution.py:363
  53.4 3.7 %all-to-all-start.1 = ((bf16[8,64,256]{2,1,0:T(8,128)(2,1)}), bf16[8,64,256]{2,1,0:T(8,128)(2,1)S(1)}, u32[]{:S(2)}, u32[]{:S(2)}) async-start(bf16[8,64,256]{2,1,0:T(8,128)(2,1)} %get-tuple-element.90), calls=%async_computation.1 | async-start | bytes 524288 | tf_op jit(solution)/shard_map/all_to_all | solution.py:1182
  57.2 1.5 collective-permute-start.8
  60.5 1.1 stage.4
  61.7 8.3 %all-to-all-done.1 = bf16[8,64,256]{2,1,0:T(8,128)(2,1)S(1)} async-done(((bf16[8,64,256]{2,1,0:T(8,128)(2,1)}), bf16[8,64,256]{2,1,0:T(8,128)(2,1)S(1)}, u32[]{:S(2)}, u32[]{:S(2)}) %all-to-all-start.1) | async-done | bytes 262176 | tf_op jit(solution)/shard_map/all_to_all | solution.py:1182
  70.0 10.7 %middle.1 = (bf16[512,512]{1,0:T(8,128)(2,1)}, f32[256,512]{1,0:T(8,128)}, bf16[512,256]{1,0:T(8,128)(2,1)}, f32[8,256]{1,0:T(8,128)S(1)}, bf16[16,144,512]{2,1,0:T(8,128)(2,1)}, /*index=5*/bf16[16,144,512]{2,1,0:T(8,128)(2,1)}) custom-call(bf16[512,256]{1,0:T(8,128)(2,1)S(1)} %bitcast.16, s32[1,256]{1,0:T(1,128)S(1)} %collective-permute-done.5.refs_1_, ...), custom_call_target="tpu_custom_call" | custom-call | flops 1000 | bytes 1024 | tf_op jit(solution)/shard_map/middle/pallas_call | solution.py:785
  80.9 3.8 %all-to-all-start.2 = ((bf16[8,64,256]{2,1,0:T(8,128)(2,1)}), bf16[8,64,256]{2,1,0:T(8,128)(2,1)S(1)}, u32[]{:S(2)}, u32[]{:S(2)}) async-start(bf16[8,64,256]{2,1,0:T(8,128)(2,1)} %bitcast.5), calls=%async_computation.2 | async-start | bytes 524288 | tf_op jit(solution)/shard_map/all_to_all | solution.py:1182
  85.5 2.5 %join.1 = (bf16[16,128,512]{2,1,0:T(8,128)(2,1)}, bf16[16,32,256]{2,1,0:T(8,128)(2,1)S(1)}) custom-call(bf16[16,144,512]{2,1,0:T(8,128)(2,1)S(1)} %collective-permute-done.12.two_ref, bf16[16,144,512]{2,1,0:T(8,128)(2,1)} %get-tuple-element.101.one_in), custom_call_target="tpu_custom_call" | custom-call | flops 1000 | bytes 1024 | tf_op jit(solution)/shard_map/join/pallas_call | solution.py:863
  88.1 1.6 prepare.1
  89.7 4.5 %all-to-all-done.2.do_ref = bf16[8,64,256]{2,1,0:T(8,128)(2,1)S(1)} async-done(((bf16[8,64,256]{2,1,0:T(8,128)(2,1)}), bf16[8,64,256]{2,1,0:T(8,128)(2,1)S(1)}, u32[]{:S(2)}, u32[]{:S(2)}) %all-to-all-start.2) | async-done | bytes 262176 | tf_op jit(solution)/shard_map/all_to_all | solution.py:1182
  94.2 8.2 %attend_back.2 = (f32[8,64,256]{2,1,0:T(8,128)S(1)}, bf16[9,256,80]{2,1,0:T(8,128)(2,1)S(1)}, bf16[8,128,256]{2,1,0:T(8,128)(2,1)S(1)}) custom-call(s32[872]{0:T(1024)} %copy-done.7, bf16[16,160,256]{2,1,0:T(8,128)(2,1)S(1)} %get-tuple-element.108.kx, bf16[9,256,160]{2,1,0:T(8,128)(2,1)S(1)} %get-tuple-element.109.qx, ...), custom_call_target="tpu_custom_call" | custom-call | flops 1000 | bytes 1024 | tf_op jit(solution)/shard_map/attend_back/pallas_call | solution.py:527
  102.5 6.3 %attend_back.3 = (bf16[8,64,256]{2,1,0:T(8,128)(2,1)S(1)}, f32[8,128,256]{2,1,0:T(8,128)S(1)}) custom-call(s32[872]{0:T(1024)} %copy-done.7, bf16[16,160,256]{2,1,0:T(8,128)(2,1)S(1)} %get-tuple-element.108.kx, bf16[9,256,160]{2,1,0:T(8,128)(2,1)S(1)} %get-tuple-element.109.qx, bf16[8,64,256]{2,1,0:T(8,128)(2,1)S(1)} %all-to-all-done.2.do_ref, ...), custom_call_target="tpu_custom_call" | custom-call | flops 1000 | bytes 1024 | tf_op jit(solution)/shard_map/attend_back/pallas_call | solution.py:527
  109.9 3.6 %all-to-all-start.4 = ((bf16[8,192,256]{2,1,0:T(8,128)(2,1)}), bf16[8,192,256]{2,1,0:T(8,128)(2,1)S(1)}, u32[]{:S(2)}, u32[]{:S(2)}) async-start(bf16[8,192,256]{2,1,0:T(8,128)(2,1)} %pack.1.back_ref), calls=%async_computation.5 | async-start | bytes 1572864 | tf_op jit(solution)/shard_map/all_to_all | solution.py:1182
  113.5 3.5 %head_grads.1 = (bf16[16,16,256]{2,1,0:T(8,128)(2,1)S(1)}, bf16[16,16,256]{2,1,0:T(8,128)(2,1)S(1)}) custom-call(bf16[8,192,256]{2,1,0:T(8,128)(2,1)} %pack.1.back_ref, bf16[8,256,512]{2,1,0:T(8,128)(2,1)} %bitcast.20, f32[8,256]{1,0:T(8,128)S(1)} %get-tuple-element.118.small_ref), custom_call_target="tpu_custom_call" | custom-call | flops 1000 | bytes 1024 | tf_op jit(solution)/shard_map/head_grads/pallas_call | solution.py:996
  117.0 2.7 %collective-permute-start.14 = (bf16[16,16,256]{2,1,0:T(8,128)(2,1)S(1)}, bf16[16,16,256]{2,1,0:T(8,128)(2,1)S(1)}, u32[]{:S(2)}, u32[]{:S(2)}) collective-permute-start(bf16[16,16,256]{2,1,0:T(8,128)(2,1)S(1)} %get-tuple-element.120), channel_id=1, source_target_pairs={{0,16},{16,0},{1,17},{17,1},{2,18},{18,2},{3,19},{19,3},{4,20},{20... | collective-permute-start | bytes 393224 | tf_op jit(solution)/shard_map/ppermute | solution.py:76
  120.8 1.1 collective-permute-start.15
  121.9 6.1 %collective-permute-done.15.two_ref = bf16[8,48,256]{2,1,0:T(8,128)(2,1)S(1)} collective-permute-done((bf16[8,48,256]{2,1,0:T(8,128)(2,1)S(1)}, bf16[8,48,256]{2,1,0:T(8,128)(2,1)S(1)}, u32[]{:S(2)}, u32[]{:S(2)}) %collective-permute-start.15) | collective-permute-done | bytes 196640 | tf_op jit(solution)/shard_map/ppermute | solution.py:76
  128.8 4.8 %all-to-all-done.4.back_ref = bf16[8,192,256]{2,1,0:T(8,128)(2,1)S(1)} async-done(((bf16[8,192,256]{2,1,0:T(8,128)(2,1)}), bf16[8,192,256]{2,1,0:T(8,128)(2,1)S(1)}, u32[]{:S(2)}, u32[]{:S(2)}) %all-to-all-start.4) | async-done | bytes 786464 | tf_op jit(solution)/shard_map/all_to_all | solution.py:1182
  133.6 4.9 %all-to-all-start.3 = ((bf16[8,48,256]{2,1,0:T(8,128)(2,1)}), bf16[8,48,256]{2,1,0:T(8,128)(2,1)S(1)}, u32[]{:S(2)}, u32[]{:S(2)}) async-start(bf16[8,48,256]{2,1,0:T(8,128)(2,1)} %merge.1), calls=%async_computation.4 | async-start | bytes 393216 | tf_op jit(solution)/shard_map/all_to_all | solution.py:1182
  139.2 1.6 stage.5
  142.1 9.2 %all-to-all-done.3.pieces_ref = bf16[8,48,256]{2,1,0:T(8,128)(2,1)S(1)} async-done(((bf16[8,48,256]{2,1,0:T(8,128)(2,1)}), bf16[8,48,256]{2,1,0:T(8,128)(2,1)S(1)}, u32[]{:S(2)}, u32[]{:S(2)}) %all-to-all-start.3) | async-done | bytes 196640 | tf_op jit(solution)/shard_map/all_to_all | solution.py:1182
  152.2 1.1 finish.1
  153.2 1.7 %spread.1 = (f32[16,2048]{1,0:T(8,128)}, f32[64,512]{1,0:T(8,128)}) custom-call(bf16[1,128,512]{2,1,0:T(8,128)(2,1)} %reduce-scatter.5.cloned.1.call-done.sums_in, f32[8,128]{1,0:T(8,128)S(1)} %get-tuple-element.128.inverse_ref), custom_call_target="tpu_custom_call" | custom-call | flops 1000 | bytes 1024 | tf_op jit(solution)/shard_map/spread/pallas_call | solution.py:1125
  (87 shorter events, 14.3 us)
Async XLA Ops:
  7.2 6.7 %collective-permute-start = (bf16[256,512]{1,0:T(8,128)(2,1)}, bf16[256,512]{1,0:T(8,128)(2,1)S(1)}, u32[]{:S(2)}, u32[]{:S(2)}) collective-permute-start(bf16[256,512]{1,0:T(8,128)(2,1)} %bitcast.25), channel_id=1, source_target_pairs={{0,0},{1,16},{2,2},{3,18},{4,4},{5,20},{6,6},{7,22},{8,8},{9,24},{... | collective-permute-start | bytes 786440 | tf_op jit(solution)/shard_map/ppermute | solution.py:1174
  8.8 5.1 %collective-permute-start.1 = (bf16[256,512]{1,0:T(8,128)(2,1)}, bf16[256,512]{1,0:T(8,128)(2,1)S(1)}, u32[]{:S(2)}, u32[]{:S(2)}) collective-permute-start(bf16[256,512]{1,0:T(8,128)(2,1)} %refs_1_.5), channel_id=1, source_target_pairs={{0,16},{16,0},{1,17},{17,1},{2,18},{18,2},{3,19},{19,3},{4,20},{20... | collective-permute-start | bytes 786440 | tf_op jit(solution)/shard_map/ppermute | solution.py:76
  12.2 1.7 %collective-permute-start.2 = (bf16[256,512]{1,0:T(8,128)(2,1)}, bf16[256,512]{1,0:T(8,128)(2,1)S(1)}, u32[]{:S(2)}, u32[]{:S(2)}) collective-permute-start(bf16[256,512]{1,0:T(8,128)(2,1)} %refs_3_.1), channel_id=1, source_target_pairs={{0,16},{16,0},{1,17},{17,1},{2,18},{18,2},{3,19},{19,3},{4,20},{20... | collective-permute-start | bytes 786440 | tf_op jit(solution)/shard_map/ppermute | solution.py:76
  12.3 2.0 %collective-permute-start.3 = (bf16[256,512]{1,0:T(8,128)(2,1)}, bf16[256,512]{1,0:T(8,128)(2,1)S(1)}, u32[]{:S(2)}, u32[]{:S(2)}) collective-permute-start(bf16[256,512]{1,0:T(8,128)(2,1)} %refs_5_.1), channel_id=1, source_target_pairs={{0,16},{16,0},{1,17},{17,1},{2,18},{18,2},{3,19},{19,3},{4,20},{20... | collective-permute-start | bytes 786440 | tf_op jit(solution)/shard_map/ppermute | solution.py:76
  15.9 26.6 %all-to-all-start = ((bf16[8,192,256]{2,1,0:T(8,128)(2,1)}), bf16[8,192,256]{2,1,0:T(8,128)(2,1)S(1)}, u32[]{:S(2)}, u32[]{:S(2)}) async-start(bf16[8,192,256]{2,1,0:T(8,128)(2,1)} %project.1), calls=%async_computation | async-start | bytes 1572864 | tf_op jit(solution)/shard_map/all_to_all | solution.py:1182
  21.8 35.4 %copy-start.9 = (bf16[256,512]{1,0:T(8,128)(2,1)S(1)}, bf16[256,512]{1,0:T(8,128)(2,1)}, u32[]{:S(2)}) copy-start(bf16[256,512]{1,0:T(8,128)(2,1)} %refs_1_.4) | copy-start | bytes 786436
  21.8 36.9 %copy-start.15 = (bf16[256]{0:T(256)(128)(2,1)S(1)}, bf16[256]{0:T(256)(128)(2,1)}, u32[]{:S(2)}) copy-start(bf16[256]{0:T(256)(128)(2,1)} %param.25) | copy-start | bytes 1540
  21.8 36.9 %copy-start.16 = (bf16[256]{0:T(256)(128)(2,1)S(1)}, bf16[256]{0:T(256)(128)(2,1)}, u32[]{:S(2)}) copy-start(bf16[256]{0:T(256)(128)(2,1)} %param.26) | copy-start | bytes 1540
  21.8 36.9 %copy-start.17 = (bf16[256]{0:T(256)(128)(2,1)S(1)}, bf16[256]{0:T(256)(128)(2,1)}, u32[]{:S(2)}) copy-start(bf16[256]{0:T(256)(128)(2,1)} %param.27) | copy-start | bytes 1540
  21.8 72.4 %all-gather.3.cloned.1.call-start = ((), (), s32[]{:S(2)}) async-start(), calls=%async_computation.9 | async-start | bytes 2359296 | tf_op jit(solution)/shard_map/all_gather | solution.py:1231
  23.1 2.8 %collective-permute-start.4 = (s32[16,256]{1,0:T(8,128)S(1)}, s32[16,256]{1,0:T(8,128)S(1)}, u32[]{:S(2)}, u32[]{:S(2)}) collective-permute-start(s32[16,256]{1,0:T(8,128)S(1)} %reshape.50.refs_0_), channel_id=1, source_target_pairs={{0,16},{16,0},{1,17},{17,1},{2,18},{18,2},{3,19},{19,3},{4,20},{20... | collective-permute-start | bytes 49160 | tf_op jit(solution)/shard_map/ppermute | solution.py:76
  25.0 4.3 %collective-permute-start.5 = (s32[1,256]{1,0:T(1,128)S(1)}, s32[1,256]{1,0:T(1,128)S(1)}, u32[]{:S(2)}, u32[]{:S(2)}) collective-permute-start(s32[1,256]{1,0:T(1,128)S(1)} %copy-done.14), channel_id=1, source_target_pairs={{0,0},{1,16},{2,2},{3,18},{4,4},{5,20},{6,6},{7,22},{8,8},{9,24},{... | collective-permute-start | bytes 3080 | tf_op jit(solution)/shard_map/ppermute | solution.py:1174
  42.5 38.2 %copy-start = (bf16[8,192,256]{2,1,0:T(8,128)(2,1)}, bf16[8,192,256]{2,1,0:T(8,128)(2,1)S(1)}, u32[]{:S(2)}) copy-start(bf16[8,192,256]{2,1,0:T(8,128)(2,1)S(1)} %all-to-all-done.refs_2_.refs_0_.refs_1_) | copy-start | bytes 2359300
  42.5 3.0 %collective-permute-start.6 = (bf16[8,192,256]{2,1,0:T(8,128)(2,1)S(1)}, bf16[8,192,256]{2,1,0:T(8,128)(2,1)S(1)}, u32[]{:S(2)}, u32[]{:S(2)}) collective-permute-start(bf16[8,192,256]{2,1,0:T(8,128)(2,1)S(1)} %all-to-all-done.refs_2_.refs_0_.refs_1_), channel_id=1, source_target_pairs={{0,16},{16,0},{1,17},{17,1},{2,18},{18,2},{3,19},{19,3},{4,20},{20... | collective-permute-start | bytes 2359304 | tf_op jit(solution)/shard_map/ppermute | solution.py:76
  43.3 26.7 %collective-permute-start.10 = (bf16[256,2048]{1,0:T(8,128)(2,1)}, bf16[256,2048]{1,0:T(8,128)(2,1)}, u32[]{:S(2)}, u32[]{:S(2)}) collective-permute-start(bf16[256,2048]{1,0:T(8,128)(2,1)} %refs_7_.1), channel_id=1, source_target_pairs={{0,16},{16,0},{1,17},{17,1},{2,18},{18,2},{3,19},{19,3},{4,20},{20... | collective-permute-start | bytes 3145736 | tf_op jit(solution)/shard_map/ppermute | solution.py:76
  43.4 26.6 %collective-permute-start.11 = (bf16[1024,512]{1,0:T(8,128)(2,1)}, bf16[1024,512]{1,0:T(8,128)(2,1)}, u32[]{:S(2)}, u32[]{:S(2)}) collective-permute-start(bf16[1024,512]{1,0:T(8,128)(2,1)} %refs_9_.1), channel_id=1, source_target_pairs={{0,16},{16,0},{1,17},{17,1},{2,18},{18,2},{3,19},{19,3},{4,20},{20... | collective-permute-start | bytes 3145736 | tf_op jit(solution)/shard_map/ppermute | solution.py:76
  43.8 9.6 %collective-permute-start.7 = (bf16[512,512]{1,0:T(8,128)(2,1)S(1)}, bf16[512,512]{1,0:T(8,128)(2,1)S(1)}, u32[]{:S(2)}, u32[]{:S(2)}) collective-permute-start(bf16[512,512]{1,0:T(8,128)(2,1)S(1)} %pad_maximum_fusion), channel_id=1, source_target_pairs={{0,0},{1,16},{2,2},{3,18},{4,4},{5,20},{6,6},{7,22},{8,8},{9,24},{... | collective-permute-start | bytes 1572872 | tf_op jit(solution)/shard_map/ppermute | solution.py:1174
  45.6 35.1 %copy-start.1 = (bf16[8,192,256]{2,1,0:T(8,128)(2,1)}, bf16[8,192,256]{2,1,0:T(8,128)(2,1)S(1)}, u32[]{:S(2)}) copy-start(bf16[8,192,256]{2,1,0:T(8,128)(2,1)S(1)} %collective-permute-done.6.refs_3_.refs_1_) | copy-start | bytes 2359300
  53.4 16.6 %all-to-all-start.1 = ((bf16[8,64,256]{2,1,0:T(8,128)(2,1)}), bf16[8,64,256]{2,1,0:T(8,128)(2,1)S(1)}, u32[]{:S(2)}, u32[]{:S(2)}) async-start(bf16[8,64,256]{2,1,0:T(8,128)(2,1)} %get-tuple-element.90), calls=%async_computation.1 | async-start | bytes 524288 | tf_op jit(solution)/shard_map/all_to_all | solution.py:1182
  57.2 2.7 %collective-permute-start.8 = (bf16[256,512]{1,0:T(8,128)(2,1)S(1)}, bf16[256,512]{1,0:T(8,128)(2,1)S(1)}, u32[]{:S(2)}, u32[]{:S(2)}) collective-permute-start(bf16[256,512]{1,0:T(8,128)(2,1)S(1)} %copy-done.9), channel_id=1, source_target_pairs={{0,16},{16,0},{1,17},{17,1},{2,18},{18,2},{3,19},{19,3},{4,20},{20... | collective-permute-start | bytes 786440 | tf_op jit(solution)/shard_map/ppermute | solution.py:76
  58.7 11.2 %collective-permute-start.9 = (bf16[3,256]{1,0:T(4,128)(2,1)S(1)}, bf16[3,256]{1,0:T(4,128)(2,1)S(1)}, u32[]{:S(2)}, u32[]{:S(2)}) collective-permute-start(bf16[3,256]{1,0:T(4,128)(2,1)S(1)} %pad_maximum_fusion.1.refs_2_), channel_id=1, source_target_pairs={{0,16},{16,0},{1,17},{17,1},{2,18},{18,2},{3,19},{19,3},{4,20},{20... | collective-permute-start | bytes 4616 | tf_op jit(solution)/shard_map/ppermute | solution.py:76
  80.7 4.8 %collective-permute-start.12 = (bf16[16,144,512]{2,1,0:T(8,128)(2,1)}, bf16[16,144,512]{2,1,0:T(8,128)(2,1)S(1)}, u32[]{:S(2)}, u32[]{:S(2)}) collective-permute-start(bf16[16,144,512]{2,1,0:T(8,128)(2,1)} %get-tuple-element.100), channel_id=1, source_target_pairs={{0,16},{16,0},{1,17},{17,1},{2,18},{18,2},{3,19},{19,3},{4,20},{20... | collective-permute-start | bytes 7077896 | tf_op jit(solution)/shard_map/ppermute | solution.py:76
  80.9 13.3 %all-to-all-start.2 = ((bf16[8,64,256]{2,1,0:T(8,128)(2,1)}), bf16[8,64,256]{2,1,0:T(8,128)(2,1)S(1)}, u32[]{:S(2)}, u32[]{:S(2)}) async-start(bf16[8,64,256]{2,1,0:T(8,128)(2,1)} %bitcast.5), calls=%async_computation.2 | async-start | bytes 524288 | tf_op jit(solution)/shard_map/all_to_all | solution.py:1182
  84.7 44.1 %reduce-scatter.3.cloned.1.call-start = ((), (), s32[]{:S(2)}) async-start(), calls=%async_computation.7 | async-start | bytes 2621440 | tf_op jit(solution)/shard_map/reduce_scatter | solution.py:1240
  102.5 6.4 %collective-permute-start.13 = (bf16[8,128,256]{2,1,0:T(8,128)(2,1)S(1)}, bf16[8,128,256]{2,1,0:T(8,128)(2,1)S(1)}, u32[]{:S(2)}, u32[]{:S(2)}) collective-permute-start(bf16[8,128,256]{2,1,0:T(8,128)(2,1)S(1)} %get-tuple-element.116), channel_id=1, source_target_pairs={{0,16},{16,0},{1,17},{17,1},{2,18},{18,2},{3,19},{19,3},{4,20},{20... | collective-permute-start | bytes 1572872 | tf_op jit(solution)/shard_map/ppermute | solution.py:76
  109.9 23.7 %all-to-all-start.4 = ((bf16[8,192,256]{2,1,0:T(8,128)(2,1)}), bf16[8,192,256]{2,1,0:T(8,128)(2,1)S(1)}, u32[]{:S(2)}, u32[]{:S(2)}) async-start(bf16[8,192,256]{2,1,0:T(8,128)(2,1)} %pack.1.back_ref), calls=%async_computation.5 | async-start | bytes 1572864 | tf_op jit(solution)/shard_map/all_to_all | solution.py:1182
  113.5 39.8 %reduce-scatter.5.cloned.1.call-start = ((), (), s32[]{:S(2)}) async-start(), calls=%async_computation.8 | async-start | bytes 655360 | tf_op jit(solution)/shard_map/reduce_scatter | solution.py:1262
  117.0 3.7 %collective-permute-start.14 = (bf16[16,16,256]{2,1,0:T(8,128)(2,1)S(1)}, bf16[16,16,256]{2,1,0:T(8,128)(2,1)S(1)}, u32[]{:S(2)}, u32[]{:S(2)}) collective-permute-start(bf16[16,16,256]{2,1,0:T(8,128)(2,1)S(1)} %get-tuple-element.120), channel_id=1, source_target_pairs={{0,16},{16,0},{1,17},{17,1},{2,18},{18,2},{3,19},{19,3},{4,20},{20... | collective-permute-start | bytes 393224 | tf_op jit(solution)/shard_map/ppermute | solution.py:76
  120.8 7.2 %collective-permute-start.15 = (bf16[8,48,256]{2,1,0:T(8,128)(2,1)S(1)}, bf16[8,48,256]{2,1,0:T(8,128)(2,1)S(1)}, u32[]{:S(2)}, u32[]{:S(2)}) collective-permute-start(bf16[8,48,256]{2,1,0:T(8,128)(2,1)S(1)} %get-tuple-element.123), channel_id=1, source_target_pairs={{0,1},{1,0},{2,3},{3,2},{4,5},{5,4},{6,7},{7,6},{8,9},{9,8},{10,11... | collective-permute-start | bytes 589832 | tf_op jit(solution)/shard_map/ppermute | solution.py:76
  133.6 17.7 %all-to-all-start.3 = ((bf16[8,48,256]{2,1,0:T(8,128)(2,1)}), bf16[8,48,256]{2,1,0:T(8,128)(2,1)S(1)}, u32[]{:S(2)}, u32[]{:S(2)}) async-start(bf16[8,48,256]{2,1,0:T(8,128)(2,1)} %merge.1), calls=%async_computation.4 | async-start | bytes 393216 | tf_op jit(solution)/shard_map/all_to_all | solution.py:1182
  138.5 13.6 %collective-permute-start.17 = (bf16[512,512]{1,0:T(8,128)(2,1)S(1)}, bf16[512,512]{1,0:T(8,128)(2,1)S(1)}, u32[]{:S(2)}, u32[]{:S(2)}) collective-permute-start(bf16[512,512]{1,0:T(8,128)(2,1)S(1)} %copy-done.13), channel_id=1, source_target_pairs={{0,0},{1,16},{2,2},{3,18},{4,4},{5,20},{6,6},{7,22},{8,8},{9,24},{... | collective-permute-start | bytes 1572872 | tf_op jit(solution)/shard_map/ppermute | solution.py:1174
  141.4 10.7 %collective-permute-start.16 = (bf16[256,512]{1,0:T(8,128)(2,1)S(1)}, bf16[256,512]{1,0:T(8,128)(2,1)S(1)}, u32[]{:S(2)}, u32[]{:S(2)}) collective-permute-start(bf16[256,512]{1,0:T(8,128)(2,1)S(1)} %last.1), channel_id=1, source_target_pairs={{0,0},{1,16},{2,2},{3,18},{4,4},{5,20},{6,6},{7,22},{8,8},{9,24},{... | collective-permute-start | bytes 786440 | tf_op jit(solution)/shard_map/ppermute | solution.py:1174
  (12 other events, 91.9 us)
Sparse Core Ops, SparseCore 0:
  42.7 36.8 all-gather.2
  94.3 27.2 reduce-scatter.2
  128.9 23.9 reduce-scatter.4

commit v6 on v5

--- a/solution.py
+++ b/solution.py
@@ -17,7 +17,6 @@
 RING = (0, 2, 4, 6, 7, 5, 3, 1)
 GROUP = 8
 GROUP_BACK = 4
-LOG2E = 1.4426950408889634
 FAR = -(2.0**100)
 CORE = 0.7978845608028654
 CUBE = 0.044715
@@ -177,15 +176,11 @@
 
 
 def query_rows(q, row, extra):
-    wide = q.astype(F32) * LOG2E
-    high, low = parts_of(wide, 2)
-    return jnp.concatenate(
-        [high.astype(BF16), low.astype(BF16), mask_rows(row, 0.0, FAR, extra)], axis=0
-    ).T
+    return jnp.concatenate([q, mask_rows(row, 0.0, FAR, extra)], axis=0).T
 
 
 def key_rows(k, row):
-    return jnp.concatenate([k, k, mask_rows(row, 1.0, 0.0, (1.0, 1.0, 1.0))], axis=0)
+    return jnp.concatenate([k, mask_rows(row, 1.0, 0.0, (1.0, 1.0, 1.0))], axis=0)
 
 
 def list_size(count):
@@ -298,7 +293,7 @@
     @pl.loop(0, plan_ref[6 * length])
     def group(g):
         tiles = tiles_of(plan_ref, 0, length, g)
-        weights = [jnp.exp2(dot(qx[i], kx[c])).astype(BF16) for i, c in tiles]
+        weights = [jnp.exp(dot(qx[i], kx[c])).astype(BF16) for i, c in tiles]
         mixed = [dot_t(vx[c], w) for (i, c), w in zip(tiles, weights)]
         for (i, c), part in zip(tiles, mixed):
             acc[i] += part
@@ -314,7 +309,7 @@
         of_ref[i] = out
         leaving += fetch([of_ref.at[i]], [of_out.at[i]], sem, i)
         o_ref[i] = out.astype(BF16)
-        lse_ref[i : i + 1, :] = jnp.log(total) * LOG2E
+        lse_ref[i : i + 1, :] = jnp.log(total)
     for copy in leaving:
         copy.wait()
     good = (jnp.min(smallest) > 2.0**-90) & (jnp.max(largest) < 2.0**90)
@@ -329,8 +324,8 @@
                 top, total, mixed = carry
                 s = dot(query, kx[c])
                 new = jnp.maximum(top, jnp.max(s, axis=1, keepdims=True))
-                fade = jnp.exp2(top - new)
-                w = jnp.exp2(s - new)
+                fade = jnp.exp(top - new)
+                w = jnp.exp(s - new)
                 total = total * fade + jnp.sum(w, axis=1, keepdims=True)
                 mixed = mixed * fade + dot_t(w.astype(BF16), vx[c])
                 return new, total, mixed
@@ -348,7 +343,7 @@
             out = (mixed / total).T[0:size, :]
             of_ref[i] = out
             o_ref[i] = out.astype(BF16)
-            lse = jnp.broadcast_to(top + jnp.log(total) * LOG2E, (tok, 128)).T
+            lse = jnp.broadcast_to(top + jnp.log(total), (tok, 128)).T
             lse_ref[pl.ds(i, 1), :] = lse[0:1, :]
 
         fetch([of_ref], [of_out], sem)[0].wait()
@@ -359,7 +354,7 @@
     _, size, tok = kvs[0].shape
     size = size // 3
     count = segs[0].shape[0]
-    depth = 2 * size + LANES
+    depth = size + LANES
     return pl.pallas_call(
         functools.partial(forward_kernel, ways, len(segs)),
         out_shape=(
@@ -418,7 +413,7 @@
     ways = len(kvs)
     count, tok = segs[0].shape
     size = kvs[0].shape[1] // 3
-    depth = 2 * size + LANES
+    depth = size + LANES
     return pl.pallas_call(
         functools.partial(prepare_kernel, ways, len(segs)),
         out_shape=(kept((count, depth, tok), BF16), kept((HEADS + 1, tok, depth), BF16)),
@@ -491,7 +486,7 @@
     @pl.loop(0, plan_ref[6 * length + kind])
     def group(g):
         tiles = tiles_of(plan_ref, kind, length, g)
-        weights = [jnp.exp2(dot(qx[i], kx[c])) for i, c in tiles]
+        weights = [jnp.exp(dot(qx[i], kx[c])) for i, c in tiles]
         pulls = [dot(dx[i], vx[c]) for i, c in tiles]
         scores = [(w * p).astype(BF16) for w, p in zip(weights, pulls)]
         for (i, c), w, ds in zip(tiles, weights, scores):

time: 162 us -> 161 us (level)
  starting transfers between devices: 39.1 us -> 41.6 us
  waiting for transfers between devices: 50.5 us -> 48.1 us
    ppermute x13, starting transfers between devices: 12.8 us -> 16.7 us  [swap(): return lax.ppermute(block, axis, [(i, i ^ bit) for i in range(size)])]
    all_to_all x5, waiting for transfers between devices: 39.9 us -> 37.6 us  [exchange(): lax.all_to_all(block, 'ctx', 0, 0, axis_index_groups=groups, tiled=True)]
    pallas_call x1, Pallas kernels: 2.54 us -> 4.19 us  [join(): pl.pallas_call(join_kernel, out_shape=(apart((blocks, depth - step, feat)...]
  transfers between devices with their start and end apart: 26 -> 26, of which waited for: 13 -> 14; matrix products, arithmetic and copies ran while one was open for 1% -> 1% of each run, Pallas kernels for 32% -> 32%
where the time goes in v6:
time: 161 us
  Pallas kernels  54 us (34%)
  waiting for transfers between devices  48.1 us (30%)
  starting transfers between devices  41.6 us (26%)
  between operations  14.2 us (9%)
  local copies, waits for them, and re-layouts  1.9 us (1%)
    all_to_all x5, waiting for transfers between devices, exchange(): lax.all_to_all(block, 'ctx', 0, 0, axis_index_groups=groups, tiled=True)  37.6 us
    all_to_all x5, starting transfers between devices, exchange(): lax.all_to_all(block, 'ctx', 0, 0, axis_index_groups=groups, tiled=True)  20.3 us
    ppermute x13, starting transfers between devices, swap(): return lax.ppermute(block, axis, [(i, i ^ bit) for i in range(size)])  16.7 us
    pallas_call x2, Pallas kernels, attend_back(): pl.pallas_call(functools.partial(backward_kernel, ways, slots, final, tex...  13 us
    pallas_call x1, Pallas kernels, middle(): pl.pallas_call(functools.partial(middle_kernel, blocks, tile), out_shape=...  10.7 us
    ppermute x13, waiting for transfers between devices, swap(): return lax.ppermute(block, axis, [(i, i ^ bit) for i in range(size)])  9.8 us
    pallas_call x1, Pallas kernels, attend(): pl.pallas_call(functools.partial(forward_kernel, ways, len(segs)), out_sh...  6.92 us
    ppermute x5, starting transfers between devices, moved(): return lax.ppermute(block, both, route)  4.44 us
  transfers between devices with their start and end apart: 26, of which 14 were waited for; matrix products, arithmetic and copies ran while one was open for 1% of the time, Pallas kernels for 32%

profile of v6, /device:TPU:0, one launch (start us, length us, event | category | flops | bytes accessed | tf_op | source)
XLA Modules:
  0.0 160.6 jit_solution(11309595867165446311)
XLA Ops:
  7.2 1.7 %collective-permute-start = (bf16[256,512]{1,0:T(8,128)(2,1)}, bf16[256,512]{1,0:T(8,128)(2,1)S(1)}, u32[]{:S(2)}, u32[]{:S(2)}) collective-permute-start(bf16[256,512]{1,0:T(8,128)(2,1)} %bitcast.25), channel_id=1, source_target_pairs={{0,0},{1,16},{2,2},{3,18},{4,4},{5,20},{6,6},{7,22},{8,8},{9,24},{... | collective-permute-start | bytes 786440 | tf_op jit(solution)/shard_map/ppermute | solution.py:1169
  9.0 3.4 %collective-permute-start.1 = (bf16[256,512]{1,0:T(8,128)(2,1)}, bf16[256,512]{1,0:T(8,128)(2,1)S(1)}, u32[]{:S(2)}, u32[]{:S(2)}) collective-permute-start(bf16[256,512]{1,0:T(8,128)(2,1)} %refs_1_.5), channel_id=1, source_target_pairs={{0,16},{16,0},{1,17},{17,1},{2,18},{18,2},{3,19},{19,3},{4,20},{20... | collective-permute-start | bytes 786440 | tf_op jit(solution)/shard_map/ppermute | solution.py:75
  12.9 1.1 stage.3
  14.5 1.6 project.1
  16.1 6.0 %all-to-all-start = ((bf16[8,192,256]{2,1,0:T(8,128)(2,1)}), bf16[8,192,256]{2,1,0:T(8,128)(2,1)S(1)}, u32[]{:S(2)}, u32[]{:S(2)}) async-start(bf16[8,192,256]{2,1,0:T(8,128)(2,1)} %project.1), calls=%async_computation | async-start | bytes 1572864 | tf_op jit(solution)/shard_map/all_to_all | solution.py:1177
  23.3 1.9 %collective-permute-start.4 = (s32[16,256]{1,0:T(8,128)S(1)}, s32[16,256]{1,0:T(8,128)S(1)}, u32[]{:S(2)}, u32[]{:S(2)}) collective-permute-start(s32[16,256]{1,0:T(8,128)S(1)} %reshape.50.refs_0_), channel_id=1, source_target_pairs={{0,16},{16,0},{1,17},{17,1},{2,18},{18,2},{3,19},{19,3},{4,20},{20... | collective-permute-start | bytes 49160 | tf_op jit(solution)/shard_map/ppermute | solution.py:75
  26.1 2.8 %plan.1.plan_ref = s32[872]{0:T(1024)S(1)} custom-call(s32[4096]{0:T(1024)S(1)} %bitcast.18, s32[4096]{0:T(1024)S(1)} %bitcast.19), custom_call_target="tpu_custom_call" | custom-call | flops 1000 | bytes 1024 | tf_op jit(solution)/shard_map/plan/pallas_call | solution.py:234
  29.5 13.4 %all-to-all-done.refs_2_.refs_0_.refs_1_ = bf16[8,192,256]{2,1,0:T(8,128)(2,1)S(1)} async-done(((bf16[8,192,256]{2,1,0:T(8,128)(2,1)}), bf16[8,192,256]{2,1,0:T(8,128)(2,1)S(1)}, u32[]{:S(2)}, u32[]{:S(2)}) %all-to-all-start) | async-done | bytes 786464 | tf_op jit(solution)/shard_map/all_to_all | solution.py:1177
  44.8 1.0 collective-permute-done.6.refs_3_.refs_1_
  45.8 6.9 %attend.1 = (bf16[8,64,256]{2,1,0:T(8,128)(2,1)}, f32[8,64,256]{2,1,0:T(8,128)}, f32[8,256]{1,0:T(8,128)S(1)}) custom-call(s32[872]{0:T(1024)} %copy-done.7, s32[16,256]{1,0:T(8,128)S(1)} %reshape.50.refs_0_, s32[16,256]{1,0:T(8,128)S(1)} %collective-permute-done.4.refs_1_, bf16[8,192,256]{2,1,0:T(8,128)(2,1)S(1)} %all-to-all-done.refs_2_.refs_0_.refs_1_, ...), custom_call_target="tpu_custom_call" | custom-call | flops 1000 | bytes 1024 | tf_op jit(solution)/shard_map/attend/pallas_call | solution.py:358
  52.8 3.7 %all-to-all-start.1 = ((bf16[8,64,256]{2,1,0:T(8,128)(2,1)}), bf16[8,64,256]{2,1,0:T(8,128)(2,1)S(1)}, u32[]{:S(2)}, u32[]{:S(2)}) async-start(bf16[8,64,256]{2,1,0:T(8,128)(2,1)} %get-tuple-element.90), calls=%async_computation.1 | async-start | bytes 524288 | tf_op jit(solution)/shard_map/all_to_all | solution.py:1177
  56.5 2.4 %collective-permute-start.8 = (bf16[256,512]{1,0:T(8,128)(2,1)S(1)}, bf16[256,512]{1,0:T(8,128)(2,1)S(1)}, u32[]{:S(2)}, u32[]{:S(2)}) collective-permute-start(bf16[256,512]{1,0:T(8,128)(2,1)S(1)} %copy-done.9), channel_id=1, source_target_pairs={{0,16},{16,0},{1,17},{17,1},{2,18},{18,2},{3,19},{19,3},{4,20},{20... | collective-permute-start | bytes 786440 | tf_op jit(solution)/shard_map/ppermute | solution.py:75
  60.8 1.1 stage.4
  62.0 7.6 %all-to-all-done.1 = bf16[8,64,256]{2,1,0:T(8,128)(2,1)S(1)} async-done(((bf16[8,64,256]{2,1,0:T(8,128)(2,1)}), bf16[8,64,256]{2,1,0:T(8,128)(2,1)S(1)}, u32[]{:S(2)}, u32[]{:S(2)}) %all-to-all-start.1) | async-done | bytes 262176 | tf_op jit(solution)/shard_map/all_to_all | solution.py:1177
  69.6 10.7 %middle.1 = (bf16[512,512]{1,0:T(8,128)(2,1)}, f32[256,512]{1,0:T(8,128)}, bf16[512,256]{1,0:T(8,128)(2,1)}, f32[8,256]{1,0:T(8,128)S(1)}, bf16[16,144,512]{2,1,0:T(8,128)(2,1)}, /*index=5*/bf16[16,144,512]{2,1,0:T(8,128)(2,1)}) custom-call(bf16[512,256]{1,0:T(8,128)(2,1)S(1)} %bitcast.16, s32[1,256]{1,0:T(1,128)S(1)} %collective-permute-done.5.refs_1_, ...), custom_call_target="tpu_custom_call" | custom-call | flops 1000 | bytes 1024 | tf_op jit(solution)/shard_map/middle/pallas_call | solution.py:780
  80.3 1.4 collective-permute-start.12
  81.6 3.4 %all-to-all-start.2 = ((bf16[8,64,256]{2,1,0:T(8,128)(2,1)}), bf16[8,64,256]{2,1,0:T(8,128)(2,1)S(1)}, u32[]{:S(2)}, u32[]{:S(2)}) async-start(bf16[8,64,256]{2,1,0:T(8,128)(2,1)} %bitcast.5), calls=%async_computation.2 | async-start | bytes 524288 | tf_op jit(solution)/shard_map/all_to_all | solution.py:1177
  86.1 4.2 %join.1 = (bf16[16,128,512]{2,1,0:T(8,128)(2,1)}, bf16[16,32,256]{2,1,0:T(8,128)(2,1)S(1)}) custom-call(bf16[16,144,512]{2,1,0:T(8,128)(2,1)} %collective-permute-done.12.two_ref, bf16[16,144,512]{2,1,0:T(8,128)(2,1)} %get-tuple-element.101.one_in), custom_call_target="tpu_custom_call" | custom-call | flops 1000 | bytes 1024 | tf_op jit(solution)/shard_map/join/pallas_call | solution.py:858
  90.3 1.5 prepare.1
  91.8 2.6 %all-to-all-done.2.do_ref = bf16[8,64,256]{2,1,0:T(8,128)(2,1)S(1)} async-done(((bf16[8,64,256]{2,1,0:T(8,128)(2,1)}), bf16[8,64,256]{2,1,0:T(8,128)(2,1)S(1)}, u32[]{:S(2)}, u32[]{:S(2)}) %all-to-all-start.2) | async-done | bytes 262176 | tf_op jit(solution)/shard_map/all_to_all | solution.py:1177
  94.4 6.7 %attend_back.2 = (f32[8,64,256]{2,1,0:T(8,128)S(1)}, bf16[9,256,80]{2,1,0:T(8,128)(2,1)S(1)}, bf16[8,128,256]{2,1,0:T(8,128)(2,1)S(1)}) custom-call(s32[872]{0:T(1024)} %copy-done.7, bf16[16,96,256]{2,1,0:T(8,128)(2,1)S(1)} %get-tuple-element.108.kx, bf16[9,256,96]{2,1,0:T(8,128)(2,1)S(1)} %get-tuple-element.109.qx, ...), custom_call_target="tpu_custom_call" | custom-call | flops 1000 | bytes 1024 | tf_op jit(solution)/shard_map/attend_back/pallas_call | solution.py:522
  101.2 6.3 %attend_back.3 = (bf16[8,64,256]{2,1,0:T(8,128)(2,1)S(1)}, f32[8,128,256]{2,1,0:T(8,128)S(1)}) custom-call(s32[872]{0:T(1024)} %copy-done.7, bf16[16,96,256]{2,1,0:T(8,128)(2,1)S(1)} %get-tuple-element.108.kx, bf16[9,256,96]{2,1,0:T(8,128)(2,1)S(1)} %get-tuple-element.109.qx, bf16[8,64,256]{2,1,0:T(8,128)(2,1)S(1)} %all-to-all-done.2.do_ref, ...), custom_call_target="tpu_custom_call" | custom-call | flops 1000 | bytes 1024 | tf_op jit(solution)/shard_map/attend_back/pallas_call | solution.py:522
  108.5 3.6 %all-to-all-start.4 = ((bf16[8,192,256]{2,1,0:T(8,128)(2,1)}), bf16[8,192,256]{2,1,0:T(8,128)(2,1)S(1)}, u32[]{:S(2)}, u32[]{:S(2)}) async-start(bf16[8,192,256]{2,1,0:T(8,128)(2,1)} %pack.1.back_ref), calls=%async_computation.5 | async-start | bytes 1572864 | tf_op jit(solution)/shard_map/all_to_all | solution.py:1177
  112.2 3.5 %head_grads.1 = (bf16[16,16,256]{2,1,0:T(8,128)(2,1)S(1)}, bf16[16,16,256]{2,1,0:T(8,128)(2,1)S(1)}) custom-call(bf16[8,192,256]{2,1,0:T(8,128)(2,1)} %pack.1.back_ref, bf16[8,256,512]{2,1,0:T(8,128)(2,1)} %bitcast.20, f32[8,256]{1,0:T(8,128)S(1)} %get-tuple-element.118.small_ref), custom_call_target="tpu_custom_call" | custom-call | flops 1000 | bytes 1024 | tf_op jit(solution)/shard_map/head_grads/pallas_call | solution.py:991
  117.3 5.1 %collective-permute-start.15 = (bf16[8,48,256]{2,1,0:T(8,128)(2,1)S(1)}, bf16[8,48,256]{2,1,0:T(8,128)(2,1)S(1)}, u32[]{:S(2)}, u32[]{:S(2)}) collective-permute-start(bf16[8,48,256]{2,1,0:T(8,128)(2,1)S(1)} %get-tuple-element.123), channel_id=1, source_target_pairs={{0,1},{1,0},{2,3},{3,2},{4,5},{5,4},{6,7},{7,6},{8,9},{9,8},{10,11... | collective-permute-start | bytes 589832 | tf_op jit(solution)/shard_map/ppermute | solution.py:75
  122.4 5.2 %collective-permute-done.15.two_ref = bf16[8,48,256]{2,1,0:T(8,128)(2,1)S(1)} collective-permute-done((bf16[8,48,256]{2,1,0:T(8,128)(2,1)S(1)}, bf16[8,48,256]{2,1,0:T(8,128)(2,1)S(1)}, u32[]{:S(2)}, u32[]{:S(2)}) %collective-permute-start.15) | collective-permute-done | bytes 196640 | tf_op jit(solution)/shard_map/ppermute | solution.py:75
  128.4 4.8 %all-to-all-done.4.back_ref = bf16[8,192,256]{2,1,0:T(8,128)(2,1)S(1)} async-done(((bf16[8,192,256]{2,1,0:T(8,128)(2,1)}), bf16[8,192,256]{2,1,0:T(8,128)(2,1)S(1)}, u32[]{:S(2)}, u32[]{:S(2)}) %all-to-all-start.4) | async-done | bytes 786464 | tf_op jit(solution)/shard_map/all_to_all | solution.py:1177
  133.1 3.6 %all-to-all-start.3 = ((bf16[8,48,256]{2,1,0:T(8,128)(2,1)}), bf16[8,48,256]{2,1,0:T(8,128)(2,1)S(1)}, u32[]{:S(2)}, u32[]{:S(2)}) async-start(bf16[8,48,256]{2,1,0:T(8,128)(2,1)} %merge.1), calls=%async_computation.4 | async-start | bytes 393216 | tf_op jit(solution)/shard_map/all_to_all | solution.py:1177
  137.5 1.6 stage.5
  140.3 9.3 %all-to-all-done.3.pieces_ref = bf16[8,48,256]{2,1,0:T(8,128)(2,1)S(1)} async-done(((bf16[8,48,256]{2,1,0:T(8,128)(2,1)}), bf16[8,48,256]{2,1,0:T(8,128)(2,1)S(1)}, u32[]{:S(2)}, u32[]{:S(2)}) %all-to-all-start.3) | async-done | bytes 196640 | tf_op jit(solution)/shard_map/all_to_all | solution.py:1177
  150.5 1.1 finish.1
  152.3 1.7 %spread.1 = (f32[16,2048]{1,0:T(8,128)}, f32[64,512]{1,0:T(8,128)}) custom-call(bf16[1,128,512]{2,1,0:T(8,128)(2,1)} %reduce-scatter.5.cloned.1.call-done.sums_in, f32[8,128]{1,0:T(8,128)S(1)} %get-tuple-element.128.inverse_ref), custom_call_target="tpu_custom_call" | custom-call | flops 1000 | bytes 1024 | tf_op jit(solution)/shard_map/spread/pallas_call | solution.py:1120
  (87 shorter events, 15.5 us)
Async XLA Ops:
  7.2 6.8 %collective-permute-start = (bf16[256,512]{1,0:T(8,128)(2,1)}, bf16[256,512]{1,0:T(8,128)(2,1)S(1)}, u32[]{:S(2)}, u32[]{:S(2)}) collective-permute-start(bf16[256,512]{1,0:T(8,128)(2,1)} %bitcast.25), channel_id=1, source_target_pairs={{0,0},{1,16},{2,2},{3,18},{4,4},{5,20},{6,6},{7,22},{8,8},{9,24},{... | collective-permute-start | bytes 786440 | tf_op jit(solution)/shard_map/ppermute | solution.py:1169
  9.0 5.1 %collective-permute-start.1 = (bf16[256,512]{1,0:T(8,128)(2,1)}, bf16[256,512]{1,0:T(8,128)(2,1)S(1)}, u32[]{:S(2)}, u32[]{:S(2)}) collective-permute-start(bf16[256,512]{1,0:T(8,128)(2,1)} %refs_1_.5), channel_id=1, source_target_pairs={{0,16},{16,0},{1,17},{17,1},{2,18},{18,2},{3,19},{19,3},{4,20},{20... | collective-permute-start | bytes 786440 | tf_op jit(solution)/shard_map/ppermute | solution.py:75
  12.4 1.7 %collective-permute-start.2 = (bf16[256,512]{1,0:T(8,128)(2,1)}, bf16[256,512]{1,0:T(8,128)(2,1)S(1)}, u32[]{:S(2)}, u32[]{:S(2)}) collective-permute-start(bf16[256,512]{1,0:T(8,128)(2,1)} %refs_3_.1), channel_id=1, source_target_pairs={{0,16},{16,0},{1,17},{17,1},{2,18},{18,2},{3,19},{19,3},{4,20},{20... | collective-permute-start | bytes 786440 | tf_op jit(solution)/shard_map/ppermute | solution.py:75
  12.5 2.0 %collective-permute-start.3 = (bf16[256,512]{1,0:T(8,128)(2,1)}, bf16[256,512]{1,0:T(8,128)(2,1)S(1)}, u32[]{:S(2)}, u32[]{:S(2)}) collective-permute-start(bf16[256,512]{1,0:T(8,128)(2,1)} %refs_5_.1), channel_id=1, source_target_pairs={{0,16},{16,0},{1,17},{17,1},{2,18},{18,2},{3,19},{19,3},{4,20},{20... | collective-permute-start | bytes 786440 | tf_op jit(solution)/shard_map/ppermute | solution.py:75
  16.1 40.5 %copy-start.9 = (bf16[256,512]{1,0:T(8,128)(2,1)S(1)}, bf16[256,512]{1,0:T(8,128)(2,1)}, u32[]{:S(2)}) copy-start(bf16[256,512]{1,0:T(8,128)(2,1)} %refs_1_.4) | copy-start | bytes 786436
  16.1 42.9 %copy-start.15 = (bf16[256]{0:T(256)(128)(2,1)S(1)}, bf16[256]{0:T(256)(128)(2,1)}, u32[]{:S(2)}) copy-start(bf16[256]{0:T(256)(128)(2,1)} %param.25) | copy-start | bytes 1540
  16.1 42.9 %copy-start.16 = (bf16[256]{0:T(256)(128)(2,1)S(1)}, bf16[256]{0:T(256)(128)(2,1)}, u32[]{:S(2)}) copy-start(bf16[256]{0:T(256)(128)(2,1)} %param.26) | copy-start | bytes 1540
  16.1 42.9 %copy-start.17 = (bf16[256]{0:T(256)(128)(2,1)S(1)}, bf16[256]{0:T(256)(128)(2,1)}, u32[]{:S(2)}) copy-start(bf16[256]{0:T(256)(128)(2,1)} %param.27) | copy-start | bytes 1540
  16.1 26.8 %all-to-all-start = ((bf16[8,192,256]{2,1,0:T(8,128)(2,1)}), bf16[8,192,256]{2,1,0:T(8,128)(2,1)S(1)}, u32[]{:S(2)}, u32[]{:S(2)}) async-start(bf16[8,192,256]{2,1,0:T(8,128)(2,1)} %project.1), calls=%async_computation | async-start | bytes 1572864 | tf_op jit(solution)/shard_map/all_to_all | solution.py:1177
  22.1 72.3 %all-gather.3.cloned.1.call-start = ((), (), s32[]{:S(2)}) async-start(), calls=%async_computation.9 | async-start | bytes 2359296 | tf_op jit(solution)/shard_map/all_gather | solution.py:1226
  23.3 2.7 %collective-permute-start.4 = (s32[16,256]{1,0:T(8,128)S(1)}, s32[16,256]{1,0:T(8,128)S(1)}, u32[]{:S(2)}, u32[]{:S(2)}) collective-permute-start(s32[16,256]{1,0:T(8,128)S(1)} %reshape.50.refs_0_), channel_id=1, source_target_pairs={{0,16},{16,0},{1,17},{17,1},{2,18},{18,2},{3,19},{19,3},{4,20},{20... | collective-permute-start | bytes 49160 | tf_op jit(solution)/shard_map/ppermute | solution.py:75
  25.2 4.2 %collective-permute-start.5 = (s32[1,256]{1,0:T(1,128)S(1)}, s32[1,256]{1,0:T(1,128)S(1)}, u32[]{:S(2)}, u32[]{:S(2)}) collective-permute-start(s32[1,256]{1,0:T(1,128)S(1)} %copy-done.14), channel_id=1, source_target_pairs={{0,0},{1,16},{2,2},{3,18},{4,4},{5,20},{6,6},{7,22},{8,8},{9,24},{... | collective-permute-start | bytes 3080 | tf_op jit(solution)/shard_map/ppermute | solution.py:1169
  42.8 37.4 %copy-start = (bf16[8,192,256]{2,1,0:T(8,128)(2,1)}, bf16[8,192,256]{2,1,0:T(8,128)(2,1)S(1)}, u32[]{:S(2)}) copy-start(bf16[8,192,256]{2,1,0:T(8,128)(2,1)S(1)} %all-to-all-done.refs_2_.refs_0_.refs_1_) | copy-start | bytes 2359300
  42.9 3.0 %collective-permute-start.6 = (bf16[8,192,256]{2,1,0:T(8,128)(2,1)S(1)}, bf16[8,192,256]{2,1,0:T(8,128)(2,1)S(1)}, u32[]{:S(2)}, u32[]{:S(2)}) collective-permute-start(bf16[8,192,256]{2,1,0:T(8,128)(2,1)S(1)} %all-to-all-done.refs_2_.refs_0_.refs_1_), channel_id=1, source_target_pairs={{0,16},{16,0},{1,17},{17,1},{2,18},{18,2},{3,19},{19,3},{4,20},{20... | collective-permute-start | bytes 2359304 | tf_op jit(solution)/shard_map/ppermute | solution.py:75
  43.6 26.0 %collective-permute-start.10 = (bf16[256,2048]{1,0:T(8,128)(2,1)}, bf16[256,2048]{1,0:T(8,128)(2,1)}, u32[]{:S(2)}, u32[]{:S(2)}) collective-permute-start(bf16[256,2048]{1,0:T(8,128)(2,1)} %refs_7_.1), channel_id=1, source_target_pairs={{0,16},{16,0},{1,17},{17,1},{2,18},{18,2},{3,19},{19,3},{4,20},{20... | collective-permute-start | bytes 3145736 | tf_op jit(solution)/shard_map/ppermute | solution.py:75
  43.7 25.9 %collective-permute-start.11 = (bf16[1024,512]{1,0:T(8,128)(2,1)}, bf16[1024,512]{1,0:T(8,128)(2,1)}, u32[]{:S(2)}, u32[]{:S(2)}) collective-permute-start(bf16[1024,512]{1,0:T(8,128)(2,1)} %refs_9_.1), channel_id=1, source_target_pairs={{0,16},{16,0},{1,17},{17,1},{2,18},{18,2},{3,19},{19,3},{4,20},{20... | collective-permute-start | bytes 3145736 | tf_op jit(solution)/shard_map/ppermute | solution.py:75
  44.1 8.7 %collective-permute-start.7 = (bf16[512,512]{1,0:T(8,128)(2,1)S(1)}, bf16[512,512]{1,0:T(8,128)(2,1)S(1)}, u32[]{:S(2)}, u32[]{:S(2)}) collective-permute-start(bf16[512,512]{1,0:T(8,128)(2,1)S(1)} %pad_maximum_fusion), channel_id=1, source_target_pairs={{0,0},{1,16},{2,2},{3,18},{4,4},{5,20},{6,6},{7,22},{8,8},{9,24},{... | collective-permute-start | bytes 1572872 | tf_op jit(solution)/shard_map/ppermute | solution.py:1169
  45.8 34.4 %copy-start.1 = (bf16[8,192,256]{2,1,0:T(8,128)(2,1)}, bf16[8,192,256]{2,1,0:T(8,128)(2,1)S(1)}, u32[]{:S(2)}) copy-start(bf16[8,192,256]{2,1,0:T(8,128)(2,1)S(1)} %collective-permute-done.6.refs_3_.refs_1_) | copy-start | bytes 2359300
  52.8 16.7 %all-to-all-start.1 = ((bf16[8,64,256]{2,1,0:T(8,128)(2,1)}), bf16[8,64,256]{2,1,0:T(8,128)(2,1)S(1)}, u32[]{:S(2)}, u32[]{:S(2)}) async-start(bf16[8,64,256]{2,1,0:T(8,128)(2,1)} %get-tuple-element.90), calls=%async_computation.1 | async-start | bytes 524288 | tf_op jit(solution)/shard_map/all_to_all | solution.py:1177
  56.5 3.6 %collective-permute-start.8 = (bf16[256,512]{1,0:T(8,128)(2,1)S(1)}, bf16[256,512]{1,0:T(8,128)(2,1)S(1)}, u32[]{:S(2)}, u32[]{:S(2)}) collective-permute-start(bf16[256,512]{1,0:T(8,128)(2,1)S(1)} %copy-done.9), channel_id=1, source_target_pairs={{0,16},{16,0},{1,17},{17,1},{2,18},{18,2},{3,19},{19,3},{4,20},{20... | collective-permute-start | bytes 786440 | tf_op jit(solution)/shard_map/ppermute | solution.py:75
  59.0 10.5 %collective-permute-start.9 = (bf16[3,256]{1,0:T(4,128)(2,1)S(1)}, bf16[3,256]{1,0:T(4,128)(2,1)S(1)}, u32[]{:S(2)}, u32[]{:S(2)}) collective-permute-start(bf16[3,256]{1,0:T(4,128)(2,1)S(1)} %pad_maximum_fusion.1.refs_2_), channel_id=1, source_target_pairs={{0,16},{16,0},{1,17},{17,1},{2,18},{18,2},{3,19},{19,3},{4,20},{20... | collective-permute-start | bytes 4616 | tf_op jit(solution)/shard_map/ppermute | solution.py:75
  80.3 5.9 %collective-permute-start.12 = (bf16[16,144,512]{2,1,0:T(8,128)(2,1)}, bf16[16,144,512]{2,1,0:T(8,128)(2,1)}, u32[]{:S(2)}, u32[]{:S(2)}) collective-permute-start(bf16[16,144,512]{2,1,0:T(8,128)(2,1)} %get-tuple-element.100), channel_id=1, source_target_pairs={{0,16},{16,0},{1,17},{17,1},{2,18},{18,2},{3,19},{19,3},{4,20},{20... | collective-permute-start | bytes 7077896 | tf_op jit(solution)/shard_map/ppermute | solution.py:75
  81.6 12.7 %all-to-all-start.2 = ((bf16[8,64,256]{2,1,0:T(8,128)(2,1)}), bf16[8,64,256]{2,1,0:T(8,128)(2,1)S(1)}, u32[]{:S(2)}, u32[]{:S(2)}) async-start(bf16[8,64,256]{2,1,0:T(8,128)(2,1)} %bitcast.5), calls=%async_computation.2 | async-start | bytes 524288 | tf_op jit(solution)/shard_map/all_to_all | solution.py:1177
  85.1 43.3 %reduce-scatter.3.cloned.1.call-start = ((), (), s32[]{:S(2)}) async-start(), calls=%async_computation.7 | async-start | bytes 2621440 | tf_op jit(solution)/shard_map/reduce_scatter | solution.py:1235
  101.2 6.4 %collective-permute-start.13 = (bf16[8,128,256]{2,1,0:T(8,128)(2,1)S(1)}, bf16[8,128,256]{2,1,0:T(8,128)(2,1)S(1)}, u32[]{:S(2)}, u32[]{:S(2)}) collective-permute-start(bf16[8,128,256]{2,1,0:T(8,128)(2,1)S(1)} %get-tuple-element.116), channel_id=1, source_target_pairs={{0,16},{16,0},{1,17},{17,1},{2,18},{18,2},{3,19},{19,3},{4,20},{20... | collective-permute-start | bytes 1572872 | tf_op jit(solution)/shard_map/ppermute | solution.py:75
  108.5 24.6 %all-to-all-start.4 = ((bf16[8,192,256]{2,1,0:T(8,128)(2,1)}), bf16[8,192,256]{2,1,0:T(8,128)(2,1)S(1)}, u32[]{:S(2)}, u32[]{:S(2)}) async-start(bf16[8,192,256]{2,1,0:T(8,128)(2,1)} %pack.1.back_ref), calls=%async_computation.5 | async-start | bytes 1572864 | tf_op jit(solution)/shard_map/all_to_all | solution.py:1177
  112.1 40.2 %reduce-scatter.5.cloned.1.call-start = ((), (), s32[]{:S(2)}) async-start(), calls=%async_computation.8 | async-start | bytes 655360 | tf_op jit(solution)/shard_map/reduce_scatter | solution.py:1257
  115.7 1.5 collective-permute-start.14
  117.3 10.3 %collective-permute-start.15 = (bf16[8,48,256]{2,1,0:T(8,128)(2,1)S(1)}, bf16[8,48,256]{2,1,0:T(8,128)(2,1)S(1)}, u32[]{:S(2)}, u32[]{:S(2)}) collective-permute-start(bf16[8,48,256]{2,1,0:T(8,128)(2,1)S(1)} %get-tuple-element.123), channel_id=1, source_target_pairs={{0,1},{1,0},{2,3},{3,2},{4,5},{5,4},{6,7},{7,6},{8,9},{9,8},{10,11... | collective-permute-start | bytes 589832 | tf_op jit(solution)/shard_map/ppermute | solution.py:75
  133.1 16.5 %all-to-all-start.3 = ((bf16[8,48,256]{2,1,0:T(8,128)(2,1)}), bf16[8,48,256]{2,1,0:T(8,128)(2,1)S(1)}, u32[]{:S(2)}, u32[]{:S(2)}) async-start(bf16[8,48,256]{2,1,0:T(8,128)(2,1)} %merge.1), calls=%async_computation.4 | async-start | bytes 393216 | tf_op jit(solution)/shard_map/all_to_all | solution.py:1177
  136.8 13.8 %collective-permute-start.17 = (bf16[512,512]{1,0:T(8,128)(2,1)S(1)}, bf16[512,512]{1,0:T(8,128)(2,1)S(1)}, u32[]{:S(2)}, u32[]{:S(2)}) collective-permute-start(bf16[512,512]{1,0:T(8,128)(2,1)S(1)} %copy-done.13), channel_id=1, source_target_pairs={{0,0},{1,16},{2,2},{3,18},{4,4},{5,20},{6,6},{7,22},{8,8},{9,24},{... | collective-permute-start | bytes 1572872 | tf_op jit(solution)/shard_map/ppermute | solution.py:1169
  139.7 10.9 %collective-permute-start.16 = (bf16[256,512]{1,0:T(8,128)(2,1)S(1)}, bf16[256,512]{1,0:T(8,128)(2,1)S(1)}, u32[]{:S(2)}, u32[]{:S(2)}) collective-permute-start(bf16[256,512]{1,0:T(8,128)(2,1)S(1)} %last.1), channel_id=1, source_target_pairs={{0,0},{1,16},{2,2},{3,18},{4,4},{5,20},{6,6},{7,22},{8,8},{9,24},{... | collective-permute-start | bytes 786440 | tf_op jit(solution)/shard_map/ppermute | solution.py:1169
  (12 other events, 160.6 us)
Sparse Core Ops, SparseCore 0:
  43.0 36.8 all-gather.2
  94.5 31.2 reduce-scatter.2
  128.5 23.8 reduce-scatter.4

commit v7 on v6

--- a/solution.py
+++ b/solution.py
@@ -11,7 +11,7 @@
 EPS = 1e-05
 LANES = 32
 DOCS = 24
-UNROLL = 4
+UNROLL = 8
 INNER = (0, 1, 3, 2)
 OUTER = (0, 1, 3, 2)
 RING = (0, 2, 4, 6, 7, 5, 3, 1)
@@ -729,20 +729,24 @@
         cols = slice(start, start + tile)
         dz = (dot_t(df_ref[...], wd_ref[start : start + tile, :]) * slope[:, cols]).astype(BF16)
         dz_ref[:, cols] = dz
-        if going is not None:
-            g = dot(xt[...], dz)
+
+    back = 0.0
+    for k in range(blocks):
+        start = k * each
+        if blocks == 2:
+            start = (start + lax.axis_index("dp") * each) % wide
+        cols = pl.ds(pl.multiple_of(start, each), each)
+        back = back + dot_t(dz_ref[:, k * each : (k + 1) * each], wu_ref[:, cols])
+    if going is not None:
+        for start in range(0, wide, tile):
+            g = dot(xt[...], dz_ref[:, start : start + tile])
             base = (start + lax.axis_index("dp") * each) % wide // feat * step
             for flip in (1, 0):
                 half_g = g[flip * (feat // 2) : (flip + 1) * (feat // 2)]
                 put(flip, 0, pl.multiple_of(base, step), step, half_g)
                 send(flip, pl.multiple_of(base, step), step)
-        part = dot_t(dz, weight_up(start))
-        if start:
-            acc[...] += part
-        else:
-            acc[...] = part
-
-    gr, dg1 = norm_back(n1, r1, g1, du + ordered(acc[...]))
+
+    gr, dg1 = norm_back(n1, r1, g1, du + ordered(back))
     gr_ref[...] = gr
     leaving = fetch(
         [gr_ref, out_ref, gy_ref],

time: 161 us -> 161 us (level)
  starting transfers between devices: 41.6 us -> 39.6 us
    ppermute x13, starting transfers between devices: 16.7 us -> 14 us  [swap(): return lax.ppermute(block, axis, [(i, i ^ bit) for i in range(size)])]
  transfers between devices with their start and end apart: 26 -> 26, of which waited for: 14 -> 13; matrix products, arithmetic and copies ran while one was open for 1% -> 1% of each run, Pallas kernels for 32% -> 32%
where the time goes in v7:
time: 161 us; the launch traced here: 160 us
  Pallas kernels  54.5 us (34%)
  waiting for transfers between devices  49.1 us (30%)
  starting transfers between devices  39.6 us (25%)
  between operations  14.2 us (9%)
  local copies, waits for them, and re-layouts  1.9 us (1%)
    all_to_all x5, waiting for transfers between devices, exchange(): lax.all_to_all(block, 'ctx', 0, 0, axis_index_groups=groups, tiled=True)  39.1 us
    all_to_all x5, starting transfers between devices, exchange(): lax.all_to_all(block, 'ctx', 0, 0, axis_index_groups=groups, tiled=True)  21 us
    ppermute x13, starting transfers between devices, swap(): return lax.ppermute(block, axis, [(i, i ^ bit) for i in range(size)])  14 us
    pallas_call x2, Pallas kernels, attend_back(): pl.pallas_call(functools.partial(backward_kernel, ways, slots, final, tex...  13.6 us
    pallas_call x1, Pallas kernels, middle(): pl.pallas_call(functools.partial(middle_kernel, blocks, tile), out_shape=...  10 us
    ppermute x13, waiting for transfers between devices, swap(): return lax.ppermute(block, axis, [(i, i ^ bit) for i in range(size)])  10 us
    pallas_call x1, Pallas kernels, attend(): pl.pallas_call(functools.partial(forward_kernel, ways, len(segs)), out_sh...  7.52 us
    ppermute x5, starting transfers between devices, moved(): return lax.ppermute(block, both, route)  4.44 us
  transfers between devices with their start and end apart: 26, of which 13 were waited for; matrix products, arithmetic and copies ran while one was open for 1% of the time, Pallas kernels for 32%

profile of v7, /device:TPU:0, one launch (start us, length us, event | category | flops | bytes accessed | tf_op | source)
XLA Modules:
  0.0 160.0 jit_solution(8032869077684706369)
XLA Ops:
  7.2 1.7 %collective-permute-start = (bf16[256,512]{1,0:T(8,128)(2,1)}, bf16[256,512]{1,0:T(8,128)(2,1)S(1)}, u32[]{:S(2)}, u32[]{:S(2)}) collective-permute-start(bf16[256,512]{1,0:T(8,128)(2,1)} %bitcast.25), channel_id=1, source_target_pairs={{0,0},{1,16},{2,2},{3,18},{4,4},{5,20},{6,6},{7,22},{8,8},{9,24},{... | collective-permute-start | bytes 786440 | tf_op jit(solution)/shard_map/ppermute | solution.py:1173
  9.0 3.4 %collective-permute-start.1 = (bf16[256,512]{1,0:T(8,128)(2,1)}, bf16[256,512]{1,0:T(8,128)(2,1)S(1)}, u32[]{:S(2)}, u32[]{:S(2)}) collective-permute-start(bf16[256,512]{1,0:T(8,128)(2,1)} %refs_1_.5), channel_id=1, source_target_pairs={{0,16},{16,0},{1,17},{17,1},{2,18},{18,2},{3,19},{19,3},{4,20},{20... | collective-permute-start | bytes 786440 | tf_op jit(solution)/shard_map/ppermute | solution.py:75
  12.9 1.1 stage.3
  14.5 1.6 project.1
  16.1 6.0 %all-to-all-start = ((bf16[8,192,256]{2,1,0:T(8,128)(2,1)}), bf16[8,192,256]{2,1,0:T(8,128)(2,1)S(1)}, u32[]{:S(2)}, u32[]{:S(2)}) async-start(bf16[8,192,256]{2,1,0:T(8,128)(2,1)} %project.1), calls=%async_computation | async-start | bytes 1572864 | tf_op jit(solution)/shard_map/all_to_all | solution.py:1181
  23.3 1.9 %collective-permute-start.4 = (s32[16,256]{1,0:T(8,128)S(1)}, s32[16,256]{1,0:T(8,128)S(1)}, u32[]{:S(2)}, u32[]{:S(2)}) collective-permute-start(s32[16,256]{1,0:T(8,128)S(1)} %reshape.50.refs_0_), channel_id=1, source_target_pairs={{0,16},{16,0},{1,17},{17,1},{2,18},{18,2},{3,19},{19,3},{4,20},{20... | collective-permute-start | bytes 49160 | tf_op jit(solution)/shard_map/ppermute | solution.py:75
  26.1 2.9 %plan.1.plan_ref = s32[872]{0:T(1024)S(1)} custom-call(s32[4096]{0:T(1024)S(1)} %bitcast.18, s32[4096]{0:T(1024)S(1)} %bitcast.19), custom_call_target="tpu_custom_call" | custom-call | flops 1000 | bytes 1024 | tf_op jit(solution)/shard_map/plan/pallas_call | solution.py:234
  29.5 13.3 %all-to-all-done.refs_2_.refs_0_.refs_1_ = bf16[8,192,256]{2,1,0:T(8,128)(2,1)S(1)} async-done(((bf16[8,192,256]{2,1,0:T(8,128)(2,1)}), bf16[8,192,256]{2,1,0:T(8,128)(2,1)S(1)}, u32[]{:S(2)}, u32[]{:S(2)}) %all-to-all-start) | async-done | bytes 786464 | tf_op jit(solution)/shard_map/all_to_all | solution.py:1181
  44.8 1.0 collective-permute-done.6.refs_3_.refs_1_
  45.8 7.5 %attend.1 = (bf16[8,64,256]{2,1,0:T(8,128)(2,1)}, f32[8,64,256]{2,1,0:T(8,128)}, f32[8,256]{1,0:T(8,128)S(1)}) custom-call(s32[872]{0:T(1024)} %copy-done.7, s32[16,256]{1,0:T(8,128)S(1)} %reshape.50.refs_0_, s32[16,256]{1,0:T(8,128)S(1)} %collective-permute-done.4.refs_1_, bf16[8,192,256]{2,1,0:T(8,128)(2,1)S(1)} %all-to-all-done.refs_2_.refs_0_.refs_1_, ...), custom_call_target="tpu_custom_call" | custom-call | flops 1000 | bytes 1024 | tf_op jit(solution)/shard_map/attend/pallas_call | solution.py:358
  53.4 3.7 %all-to-all-start.1 = ((bf16[8,64,256]{2,1,0:T(8,128)(2,1)}), bf16[8,64,256]{2,1,0:T(8,128)(2,1)S(1)}, u32[]{:S(2)}, u32[]{:S(2)}) async-start(bf16[8,64,256]{2,1,0:T(8,128)(2,1)} %get-tuple-element.90), calls=%async_computation.1 | async-start | bytes 524288 | tf_op jit(solution)/shard_map/all_to_all | solution.py:1181
  57.1 1.8 %collective-permute-start.8 = (bf16[256,512]{1,0:T(8,128)(2,1)S(1)}, bf16[256,512]{1,0:T(8,128)(2,1)S(1)}, u32[]{:S(2)}, u32[]{:S(2)}) collective-permute-start(bf16[256,512]{1,0:T(8,128)(2,1)S(1)} %copy-done.9), channel_id=1, source_target_pairs={{0,16},{16,0},{1,17},{17,1},{2,18},{18,2},{3,19},{19,3},{4,20},{20... | collective-permute-start | bytes 786440 | tf_op jit(solution)/shard_map/ppermute | solution.py:75
  60.8 1.1 stage.4
  62.0 7.6 %all-to-all-done.1 = bf16[8,64,256]{2,1,0:T(8,128)(2,1)S(1)} async-done(((bf16[8,64,256]{2,1,0:T(8,128)(2,1)}), bf16[8,64,256]{2,1,0:T(8,128)(2,1)S(1)}, u32[]{:S(2)}, u32[]{:S(2)}) %all-to-all-start.1) | async-done | bytes 262176 | tf_op jit(solution)/shard_map/all_to_all | solution.py:1181
  69.6 10.0 %middle.1 = (bf16[512,512]{1,0:T(8,128)(2,1)}, f32[256,512]{1,0:T(8,128)}, bf16[512,256]{1,0:T(8,128)(2,1)}, f32[8,256]{1,0:T(8,128)S(1)}, bf16[16,144,512]{2,1,0:T(8,128)(2,1)}, /*index=5*/bf16[16,144,512]{2,1,0:T(8,128)(2,1)}) custom-call(bf16[512,256]{1,0:T(8,128)(2,1)S(1)} %bitcast.16, s32[1,256]{1,0:T(1,128)S(1)} %collective-permute-done.5.refs_1_, ...), custom_call_target="tpu_custom_call" | custom-call | flops 1000 | bytes 1024 | tf_op jit(solution)/shard_map/middle/pallas_call | solution.py:784
  80.6 3.4 %all-to-all-start.2 = ((bf16[8,64,256]{2,1,0:T(8,128)(2,1)}), bf16[8,64,256]{2,1,0:T(8,128)(2,1)S(1)}, u32[]{:S(2)}, u32[]{:S(2)}) async-start(bf16[8,64,256]{2,1,0:T(8,128)(2,1)} %bitcast.5), calls=%async_computation.2 | async-start | bytes 524288 | tf_op jit(solution)/shard_map/all_to_all | solution.py:1181
  85.1 4.2 %join.1 = (bf16[16,128,512]{2,1,0:T(8,128)(2,1)}, bf16[16,32,256]{2,1,0:T(8,128)(2,1)S(1)}) custom-call(bf16[16,144,512]{2,1,0:T(8,128)(2,1)} %collective-permute-done.12.two_ref, bf16[16,144,512]{2,1,0:T(8,128)(2,1)} %get-tuple-element.101.one_in), custom_call_target="tpu_custom_call" | custom-call | flops 1000 | bytes 1024 | tf_op jit(solution)/shard_map/join/pallas_call | solution.py:862
  89.3 1.4 prepare.1
  90.6 2.7 %all-to-all-done.2.do_ref = bf16[8,64,256]{2,1,0:T(8,128)(2,1)S(1)} async-done(((bf16[8,64,256]{2,1,0:T(8,128)(2,1)}), bf16[8,64,256]{2,1,0:T(8,128)(2,1)S(1)}, u32[]{:S(2)}, u32[]{:S(2)}) %all-to-all-start.2) | async-done | bytes 262176 | tf_op jit(solution)/shard_map/all_to_all | solution.py:1181
  93.4 7.4 %attend_back.2 = (f32[8,64,256]{2,1,0:T(8,128)S(1)}, bf16[9,256,80]{2,1,0:T(8,128)(2,1)S(1)}, bf16[8,128,256]{2,1,0:T(8,128)(2,1)S(1)}) custom-call(s32[872]{0:T(1024)} %copy-done.7, bf16[16,96,256]{2,1,0:T(8,128)(2,1)S(1)} %get-tuple-element.108.kx, bf16[9,256,96]{2,1,0:T(8,128)(2,1)S(1)} %get-tuple-element.109.qx, ...), custom_call_target="tpu_custom_call" | custom-call | flops 1000 | bytes 1024 | tf_op jit(solution)/shard_map/attend_back/pallas_call | solution.py:522
  100.8 6.3 %attend_back.3 = (bf16[8,64,256]{2,1,0:T(8,128)(2,1)S(1)}, f32[8,128,256]{2,1,0:T(8,128)S(1)}) custom-call(s32[872]{0:T(1024)} %copy-done.7, bf16[16,96,256]{2,1,0:T(8,128)(2,1)S(1)} %get-tuple-element.108.kx, bf16[9,256,96]{2,1,0:T(8,128)(2,1)S(1)} %get-tuple-element.109.qx, bf16[8,64,256]{2,1,0:T(8,128)(2,1)S(1)} %all-to-all-done.2.do_ref, ...), custom_call_target="tpu_custom_call" | custom-call | flops 1000 | bytes 1024 | tf_op jit(solution)/shard_map/attend_back/pallas_call | solution.py:522
  108.1 3.6 %all-to-all-start.4 = ((bf16[8,192,256]{2,1,0:T(8,128)(2,1)}), bf16[8,192,256]{2,1,0:T(8,128)(2,1)S(1)}, u32[]{:S(2)}, u32[]{:S(2)}) async-start(bf16[8,192,256]{2,1,0:T(8,128)(2,1)} %pack.1.back_ref), calls=%async_computation.5 | async-start | bytes 1572864 | tf_op jit(solution)/shard_map/all_to_all | solution.py:1181
  111.7 3.5 %head_grads.1 = (bf16[16,16,256]{2,1,0:T(8,128)(2,1)S(1)}, bf16[16,16,256]{2,1,0:T(8,128)(2,1)S(1)}) custom-call(bf16[8,192,256]{2,1,0:T(8,128)(2,1)} %pack.1.back_ref, bf16[8,256,512]{2,1,0:T(8,128)(2,1)} %bitcast.20, f32[8,256]{1,0:T(8,128)S(1)} %get-tuple-element.118.small_ref), custom_call_target="tpu_custom_call" | custom-call | flops 1000 | bytes 1024 | tf_op jit(solution)/shard_map/head_grads/pallas_call | solution.py:995
  115.2 2.0 %collective-permute-start.14 = (bf16[16,16,256]{2,1,0:T(8,128)(2,1)S(1)}, bf16[16,16,256]{2,1,0:T(8,128)(2,1)S(1)}, u32[]{:S(2)}, u32[]{:S(2)}) collective-permute-start(bf16[16,16,256]{2,1,0:T(8,128)(2,1)S(1)} %get-tuple-element.120), channel_id=1, source_target_pairs={{0,16},{16,0},{1,17},{17,1},{2,18},{18,2},{3,19},{19,3},{4,20},{20... | collective-permute-start | bytes 393224 | tf_op jit(solution)/shard_map/ppermute | solution.py:75
  118.3 2.0 %collective-permute-start.15 = (bf16[8,48,256]{2,1,0:T(8,128)(2,1)S(1)}, bf16[8,48,256]{2,1,0:T(8,128)(2,1)S(1)}, u32[]{:S(2)}, u32[]{:S(2)}) collective-permute-start(bf16[8,48,256]{2,1,0:T(8,128)(2,1)S(1)} %get-tuple-element.123), channel_id=1, source_target_pairs={{0,1},{1,0},{2,3},{3,2},{4,5},{5,4},{6,7},{7,6},{8,9},{9,8},{10,11... | collective-permute-start | bytes 589832 | tf_op jit(solution)/shard_map/ppermute | solution.py:75
  120.3 5.4 %collective-permute-done.15.two_ref = bf16[8,48,256]{2,1,0:T(8,128)(2,1)S(1)} collective-permute-done((bf16[8,48,256]{2,1,0:T(8,128)(2,1)S(1)}, bf16[8,48,256]{2,1,0:T(8,128)(2,1)S(1)}, u32[]{:S(2)}, u32[]{:S(2)}) %collective-permute-start.15) | collective-permute-done | bytes 196640 | tf_op jit(solution)/shard_map/ppermute | solution.py:75
  126.5 6.0 %all-to-all-done.4.back_ref = bf16[8,192,256]{2,1,0:T(8,128)(2,1)S(1)} async-done(((bf16[8,192,256]{2,1,0:T(8,128)(2,1)}), bf16[8,192,256]{2,1,0:T(8,128)(2,1)S(1)}, u32[]{:S(2)}, u32[]{:S(2)}) %all-to-all-start.4) | async-done | bytes 786464 | tf_op jit(solution)/shard_map/all_to_all | solution.py:1181
  132.5 4.3 %all-to-all-start.3 = ((bf16[8,48,256]{2,1,0:T(8,128)(2,1)}), bf16[8,48,256]{2,1,0:T(8,128)(2,1)S(1)}, u32[]{:S(2)}, u32[]{:S(2)}) async-start(bf16[8,48,256]{2,1,0:T(8,128)(2,1)} %merge.1), calls=%async_computation.4 | async-start | bytes 393216 | tf_op jit(solution)/shard_map/all_to_all | solution.py:1181
  137.6 1.6 stage.5
  140.4 9.4 %all-to-all-done.3.pieces_ref = bf16[8,48,256]{2,1,0:T(8,128)(2,1)S(1)} async-done(((bf16[8,48,256]{2,1,0:T(8,128)(2,1)}), bf16[8,48,256]{2,1,0:T(8,128)(2,1)S(1)}, u32[]{:S(2)}, u32[]{:S(2)}) %all-to-all-start.3) | async-done | bytes 196640 | tf_op jit(solution)/shard_map/all_to_all | solution.py:1181
  150.7 1.1 finish.1
  151.8 1.7 %spread.1 = (f32[16,2048]{1,0:T(8,128)}, f32[64,512]{1,0:T(8,128)}) custom-call(bf16[1,128,512]{2,1,0:T(8,128)(2,1)} %reduce-scatter.5.cloned.1.call-done.sums_in, f32[8,128]{1,0:T(8,128)S(1)} %get-tuple-element.128.inverse_ref), custom_call_target="tpu_custom_call" | custom-call | flops 1000 | bytes 1024 | tf_op jit(solution)/shard_map/spread/pallas_call | solution.py:1124
  (87 shorter events, 15.2 us)
Async XLA Ops:
  7.2 6.8 %collective-permute-start = (bf16[256,512]{1,0:T(8,128)(2,1)}, bf16[256,512]{1,0:T(8,128)(2,1)S(1)}, u32[]{:S(2)}, u32[]{:S(2)}) collective-permute-start(bf16[256,512]{1,0:T(8,128)(2,1)} %bitcast.25), channel_id=1, source_target_pairs={{0,0},{1,16},{2,2},{3,18},{4,4},{5,20},{6,6},{7,22},{8,8},{9,24},{... | collective-permute-start | bytes 786440 | tf_op jit(solution)/shard_map/ppermute | solution.py:1173
  9.0 5.1 %collective-permute-start.1 = (bf16[256,512]{1,0:T(8,128)(2,1)}, bf16[256,512]{1,0:T(8,128)(2,1)S(1)}, u32[]{:S(2)}, u32[]{:S(2)}) collective-permute-start(bf16[256,512]{1,0:T(8,128)(2,1)} %refs_1_.5), channel_id=1, source_target_pairs={{0,16},{16,0},{1,17},{17,1},{2,18},{18,2},{3,19},{19,3},{4,20},{20... | collective-permute-start | bytes 786440 | tf_op jit(solution)/shard_map/ppermute | solution.py:75
  12.4 1.7 %collective-permute-start.2 = (bf16[256,512]{1,0:T(8,128)(2,1)}, bf16[256,512]{1,0:T(8,128)(2,1)S(1)}, u32[]{:S(2)}, u32[]{:S(2)}) collective-permute-start(bf16[256,512]{1,0:T(8,128)(2,1)} %refs_3_.1), channel_id=1, source_target_pairs={{0,16},{16,0},{1,17},{17,1},{2,18},{18,2},{3,19},{19,3},{4,20},{20... | collective-permute-start | bytes 786440 | tf_op jit(solution)/shard_map/ppermute | solution.py:75
  12.5 2.0 %collective-permute-start.3 = (bf16[256,512]{1,0:T(8,128)(2,1)}, bf16[256,512]{1,0:T(8,128)(2,1)S(1)}, u32[]{:S(2)}, u32[]{:S(2)}) collective-permute-start(bf16[256,512]{1,0:T(8,128)(2,1)} %refs_5_.1), channel_id=1, source_target_pairs={{0,16},{16,0},{1,17},{17,1},{2,18},{18,2},{3,19},{19,3},{4,20},{20... | collective-permute-start | bytes 786440 | tf_op jit(solution)/shard_map/ppermute | solution.py:75
  16.1 41.1 %copy-start.9 = (bf16[256,512]{1,0:T(8,128)(2,1)S(1)}, bf16[256,512]{1,0:T(8,128)(2,1)}, u32[]{:S(2)}) copy-start(bf16[256,512]{1,0:T(8,128)(2,1)} %refs_1_.4) | copy-start | bytes 786436
  16.1 42.9 %copy-start.15 = (bf16[256]{0:T(256)(128)(2,1)S(1)}, bf16[256]{0:T(256)(128)(2,1)}, u32[]{:S(2)}) copy-start(bf16[256]{0:T(256)(128)(2,1)} %param.25) | copy-start | bytes 1540
  16.1 42.9 %copy-start.16 = (bf16[256]{0:T(256)(128)(2,1)S(1)}, bf16[256]{0:T(256)(128)(2,1)}, u32[]{:S(2)}) copy-start(bf16[256]{0:T(256)(128)(2,1)} %param.26) | copy-start | bytes 1540
  16.1 42.9 %copy-start.17 = (bf16[256]{0:T(256)(128)(2,1)S(1)}, bf16[256]{0:T(256)(128)(2,1)}, u32[]{:S(2)}) copy-start(bf16[256]{0:T(256)(128)(2,1)} %param.27) | copy-start | bytes 1540
  16.1 26.8 %all-to-all-start = ((bf16[8,192,256]{2,1,0:T(8,128)(2,1)}), bf16[8,192,256]{2,1,0:T(8,128)(2,1)S(1)}, u32[]{:S(2)}, u32[]{:S(2)}) async-start(bf16[8,192,256]{2,1,0:T(8,128)(2,1)} %project.1), calls=%async_computation | async-start | bytes 1572864 | tf_op jit(solution)/shard_map/all_to_all | solution.py:1181
  22.1 71.3 %all-gather.3.cloned.1.call-start = ((), (), s32[]{:S(2)}) async-start(), calls=%async_computation.9 | async-start | bytes 2359296 | tf_op jit(solution)/shard_map/all_gather | solution.py:1230
  23.3 2.7 %collective-permute-start.4 = (s32[16,256]{1,0:T(8,128)S(1)}, s32[16,256]{1,0:T(8,128)S(1)}, u32[]{:S(2)}, u32[]{:S(2)}) collective-permute-start(s32[16,256]{1,0:T(8,128)S(1)} %reshape.50.refs_0_), channel_id=1, source_target_pairs={{0,16},{16,0},{1,17},{17,1},{2,18},{18,2},{3,19},{19,3},{4,20},{20... | collective-permute-start | bytes 49160 | tf_op jit(solution)/shard_map/ppermute | solution.py:75
  25.2 4.3 %collective-permute-start.5 = (s32[1,256]{1,0:T(1,128)S(1)}, s32[1,256]{1,0:T(1,128)S(1)}, u32[]{:S(2)}, u32[]{:S(2)}) collective-permute-start(s32[1,256]{1,0:T(1,128)S(1)} %copy-done.14), channel_id=1, source_target_pairs={{0,0},{1,16},{2,2},{3,18},{4,4},{5,20},{6,6},{7,22},{8,8},{9,24},{... | collective-permute-start | bytes 3080 | tf_op jit(solution)/shard_map/ppermute | solution.py:1173
  42.8 36.8 %copy-start = (bf16[8,192,256]{2,1,0:T(8,128)(2,1)}, bf16[8,192,256]{2,1,0:T(8,128)(2,1)S(1)}, u32[]{:S(2)}) copy-start(bf16[8,192,256]{2,1,0:T(8,128)(2,1)S(1)} %all-to-all-done.refs_2_.refs_0_.refs_1_) | copy-start | bytes 2359300
  42.9 3.0 %collective-permute-start.6 = (bf16[8,192,256]{2,1,0:T(8,128)(2,1)S(1)}, bf16[8,192,256]{2,1,0:T(8,128)(2,1)S(1)}, u32[]{:S(2)}, u32[]{:S(2)}) collective-permute-start(bf16[8,192,256]{2,1,0:T(8,128)(2,1)S(1)} %all-to-all-done.refs_2_.refs_0_.refs_1_), channel_id=1, source_target_pairs={{0,16},{16,0},{1,17},{17,1},{2,18},{18,2},{3,19},{19,3},{4,20},{20... | collective-permute-start | bytes 2359304 | tf_op jit(solution)/shard_map/ppermute | solution.py:75
  43.6 26.0 %collective-permute-start.10 = (bf16[256,2048]{1,0:T(8,128)(2,1)}, bf16[256,2048]{1,0:T(8,128)(2,1)}, u32[]{:S(2)}, u32[]{:S(2)}) collective-permute-start(bf16[256,2048]{1,0:T(8,128)(2,1)} %refs_7_.1), channel_id=1, source_target_pairs={{0,16},{16,0},{1,17},{17,1},{2,18},{18,2},{3,19},{19,3},{4,20},{20... | collective-permute-start | bytes 3145736 | tf_op jit(solution)/shard_map/ppermute | solution.py:75
  43.7 25.9 %collective-permute-start.11 = (bf16[1024,512]{1,0:T(8,128)(2,1)}, bf16[1024,512]{1,0:T(8,128)(2,1)}, u32[]{:S(2)}, u32[]{:S(2)}) collective-permute-start(bf16[1024,512]{1,0:T(8,128)(2,1)} %refs_9_.1), channel_id=1, source_target_pairs={{0,16},{16,0},{1,17},{17,1},{2,18},{18,2},{3,19},{19,3},{4,20},{20... | collective-permute-start | bytes 3145736 | tf_op jit(solution)/shard_map/ppermute | solution.py:75
  44.1 9.3 %collective-permute-start.7 = (bf16[512,512]{1,0:T(8,128)(2,1)S(1)}, bf16[512,512]{1,0:T(8,128)(2,1)S(1)}, u32[]{:S(2)}, u32[]{:S(2)}) collective-permute-start(bf16[512,512]{1,0:T(8,128)(2,1)S(1)} %pad_maximum_fusion), channel_id=1, source_target_pairs={{0,0},{1,16},{2,2},{3,18},{4,4},{5,20},{6,6},{7,22},{8,8},{9,24},{... | collective-permute-start | bytes 1572872 | tf_op jit(solution)/shard_map/ppermute | solution.py:1173
  45.8 33.8 %copy-start.1 = (bf16[8,192,256]{2,1,0:T(8,128)(2,1)}, bf16[8,192,256]{2,1,0:T(8,128)(2,1)S(1)}, u32[]{:S(2)}) copy-start(bf16[8,192,256]{2,1,0:T(8,128)(2,1)S(1)} %collective-permute-done.6.refs_3_.refs_1_) | copy-start | bytes 2359300
  53.4 16.2 %all-to-all-start.1 = ((bf16[8,64,256]{2,1,0:T(8,128)(2,1)}), bf16[8,64,256]{2,1,0:T(8,128)(2,1)S(1)}, u32[]{:S(2)}, u32[]{:S(2)}) async-start(bf16[8,64,256]{2,1,0:T(8,128)(2,1)} %get-tuple-element.90), calls=%async_computation.1 | async-start | bytes 524288 | tf_op jit(solution)/shard_map/all_to_all | solution.py:1181
  57.1 3.0 %collective-permute-start.8 = (bf16[256,512]{1,0:T(8,128)(2,1)S(1)}, bf16[256,512]{1,0:T(8,128)(2,1)S(1)}, u32[]{:S(2)}, u32[]{:S(2)}) collective-permute-start(bf16[256,512]{1,0:T(8,128)(2,1)S(1)} %copy-done.9), channel_id=1, source_target_pairs={{0,16},{16,0},{1,17},{17,1},{2,18},{18,2},{3,19},{19,3},{4,20},{20... | collective-permute-start | bytes 786440 | tf_op jit(solution)/shard_map/ppermute | solution.py:75
  59.0 10.6 %collective-permute-start.9 = (bf16[3,256]{1,0:T(4,128)(2,1)S(1)}, bf16[3,256]{1,0:T(4,128)(2,1)S(1)}, u32[]{:S(2)}, u32[]{:S(2)}) collective-permute-start(bf16[3,256]{1,0:T(4,128)(2,1)S(1)} %pad_maximum_fusion.1.refs_2_), channel_id=1, source_target_pairs={{0,16},{16,0},{1,17},{17,1},{2,18},{18,2},{3,19},{19,3},{4,20},{20... | collective-permute-start | bytes 4616 | tf_op jit(solution)/shard_map/ppermute | solution.py:75
  79.7 5.4 %collective-permute-start.12 = (bf16[16,144,512]{2,1,0:T(8,128)(2,1)}, bf16[16,144,512]{2,1,0:T(8,128)(2,1)}, u32[]{:S(2)}, u32[]{:S(2)}) collective-permute-start(bf16[16,144,512]{2,1,0:T(8,128)(2,1)} %get-tuple-element.100), channel_id=1, source_target_pairs={{0,16},{16,0},{1,17},{17,1},{2,18},{18,2},{3,19},{19,3},{4,20},{20... | collective-permute-start | bytes 7077896 | tf_op jit(solution)/shard_map/ppermute | solution.py:75
  80.6 12.8 %all-to-all-start.2 = ((bf16[8,64,256]{2,1,0:T(8,128)(2,1)}), bf16[8,64,256]{2,1,0:T(8,128)(2,1)S(1)}, u32[]{:S(2)}, u32[]{:S(2)}) async-start(bf16[8,64,256]{2,1,0:T(8,128)(2,1)} %bitcast.5), calls=%async_computation.2 | async-start | bytes 524288 | tf_op jit(solution)/shard_map/all_to_all | solution.py:1181
  84.0 42.4 %reduce-scatter.3.cloned.1.call-start = ((), (), s32[]{:S(2)}) async-start(), calls=%async_computation.7 | async-start | bytes 2621440 | tf_op jit(solution)/shard_map/reduce_scatter | solution.py:1239
  100.7 6.3 %collective-permute-start.13 = (bf16[8,128,256]{2,1,0:T(8,128)(2,1)S(1)}, bf16[8,128,256]{2,1,0:T(8,128)(2,1)S(1)}, u32[]{:S(2)}, u32[]{:S(2)}) collective-permute-start(bf16[8,128,256]{2,1,0:T(8,128)(2,1)S(1)} %get-tuple-element.116), channel_id=1, source_target_pairs={{0,16},{16,0},{1,17},{17,1},{2,18},{18,2},{3,19},{19,3},{4,20},{20... | collective-permute-start | bytes 1572872 | tf_op jit(solution)/shard_map/ppermute | solution.py:75
  108.1 24.4 %all-to-all-start.4 = ((bf16[8,192,256]{2,1,0:T(8,128)(2,1)}), bf16[8,192,256]{2,1,0:T(8,128)(2,1)S(1)}, u32[]{:S(2)}, u32[]{:S(2)}) async-start(bf16[8,192,256]{2,1,0:T(8,128)(2,1)} %pack.1.back_ref), calls=%async_computation.5 | async-start | bytes 1572864 | tf_op jit(solution)/shard_map/all_to_all | solution.py:1181
  111.7 40.1 %reduce-scatter.5.cloned.1.call-start = ((), (), s32[]{:S(2)}) async-start(), calls=%async_computation.8 | async-start | bytes 655360 | tf_op jit(solution)/shard_map/reduce_scatter | solution.py:1261
  115.2 2.9 %collective-permute-start.14 = (bf16[16,16,256]{2,1,0:T(8,128)(2,1)S(1)}, bf16[16,16,256]{2,1,0:T(8,128)(2,1)S(1)}, u32[]{:S(2)}, u32[]{:S(2)}) collective-permute-start(bf16[16,16,256]{2,1,0:T(8,128)(2,1)S(1)} %get-tuple-element.120), channel_id=1, source_target_pairs={{0,16},{16,0},{1,17},{17,1},{2,18},{18,2},{3,19},{19,3},{4,20},{20... | collective-permute-start | bytes 393224 | tf_op jit(solution)/shard_map/ppermute | solution.py:75
  118.3 7.4 %collective-permute-start.15 = (bf16[8,48,256]{2,1,0:T(8,128)(2,1)S(1)}, bf16[8,48,256]{2,1,0:T(8,128)(2,1)S(1)}, u32[]{:S(2)}, u32[]{:S(2)}) collective-permute-start(bf16[8,48,256]{2,1,0:T(8,128)(2,1)S(1)} %get-tuple-element.123), channel_id=1, source_target_pairs={{0,1},{1,0},{2,3},{3,2},{4,5},{5,4},{6,7},{7,6},{8,9},{9,8},{10,11... | collective-permute-start | bytes 589832 | tf_op jit(solution)/shard_map/ppermute | solution.py:75
  132.5 17.3 %all-to-all-start.3 = ((bf16[8,48,256]{2,1,0:T(8,128)(2,1)}), bf16[8,48,256]{2,1,0:T(8,128)(2,1)S(1)}, u32[]{:S(2)}, u32[]{:S(2)}) async-start(bf16[8,48,256]{2,1,0:T(8,128)(2,1)} %merge.1), calls=%async_computation.4 | async-start | bytes 393216 | tf_op jit(solution)/shard_map/all_to_all | solution.py:1181
  136.9 13.9 %collective-permute-start.17 = (bf16[512,512]{1,0:T(8,128)(2,1)S(1)}, bf16[512,512]{1,0:T(8,128)(2,1)S(1)}, u32[]{:S(2)}, u32[]{:S(2)}) collective-permute-start(bf16[512,512]{1,0:T(8,128)(2,1)S(1)} %copy-done.13), channel_id=1, source_target_pairs={{0,0},{1,16},{2,2},{3,18},{4,4},{5,20},{6,6},{7,22},{8,8},{9,24},{... | collective-permute-start | bytes 1572872 | tf_op jit(solution)/shard_map/ppermute | solution.py:1173
  139.7 11.0 %collective-permute-start.16 = (bf16[256,512]{1,0:T(8,128)(2,1)S(1)}, bf16[256,512]{1,0:T(8,128)(2,1)S(1)}, u32[]{:S(2)}, u32[]{:S(2)}) collective-permute-start(bf16[256,512]{1,0:T(8,128)(2,1)S(1)} %last.1), channel_id=1, source_target_pairs={{0,0},{1,16},{2,2},{3,18},{4,4},{5,20},{6,6},{7,22},{8,8},{9,24},{... | collective-permute-start | bytes 786440 | tf_op jit(solution)/shard_map/ppermute | solution.py:1173
  (12 other events, 160.6 us)
Sparse Core Ops, SparseCore 0:
  43.0 36.5 all-gather.2
  93.5 31.2 reduce-scatter.2
  127.2 24.1 reduce-scatter.4

commit v8 on v7

--- a/solution.py
+++ b/solution.py
@@ -13,7 +13,7 @@
 DOCS = 24
 UNROLL = 8
 INNER = (0, 1, 3, 2)
-OUTER = (0, 1, 3, 2)
+OUTER = (0, 1, 2, 3)
 RING = (0, 2, 4, 6, 7, 5, 3, 1)
 GROUP = 8
 GROUP_BACK = 4

time: 161 us -> 161 us (level)
  no operation moved by 1% of the time
where the time goes in v8:
time: 161 us; the launch traced here: 160 us
  Pallas kernels  54.5 us (34%)
  waiting for transfers between devices  49.4 us (31%)
  starting transfers between devices  39.6 us (25%)
  between operations  14.2 us (9%)
  local copies, waits for them, and re-layouts  1.9 us (1%)
    all_to_all x5, waiting for transfers between devices, exchange(): lax.all_to_all(block, 'ctx', 0, 0, axis_index_groups=groups, tiled=True)  39.4 us
    all_to_all x5, starting transfers between devices, exchange(): lax.all_to_all(block, 'ctx', 0, 0, axis_index_groups=groups, tiled=True)  21 us
    ppermute x13, starting transfers between devices, swap(): return lax.ppermute(block, axis, [(i, i ^ bit) for i in range(size)])  14 us
    pallas_call x2, Pallas kernels, attend_back(): pl.pallas_call(functools.partial(backward_kernel, ways, slots, final, tex...  13.6 us
    pallas_call x1, Pallas kernels, middle(): pl.pallas_call(functools.partial(middle_kernel, blocks, tile), out_shape=...  10 us
    ppermute x13, waiting for transfers between devices, swap(): return lax.ppermute(block, axis, [(i, i ^ bit) for i in range(size)])  10 us
    pallas_call x1, Pallas kernels, attend(): pl.pallas_call(functools.partial(forward_kernel, ways, len(segs)), out_sh...  7.52 us
    ppermute x5, starting transfers between devices, moved(): return lax.ppermute(block, both, route)  4.44 us
  transfers between devices with their start and end apart: 26, of which 13 were waited for; matrix products, arithmetic and copies ran while one was open for 1% of the time, Pallas kernels for 32%

profile of v8, /device:TPU:0, one launch (start us, length us, event | category | flops | bytes accessed | tf_op | source)
XLA Modules:
  0.0 160.3 jit_solution(11088417026998132584)
XLA Ops:
  7.2 1.7 %collective-permute-start = (bf16[256,512]{1,0:T(8,128)(2,1)}, bf16[256,512]{1,0:T(8,128)(2,1)S(1)}, u32[]{:S(2)}, u32[]{:S(2)}) collective-permute-start(bf16[256,512]{1,0:T(8,128)(2,1)} %bitcast.25), channel_id=1, source_target_pairs={{0,0},{1,16},{2,2},{3,18},{4,4},{5,20},{6,6},{7,22},{8,8},{9,24},{... | collective-permute-start | bytes 786440 | tf_op jit(solution)/shard_map/ppermute | solution.py:1173
  9.0 3.4 %collective-permute-start.1 = (bf16[256,512]{1,0:T(8,128)(2,1)}, bf16[256,512]{1,0:T(8,128)(2,1)S(1)}, u32[]{:S(2)}, u32[]{:S(2)}) collective-permute-start(bf16[256,512]{1,0:T(8,128)(2,1)} %refs_1_.5), channel_id=1, source_target_pairs={{0,16},{16,0},{1,17},{17,1},{2,18},{18,2},{3,19},{19,3},{4,20},{20... | collective-permute-start | bytes 786440 | tf_op jit(solution)/shard_map/ppermute | solution.py:75
  12.9 1.1 stage.3
  14.5 1.6 project.1
  16.1 6.0 %all-to-all-start = ((bf16[8,192,256]{2,1,0:T(8,128)(2,1)}), bf16[8,192,256]{2,1,0:T(8,128)(2,1)S(1)}, u32[]{:S(2)}, u32[]{:S(2)}) async-start(bf16[8,192,256]{2,1,0:T(8,128)(2,1)} %project.1), calls=%async_computation | async-start | bytes 1572864 | tf_op jit(solution)/shard_map/all_to_all | solution.py:1181
  23.3 1.9 %collective-permute-start.4 = (s32[16,256]{1,0:T(8,128)S(1)}, s32[16,256]{1,0:T(8,128)S(1)}, u32[]{:S(2)}, u32[]{:S(2)}) collective-permute-start(s32[16,256]{1,0:T(8,128)S(1)} %reshape.50.refs_0_), channel_id=1, source_target_pairs={{0,16},{16,0},{1,17},{17,1},{2,18},{18,2},{3,19},{19,3},{4,20},{20... | collective-permute-start | bytes 49160 | tf_op jit(solution)/shard_map/ppermute | solution.py:75
  26.1 2.8 %plan.1.plan_ref = s32[872]{0:T(1024)S(1)} custom-call(s32[4096]{0:T(1024)S(1)} %bitcast.18, s32[4096]{0:T(1024)S(1)} %bitcast.19), custom_call_target="tpu_custom_call" | custom-call | flops 1000 | bytes 1024 | tf_op jit(solution)/shard_map/plan/pallas_call | solution.py:234
  29.5 13.3 %all-to-all-done.refs_2_.refs_0_.refs_1_ = bf16[8,192,256]{2,1,0:T(8,128)(2,1)S(1)} async-done(((bf16[8,192,256]{2,1,0:T(8,128)(2,1)}), bf16[8,192,256]{2,1,0:T(8,128)(2,1)S(1)}, u32[]{:S(2)}, u32[]{:S(2)}) %all-to-all-start) | async-done | bytes 786464 | tf_op jit(solution)/shard_map/all_to_all | solution.py:1181
  44.8 1.0 collective-permute-done.6.refs_3_.refs_1_
  45.8 7.5 %attend.1 = (bf16[8,64,256]{2,1,0:T(8,128)(2,1)}, f32[8,64,256]{2,1,0:T(8,128)}, f32[8,256]{1,0:T(8,128)S(1)}) custom-call(s32[872]{0:T(1024)} %copy-done.7, s32[16,256]{1,0:T(8,128)S(1)} %reshape.50.refs_0_, s32[16,256]{1,0:T(8,128)S(1)} %collective-permute-done.4.refs_1_, bf16[8,192,256]{2,1,0:T(8,128)(2,1)S(1)} %all-to-all-done.refs_2_.refs_0_.refs_1_, ...), custom_call_target="tpu_custom_call" | custom-call | flops 1000 | bytes 1024 | tf_op jit(solution)/shard_map/attend/pallas_call | solution.py:358
  53.4 3.7 %all-to-all-start.1 = ((bf16[8,64,256]{2,1,0:T(8,128)(2,1)}), bf16[8,64,256]{2,1,0:T(8,128)(2,1)S(1)}, u32[]{:S(2)}, u32[]{:S(2)}) async-start(bf16[8,64,256]{2,1,0:T(8,128)(2,1)} %get-tuple-element.90), calls=%async_computation.1 | async-start | bytes 524288 | tf_op jit(solution)/shard_map/all_to_all | solution.py:1181
  57.1 1.8 %collective-permute-start.8 = (bf16[256,512]{1,0:T(8,128)(2,1)S(1)}, bf16[256,512]{1,0:T(8,128)(2,1)S(1)}, u32[]{:S(2)}, u32[]{:S(2)}) collective-permute-start(bf16[256,512]{1,0:T(8,128)(2,1)S(1)} %copy-done.9), channel_id=1, source_target_pairs={{0,16},{16,0},{1,17},{17,1},{2,18},{18,2},{3,19},{19,3},{4,20},{20... | collective-permute-start | bytes 786440 | tf_op jit(solution)/shard_map/ppermute | solution.py:75
  60.8 1.1 stage.4
  62.0 7.6 %all-to-all-done.1 = bf16[8,64,256]{2,1,0:T(8,128)(2,1)S(1)} async-done(((bf16[8,64,256]{2,1,0:T(8,128)(2,1)}), bf16[8,64,256]{2,1,0:T(8,128)(2,1)S(1)}, u32[]{:S(2)}, u32[]{:S(2)}) %all-to-all-start.1) | async-done | bytes 262176 | tf_op jit(solution)/shard_map/all_to_all | solution.py:1181
  69.6 10.0 %middle.1 = (bf16[512,512]{1,0:T(8,128)(2,1)}, f32[256,512]{1,0:T(8,128)}, bf16[512,256]{1,0:T(8,128)(2,1)}, f32[8,256]{1,0:T(8,128)S(1)}, bf16[16,144,512]{2,1,0:T(8,128)(2,1)}, /*index=5*/bf16[16,144,512]{2,1,0:T(8,128)(2,1)}) custom-call(bf16[512,256]{1,0:T(8,128)(2,1)S(1)} %bitcast.16, s32[1,256]{1,0:T(1,128)S(1)} %collective-permute-done.5.refs_1_, ...), custom_call_target="tpu_custom_call" | custom-call | flops 1000 | bytes 1024 | tf_op jit(solution)/shard_map/middle/pallas_call | solution.py:784
  80.6 3.4 %all-to-all-start.2 = ((bf16[8,64,256]{2,1,0:T(8,128)(2,1)}), bf16[8,64,256]{2,1,0:T(8,128)(2,1)S(1)}, u32[]{:S(2)}, u32[]{:S(2)}) async-start(bf16[8,64,256]{2,1,0:T(8,128)(2,1)} %bitcast.5), calls=%async_computation.2 | async-start | bytes 524288 | tf_op jit(solution)/shard_map/all_to_all | solution.py:1181
  85.1 4.2 %join.1 = (bf16[16,128,512]{2,1,0:T(8,128)(2,1)}, bf16[16,32,256]{2,1,0:T(8,128)(2,1)S(1)}) custom-call(bf16[16,144,512]{2,1,0:T(8,128)(2,1)} %collective-permute-done.12.two_ref, bf16[16,144,512]{2,1,0:T(8,128)(2,1)} %get-tuple-element.101.one_in), custom_call_target="tpu_custom_call" | custom-call | flops 1000 | bytes 1024 | tf_op jit(solution)/shard_map/join/pallas_call | solution.py:862
  89.3 1.4 prepare.1
  90.7 2.7 %all-to-all-done.2.do_ref = bf16[8,64,256]{2,1,0:T(8,128)(2,1)S(1)} async-done(((bf16[8,64,256]{2,1,0:T(8,128)(2,1)}), bf16[8,64,256]{2,1,0:T(8,128)(2,1)S(1)}, u32[]{:S(2)}, u32[]{:S(2)}) %all-to-all-start.2) | async-done | bytes 262176 | tf_op jit(solution)/shard_map/all_to_all | solution.py:1181
  93.4 7.4 %attend_back.2 = (f32[8,64,256]{2,1,0:T(8,128)S(1)}, bf16[9,256,80]{2,1,0:T(8,128)(2,1)S(1)}, bf16[8,128,256]{2,1,0:T(8,128)(2,1)S(1)}) custom-call(s32[872]{0:T(1024)} %copy-done.7, bf16[16,96,256]{2,1,0:T(8,128)(2,1)S(1)} %get-tuple-element.108.kx, bf16[9,256,96]{2,1,0:T(8,128)(2,1)S(1)} %get-tuple-element.109.qx, ...), custom_call_target="tpu_custom_call" | custom-call | flops 1000 | bytes 1024 | tf_op jit(solution)/shard_map/attend_back/pallas_call | solution.py:522
  100.8 6.3 %attend_back.3 = (bf16[8,64,256]{2,1,0:T(8,128)(2,1)S(1)}, f32[8,128,256]{2,1,0:T(8,128)S(1)}) custom-call(s32[872]{0:T(1024)} %copy-done.7, bf16[16,96,256]{2,1,0:T(8,128)(2,1)S(1)} %get-tuple-element.108.kx, bf16[9,256,96]{2,1,0:T(8,128)(2,1)S(1)} %get-tuple-element.109.qx, bf16[8,64,256]{2,1,0:T(8,128)(2,1)S(1)} %all-to-all-done.2.do_ref, ...), custom_call_target="tpu_custom_call" | custom-call | flops 1000 | bytes 1024 | tf_op jit(solution)/shard_map/attend_back/pallas_call | solution.py:522
  108.1 3.6 %all-to-all-start.4 = ((bf16[8,192,256]{2,1,0:T(8,128)(2,1)}), bf16[8,192,256]{2,1,0:T(8,128)(2,1)S(1)}, u32[]{:S(2)}, u32[]{:S(2)}) async-start(bf16[8,192,256]{2,1,0:T(8,128)(2,1)} %pack.1.back_ref), calls=%async_computation.5 | async-start | bytes 1572864 | tf_op jit(solution)/shard_map/all_to_all | solution.py:1181
  111.7 3.5 %head_grads.1 = (bf16[16,16,256]{2,1,0:T(8,128)(2,1)S(1)}, bf16[16,16,256]{2,1,0:T(8,128)(2,1)S(1)}) custom-call(bf16[8,192,256]{2,1,0:T(8,128)(2,1)} %pack.1.back_ref, bf16[8,256,512]{2,1,0:T(8,128)(2,1)} %bitcast.20, f32[8,256]{1,0:T(8,128)S(1)} %get-tuple-element.118.small_ref), custom_call_target="tpu_custom_call" | custom-call | flops 1000 | bytes 1024 | tf_op jit(solution)/shard_map/head_grads/pallas_call | solution.py:995
  115.2 2.0 %collective-permute-start.14 = (bf16[16,16,256]{2,1,0:T(8,128)(2,1)S(1)}, bf16[16,16,256]{2,1,0:T(8,128)(2,1)S(1)}, u32[]{:S(2)}, u32[]{:S(2)}) collective-permute-start(bf16[16,16,256]{2,1,0:T(8,128)(2,1)S(1)} %get-tuple-element.120), channel_id=1, source_target_pairs={{0,16},{16,0},{1,17},{17,1},{2,18},{18,2},{3,19},{19,3},{4,20},{20... | collective-permute-start | bytes 393224 | tf_op jit(solution)/shard_map/ppermute | solution.py:75
  118.3 2.0 %collective-permute-start.15 = (bf16[8,48,256]{2,1,0:T(8,128)(2,1)S(1)}, bf16[8,48,256]{2,1,0:T(8,128)(2,1)S(1)}, u32[]{:S(2)}, u32[]{:S(2)}) collective-permute-start(bf16[8,48,256]{2,1,0:T(8,128)(2,1)S(1)} %get-tuple-element.123), channel_id=1, source_target_pairs={{0,1},{1,0},{2,3},{3,2},{4,5},{5,4},{6,7},{7,6},{8,9},{9,8},{10,11... | collective-permute-start | bytes 589832 | tf_op jit(solution)/shard_map/ppermute | solution.py:75
  120.3 5.4 %collective-permute-done.15.two_ref = bf16[8,48,256]{2,1,0:T(8,128)(2,1)S(1)} collective-permute-done((bf16[8,48,256]{2,1,0:T(8,128)(2,1)S(1)}, bf16[8,48,256]{2,1,0:T(8,128)(2,1)S(1)}, u32[]{:S(2)}, u32[]{:S(2)}) %collective-permute-start.15) | collective-permute-done | bytes 196640 | tf_op jit(solution)/shard_map/ppermute | solution.py:75
  126.5 6.0 %all-to-all-done.4.back_ref = bf16[8,192,256]{2,1,0:T(8,128)(2,1)S(1)} async-done(((bf16[8,192,256]{2,1,0:T(8,128)(2,1)}), bf16[8,192,256]{2,1,0:T(8,128)(2,1)S(1)}, u32[]{:S(2)}, u32[]{:S(2)}) %all-to-all-start.4) | async-done | bytes 786464 | tf_op jit(solution)/shard_map/all_to_all | solution.py:1181
  132.5 4.3 %all-to-all-start.3 = ((bf16[8,48,256]{2,1,0:T(8,128)(2,1)}), bf16[8,48,256]{2,1,0:T(8,128)(2,1)S(1)}, u32[]{:S(2)}, u32[]{:S(2)}) async-start(bf16[8,48,256]{2,1,0:T(8,128)(2,1)} %merge.1), calls=%async_computation.4 | async-start | bytes 393216 | tf_op jit(solution)/shard_map/all_to_all | solution.py:1181
  137.6 1.6 stage.5
  140.4 9.7 %all-to-all-done.3.pieces_ref = bf16[8,48,256]{2,1,0:T(8,128)(2,1)S(1)} async-done(((bf16[8,48,256]{2,1,0:T(8,128)(2,1)}), bf16[8,48,256]{2,1,0:T(8,128)(2,1)S(1)}, u32[]{:S(2)}, u32[]{:S(2)}) %all-to-all-start.3) | async-done | bytes 196640 | tf_op jit(solution)/shard_map/all_to_all | solution.py:1181
  151.0 1.1 finish.1
  152.1 1.7 %spread.1 = (f32[16,2048]{1,0:T(8,128)}, f32[64,512]{1,0:T(8,128)}) custom-call(bf16[1,128,512]{2,1,0:T(8,128)(2,1)} %reduce-scatter.5.cloned.1.call-done.sums_in, f32[8,128]{1,0:T(8,128)S(1)} %get-tuple-element.128.inverse_ref), custom_call_target="tpu_custom_call" | custom-call | flops 1000 | bytes 1024 | tf_op jit(solution)/shard_map/spread/pallas_call | solution.py:1124
  (87 shorter events, 15.2 us)
Async XLA Ops:
  7.2 6.8 %collective-permute-start = (bf16[256,512]{1,0:T(8,128)(2,1)}, bf16[256,512]{1,0:T(8,128)(2,1)S(1)}, u32[]{:S(2)}, u32[]{:S(2)}) collective-permute-start(bf16[256,512]{1,0:T(8,128)(2,1)} %bitcast.25), channel_id=1, source_target_pairs={{0,0},{1,16},{2,2},{3,18},{4,4},{5,20},{6,6},{7,22},{8,8},{9,24},{... | collective-permute-start | bytes 786440 | tf_op jit(solution)/shard_map/ppermute | solution.py:1173
  9.0 5.1 %collective-permute-start.1 = (bf16[256,512]{1,0:T(8,128)(2,1)}, bf16[256,512]{1,0:T(8,128)(2,1)S(1)}, u32[]{:S(2)}, u32[]{:S(2)}) collective-permute-start(bf16[256,512]{1,0:T(8,128)(2,1)} %refs_1_.5), channel_id=1, source_target_pairs={{0,16},{16,0},{1,17},{17,1},{2,18},{18,2},{3,19},{19,3},{4,20},{20... | collective-permute-start | bytes 786440 | tf_op jit(solution)/shard_map/ppermute | solution.py:75
  12.4 1.7 %collective-permute-start.2 = (bf16[256,512]{1,0:T(8,128)(2,1)}, bf16[256,512]{1,0:T(8,128)(2,1)S(1)}, u32[]{:S(2)}, u32[]{:S(2)}) collective-permute-start(bf16[256,512]{1,0:T(8,128)(2,1)} %refs_3_.1), channel_id=1, source_target_pairs={{0,16},{16,0},{1,17},{17,1},{2,18},{18,2},{3,19},{19,3},{4,20},{20... | collective-permute-start | bytes 786440 | tf_op jit(solution)/shard_map/ppermute | solution.py:75
  12.5 2.0 %collective-permute-start.3 = (bf16[256,512]{1,0:T(8,128)(2,1)}, bf16[256,512]{1,0:T(8,128)(2,1)S(1)}, u32[]{:S(2)}, u32[]{:S(2)}) collective-permute-start(bf16[256,512]{1,0:T(8,128)(2,1)} %refs_5_.1), channel_id=1, source_target_pairs={{0,16},{16,0},{1,17},{17,1},{2,18},{18,2},{3,19},{19,3},{4,20},{20... | collective-permute-start | bytes 786440 | tf_op jit(solution)/shard_map/ppermute | solution.py:75
  16.1 41.1 %copy-start.9 = (bf16[256,512]{1,0:T(8,128)(2,1)S(1)}, bf16[256,512]{1,0:T(8,128)(2,1)}, u32[]{:S(2)}) copy-start(bf16[256,512]{1,0:T(8,128)(2,1)} %refs_1_.4) | copy-start | bytes 786436
  16.1 42.9 %copy-start.15 = (bf16[256]{0:T(256)(128)(2,1)S(1)}, bf16[256]{0:T(256)(128)(2,1)}, u32[]{:S(2)}) copy-start(bf16[256]{0:T(256)(128)(2,1)} %param.25) | copy-start | bytes 1540
  16.1 42.9 %copy-start.16 = (bf16[256]{0:T(256)(128)(2,1)S(1)}, bf16[256]{0:T(256)(128)(2,1)}, u32[]{:S(2)}) copy-start(bf16[256]{0:T(256)(128)(2,1)} %param.26) | copy-start | bytes 1540
  16.1 42.9 %copy-start.17 = (bf16[256]{0:T(256)(128)(2,1)S(1)}, bf16[256]{0:T(256)(128)(2,1)}, u32[]{:S(2)}) copy-start(bf16[256]{0:T(256)(128)(2,1)} %param.27) | copy-start | bytes 1540
  16.1 26.8 %all-to-all-start = ((bf16[8,192,256]{2,1,0:T(8,128)(2,1)}), bf16[8,192,256]{2,1,0:T(8,128)(2,1)S(1)}, u32[]{:S(2)}, u32[]{:S(2)}) async-start(bf16[8,192,256]{2,1,0:T(8,128)(2,1)} %project.1), calls=%async_computation | async-start | bytes 1572864 | tf_op jit(solution)/shard_map/all_to_all | solution.py:1181
  22.1 71.3 %all-gather.3.cloned.1.call-start = ((), (), s32[]{:S(2)}) async-start(), calls=%async_computation.9 | async-start | bytes 2359296 | tf_op jit(solution)/shard_map/all_gather | solution.py:1230
  23.3 2.7 %collective-permute-start.4 = (s32[16,256]{1,0:T(8,128)S(1)}, s32[16,256]{1,0:T(8,128)S(1)}, u32[]{:S(2)}, u32[]{:S(2)}) collective-permute-start(s32[16,256]{1,0:T(8,128)S(1)} %reshape.50.refs_0_), channel_id=1, source_target_pairs={{0,16},{16,0},{1,17},{17,1},{2,18},{18,2},{3,19},{19,3},{4,20},{20... | collective-permute-start | bytes 49160 | tf_op jit(solution)/shard_map/ppermute | solution.py:75
  25.2 4.3 %collective-permute-start.5 = (s32[1,256]{1,0:T(1,128)S(1)}, s32[1,256]{1,0:T(1,128)S(1)}, u32[]{:S(2)}, u32[]{:S(2)}) collective-permute-start(s32[1,256]{1,0:T(1,128)S(1)} %copy-done.14), channel_id=1, source_target_pairs={{0,0},{1,16},{2,2},{3,18},{4,4},{5,20},{6,6},{7,22},{8,8},{9,24},{... | collective-permute-start | bytes 3080 | tf_op jit(solution)/shard_map/ppermute | solution.py:1173
  42.8 36.8 %copy-start = (bf16[8,192,256]{2,1,0:T(8,128)(2,1)}, bf16[8,192,256]{2,1,0:T(8,128)(2,1)S(1)}, u32[]{:S(2)}) copy-start(bf16[8,192,256]{2,1,0:T(8,128)(2,1)S(1)} %all-to-all-done.refs_2_.refs_0_.refs_1_) | copy-start | bytes 2359300
  42.9 3.0 %collective-permute-start.6 = (bf16[8,192,256]{2,1,0:T(8,128)(2,1)S(1)}, bf16[8,192,256]{2,1,0:T(8,128)(2,1)S(1)}, u32[]{:S(2)}, u32[]{:S(2)}) collective-permute-start(bf16[8,192,256]{2,1,0:T(8,128)(2,1)S(1)} %all-to-all-done.refs_2_.refs_0_.refs_1_), channel_id=1, source_target_pairs={{0,16},{16,0},{1,17},{17,1},{2,18},{18,2},{3,19},{19,3},{4,20},{20... | collective-permute-start | bytes 2359304 | tf_op jit(solution)/shard_map/ppermute | solution.py:75
  43.6 26.0 %collective-permute-start.10 = (bf16[256,2048]{1,0:T(8,128)(2,1)}, bf16[256,2048]{1,0:T(8,128)(2,1)}, u32[]{:S(2)}, u32[]{:S(2)}) collective-permute-start(bf16[256,2048]{1,0:T(8,128)(2,1)} %refs_7_.1), channel_id=1, source_target_pairs={{0,16},{16,0},{1,17},{17,1},{2,18},{18,2},{3,19},{19,3},{4,20},{20... | collective-permute-start | bytes 3145736 | tf_op jit(solution)/shard_map/ppermute | solution.py:75
  43.7 25.9 %collective-permute-start.11 = (bf16[1024,512]{1,0:T(8,128)(2,1)}, bf16[1024,512]{1,0:T(8,128)(2,1)}, u32[]{:S(2)}, u32[]{:S(2)}) collective-permute-start(bf16[1024,512]{1,0:T(8,128)(2,1)} %refs_9_.1), channel_id=1, source_target_pairs={{0,16},{16,0},{1,17},{17,1},{2,18},{18,2},{3,19},{19,3},{4,20},{20... | collective-permute-start | bytes 3145736 | tf_op jit(solution)/shard_map/ppermute | solution.py:75
  44.1 9.3 %collective-permute-start.7 = (bf16[512,512]{1,0:T(8,128)(2,1)S(1)}, bf16[512,512]{1,0:T(8,128)(2,1)S(1)}, u32[]{:S(2)}, u32[]{:S(2)}) collective-permute-start(bf16[512,512]{1,0:T(8,128)(2,1)S(1)} %pad_maximum_fusion), channel_id=1, source_target_pairs={{0,0},{1,16},{2,2},{3,18},{4,4},{5,20},{6,6},{7,22},{8,8},{9,24},{... | collective-permute-start | bytes 1572872 | tf_op jit(solution)/shard_map/ppermute | solution.py:1173
  45.8 33.8 %copy-start.1 = (bf16[8,192,256]{2,1,0:T(8,128)(2,1)}, bf16[8,192,256]{2,1,0:T(8,128)(2,1)S(1)}, u32[]{:S(2)}) copy-start(bf16[8,192,256]{2,1,0:T(8,128)(2,1)S(1)} %collective-permute-done.6.refs_3_.refs_1_) | copy-start | bytes 2359300
  53.4 16.2 %all-to-all-start.1 = ((bf16[8,64,256]{2,1,0:T(8,128)(2,1)}), bf16[8,64,256]{2,1,0:T(8,128)(2,1)S(1)}, u32[]{:S(2)}, u32[]{:S(2)}) async-start(bf16[8,64,256]{2,1,0:T(8,128)(2,1)} %get-tuple-element.90), calls=%async_computation.1 | async-start | bytes 524288 | tf_op jit(solution)/shard_map/all_to_all | solution.py:1181
  57.1 3.0 %collective-permute-start.8 = (bf16[256,512]{1,0:T(8,128)(2,1)S(1)}, bf16[256,512]{1,0:T(8,128)(2,1)S(1)}, u32[]{:S(2)}, u32[]{:S(2)}) collective-permute-start(bf16[256,512]{1,0:T(8,128)(2,1)S(1)} %copy-done.9), channel_id=1, source_target_pairs={{0,16},{16,0},{1,17},{17,1},{2,18},{18,2},{3,19},{19,3},{4,20},{20... | collective-permute-start | bytes 786440 | tf_op jit(solution)/shard_map/ppermute | solution.py:75
  59.0 10.6 %collective-permute-start.9 = (bf16[3,256]{1,0:T(4,128)(2,1)S(1)}, bf16[3,256]{1,0:T(4,128)(2,1)S(1)}, u32[]{:S(2)}, u32[]{:S(2)}) collective-permute-start(bf16[3,256]{1,0:T(4,128)(2,1)S(1)} %pad_maximum_fusion.1.refs_2_), channel_id=1, source_target_pairs={{0,16},{16,0},{1,17},{17,1},{2,18},{18,2},{3,19},{19,3},{4,20},{20... | collective-permute-start | bytes 4616 | tf_op jit(solution)/shard_map/ppermute | solution.py:75
  79.6 5.4 %collective-permute-start.12 = (bf16[16,144,512]{2,1,0:T(8,128)(2,1)}, bf16[16,144,512]{2,1,0:T(8,128)(2,1)}, u32[]{:S(2)}, u32[]{:S(2)}) collective-permute-start(bf16[16,144,512]{2,1,0:T(8,128)(2,1)} %get-tuple-element.100), channel_id=1, source_target_pairs={{0,16},{16,0},{1,17},{17,1},{2,18},{18,2},{3,19},{19,3},{4,20},{20... | collective-permute-start | bytes 7077896 | tf_op jit(solution)/shard_map/ppermute | solution.py:75
  80.6 12.8 %all-to-all-start.2 = ((bf16[8,64,256]{2,1,0:T(8,128)(2,1)}), bf16[8,64,256]{2,1,0:T(8,128)(2,1)S(1)}, u32[]{:S(2)}, u32[]{:S(2)}) async-start(bf16[8,64,256]{2,1,0:T(8,128)(2,1)} %bitcast.5), calls=%async_computation.2 | async-start | bytes 524288 | tf_op jit(solution)/shard_map/all_to_all | solution.py:1181
  84.0 42.4 %reduce-scatter.3.cloned.1.call-start = ((), (), s32[]{:S(2)}) async-start(), calls=%async_computation.7 | async-start | bytes 2621440 | tf_op jit(solution)/shard_map/reduce_scatter | solution.py:1239
  100.7 6.3 %collective-permute-start.13 = (bf16[8,128,256]{2,1,0:T(8,128)(2,1)S(1)}, bf16[8,128,256]{2,1,0:T(8,128)(2,1)S(1)}, u32[]{:S(2)}, u32[]{:S(2)}) collective-permute-start(bf16[8,128,256]{2,1,0:T(8,128)(2,1)S(1)} %get-tuple-element.116), channel_id=1, source_target_pairs={{0,16},{16,0},{1,17},{17,1},{2,18},{18,2},{3,19},{19,3},{4,20},{20... | collective-permute-start | bytes 1572872 | tf_op jit(solution)/shard_map/ppermute | solution.py:75
  108.1 24.4 %all-to-all-start.4 = ((bf16[8,192,256]{2,1,0:T(8,128)(2,1)}), bf16[8,192,256]{2,1,0:T(8,128)(2,1)S(1)}, u32[]{:S(2)}, u32[]{:S(2)}) async-start(bf16[8,192,256]{2,1,0:T(8,128)(2,1)} %pack.1.back_ref), calls=%async_computation.5 | async-start | bytes 1572864 | tf_op jit(solution)/shard_map/all_to_all | solution.py:1181
  111.7 40.4 %reduce-scatter.5.cloned.1.call-start = ((), (), s32[]{:S(2)}) async-start(), calls=%async_computation.8 | async-start | bytes 655360 | tf_op jit(solution)/shard_map/reduce_scatter | solution.py:1261
  115.2 2.9 %collective-permute-start.14 = (bf16[16,16,256]{2,1,0:T(8,128)(2,1)S(1)}, bf16[16,16,256]{2,1,0:T(8,128)(2,1)S(1)}, u32[]{:S(2)}, u32[]{:S(2)}) collective-permute-start(bf16[16,16,256]{2,1,0:T(8,128)(2,1)S(1)} %get-tuple-element.120), channel_id=1, source_target_pairs={{0,16},{16,0},{1,17},{17,1},{2,18},{18,2},{3,19},{19,3},{4,20},{20... | collective-permute-start | bytes 393224 | tf_op jit(solution)/shard_map/ppermute | solution.py:75
  118.3 7.4 %collective-permute-start.15 = (bf16[8,48,256]{2,1,0:T(8,128)(2,1)S(1)}, bf16[8,48,256]{2,1,0:T(8,128)(2,1)S(1)}, u32[]{:S(2)}, u32[]{:S(2)}) collective-permute-start(bf16[8,48,256]{2,1,0:T(8,128)(2,1)S(1)} %get-tuple-element.123), channel_id=1, source_target_pairs={{0,1},{1,0},{2,3},{3,2},{4,5},{5,4},{6,7},{7,6},{8,9},{9,8},{10,11... | collective-permute-start | bytes 589832 | tf_op jit(solution)/shard_map/ppermute | solution.py:75
  132.5 17.6 %all-to-all-start.3 = ((bf16[8,48,256]{2,1,0:T(8,128)(2,1)}), bf16[8,48,256]{2,1,0:T(8,128)(2,1)S(1)}, u32[]{:S(2)}, u32[]{:S(2)}) async-start(bf16[8,48,256]{2,1,0:T(8,128)(2,1)} %merge.1), calls=%async_computation.4 | async-start | bytes 393216 | tf_op jit(solution)/shard_map/all_to_all | solution.py:1181
  136.9 14.2 %collective-permute-start.17 = (bf16[512,512]{1,0:T(8,128)(2,1)S(1)}, bf16[512,512]{1,0:T(8,128)(2,1)S(1)}, u32[]{:S(2)}, u32[]{:S(2)}) collective-permute-start(bf16[512,512]{1,0:T(8,128)(2,1)S(1)} %copy-done.13), channel_id=1, source_target_pairs={{0,0},{1,16},{2,2},{3,18},{4,4},{5,20},{6,6},{7,22},{8,8},{9,24},{... | collective-permute-start | bytes 1572872 | tf_op jit(solution)/shard_map/ppermute | solution.py:1173
  139.7 11.3 %collective-permute-start.16 = (bf16[256,512]{1,0:T(8,128)(2,1)S(1)}, bf16[256,512]{1,0:T(8,128)(2,1)S(1)}, u32[]{:S(2)}, u32[]{:S(2)}) collective-permute-start(bf16[256,512]{1,0:T(8,128)(2,1)S(1)} %last.1), channel_id=1, source_target_pairs={{0,0},{1,16},{2,2},{3,18},{4,4},{5,20},{6,6},{7,22},{8,8},{9,24},{... | collective-permute-start | bytes 786440 | tf_op jit(solution)/shard_map/ppermute | solution.py:1173
  (12 other events, 160.6 us)
Sparse Core Ops, SparseCore 0:
  43.0 36.5 all-gather.2
  93.5 31.2 reduce-scatter.2
  127.2 24.4 reduce-scatter.4
